TPU v7x, 32 devices: a whole 2x2x4 slice. The times are simulated.
32 devices in a mesh: row: 8 (over y, x, core), col: 4 (over z).
Axes of the slice: x: 2, y: 2, z: 4, core: 2. Of those that a mesh axis runs over, the one named last changes fastest.
Arguments:
- rhs: float32 [4, 2048, 1024], P(None, 'row', 'col'), may hold values from -6 to 6
- l_panel: bfloat16 [4, 2048, 16384], P(None, 'row', 'col'), may hold values from -0.046875 to 0.046875
- x_solved: bfloat16 [16384, 1024], P('col'), may hold values from -6 to 6
- diag_inv: bfloat16 [4, 2048, 2048], P(None, 'row'), may hold values from -1 to 1.5, as said below
- l_inner: bfloat16 [6, 2048, 2048], P(None, 'row'), may hold values from -0.0625 to 0.0625
Outputs:
- x_window: float32 [4, 2048, 1024], P(None, 'row', 'col')
Inputs may be any that keep to these rules, and one draw needn't show every extreme that they name: `diag_inv`: each block is lower triangular with diagonal entries between one half and three halves.
All inputs are finite; a program needn't handle non-finite values.
Results may differ from a plain program's by a relative error of at most 0.0045.
Values may be sent and summed in bfloat16 or wider, within the bound.
No kernel may reach another device: no remote copies, remote signals or barrier semaphores. Data moves between devices by JAX's collectives and lax.ppermute only.
A program may use at most 64 MiB of HBM per device.

v0:
```python
import jax
import jax.numpy as jnp
from jax import lax
from jax.sharding import PartitionSpec as P


def inner_index(target, earlier):
    return target * (target - 1) // 2 + earlier


def local(rhs, l_panel, x_solved, diag_inv, l_inner):
    step_count, local_rows, solved_count = l_panel.shape
    local_width = rhs.shape[2]
    reduced = []
    products = jnp.dot(
        l_panel.reshape(step_count * local_rows, solved_count),
        x_solved,
        preferred_element_type=jnp.float32,
    )
    products = products.reshape(step_count, local_rows, x_solved.shape[1])
    shares = lax.psum_scatter(products, "col", scatter_dimension=2, tiled=True)
    for target in range(step_count):
        reduced.append(rhs[target] - shares[target])
    empty = jnp.zeros((local_rows, local_width), jnp.float32)
    results = []
    pending = list(reduced)
    for target in range(step_count):
        resid = pending[target]
        resid_low = resid.astype(jnp.bfloat16)
        apply_columns = diag_inv[target]
        current = jnp.dot(
            apply_columns,
            lax.all_gather(resid_low, "row", axis=0, tiled=True),
            preferred_element_type=jnp.float32,
        )
        results.append(current)
        if target + 1 < step_count:
            current_low = current.astype(jnp.bfloat16)
            later = tuple(range(target + 1, step_count))

            def subtract_later(carried, segment, offset, target=target, later=later):
                updated = []
                for position, follower in enumerate(later):
                    columns = l_inner[inner_index(follower, target)]
                    updated.append(jnp.dot(columns, segment, preferred_element_type=jnp.float32))
                return tuple(updated)

            updates = subtract_later(
                tuple((empty for follower in later)),
                lax.all_gather(current_low, "row", axis=0, tiled=True),
                jnp.int32(0),
            )
            for position, follower in enumerate(later):
                pending[follower] = pending[follower] - updates[position]
    return jnp.stack(results, axis=0)


def solution(mesh):
    in_specs = (
        P(None, "row", "col"),
        P(None, "row", "col"),
        P("col", None),
        P(None, "row", None),
        P(None, "row", None),
    )
    out_specs = P(None, "row", "col")
    return jax.shard_map(local, mesh=mesh, in_specs=in_specs, out_specs=out_specs, check_vma=False)
```

profile of v0, /device:TPU:0, one launch (start us, length us, event | category | flops | bytes accessed | tf_op | source)
XLA Modules:
  0.0 295.9 jit_solution(694731258520664546)
XLA Ops:
  6.5 0.0 copy-start
  6.5 0.0 reduce-scatter.2.cloned.1.call-start
  6.5 15.1 %fusion = f32[4,256,1024]{2,1,0:T(8,128)} fusion(bf16[4,256,4096]{2,1,0:T(8,128)(2,1)} %param.6, bf16[4096,1024]{1,0:T(8,128)(2,1)} %param.7), kind=kOutput, calls=%fused_computation | convolution fusion | flops 8589934592 | bytes 20971520 | tf_op jit(solution)/shard_map/dot_general | solution.py:15
  21.6 0.0 reduce-scatter.2.cloned.1.call-update
  21.6 0.0 all-gather.21.cloned.1.call-start
  21.7 79.6 %reduce-scatter.2.cloned.1.call-done = f32[4,256,256]{2,1,0:T(8,128)} async-done(((f32[4,256,1024]{2,1,0:T(8,128)}), f32[4,256,256]{2,1,0:T(8,128)}) %reduce-scatter.2.cloned.1.call-update) | async-done | bytes 1048592 | tf_op jit(solution)/shard_map/reduce_scatter | solution.py:21
  101.2 0.0 copy-done
  101.2 0.0 copy-start.1
  101.2 1.7 fusion.38
  103.0 0.0 all-gather.21.cloned.1.call-update
  103.0 0.0 all-gather.9.cloned.1.call-start
  103.0 24.3 %all-gather.21.cloned.1.call-done = bf16[1,2048,256]{2,1,0:T(8,128)(2,1)} async-done(((bf16[1,256,256]{2,1,0:T(8,128)(2,1)}), bf16[1,2048,256]{2,1,0:T(8,128)(2,1)}) %all-gather.21.cloned.1.call-update) | async-done | bytes 1048592 | tf_op jit(solution)/shard_map/all_gather | solution.py:33
  127.3 2.7 bitcast_convert_fusion.2
  130.0 0.0 all-gather.9.cloned.1.call-update
  130.0 0.0 all-gather.11.cloned.1.call-start
  130.1 23.7 %all-gather.9.cloned.1.call-done = bf16[2048,256]{0,1:T(8,128)(2,1)} async-done(((bf16[256,256]{0,1:T(8,128)(2,1)}), bf16[2048,256]{0,1:T(8,128)(2,1)}) %all-gather.9.cloned.1.call-update) | async-done | bytes 1048592 | tf_op jit(solution)/shard_map/all_gather | solution.py:50
  153.8 2.7 fusion.8
  156.5 0.0 all-gather.11.cloned.1.call-update
  156.5 0.0 all-gather.13.cloned.1.call-start
  156.5 23.6 %all-gather.11.cloned.1.call-done = bf16[2048,256]{1,0:T(8,128)(2,1)} async-done(((bf16[256,256]{1,0:T(8,128)(2,1)}), bf16[2048,256]{1,0:T(8,128)(2,1)}) %all-gather.11.cloned.1.call-update) | async-done | bytes 1048592 | tf_op jit(solution)/shard_map/all_gather | solution.py:33
  180.1 2.7 bitcast_convert_fusion.1
  182.8 0.0 all-gather.13.cloned.1.call-update
  182.8 0.0 all-gather.15.cloned.1.call-start
  182.9 0.0 copy-done.1
  182.9 2.0 fusion.6
  184.9 21.6 %all-gather.13.cloned.1.call-done = bf16[2048,256]{0,1:T(8,128)(2,1)} async-done(((bf16[256,256]{0,1:T(8,128)(2,1)}), bf16[2048,256]{0,1:T(8,128)(2,1)}) %all-gather.13.cloned.1.call-update) | async-done | bytes 1048592 | tf_op jit(solution)/shard_map/all_gather | solution.py:50
  206.6 2.7 fusion.9
  209.2 0.0 all-gather.15.cloned.1.call-update
  209.3 0.0 all-gather.17.cloned.1.call-start
  209.3 23.6 %all-gather.15.cloned.1.call-done = bf16[2048,256]{1,0:T(8,128)(2,1)} async-done(((bf16[256,256]{1,0:T(8,128)(2,1)}), bf16[2048,256]{1,0:T(8,128)(2,1)}) %all-gather.15.cloned.1.call-update) | async-done | bytes 1048592 | tf_op jit(solution)/shard_map/all_gather | solution.py:33
  232.9 2.7 bitcast_convert_fusion
  235.6 0.0 all-gather.17.cloned.1.call-update
  235.6 0.0 all-gather.19.cloned.1.call-start
  235.7 2.0 fusion.4
  237.7 2.0 fusion.3
  239.7 19.6 %all-gather.17.cloned.1.call-done = bf16[2048,256]{0,1:T(8,128)(2,1)} async-done(((bf16[256,256]{0,1:T(8,128)(2,1)}), bf16[2048,256]{0,1:T(8,128)(2,1)}) %all-gather.17.cloned.1.call-update) | async-done | bytes 1048592 | tf_op jit(solution)/shard_map/all_gather | solution.py:50
  259.3 2.7 fusion.10
  262.0 0.0 all-gather.19.cloned.1.call-update
  262.0 23.6 %all-gather.19.cloned.1.call-done = bf16[2048,256]{1,0:T(8,128)(2,1)} async-done(((bf16[256,256]{1,0:T(8,128)(2,1)}), bf16[2048,256]{1,0:T(8,128)(2,1)}) %all-gather.19.cloned.1.call-update) | async-done | bytes 1048592 | tf_op jit(solution)/shard_map/all_gather | solution.py:33
  285.7 2.0 convolution_bitcast_fusion
  287.7 0.1 pad_maximum_fusion
  287.8 1.3 copy.6
Async XLA Ops:
  6.5 94.7 %copy-start = (f32[4,256,256]{2,1,0:T(8,128)S(1)}, f32[4,256,256]{2,1,0:T(8,128)}, u32[]{:S(2)}) copy-start(f32[4,256,256]{2,1,0:T(8,128)} %param.5) | copy-start | bytes 3145732
  6.5 94.7 %reduce-scatter.2.cloned.1.call-start = ((), (), s32[]{:S(2)}) async-start(), calls=%async_computation.1 | async-start | bytes 5242880 | tf_op jit(solution)/shard_map/reduce_scatter | solution.py:21
  21.6 105.7 %all-gather.21.cloned.1.call-start = ((), (), s32[]{:S(2)}) async-start(), calls=%async_computation.8 | async-start | bytes 1179648 | tf_op jit(solution)/shard_map/all_gather | solution.py:33
  101.2 81.6 %copy-start.1 = (f32[4,256,256]{2,1,0:T(8,128)S(1)}, f32[4,256,256]{2,1,0:T(8,128)}, u32[]{:S(2)}) copy-start(f32[4,256,256]{2,1,0:T(8,128)} %reduce-scatter.2.cloned.1.call-done) | copy-start | bytes 3145732
  103.0 50.8 %all-gather.9.cloned.1.call-start = ((), (), s32[]{:S(2)}) async-start(), calls=%async_computation.2 | async-start | bytes 1179648 | tf_op jit(solution)/shard_map/all_gather | solution.py:50
  130.0 50.1 %all-gather.11.cloned.1.call-start = ((), (), s32[]{:S(2)}) async-start(), calls=%async_computation.3 | async-start | bytes 1179648 | tf_op jit(solution)/shard_map/all_gather | solution.py:33
  156.5 50.1 %all-gather.13.cloned.1.call-start = ((), (), s32[]{:S(2)}) async-start(), calls=%async_computation.4 | async-start | bytes 1179648 | tf_op jit(solution)/shard_map/all_gather | solution.py:50
  182.8 50.1 %all-gather.15.cloned.1.call-start = ((), (), s32[]{:S(2)}) async-start(), calls=%async_computation.5 | async-start | bytes 1179648 | tf_op jit(solution)/shard_map/all_gather | solution.py:33
  209.3 50.1 %all-gather.17.cloned.1.call-start = ((), (), s32[]{:S(2)}) async-start(), calls=%async_computation.6 | async-start | bytes 1179648 | tf_op jit(solution)/shard_map/all_gather | solution.py:50
  235.6 50.1 %all-gather.19.cloned.1.call-start = ((), (), s32[]{:S(2)}) async-start(), calls=%async_computation.7 | async-start | bytes 1179648 | tf_op jit(solution)/shard_map/all_gather | solution.py:33
Sparse Core Ops, SparseCore 0:
  21.8 79.4 reduce-scatter.1
  103.3 23.9 all-gather.20
  130.2 23.5 all-gather.8
  156.6 23.4 all-gather.10
  183.0 23.5 all-gather.12
  209.4 23.4 all-gather.14
  235.7 23.5 all-gather.16
  262.1 23.4 all-gather.18
where the time goes:
time: 296 us
  waiting for transfers between devices  240 us (81%)
  matrix products  39.2 us (13%)
  between operations  13.5 us (5%)
    all_gather x4, waiting for transfers between devices, local(): lax.all_gather(resid_low, 'row', axis=0, tiled=True)  95.1 us
    reduce_scatter x1, waiting for transfers between devices, local(): shares = lax.psum_scatter(products, 'col', scatter_dimension=2, tiled=True)  79.6 us
    all_gather x3, waiting for transfers between devices, local(): lax.all_gather(current_low, 'row', axis=0, tiled=True)  64.9 us
    dot_general x1, matrix products, local(): jnp.dot(l_panel.reshape(step_count * local_rows, solved_count), x_solved,...  15.1 us
    dot_general x6, matrix products, subtract_later(): jnp.dot(columns, segment, preferred_element_type=jnp.float32)  14.1 us
    dot_general x4, matrix products, local(): jnp.dot(apply_columns, lax.all_gather(resid_low, 'row', axis=0, tiled=Tru...  10.1 us
  transfers between devices with their start and end apart: 8, of which 8 were waited for; matrix products, arithmetic and copies ran while one was open for 2% of the time, Pallas kernels for 0%

commit v1 on v0

v1 whole, which is shorter than its diff:
```python
import functools

import jax
import jax.numpy as jnp
from jax import lax
from jax.experimental import pallas as pl
from jax.experimental.pallas import tpu as pltpu
from jax.sharding import PartitionSpec as P

F32, BF16 = jnp.float32, jnp.bfloat16


def inner_index(target, earlier):
    return target * (target - 1) // 2 + earlier


def product_kernel(l_ref, x_ref, out_ref):
    out_ref[...] = jnp.dot(l_ref[...], x_ref[...], preferred_element_type=F32)


def panel_product(l_block, x_solved, width):
    rows, depth = l_block.shape
    total = x_solved.shape[1]
    return pl.pallas_call(
        product_kernel,
        grid=(total // width,),
        in_specs=[
            pl.BlockSpec((rows, depth), lambda i: (0, 0)),
            pl.BlockSpec((depth, width), lambda i: (0, i)),
        ],
        out_specs=pl.BlockSpec((rows, width), lambda i: (0, i)),
        out_shape=jax.ShapeDtypeStruct((rows, total), F32),
        compiler_params=pltpu.CompilerParams(vmem_limit_bytes=40 << 20),
        cost_estimate=pl.CostEstimate(
            flops=2 * rows * depth * total,
            bytes_accessed=2 * (rows + total) * depth + 4 * rows * total,
            transcendentals=0,
        ),
    )(l_block, x_solved)


def apply_kernel(parts, subtract, low, place_ref, *refs):
    own_ref, other_ref = refs[0], refs[1]
    shards = refs[2 : 2 + parts]
    pending_ref = refs[2 + parts] if subtract else None
    outs = refs[2 + parts + (1 if subtract else 0) :]
    rows, high = own_ref.shape[0], 2 * own_ref.shape[0]
    for ref, offset in ((own_ref, place_ref[0]), (other_ref, place_ref[1])):
        there = pl.ds(pl.multiple_of(offset, rows), rows)
        total = jnp.zeros((rows, shards[0].shape[1]), F32)
        entry = 0
        for shard in shards:
            for piece in range(shard.shape[0] // high):
                begin = pl.multiple_of(place_ref[2 + entry], high)
                total += jnp.dot(
                    ref[:, pl.ds(begin, high)],
                    shard[piece * high : (piece + 1) * high, :],
                    preferred_element_type=F32,
                )
                entry += 1
        if subtract:
            total = pending_ref[there, :] - total
        outs[0][there, :] = total
        if low:
            outs[1][there, :] = total.astype(BF16)


def apply_rows(place, own, other, shards, pending, low):
    high, width = shards[0].shape
    flops = 4 * own.shape[0] * own.shape[1] * width
    shapes = [jax.ShapeDtypeStruct((high, width), F32)]
    if low:
        shapes.append(jax.ShapeDtypeStruct((high, width), BF16))
    operands = [own, other, *shards] + ([] if pending is None else [pending])
    return pl.pallas_call(
        functools.partial(apply_kernel, len(shards), pending is not None, low),
        in_specs=[pl.BlockSpec(memory_space=pltpu.SMEM)]
        + [pl.BlockSpec(memory_space=pltpu.VMEM)] * len(operands),
        out_specs=[pl.BlockSpec(memory_space=pltpu.VMEM)] * len(shapes),
        out_shape=shapes,
        compiler_params=pltpu.CompilerParams(vmem_limit_bytes=16 << 20),
        cost_estimate=pl.CostEstimate(
            flops=flops, bytes_accessed=4 * own.size + 4 * high * width, transcendentals=0
        ),
    )(place, *operands)


def local(rhs, l_panel, x_solved, diag_inv, l_inner, row_count, col_count):
    steps, rows, _ = l_panel.shape
    width = rhs.shape[2]
    half = width // 2
    high = 2 * rows
    me, place_col = lax.axis_index("row"), lax.axis_index("col")
    core, chip = me % 2, me // 2
    bits = [1 << k for k in range((row_count // 2 - 1).bit_length())]
    orders = (bits, bits[::-1])

    def masks(order):
        found = [0]
        for bit in order:
            found += [mask ^ bit for mask in found]
        return found

    first, second = (jnp.array(masks(order), jnp.int32) for order in orders)
    shard_chip = chip ^ jnp.where(core == 0, first, second)
    place = jnp.concatenate(
        [jnp.stack([core * rows, (1 - core) * rows]), shard_chip * high]
    ).astype(jnp.int32)

    def swap(value):
        return lax.ppermute(value, "row", [(i, i ^ 1) for i in range(row_count)])

    def gather(value):
        shards = [value]
        for stage in range(len(bits)):
            pairs = [(i, i ^ (2 * orders[i % 2][stage])) for i in range(row_count)]
            send = shards[0] if stage == 0 else jnp.concatenate(shards, axis=0)
            shards.append(lax.ppermute(send, "row", pairs))
        return shards

    def chunk(block, index):
        return lax.dynamic_slice_in_dim(block, jnp.clip(index, 0, col_count - 1) * width, width, 1)

    def reduce_block(block):
        up = down = None
        for step in range(col_count - 1):
            high_chunk = chunk(block, place_col + col_count - 1 - step)
            low_chunk = chunk(block, place_col - col_count + 1 + step)
            if step:
                high_chunk += up.astype(F32)
                low_chunk += down.astype(F32)
            pairs = [(i, i + 1) for i in range(step + 1)]
            up = lax.ppermute(high_chunk.astype(BF16), "col", pairs)
            last = col_count - 1
            down = lax.ppermute(
                low_chunk.astype(BF16), "col", [(last - i, last - j) for i, j in pairs]
            )
        return up.astype(F32) + down.astype(F32) + chunk(block, place_col)

    def to_halves(value):
        mine = lax.dynamic_slice_in_dim(value, core * half, half, 1)
        other = swap(lax.dynamic_slice_in_dim(value, (1 - core) * half, half, 1))
        return jnp.where(
            core == 0,
            jnp.concatenate([mine, other], axis=0),
            jnp.concatenate([other, mine], axis=0),
        )

    def from_halves(value):
        mine = lax.dynamic_slice_in_dim(value, core * rows, rows, 0)
        other = swap(lax.dynamic_slice_in_dim(value, (1 - core) * rows, rows, 0))
        return jnp.where(
            core == 0,
            jnp.concatenate([mine, other], axis=1),
            jnp.concatenate([other, mine], axis=1),
        )

    pending = []
    for target in range(steps):
        block = panel_product(l_panel[target], x_solved, width)
        pending.append(to_halves(rhs[target] - reduce_block(block)))
    diag_other = [swap(diag_inv[target]) for target in range(steps)]
    inner_other = {}
    for earlier in range(steps):
        for target in range(earlier + 1, steps):
            index = inner_index(target, earlier)
            inner_other[index] = swap(l_inner[index])
    results = []
    resid_low = pending[0].astype(BF16)
    for target in range(steps):
        last = target + 1 == steps
        current = apply_rows(
            place, diag_inv[target], diag_other[target], gather(resid_low), None, not last
        )
        results.append(from_halves(current[0]))
        if last:
            break
        shards = gather(current[1])
        for follower in range(target + 1, steps):
            index = inner_index(follower, target)
            updated = apply_rows(
                place, l_inner[index], inner_other[index], shards, pending[follower], follower == target + 1
            )
            pending[follower] = updated[0]
            if follower == target + 1:
                resid_low = updated[1]
    return jnp.stack(results, axis=0)


def solution(mesh):
    in_specs = (
        P(None, "row", "col"),
        P(None, "row", "col"),
        P("col", None),
        P(None, "row", None),
        P(None, "row", None),
    )
    out_specs = P(None, "row", "col")
    body = functools.partial(
        local, row_count=mesh.shape["row"], col_count=mesh.shape["col"]
    )
    return jax.shard_map(body, mesh=mesh, in_specs=in_specs, out_specs=out_specs, check_vma=False)
```

time: 296 us -> 224 us (0.76)
  waiting for transfers between devices: 240 us -> 70.8 us
  starting transfers between devices: 0.3 us -> 86.5 us
  matrix products: 39.2 us -> 0 us
  Pallas kernels: 0 us -> 31.6 us
  local copies, waits for them, and re-layouts: 1.32 us -> 29.9 us
  between operations: 13.5 us -> 0.95 us
    all_gather x7 -> x0, waiting for transfers between devices: 160 us -> none  [the longest x4 95.1 us: local(): lax.all_gather(resid_low, 'row', axis=0, tiled=True)]
    ppermute x0 -> x56, starting transfers between devices: none -> 86.5 us  [the longest x12 53.6 us: reduce_block(): up = lax.ppermute(high_chunk.astype(BF16), 'col', pairs)]
    reduce_scatter x1 -> x0, waiting for transfers between devices: 79.6 us -> none  [local(): shares = lax.psum_scatter(products, 'col', scatter_dimension=2, tiled=True)]
    ppermute x0 -> x56, waiting for transfers between devices: none -> 70.8 us  [the longest x14 52.2 us: gather(): shards.append(lax.ppermute(send, 'row', pairs))]
    dot_general x11 -> x0, matrix products: 39.2 us -> none  [the longest x1 15.1 us: local(): jnp.dot(l_panel.reshape(step_count * local_rows, solved_count), x_solved,...]
    pallas_call x0 -> x14, Pallas kernels: none -> 31.6 us  [the longest x4 16.1 us: panel_product(): pl.pallas_call(product_kernel, grid=(total // width,), in_specs=[pl.Block...]
    unnamed x4 -> x52, local copies, waits for them, and re-layouts: 0.01 us -> 15.5 us
    squeeze x0 -> x3, local copies, waits for them, and re-layouts: none -> 10.7 us  [the longest x1 5.68 us: local(): block = panel_product(l_panel[target], x_solved, width)]
  transfers between devices with their start and end apart: 8 -> 56, of which waited for: 8 -> 28; matrix products, arithmetic and copies ran while one was open for 2% -> 5% of each run, Pallas kernels for 0% -> 12%
where the time goes in v1:
time: 224 us; the launch traced here: 223 us
  starting transfers between devices  86.5 us (39%)
  waiting for transfers between devices  70.8 us (32%)
  Pallas kernels  31.6 us (14%)
  local copies, waits for them, and re-layouts  29.9 us (13%)
  other arithmetic  3.38 us (2%)
    ppermute x12, starting transfers between devices, reduce_block(): up = lax.ppermute(high_chunk.astype(BF16), 'col', pairs)  53.6 us
    ppermute x14, waiting for transfers between devices, gather(): shards.append(lax.ppermute(send, 'row', pairs))  52.2 us
    ppermute x14, starting transfers between devices, gather(): shards.append(lax.ppermute(send, 'row', pairs))  19.6 us
    pallas_call x4, Pallas kernels, panel_product(): pl.pallas_call(product_kernel, grid=(total // width,), in_specs=[pl.Block...  16.1 us
    pallas_call x10, Pallas kernels, apply_rows(): pl.pallas_call(functools.partial(apply_kernel, len(shards), pending is no...  15.5 us
    unnamed x52, local copies, waits for them, and re-layouts  15.5 us
    ppermute x12, starting transfers between devices, reduce_block(): lax.ppermute(low_chunk.astype(BF16), 'col', [(last - i, last - j) for i,...  10.6 us
    ppermute x12, waiting for transfers between devices, reduce_block(): up = lax.ppermute(high_chunk.astype(BF16), 'col', pairs)  10.6 us
  transfers between devices with their start and end apart: 56, of which 28 were waited for; matrix products, arithmetic and copies ran while one was open for 5% of the time, Pallas kernels for 12%

profile of v1, /device:TPU:0, one launch (start us, length us, event | category | flops | bytes accessed | tf_op | source)
XLA Modules:
  0.0 223.0 jit_solution(13670000893248982102)
XLA Ops:
  0.0 5.7 %slice_bitcast_fusion = (bf16[256,4096]{1,0:T(8,128)(2,1)S(1)}, bf16[256,4096]{1,0:T(8,128)(2,1)}, bf16[256,4096]{1,0:T(8,128)(2,1)}, bf16[256,4096]{1,0:T(8,128)(2,1)}) fusion(bf16[4,256,4096]{2,1,0:T(8,128)(2,1)} %param.8), kind=kLoop, calls=%fused_computation | loop fusion | bytes 16777216 | tf_op jit(solution)/shard_map/squeeze | solution.py:160
  5.7 3.4 %copy-done = bf16[4096,1024]{1,0:T(8,128)(2,1)S(1)} copy-done((bf16[4096,1024]{1,0:T(8,128)(2,1)S(1)}, bf16[4096,1024]{1,0:T(8,128)(2,1)}, u32[]{:S(2)}) %copy-start) | copy-done | bytes 8388632
  9.1 1.6 copy-done.5
  10.7 4.0 %shard_map.73 = f32[256,1024]{1,0:T(8,128)S(1)} custom-call(bf16[256,4096]{1,0:T(8,128)(2,1)S(1)} %copy-done.5, bf16[4096,1024]{1,0:T(8,128)(2,1)S(1)} %copy-done), custom_call_target="tpu_custom_call" | custom-call | flops 2147483648 | bytes 11534336 | tf_op jit(solution)/shard_map/pallas_call | solution.py:24
  15.5 4.9 %collective-permute-start.1 = (bf16[256,256]{1,0:T(8,128)(2,1)}, bf16[256,256]{1,0:T(8,128)(2,1)S(1)}, u32[]{:S(2)}, u32[]{:S(2)}) collective-permute-start(bf16[256,256]{1,0:T(8,128)(2,1)} %get-tuple-element.54), channel_id=1, source_target_pairs={{0,1},{4,5},{8,9},{12,13},{16,17},{20,21},{24,25},{28,29}} | collective-permute-start | bytes 393224 | tf_op jit(solution)/shard_map/ppermute | solution.py:133
  21.1 2.2 %slice_bitcast_fusion.13 = (bf16[256,2048]{1,0:T(8,128)(2,1)}, bf16[256,2048]{1,0:T(8,128)(2,1)}, bf16[256,2048]{1,0:T(8,128)(2,1)}, bf16[256,2048]{1,0:T(8,128)(2,1)}) fusion(bf16[4,256,2048]{2,1,0:T(8,128)(2,1)S(1)} %copy-done.21), kind=kLoop, calls=%fused_computation.14 | loop fusion | bytes 8388608 | tf_op jit(solution)/shard_map/squeeze | solution.py:173
  23.3 2.6 %copy-done.1 = bf16[4096,1024]{1,0:T(8,128)(2,1)S(1)} copy-done((bf16[4096,1024]{1,0:T(8,128)(2,1)S(1)}, bf16[4096,1024]{1,0:T(8,128)(2,1)}, u32[]{:S(2)}) %copy-start.1) | copy-done | bytes 8388632
  26.0 4.0 %shard_map.75 = f32[256,1024]{1,0:T(8,128)S(1)} custom-call(bf16[256,4096]{1,0:T(8,128)(2,1)S(1)} %copy-done.4, bf16[4096,1024]{1,0:T(8,128)(2,1)S(1)} %copy-done.1), custom_call_target="tpu_custom_call" | custom-call | flops 2147483648 | bytes 11534336 | tf_op jit(solution)/shard_map/pallas_call | solution.py:24
  31.7 1.9 collective-permute-start.15
  34.3 3.4 %copy-done.2 = bf16[4096,1024]{1,0:T(8,128)(2,1)S(1)} copy-done((bf16[4096,1024]{1,0:T(8,128)(2,1)S(1)}, bf16[4096,1024]{1,0:T(8,128)(2,1)}, u32[]{:S(2)}) %copy-start.2) | copy-done | bytes 8388632
  37.7 1.6 copy-done.3
  39.3 4.0 %shard_map.78 = f32[256,1024]{1,0:T(8,128)S(1)} custom-call(bf16[256,4096]{1,0:T(8,128)(2,1)S(1)} %copy-done.3, bf16[4096,1024]{1,0:T(8,128)(2,1)S(1)} %copy-done.2), custom_call_target="tpu_custom_call" | custom-call | flops 2147483648 | bytes 11534336 | tf_op jit(solution)/shard_map/pallas_call | solution.py:24
  44.3 4.0 %shard_map.82 = f32[256,1024]{1,0:T(8,128)S(1)} custom-call(bf16[256,4096]{1,0:T(8,128)(2,1)S(1)} %get-tuple-element.23.l_ref, bf16[4096,1024]{1,0:T(8,128)(2,1)S(1)} %copy-done.2), custom_call_target="tpu_custom_call" | custom-call | flops 2147483648 | bytes 11534336 | tf_op jit(solution)/shard_map/pallas_call | solution.py:24
  49.3 2.8 %slice_bitcast_fusion.4 = (bf16[256,2048]{1,0:T(8,128)(2,1)}, bf16[256,2048]{1,0:T(8,128)(2,1)}, bf16[256,2048]{1,0:T(8,128)(2,1)}, bf16[256,2048]{1,0:T(8,128)(...) fusion(bf16[6,256,2048]{2,1,0:T(8,128)(2,1)S(1)} %bitcast.51), kind=kLoop, calls=%fused_computation.5 | loop fusion | bytes 12582912 | tf_op jit(solution)/shard_map/squeeze | solution.py:182
  54.1 1.3 collective-permute-start.30
  57.1 1.3 collective-permute-done.30
  58.4 4.3 %collective-permute-start.46 = (bf16[256,256]{1,0:T(8,128)(2,1)S(1)}, bf16[256,256]{1,0:T(8,128)(2,1)S(1)}, u32[]{:S(2)}, u32[]{:S(2)}) collective-permute-start(bf16[256,256]{1,0:T(8,128)(2,1)S(1)} %get-tuple-element.42), channel_id=1, source_target_pairs={{0,1},{4,5},{8,9},{12,13},{16,17},{20,21},{24,25},{28,29}} | collective-permute-start | bytes 393224 | tf_op jit(solution)/shard_map/ppermute | solution.py:133
  62.8 2.4 %collective-permute-done.46 = bf16[256,256]{1,0:T(8,128)(2,1)S(1)} collective-permute-done((bf16[256,256]{1,0:T(8,128)(2,1)S(1)}, bf16[256,256]{1,0:T(8,128)(2,1)S(1)}, u32[]{:S(2)}, u32[]{:S(2)}) %collective-permute-start.46) | collective-permute-done | bytes 131104 | tf_op jit(solution)/shard_map/ppermute | solution.py:133
  65.2 4.3 %collective-permute-start.2 = (bf16[256,256]{1,0:T(8,128)(2,1)S(1)}, bf16[256,256]{1,0:T(8,128)(2,1)S(1)}, u32[]{:S(2)}, u32[]{:S(2)}) collective-permute-start(bf16[256,256]{1,0:T(8,128)(2,1)S(1)} %add_convert_fusion.15), channel_id=1, source_target_pairs={{0,1},{1,2},{4,5},{5,6},{8,9},{9,10},{12,13},{13,14},{16,17},{17,1... | collective-permute-start | bytes 393224 | tf_op jit(solution)/shard_map/ppermute | solution.py:133
  70.3 1.7 collective-permute-done.2
  72.1 4.3 %collective-permute-start.16 = (bf16[256,256]{1,0:T(8,128)(2,1)S(1)}, bf16[256,256]{1,0:T(8,128)(2,1)S(1)}, u32[]{:S(2)}, u32[]{:S(2)}) collective-permute-start(bf16[256,256]{1,0:T(8,128)(2,1)S(1)} %add_convert_fusion.11), channel_id=1, source_target_pairs={{0,1},{1,2},{4,5},{5,6},{8,9},{9,10},{12,13},{13,14},{16,17},{17,1... | collective-permute-start | bytes 393224 | tf_op jit(solution)/shard_map/ppermute | solution.py:133
  76.6 2.3 %collective-permute-done.16 = bf16[256,256]{1,0:T(8,128)(2,1)S(1)} collective-permute-done((bf16[256,256]{1,0:T(8,128)(2,1)S(1)}, bf16[256,256]{1,0:T(8,128)(2,1)S(1)}, u32[]{:S(2)}, u32[]{:S(2)}) %collective-permute-start.16) | collective-permute-done | bytes 131104 | tf_op jit(solution)/shard_map/ppermute | solution.py:133
  79.7 10.4 %collective-permute-start.31 = (bf16[256,256]{1,0:T(8,128)(2,1)S(1)}, bf16[256,256]{1,0:T(8,128)(2,1)S(1)}, u32[]{:S(2)}, u32[]{:S(2)}) collective-permute-start(bf16[256,256]{1,0:T(8,128)(2,1)S(1)} %add_convert_fusion.7), channel_id=1, source_target_pairs={{0,1},{1,2},{4,5},{5,6},{8,9},{9,10},{12,13},{13,14},{16,17},{17,1... | collective-permute-start | bytes 393224 | tf_op jit(solution)/shard_map/ppermute | solution.py:133
  90.2 1.9 collective-permute-start.3
  92.6 1.3 collective-permute-start.6
  94.0 1.4 collective-permute-done.3
  95.4 4.4 %collective-permute-start.47 = (bf16[256,256]{1,0:T(8,128)(2,1)S(1)}, bf16[256,256]{1,0:T(8,128)(2,1)S(1)}, u32[]{:S(2)}, u32[]{:S(2)}) collective-permute-start(bf16[256,256]{1,0:T(8,128)(2,1)S(1)} %add_convert_fusion.3), channel_id=1, source_target_pairs={{0,1},{1,2},{4,5},{5,6},{8,9},{9,10},{12,13},{13,14},{16,17},{17,1... | collective-permute-start | bytes 393224 | tf_op jit(solution)/shard_map/ppermute | solution.py:133
  104.3 1.6 collective-permute-start.8
  105.9 3.4 %collective-permute-done.8.refs_3_ = bf16[512,128]{1,0:T(8,128)(2,1)S(1)} collective-permute-done((bf16[512,128]{1,0:T(8,128)(2,1)S(1)}, bf16[512,128]{1,0:T(8,128)(2,1)S(1)}, u32[]{:S(2)}, u32[]{:S(2)}) %collective-permute-start.8) | collective-permute-done | bytes 131104 | tf_op jit(solution)/shard_map/ppermute | solution.py:118
  109.3 7.4 %collective-permute-start.17 = (bf16[256,256]{1,0:T(8,128)(2,1)S(1)}, bf16[256,256]{1,0:T(8,128)(2,1)S(1)}, u32[]{:S(2)}, u32[]{:S(2)}) collective-permute-start(bf16[256,256]{1,0:T(8,128)(2,1)S(1)} %get-tuple-element.48), channel_id=1, source_target_pairs={{0,1},{1,2},{2,3},{4,5},{5,6},{6,7},{8,9},{9,10},{10,11},{12,13},{... | collective-permute-start | bytes 393224 | tf_op jit(solution)/shard_map/ppermute | solution.py:133
  116.7 1.6 collective-permute-start.9
  118.4 4.4 %collective-permute-start.32 = (bf16[256,256]{1,0:T(8,128)(2,1)S(1)}, bf16[256,256]{1,0:T(8,128)(2,1)S(1)}, u32[]{:S(2)}, u32[]{:S(2)}) collective-permute-start(bf16[256,256]{1,0:T(8,128)(2,1)S(1)} %get-tuple-element.44), channel_id=1, source_target_pairs={{0,1},{1,2},{2,3},{4,5},{5,6},{6,7},{8,9},{9,10},{10,11},{12,13},{... | collective-permute-start | bytes 393224 | tf_op jit(solution)/shard_map/ppermute | solution.py:133
  122.9 3.9 %collective-permute-start.48 = (bf16[256,256]{1,0:T(8,128)(2,1)S(1)}, bf16[256,256]{1,0:T(8,128)(2,1)S(1)}, u32[]{:S(2)}, u32[]{:S(2)}) collective-permute-start(bf16[256,256]{1,0:T(8,128)(2,1)S(1)} %get-tuple-element.40), channel_id=1, source_target_pairs={{0,1},{1,2},{2,3},{4,5},{5,6},{6,7},{8,9},{9,10},{10,11},{12,13},{... | collective-permute-start | bytes 393224 | tf_op jit(solution)/shard_map/ppermute | solution.py:133
  126.8 1.3 collective-permute-start.20
  128.1 1.3 collective-permute-start.35
  129.4 1.5 collective-permute-start.51
  131.0 2.3 %shard_map.74 = (f32[512,128]{1,0:T(8,128)S(1)}, bf16[512,128]{1,0:T(8,128)(2,1)S(1)}) custom-call(s32[6]{0:T(128)S(1)} %pad_add_fusion.place_ref, bf16[256,2048]{1,0:T(8,128)(2,1)} %get-tuple-element.33.refs_0_, bf16[256,2048]{1,0:T(8,128)(2,1)} %collective-permute-done.refs_1_, bf16[512,128]{1,0:T(8,128)(2,1)S(1)} %fusion.refs_2_, ...), custom_call_target="tpu_custom_call" | custom-call | flops 268435456 | bytes 2359296 | tf_op jit(solution)/shard_map/pallas_call | solution.py:75
  133.3 1.5 collective-permute-done.20
  134.8 1.6 collective-permute-start.13
  136.7 1.4 collective-permute-done.51
  138.3 1.4 collective-permute-done.13.refs_3_
  142.1 4.1 %collective-permute-done.14.refs_4_ = bf16[1024,128]{1,0:T(8,128)(2,1)S(1)} collective-permute-done((bf16[1024,128]{1,0:T(8,128)(2,1)S(1)}, bf16[1024,128]{1,0:T(8,128)(2,1)S(1)}, u32[]{:S(2)}, u32[]{:S(2)}) %collective-permute-start.14) | collective-permute-done | bytes 262176 | tf_op jit(solution)/shard_map/ppermute | solution.py:118
  146.2 1.9 shard_map.76
  148.2 1.6 collective-permute-start.22
  149.8 3.8 %collective-permute-done.22.refs_3_ = bf16[512,128]{1,0:T(8,128)(2,1)S(1)} collective-permute-done((bf16[512,128]{1,0:T(8,128)(2,1)S(1)}, bf16[512,128]{1,0:T(8,128)(2,1)S(1)}, u32[]{:S(2)}, u32[]{:S(2)}) %collective-permute-start.22) | collective-permute-done | bytes 131104 | tf_op jit(solution)/shard_map/ppermute | solution.py:118
  154.5 5.8 %collective-permute-done.23.refs_4_ = bf16[1024,128]{1,0:T(8,128)(2,1)S(1)} collective-permute-done((bf16[1024,128]{1,0:T(8,128)(2,1)S(1)}, bf16[1024,128]{1,0:T(8,128)(2,1)S(1)}, u32[]{:S(2)}, u32[]{:S(2)}) %collective-permute-start.23) | collective-permute-done | bytes 262176 | tf_op jit(solution)/shard_map/ppermute | solution.py:118
  161.5 3.4 %collective-permute-start.27 = (bf16[512,128]{1,0:T(8,128)(2,1)S(1)}, bf16[512,128]{1,0:T(8,128)(2,1)S(1)}, u32[]{:S(2)}, u32[]{:S(2)}) collective-permute-start(bf16[512,128]{1,0:T(8,128)(2,1)S(1)} %get-tuple-element.18.refs_2_), channel_id=1, source_target_pairs={{0,8},{4,20},{8,0},{12,28},{16,24},{20,4},{24,16},{28,12},{1,9},{5... | collective-permute-start | bytes 393224 | tf_op jit(solution)/shard_map/ppermute | solution.py:118
  165.6 3.3 %collective-permute-done.27.refs_3_ = bf16[512,128]{1,0:T(8,128)(2,1)S(1)} collective-permute-done((bf16[512,128]{1,0:T(8,128)(2,1)S(1)}, bf16[512,128]{1,0:T(8,128)(2,1)S(1)}, u32[]{:S(2)}, u32[]{:S(2)}) %collective-permute-start.27) | collective-permute-done | bytes 131104 | tf_op jit(solution)/shard_map/ppermute | solution.py:118
  170.9 4.4 %collective-permute-done.28.refs_4_ = bf16[1024,128]{1,0:T(8,128)(2,1)S(1)} collective-permute-done((bf16[1024,128]{1,0:T(8,128)(2,1)S(1)}, bf16[1024,128]{1,0:T(8,128)(2,1)S(1)}, u32[]{:S(2)}, u32[]{:S(2)}) %collective-permute-start.28) | collective-permute-done | bytes 262176 | tf_op jit(solution)/shard_map/ppermute | solution.py:118
  175.3 1.9 shard_map.80
  177.2 2.5 %collective-permute-start.37 = (bf16[512,128]{1,0:T(8,128)(2,1)S(1)}, bf16[512,128]{1,0:T(8,128)(2,1)S(1)}, u32[]{:S(2)}, u32[]{:S(2)}) collective-permute-start(bf16[512,128]{1,0:T(8,128)(2,1)S(1)} %get-tuple-element.19.refs_2_), channel_id=1, source_target_pairs={{0,8},{4,20},{8,0},{12,28},{16,24},{20,4},{24,16},{28,12},{1,9},{5... | collective-permute-start | bytes 393224 | tf_op jit(solution)/shard_map/ppermute | solution.py:118
  179.7 3.9 %collective-permute-done.37.refs_3_ = bf16[512,128]{1,0:T(8,128)(2,1)S(1)} collective-permute-done((bf16[512,128]{1,0:T(8,128)(2,1)S(1)}, bf16[512,128]{1,0:T(8,128)(2,1)S(1)}, u32[]{:S(2)}, u32[]{:S(2)}) %collective-permute-start.37) | collective-permute-done | bytes 131104 | tf_op jit(solution)/shard_map/ppermute | solution.py:118
  183.7 6.9 %collective-permute-done.38.refs_4_ = bf16[1024,128]{1,0:T(8,128)(2,1)S(1)} collective-permute-done((bf16[1024,128]{1,0:T(8,128)(2,1)S(1)}, bf16[1024,128]{1,0:T(8,128)(2,1)S(1)}, u32[]{:S(2)}, u32[]{:S(2)}) %collective-permute-start.38) | collective-permute-done | bytes 262176 | tf_op jit(solution)/shard_map/ppermute | solution.py:118
  191.9 3.3 %collective-permute-start.42 = (bf16[512,128]{1,0:T(8,128)(2,1)S(1)}, bf16[512,128]{1,0:T(8,128)(2,1)S(1)}, u32[]{:S(2)}, u32[]{:S(2)}) collective-permute-start(bf16[512,128]{1,0:T(8,128)(2,1)S(1)} %get-tuple-element.21.refs_2_), channel_id=1, source_target_pairs={{0,8},{4,20},{8,0},{12,28},{16,24},{20,4},{24,16},{28,12},{1,9},{5... | collective-permute-start | bytes 393224 | tf_op jit(solution)/shard_map/ppermute | solution.py:118
  195.2 2.9 %collective-permute-done.42.refs_3_ = bf16[512,128]{1,0:T(8,128)(2,1)S(1)} collective-permute-done((bf16[512,128]{1,0:T(8,128)(2,1)S(1)}, bf16[512,128]{1,0:T(8,128)(2,1)S(1)}, u32[]{:S(2)}, u32[]{:S(2)}) %collective-permute-start.42) | collective-permute-done | bytes 131104 | tf_op jit(solution)/shard_map/ppermute | solution.py:118
  198.2 1.3 collective-permute-done.52
  199.5 1.2 shard_map.83.refs_5_
  200.8 1.2 shard_map.84.refs_5_
  202.1 3.8 %collective-permute-done.43.refs_4_ = bf16[1024,128]{1,0:T(8,128)(2,1)S(1)} collective-permute-done((bf16[1024,128]{1,0:T(8,128)(2,1)S(1)}, bf16[1024,128]{1,0:T(8,128)(2,1)S(1)}, u32[]{:S(2)}, u32[]{:S(2)}) %collective-permute-start.43) | collective-permute-done | bytes 262176 | tf_op jit(solution)/shard_map/ppermute | solution.py:118
  205.9 1.9 shard_map.85
  207.8 2.0 collective-permute-start.53
  209.9 2.9 %collective-permute-done.53.refs_3_ = bf16[512,128]{1,0:T(8,128)(2,1)S(1)} collective-permute-done((bf16[512,128]{1,0:T(8,128)(2,1)S(1)}, bf16[512,128]{1,0:T(8,128)(2,1)S(1)}, u32[]{:S(2)}, u32[]{:S(2)}) %collective-permute-start.53) | collective-permute-done | bytes 131104 | tf_op jit(solution)/shard_map/ppermute | solution.py:118
  213.6 5.6 %collective-permute-done.54.refs_4_ = bf16[1024,128]{1,0:T(8,128)(2,1)S(1)} collective-permute-done((bf16[1024,128]{1,0:T(8,128)(2,1)S(1)}, bf16[1024,128]{1,0:T(8,128)(2,1)S(1)}, u32[]{:S(2)}, u32[]{:S(2)}) %collective-permute-start.54) | collective-permute-done | bytes 262176 | tf_op jit(solution)/shard_map/ppermute | solution.py:118
  220.7 1.3 collective-permute-done.55
  (162 shorter events, 28.8 us)
Async XLA Ops:
  15.5 38.6 %collective-permute-start.1 = (bf16[256,256]{1,0:T(8,128)(2,1)}, bf16[256,256]{1,0:T(8,128)(2,1)S(1)}, u32[]{:S(2)}, u32[]{:S(2)}) collective-permute-start(bf16[256,256]{1,0:T(8,128)(2,1)} %get-tuple-element.54), channel_id=1, source_target_pairs={{0,1},{4,5},{8,9},{12,13},{16,17},{20,21},{24,25},{28,29}} | collective-permute-start | bytes 393224 | tf_op jit(solution)/shard_map/ppermute | solution.py:133
  20.4 49.2 %collective-permute-start.4 = (bf16[256,256]{1,0:T(8,128)(2,1)}, bf16[256,256]{1,0:T(8,128)(2,1)S(1)}, u32[]{:S(2)}, u32[]{:S(2)}) collective-permute-start(bf16[256,256]{1,0:T(8,128)(2,1)} %get-tuple-element.55), channel_id=1, source_target_pairs={{3,2},{7,6},{11,10},{15,14},{19,18},{23,22},{27,26},{31,30}} | collective-permute-start | bytes 393224 | tf_op jit(solution)/shard_map/ppermute | solution.py:135
  23.3 106.1 %collective-permute-start = (bf16[256,2048]{1,0:T(8,128)(2,1)}, bf16[256,2048]{1,0:T(8,128)(2,1)}, u32[]{:S(2)}, u32[]{:S(2)}) collective-permute-start(bf16[256,2048]{1,0:T(8,128)(2,1)} %get-tuple-element.33.refs_0_), channel_id=1, source_target_pairs={{0,4},{4,0},{8,12},{12,8},{16,20},{20,16},{24,28},{28,24},{1,5},{5... | collective-permute-start | bytes 3145736 | tf_op jit(solution)/shard_map/ppermute | solution.py:111
  31.7 23.8 %collective-permute-start.15 = (bf16[256,256]{1,0:T(8,128)(2,1)}, bf16[256,256]{1,0:T(8,128)(2,1)}, u32[]{:S(2)}, u32[]{:S(2)}) collective-permute-start(bf16[256,256]{1,0:T(8,128)(2,1)} %get-tuple-element.50), channel_id=1, source_target_pairs={{0,1},{4,5},{8,9},{12,13},{16,17},{20,21},{24,25},{28,29}} | collective-permute-start | bytes 393224 | tf_op jit(solution)/shard_map/ppermute | solution.py:133
  33.6 42.9 %collective-permute-start.18 = (bf16[256,256]{1,0:T(8,128)(2,1)}, bf16[256,256]{1,0:T(8,128)(2,1)S(1)}, u32[]{:S(2)}, u32[]{:S(2)}) collective-permute-start(bf16[256,256]{1,0:T(8,128)(2,1)} %get-tuple-element.51), channel_id=1, source_target_pairs={{3,2},{7,6},{11,10},{15,14},{19,18},{23,22},{27,26},{31,30}} | collective-permute-start | bytes 393224 | tf_op jit(solution)/shard_map/ppermute | solution.py:135
  52.9 16.7 %copy-start.11 = (f32[256,1024]{1,0:T(8,128)S(1)}, f32[256,1024]{1,0:T(8,128)}, u32[]{:S(2)}) copy-start(f32[256,1024]{1,0:T(8,128)} %copy-done.10) | copy-start | bytes 3145732
  52.9 23.7 %copy-start.14 = (bf16[256,2048]{1,0:T(8,128)(2,1)S(1)}, bf16[256,2048]{1,0:T(8,128)(2,1)}, u32[]{:S(2)}) copy-start(bf16[256,2048]{1,0:T(8,128)(2,1)} %get-tuple-element.31.refs_0_) | copy-start | bytes 3145732
  54.1 4.4 %collective-permute-start.30 = (bf16[256,256]{1,0:T(8,128)(2,1)}, bf16[256,256]{1,0:T(8,128)(2,1)S(1)}, u32[]{:S(2)}, u32[]{:S(2)}) collective-permute-start(bf16[256,256]{1,0:T(8,128)(2,1)} %get-tuple-element.46), channel_id=1, source_target_pairs={{0,1},{4,5},{8,9},{12,13},{16,17},{20,21},{24,25},{28,29}} | collective-permute-start | bytes 393224 | tf_op jit(solution)/shard_map/ppermute | solution.py:133
  55.5 34.7 %collective-permute-start.33 = (bf16[256,256]{1,0:T(8,128)(2,1)}, bf16[256,256]{1,0:T(8,128)(2,1)S(1)}, u32[]{:S(2)}, u32[]{:S(2)}) collective-permute-start(bf16[256,256]{1,0:T(8,128)(2,1)} %get-tuple-element.47), channel_id=1, source_target_pairs={{3,2},{7,6},{11,10},{15,14},{19,18},{23,22},{27,26},{31,30}} | collective-permute-start | bytes 393224 | tf_op jit(solution)/shard_map/ppermute | solution.py:135
  58.4 6.8 %collective-permute-start.46 = (bf16[256,256]{1,0:T(8,128)(2,1)S(1)}, bf16[256,256]{1,0:T(8,128)(2,1)S(1)}, u32[]{:S(2)}, u32[]{:S(2)}) collective-permute-start(bf16[256,256]{1,0:T(8,128)(2,1)S(1)} %get-tuple-element.42), channel_id=1, source_target_pairs={{0,1},{4,5},{8,9},{12,13},{16,17},{20,21},{24,25},{28,29}} | collective-permute-start | bytes 393224 | tf_op jit(solution)/shard_map/ppermute | solution.py:133
  62.8 37.8 %copy-start.22 = (f32[4,256,256]{2,1,0:T(8,128)S(1)}, f32[4,256,256]{2,1,0:T(8,128)}, u32[]{:S(2)}) copy-start(f32[4,256,256]{2,1,0:T(8,128)} %param.7) | copy-start | bytes 3145732
  65.2 6.8 %collective-permute-start.2 = (bf16[256,256]{1,0:T(8,128)(2,1)S(1)}, bf16[256,256]{1,0:T(8,128)(2,1)S(1)}, u32[]{:S(2)}, u32[]{:S(2)}) collective-permute-start(bf16[256,256]{1,0:T(8,128)(2,1)S(1)} %add_convert_fusion.15), channel_id=1, source_target_pairs={{0,1},{1,2},{4,5},{5,6},{8,9},{9,10},{12,13},{13,14},{16,17},{17,1... | collective-permute-start | bytes 393224 | tf_op jit(solution)/shard_map/ppermute | solution.py:133
  69.6 31.0 %collective-permute-start.49 = (bf16[256,256]{1,0:T(8,128)(2,1)S(1)}, bf16[256,256]{1,0:T(8,128)(2,1)S(1)}, u32[]{:S(2)}, u32[]{:S(2)}) collective-permute-start(bf16[256,256]{1,0:T(8,128)(2,1)S(1)} %get-tuple-element.43), channel_id=1, source_target_pairs={{3,2},{7,6},{11,10},{15,14},{19,18},{23,22},{27,26},{31,30}} | collective-permute-start | bytes 393224 | tf_op jit(solution)/shard_map/ppermute | solution.py:135
  72.1 6.8 %collective-permute-start.16 = (bf16[256,256]{1,0:T(8,128)(2,1)S(1)}, bf16[256,256]{1,0:T(8,128)(2,1)S(1)}, u32[]{:S(2)}, u32[]{:S(2)}) collective-permute-start(bf16[256,256]{1,0:T(8,128)(2,1)S(1)} %add_convert_fusion.11), channel_id=1, source_target_pairs={{0,1},{1,2},{4,5},{5,6},{8,9},{9,10},{12,13},{13,14},{16,17},{17,1... | collective-permute-start | bytes 393224 | tf_op jit(solution)/shard_map/ppermute | solution.py:133
  76.5 65.6 %collective-permute-start.12 = (bf16[256,2048]{1,0:T(8,128)(2,1)S(1)}, bf16[256,2048]{1,0:T(8,128)(2,1)S(1)}, u32[]{:S(2)}, u32[]{:S(2)}) collective-permute-start(bf16[256,2048]{1,0:T(8,128)(2,1)S(1)} %copy-done.14), channel_id=1, source_target_pairs={{0,4},{4,0},{8,12},{12,8},{16,20},{20,16},{24,28},{28,24},{1,5},{5... | collective-permute-start | bytes 3145736 | tf_op jit(solution)/shard_map/ppermute | solution.py:111
  78.9 0.8 collective-permute-start.5
  79.7 12.9 %collective-permute-start.31 = (bf16[256,256]{1,0:T(8,128)(2,1)S(1)}, bf16[256,256]{1,0:T(8,128)(2,1)S(1)}, u32[]{:S(2)}, u32[]{:S(2)}) collective-permute-start(bf16[256,256]{1,0:T(8,128)(2,1)S(1)} %add_convert_fusion.7), channel_id=1, source_target_pairs={{0,1},{1,2},{4,5},{5,6},{8,9},{9,10},{12,13},{13,14},{16,17},{17,1... | collective-permute-start | bytes 393224 | tf_op jit(solution)/shard_map/ppermute | solution.py:133
  90.2 5.2 %collective-permute-start.3 = (bf16[256,256]{1,0:T(8,128)(2,1)S(1)}, bf16[256,256]{1,0:T(8,128)(2,1)S(1)}, u32[]{:S(2)}, u32[]{:S(2)}) collective-permute-start(bf16[256,256]{1,0:T(8,128)(2,1)S(1)} %get-tuple-element.52), channel_id=1, source_target_pairs={{0,1},{1,2},{2,3},{4,5},{5,6},{6,7},{8,9},{9,10},{10,11},{12,13},{... | collective-permute-start | bytes 393224 | tf_op jit(solution)/shard_map/ppermute | solution.py:133
  92.6 7.3 %collective-permute-start.6 = (bf16[256,256]{1,0:T(8,128)(2,1)S(1)}, bf16[256,256]{1,0:T(8,128)(2,1)S(1)}, u32[]{:S(2)}, u32[]{:S(2)}) collective-permute-start(bf16[256,256]{1,0:T(8,128)(2,1)S(1)} %add_convert_fusion.12), channel_id=1, source_target_pairs={{3,2},{2,1},{1,0},{7,6},{6,5},{5,4},{11,10},{10,9},{9,8},{15,14},{... | collective-permute-start | bytes 393224 | tf_op jit(solution)/shard_map/ppermute | solution.py:135
  95.4 6.9 %collective-permute-start.47 = (bf16[256,256]{1,0:T(8,128)(2,1)S(1)}, bf16[256,256]{1,0:T(8,128)(2,1)S(1)}, u32[]{:S(2)}, u32[]{:S(2)}) collective-permute-start(bf16[256,256]{1,0:T(8,128)(2,1)S(1)} %add_convert_fusion.3), channel_id=1, source_target_pairs={{0,1},{1,2},{4,5},{5,6},{8,9},{9,10},{12,13},{13,14},{16,17},{17,1... | collective-permute-start | bytes 393224 | tf_op jit(solution)/shard_map/ppermute | solution.py:133
  99.9 4.3 %collective-permute-start.19 = (bf16[256,256]{1,0:T(8,128)(2,1)S(1)}, bf16[256,256]{1,0:T(8,128)(2,1)S(1)}, u32[]{:S(2)}, u32[]{:S(2)}) collective-permute-start(bf16[256,256]{1,0:T(8,128)(2,1)S(1)} %get-tuple-element.49), channel_id=1, source_target_pairs={{3,2},{2,1},{7,6},{6,5},{11,10},{10,9},{15,14},{14,13},{19,18},{18... | collective-permute-start | bytes 393224 | tf_op jit(solution)/shard_map/ppermute | solution.py:135
  100.7 16.0 %collective-permute-start.34 = (bf16[256,256]{1,0:T(8,128)(2,1)S(1)}, bf16[256,256]{1,0:T(8,128)(2,1)S(1)}, u32[]{:S(2)}, u32[]{:S(2)}) collective-permute-start(bf16[256,256]{1,0:T(8,128)(2,1)S(1)} %get-tuple-element.45), channel_id=1, source_target_pairs={{3,2},{2,1},{7,6},{6,5},{11,10},{10,9},{15,14},{14,13},{19,18},{18... | collective-permute-start | bytes 393224 | tf_op jit(solution)/shard_map/ppermute | solution.py:135
  102.3 1.3 collective-permute-start.7
  103.5 14.8 %collective-permute-start.50 = (bf16[256,256]{1,0:T(8,128)(2,1)S(1)}, bf16[256,256]{1,0:T(8,128)(2,1)S(1)}, u32[]{:S(2)}, u32[]{:S(2)}) collective-permute-start(bf16[256,256]{1,0:T(8,128)(2,1)S(1)} %get-tuple-element.41), channel_id=1, source_target_pairs={{3,2},{2,1},{7,6},{6,5},{11,10},{10,9},{15,14},{14,13},{19,18},{18... | collective-permute-start | bytes 393224 | tf_op jit(solution)/shard_map/ppermute | solution.py:135
  104.3 5.0 %collective-permute-start.8 = (bf16[512,128]{1,0:T(8,128)(2,1)S(1)}, bf16[512,128]{1,0:T(8,128)(2,1)S(1)}, u32[]{:S(2)}, u32[]{:S(2)}) collective-permute-start(bf16[512,128]{1,0:T(8,128)(2,1)S(1)} %fusion.refs_2_), channel_id=1, source_target_pairs={{0,8},{4,20},{8,0},{12,28},{16,24},{20,4},{24,16},{28,12},{1,9},{5... | collective-permute-start | bytes 393224 | tf_op jit(solution)/shard_map/ppermute | solution.py:118
  109.3 24.0 %copy-start.20 = (bf16[256,2048]{1,0:T(8,128)(2,1)S(1)}, bf16[256,2048]{1,0:T(8,128)(2,1)}, u32[]{:S(2)}) copy-start(bf16[256,2048]{1,0:T(8,128)(2,1)} %get-tuple-element.34.refs_0_) | copy-start | bytes 3145732
  109.3 13.6 %collective-permute-start.17 = (bf16[256,256]{1,0:T(8,128)(2,1)S(1)}, bf16[256,256]{1,0:T(8,128)(2,1)S(1)}, u32[]{:S(2)}, u32[]{:S(2)}) collective-permute-start(bf16[256,256]{1,0:T(8,128)(2,1)S(1)} %get-tuple-element.48), channel_id=1, source_target_pairs={{0,1},{1,2},{2,3},{4,5},{5,6},{6,7},{8,9},{9,10},{10,11},{12,13},{... | collective-permute-start | bytes 393224 | tf_op jit(solution)/shard_map/ppermute | solution.py:133
  116.7 11.4 %collective-permute-start.9 = (bf16[1024,128]{1,0:T(8,128)(2,1)S(1)}, bf16[1024,128]{1,0:T(8,128)(2,1)S(1)}, u32[]{:S(2)}, u32[]{:S(2)}) collective-permute-start(bf16[1024,128]{1,0:T(8,128)(2,1)S(1)} %pad_maximum_fusion.1), channel_id=1, source_target_pairs={{0,16},{4,12},{8,24},{12,4},{16,0},{20,28},{24,8},{28,20},{1,17},{... | collective-permute-start | bytes 786440 | tf_op jit(solution)/shard_map/ppermute | solution.py:118
  118.4 8.4 %collective-permute-start.32 = (bf16[256,256]{1,0:T(8,128)(2,1)S(1)}, bf16[256,256]{1,0:T(8,128)(2,1)S(1)}, u32[]{:S(2)}, u32[]{:S(2)}) collective-permute-start(bf16[256,256]{1,0:T(8,128)(2,1)S(1)} %get-tuple-element.44), channel_id=1, source_target_pairs={{0,1},{1,2},{2,3},{4,5},{5,6},{6,7},{8,9},{9,10},{10,11},{12,13},{... | collective-permute-start | bytes 393224 | tf_op jit(solution)/shard_map/ppermute | solution.py:133
  122.9 10.4 %collective-permute-start.48 = (bf16[256,256]{1,0:T(8,128)(2,1)S(1)}, bf16[256,256]{1,0:T(8,128)(2,1)S(1)}, u32[]{:S(2)}, u32[]{:S(2)}) collective-permute-start(bf16[256,256]{1,0:T(8,128)(2,1)S(1)} %get-tuple-element.40), channel_id=1, source_target_pairs={{0,1},{1,2},{2,3},{4,5},{5,6},{6,7},{8,9},{9,10},{10,11},{12,13},{... | collective-permute-start | bytes 393224 | tf_op jit(solution)/shard_map/ppermute | solution.py:133
  126.8 8.0 %collective-permute-start.20 = (bf16[256,256]{1,0:T(8,128)(2,1)S(1)}, bf16[256,256]{1,0:T(8,128)(2,1)S(1)}, u32[]{:S(2)}, u32[]{:S(2)}) collective-permute-start(bf16[256,256]{1,0:T(8,128)(2,1)S(1)} %add_convert_fusion.8), channel_id=1, source_target_pairs={{3,2},{2,1},{1,0},{7,6},{6,5},{5,4},{11,10},{10,9},{9,8},{15,14},{... | collective-permute-start | bytes 393224 | tf_op jit(solution)/shard_map/ppermute | solution.py:135
  128.1 8.6 %collective-permute-start.35 = (bf16[256,256]{1,0:T(8,128)(2,1)S(1)}, bf16[256,256]{1,0:T(8,128)(2,1)S(1)}, u32[]{:S(2)}, u32[]{:S(2)}) collective-permute-start(bf16[256,256]{1,0:T(8,128)(2,1)S(1)} %add_convert_fusion.4), channel_id=1, source_target_pairs={{3,2},{2,1},{1,0},{7,6},{6,5},{5,4},{11,10},{10,9},{9,8},{15,14},{... | collective-permute-start | bytes 393224 | tf_op jit(solution)/shard_map/ppermute | solution.py:135
  129.4 8.7 %collective-permute-start.51 = (bf16[256,256]{1,0:T(8,128)(2,1)S(1)}, bf16[256,256]{1,0:T(8,128)(2,1)S(1)}, u32[]{:S(2)}, u32[]{:S(2)}) collective-permute-start(bf16[256,256]{1,0:T(8,128)(2,1)S(1)} %add_convert_fusion), channel_id=1, source_target_pairs={{3,2},{2,1},{1,0},{7,6},{6,5},{5,4},{11,10},{10,9},{9,8},{15,14},{... | collective-permute-start | bytes 393224 | tf_op jit(solution)/shard_map/ppermute | solution.py:135
  133.3 21.3 %collective-permute-start.11 = (bf16[256,2048]{1,0:T(8,128)(2,1)S(1)}, bf16[256,2048]{1,0:T(8,128)(2,1)S(1)}, u32[]{:S(2)}, u32[]{:S(2)}) collective-permute-start(bf16[256,2048]{1,0:T(8,128)(2,1)S(1)} %copy-done.20), channel_id=1, source_target_pairs={{0,4},{4,0},{8,12},{12,8},{16,20},{20,16},{24,28},{28,24},{1,5},{5... | collective-permute-start | bytes 3145736 | tf_op jit(solution)/shard_map/ppermute | solution.py:111
  134.8 5.0 %collective-permute-start.13 = (bf16[512,128]{1,0:T(8,128)(2,1)S(1)}, bf16[512,128]{1,0:T(8,128)(2,1)S(1)}, u32[]{:S(2)}, u32[]{:S(2)}) collective-permute-start(bf16[512,128]{1,0:T(8,128)(2,1)S(1)} %get-tuple-element.15.refs_2_), channel_id=1, source_target_pairs={{0,8},{4,20},{8,0},{12,28},{16,24},{20,4},{24,16},{28,12},{1,9},{5... | collective-permute-start | bytes 393224 | tf_op jit(solution)/shard_map/ppermute | solution.py:118
  139.8 6.4 %collective-permute-start.14 = (bf16[1024,128]{1,0:T(8,128)(2,1)S(1)}, bf16[1024,128]{1,0:T(8,128)(2,1)S(1)}, u32[]{:S(2)}, u32[]{:S(2)}) collective-permute-start(bf16[1024,128]{1,0:T(8,128)(2,1)S(1)} %pad_maximum_fusion.2), channel_id=1, source_target_pairs={{0,16},{4,12},{8,24},{12,4},{16,0},{20,28},{24,8},{28,20},{1,17},{... | collective-permute-start | bytes 786440 | tf_op jit(solution)/shard_map/ppermute | solution.py:118
  140.7 1.4 collective-permute-start.21
  140.8 28.3 %collective-permute-start.29 = (bf16[256,2048]{1,0:T(8,128)(2,1)S(1)}, bf16[256,2048]{1,0:T(8,128)(2,1)S(1)}, u32[]{:S(2)}, u32[]{:S(2)}) collective-permute-start(bf16[256,2048]{1,0:T(8,128)(2,1)S(1)} %copy-done.17), channel_id=1, source_target_pairs={{0,4},{4,0},{8,12},{12,8},{16,20},{20,16},{24,28},{28,24},{1,5},{5... | collective-permute-start | bytes 3145736 | tf_op jit(solution)/shard_map/ppermute | solution.py:111
  148.2 16.8 %copy-start.19 = (bf16[256,2048]{1,0:T(8,128)(2,1)S(1)}, bf16[256,2048]{1,0:T(8,128)(2,1)}, u32[]{:S(2)}) copy-start(bf16[256,2048]{1,0:T(8,128)(2,1)} %get-tuple-element.36.refs_0_) | copy-start | bytes 3145732
  148.2 5.4 %collective-permute-start.22 = (bf16[512,128]{1,0:T(8,128)(2,1)S(1)}, bf16[512,128]{1,0:T(8,128)(2,1)S(1)}, u32[]{:S(2)}, u32[]{:S(2)}) collective-permute-start(bf16[512,128]{1,0:T(8,128)(2,1)S(1)} %get-tuple-element.16.refs_2_), channel_id=1, source_target_pairs={{0,8},{4,20},{8,0},{12,28},{16,24},{20,4},{24,16},{28,12},{1,9},{5... | collective-permute-start | bytes 393224 | tf_op jit(solution)/shard_map/ppermute | solution.py:118
  149.8 19.2 %copy-start.16 = (bf16[256,2048]{1,0:T(8,128)(2,1)S(1)}, bf16[256,2048]{1,0:T(8,128)(2,1)}, u32[]{:S(2)}) copy-start(bf16[256,2048]{1,0:T(8,128)(2,1)} %get-tuple-element.27.refs_0_) | copy-start | bytes 3145732
  149.8 21.1 %collective-permute-start.26 = (bf16[256,2048]{1,0:T(8,128)(2,1)S(1)}, bf16[256,2048]{1,0:T(8,128)(2,1)S(1)}, u32[]{:S(2)}, u32[]{:S(2)}) collective-permute-start(bf16[256,2048]{1,0:T(8,128)(2,1)S(1)} %copy-done.13), channel_id=1, source_target_pairs={{0,4},{4,0},{8,12},{12,8},{16,20},{20,16},{24,28},{28,24},{1,5},{5... | collective-permute-start | bytes 3145736 | tf_op jit(solution)/shard_map/ppermute | solution.py:111
  153.6 15.5 %copy-start.15 = (bf16[256,2048]{1,0:T(8,128)(2,1)S(1)}, bf16[256,2048]{1,0:T(8,128)(2,1)}, u32[]{:S(2)}) copy-start(bf16[256,2048]{1,0:T(8,128)(2,1)} %get-tuple-element.32.refs_0_) | copy-start | bytes 3145732
  153.6 6.7 %collective-permute-start.23 = (bf16[1024,128]{1,0:T(8,128)(2,1)S(1)}, bf16[1024,128]{1,0:T(8,128)(2,1)S(1)}, u32[]{:S(2)}, u32[]{:S(2)}) collective-permute-start(bf16[1024,128]{1,0:T(8,128)(2,1)S(1)} %pad_maximum_fusion.3), channel_id=1, source_target_pairs={{0,16},{4,12},{8,24},{12,4},{16,0},{20,28},{24,8},{28,20},{1,17},{... | collective-permute-start | bytes 786440 | tf_op jit(solution)/shard_map/ppermute | solution.py:118
  161.5 7.3 %collective-permute-start.27 = (bf16[512,128]{1,0:T(8,128)(2,1)S(1)}, bf16[512,128]{1,0:T(8,128)(2,1)S(1)}, u32[]{:S(2)}, u32[]{:S(2)}) collective-permute-start(bf16[512,128]{1,0:T(8,128)(2,1)S(1)} %get-tuple-element.18.refs_2_), channel_id=1, source_target_pairs={{0,8},{4,20},{8,0},{12,28},{16,24},{20,4},{24,16},{28,12},{1,9},{5... | collective-permute-start | bytes 393224 | tf_op jit(solution)/shard_map/ppermute | solution.py:118
  165.0 18.7 %collective-permute-start.25 = (bf16[256,2048]{1,0:T(8,128)(2,1)S(1)}, bf16[256,2048]{1,0:T(8,128)(2,1)S(1)}, u32[]{:S(2)}, u32[]{:S(2)}) collective-permute-start(bf16[256,2048]{1,0:T(8,128)(2,1)S(1)} %copy-done.19), channel_id=1, source_target_pairs={{0,4},{4,0},{8,12},{12,8},{16,20},{20,16},{24,28},{28,24},{1,5},{5... | collective-permute-start | bytes 3145736 | tf_op jit(solution)/shard_map/ppermute | solution.py:111
  165.0 4.0 %collective-permute-start.36 = (f32[256,128]{1,0:T(8,128)S(1)}, f32[256,128]{1,0:T(8,128)S(1)}, u32[]{:S(2)}, u32[]{:S(2)}) collective-permute-start(f32[256,128]{1,0:T(8,128)S(1)} %get-tuple-element.67), channel_id=1, source_target_pairs={{0,4},{4,0},{8,12},{12,8},{16,20},{20,16},{24,28},{28,24},{1,5},{5... | collective-permute-start | bytes 393224 | tf_op jit(solution)/shard_map/ppermute | solution.py:111
  168.9 6.4 %collective-permute-start.28 = (bf16[1024,128]{1,0:T(8,128)(2,1)S(1)}, bf16[1024,128]{1,0:T(8,128)(2,1)S(1)}, u32[]{:S(2)}, u32[]{:S(2)}) collective-permute-start(bf16[1024,128]{1,0:T(8,128)(2,1)S(1)} %pad_maximum_fusion.4), channel_id=1, source_target_pairs={{0,16},{4,12},{8,24},{12,4},{16,0},{20,28},{24,8},{28,20},{1,17},{... | collective-permute-start | bytes 786440 | tf_op jit(solution)/shard_map/ppermute | solution.py:118
  169.0 30.5 %collective-permute-start.45 = (bf16[256,2048]{1,0:T(8,128)(2,1)S(1)}, bf16[256,2048]{1,0:T(8,128)(2,1)S(1)}, u32[]{:S(2)}, u32[]{:S(2)}) collective-permute-start(bf16[256,2048]{1,0:T(8,128)(2,1)S(1)} %copy-done.16), channel_id=1, source_target_pairs={{0,4},{4,0},{8,12},{12,8},{16,20},{20,16},{24,28},{28,24},{1,5},{5... | collective-permute-start | bytes 3145736 | tf_op jit(solution)/shard_map/ppermute | solution.py:111
  169.1 31.7 %collective-permute-start.44 = (bf16[256,2048]{1,0:T(8,128)(2,1)S(1)}, bf16[256,2048]{1,0:T(8,128)(2,1)S(1)}, u32[]{:S(2)}, u32[]{:S(2)}) collective-permute-start(bf16[256,2048]{1,0:T(8,128)(2,1)S(1)} %copy-done.15), channel_id=1, source_target_pairs={{0,4},{4,0},{8,12},{12,8},{16,20},{20,16},{24,28},{28,24},{1,5},{5... | collective-permute-start | bytes 3145736 | tf_op jit(solution)/shard_map/ppermute | solution.py:111
  177.2 18.0 %copy-start.18 = (bf16[256,2048]{1,0:T(8,128)(2,1)S(1)}, bf16[256,2048]{1,0:T(8,128)(2,1)}, u32[]{:S(2)}) copy-start(bf16[256,2048]{1,0:T(8,128)(2,1)} %get-tuple-element.35.refs_0_) | copy-start | bytes 3145732
  177.2 6.4 %collective-permute-start.37 = (bf16[512,128]{1,0:T(8,128)(2,1)S(1)}, bf16[512,128]{1,0:T(8,128)(2,1)S(1)}, u32[]{:S(2)}, u32[]{:S(2)}) collective-permute-start(bf16[512,128]{1,0:T(8,128)(2,1)S(1)} %get-tuple-element.19.refs_2_), channel_id=1, source_target_pairs={{0,8},{4,20},{8,0},{12,28},{16,24},{20,4},{24,16},{28,12},{1,9},{5... | collective-permute-start | bytes 393224 | tf_op jit(solution)/shard_map/ppermute | solution.py:118
  179.7 22.3 %collective-permute-start.41 = (bf16[256,2048]{1,0:T(8,128)(2,1)S(1)}, bf16[256,2048]{1,0:T(8,128)(2,1)S(1)}, u32[]{:S(2)}, u32[]{:S(2)}) collective-permute-start(bf16[256,2048]{1,0:T(8,128)(2,1)S(1)} %copy-done.12), channel_id=1, source_target_pairs={{0,4},{4,0},{8,12},{12,8},{16,20},{20,16},{24,28},{28,24},{1,5},{5... | collective-permute-start | bytes 3145736 | tf_op jit(solution)/shard_map/ppermute | solution.py:111
  183.6 7.0 %collective-permute-start.38 = (bf16[1024,128]{1,0:T(8,128)(2,1)S(1)}, bf16[1024,128]{1,0:T(8,128)(2,1)S(1)}, u32[]{:S(2)}, u32[]{:S(2)}) collective-permute-start(bf16[1024,128]{1,0:T(8,128)(2,1)S(1)} %pad_maximum_fusion.5), channel_id=1, source_target_pairs={{0,16},{4,12},{8,24},{12,4},{16,0},{20,28},{24,8},{28,20},{1,17},{... | collective-permute-start | bytes 786440 | tf_op jit(solution)/shard_map/ppermute | solution.py:118
  191.9 6.3 %collective-permute-start.42 = (bf16[512,128]{1,0:T(8,128)(2,1)S(1)}, bf16[512,128]{1,0:T(8,128)(2,1)S(1)}, u32[]{:S(2)}, u32[]{:S(2)}) collective-permute-start(bf16[512,128]{1,0:T(8,128)(2,1)S(1)} %get-tuple-element.21.refs_2_), channel_id=1, source_target_pairs={{0,8},{4,20},{8,0},{12,28},{16,24},{20,4},{24,16},{28,12},{1,9},{5... | collective-permute-start | bytes 393224 | tf_op jit(solution)/shard_map/ppermute | solution.py:118
  195.2 18.4 %collective-permute-start.40 = (bf16[256,2048]{1,0:T(8,128)(2,1)S(1)}, bf16[256,2048]{1,0:T(8,128)(2,1)S(1)}, u32[]{:S(2)}, u32[]{:S(2)}) collective-permute-start(bf16[256,2048]{1,0:T(8,128)(2,1)S(1)} %copy-done.18), channel_id=1, source_target_pairs={{0,4},{4,0},{8,12},{12,8},{16,20},{20,16},{24,28},{28,24},{1,5},{5... | collective-permute-start | bytes 3145736 | tf_op jit(solution)/shard_map/ppermute | solution.py:111
  198.2 1.3 collective-permute-start.52
  199.5 6.4 %collective-permute-start.43 = (bf16[1024,128]{1,0:T(8,128)(2,1)S(1)}, bf16[1024,128]{1,0:T(8,128)(2,1)S(1)}, u32[]{:S(2)}, u32[]{:S(2)}) collective-permute-start(bf16[1024,128]{1,0:T(8,128)(2,1)S(1)} %pad_maximum_fusion.6), channel_id=1, source_target_pairs={{0,16},{4,12},{8,24},{12,4},{16,0},{20,28},{24,8},{28,20},{1,17},{... | collective-permute-start | bytes 786440 | tf_op jit(solution)/shard_map/ppermute | solution.py:118
  207.8 5.0 %collective-permute-start.53 = (bf16[512,128]{1,0:T(8,128)(2,1)S(1)}, bf16[512,128]{1,0:T(8,128)(2,1)S(1)}, u32[]{:S(2)}, u32[]{:S(2)}) collective-permute-start(bf16[512,128]{1,0:T(8,128)(2,1)S(1)} %get-tuple-element.22.refs_2_), channel_id=1, source_target_pairs={{0,8},{4,20},{8,0},{12,28},{16,24},{20,4},{24,16},{28,12},{1,9},{5... | collective-permute-start | bytes 393224 | tf_op jit(solution)/shard_map/ppermute | solution.py:118
  209.9 3.0 %collective-permute-start.10 = (f32[256,128]{1,0:T(8,128)S(1)}, f32[256,128]{1,0:T(8,128)S(1)}, u32[]{:S(2)}, u32[]{:S(2)}) collective-permute-start(f32[256,128]{1,0:T(8,128)S(1)} %get-tuple-element.57), channel_id=1, source_target_pairs={{0,4},{4,0},{8,12},{12,8},{16,20},{20,16},{24,28},{28,24},{1,5},{5... | collective-permute-start | bytes 393224 | tf_op jit(solution)/shard_map/ppermute | solution.py:111
  212.8 6.4 %collective-permute-start.54 = (bf16[1024,128]{1,0:T(8,128)(2,1)S(1)}, bf16[1024,128]{1,0:T(8,128)(2,1)S(1)}, u32[]{:S(2)}, u32[]{:S(2)}) collective-permute-start(bf16[1024,128]{1,0:T(8,128)(2,1)S(1)} %pad_maximum_fusion.7), channel_id=1, source_target_pairs={{0,16},{4,12},{8,24},{12,4},{16,0},{20,28},{24,8},{28,20},{1,17},{... | collective-permute-start | bytes 786440 | tf_op jit(solution)/shard_map/ppermute | solution.py:118
  213.0 7.6 %collective-permute-start.24 = (f32[256,128]{1,0:T(8,128)S(1)}, f32[256,128]{1,0:T(8,128)S(1)}, u32[]{:S(2)}, u32[]{:S(2)}) collective-permute-start(f32[256,128]{1,0:T(8,128)S(1)} %get-tuple-element.59), channel_id=1, source_target_pairs={{0,4},{4,0},{8,12},{12,8},{16,20},{20,16},{24,28},{28,24},{1,5},{5... | collective-permute-start | bytes 393224 | tf_op jit(solution)/shard_map/ppermute | solution.py:111
  213.1 7.6 %collective-permute-start.39 = (f32[256,128]{1,0:T(8,128)S(1)}, f32[256,128]{1,0:T(8,128)S(1)}, u32[]{:S(2)}, u32[]{:S(2)}) collective-permute-start(f32[256,128]{1,0:T(8,128)S(1)} %get-tuple-element.61), channel_id=1, source_target_pairs={{0,4},{4,0},{8,12},{12,8},{16,20},{20,16},{24,28},{28,24},{1,5},{5... | collective-permute-start | bytes 393224 | tf_op jit(solution)/shard_map/ppermute | solution.py:111
  220.5 1.4 collective-permute-start.55
  (18 other events, 93.1 us)

commit v2 on v0

v2 whole, which is shorter than its diff:
```python
import functools

import jax
import jax.numpy as jnp
from jax import lax
from jax.experimental import pallas as pl
from jax.experimental.pallas import tpu as pltpu
from jax.sharding import PartitionSpec as P

F32, BF16 = jnp.float32, jnp.bfloat16
VMEM = pl.BlockSpec(memory_space=pltpu.VMEM)
SMEM = pl.BlockSpec(memory_space=pltpu.SMEM)
ANY = pl.BlockSpec(memory_space=pl.ANY)


def inner_index(target, earlier):
    return target * (target - 1) // 2 + earlier


def product_kernel(blocks, count, place_ref, *refs):
    l_refs, x_ref, outs = refs[:blocks], refs[blocks], refs[blocks + 1 :]
    for turn in range(count):

        @pl.when(pl.program_id(0) == turn)
        def _():
            for block in range(blocks):
                out = outs[block * count + turn]
                out[...] = jnp.dot(
                    l_refs[block][...], x_ref[...], preferred_element_type=F32
                ).astype(out.dtype)


def panel_products(place, l_panel, x_solved, targets, width):
    _, rows, depth = l_panel.shape
    count = x_solved.shape[1] // width
    types = [BF16] * (count - 1) + [F32]
    found = pl.pallas_call(
        functools.partial(product_kernel, len(targets), count),
        grid_spec=pltpu.PrefetchScalarGridSpec(
            num_scalar_prefetch=1,
            grid=(count,),
            in_specs=[
                pl.BlockSpec((None, rows, depth), lambda i, place, t=t: (t, 0, 0)) for t in targets
            ]
            + [pl.BlockSpec((depth, width), lambda i, place: (0, place[i]))],
            out_specs=[pl.BlockSpec((rows, width), lambda i, place: (0, 0))]
            * (count * len(targets)),
        ),
        out_shape=[jax.ShapeDtypeStruct((rows, width), t) for t in types] * len(targets),
        compiler_params=pltpu.CompilerParams(vmem_limit_bytes=40 << 20),
        cost_estimate=pl.CostEstimate(
            flops=2 * rows * depth * x_solved.shape[1] * len(targets),
            bytes_accessed=2 * (rows * len(targets) + x_solved.shape[1]) * depth,
            transcendentals=0,
        ),
    )(place, *[l_panel] * len(targets), x_solved)
    return [found[i * count : (i + 1) * count] for i in range(len(targets))]


def load_kernel(index, place_ref, own_ref, other_ref, out_ref, sems):
    rows = own_ref.shape[1]
    copies = [
        pltpu.make_async_copy(
            ref.at[index],
            out_ref.at[pl.ds(pl.multiple_of(place_ref[k], rows), rows)],
            sems.at[k],
        )
        for k, ref in enumerate((own_ref, other_ref))
    ]
    for copy in copies:
        copy.start()
    for copy in copies:
        copy.wait()


def load_rows(place, own, other, index):
    _, rows, depth = own.shape
    return pl.pallas_call(
        functools.partial(load_kernel, index),
        in_specs=[SMEM, ANY, ANY],
        out_specs=VMEM,
        out_shape=jax.ShapeDtypeStruct((2 * rows, depth), own.dtype),
        scratch_shapes=[pltpu.SemaphoreType.DMA((2,))],
        compiler_params=pltpu.CompilerParams(vmem_limit_bytes=8 << 20),
        cost_estimate=pl.CostEstimate(
            flops=0, bytes_accessed=8 * rows * depth, transcendentals=0
        ),
    )(place, own, other)


def apply_kernel(parts, subtract, types, place_ref, matrix_ref, *refs):
    shards = refs[:parts]
    outs = refs[parts + subtract :]
    high, width = shards[0].shape
    total = jnp.zeros((high, width), F32)
    for entry, shard in enumerate(shards):
        begin = pl.multiple_of(place_ref[2 + entry], high)
        total += jnp.dot(
            matrix_ref[:, pl.ds(begin, high)], shard[...], preferred_element_type=F32
        )
    if subtract:
        total = refs[parts][...] - total
    for out in outs:
        out[...] = total.astype(out.dtype)


def apply_rows(place, matrix, shards, pending, types):
    high, width = shards[0].shape
    operands = [matrix, *shards] + ([] if pending is None else [pending])
    return pl.pallas_call(
        functools.partial(apply_kernel, len(shards), int(pending is not None), types),
        in_specs=[SMEM] + [VMEM] * len(operands),
        out_specs=[VMEM] * len(types),
        out_shape=[jax.ShapeDtypeStruct((high, width), t) for t in types],
        compiler_params=pltpu.CompilerParams(vmem_limit_bytes=16 << 20),
        cost_estimate=pl.CostEstimate(
            flops=4 * matrix.size * width, bytes_accessed=2 * matrix.size, transcendentals=0
        ),
    )(place, *operands)


def local(rhs, l_panel, x_solved, diag_inv, l_inner, row_count, col_count):
    steps, rows, _ = l_panel.shape
    width = rhs.shape[2]
    half = width // 2
    high = 2 * rows
    chips = row_count // 2
    me, mine = lax.axis_index("row"), lax.axis_index("col")
    core, chip = me % 2, me // 2
    order = jnp.arange(chips, dtype=jnp.int32)
    place = jnp.concatenate(
        [jnp.stack([core * rows, (1 - core) * rows]), (chip ^ order) * high]
    ).astype(jnp.int32)
    turns = (mine + 1 + jnp.arange(col_count, dtype=jnp.int32)) % col_count

    def swap(value):
        return lax.ppermute(value, "row", [(i, i ^ 1) for i in range(row_count)])

    def gather(value):
        far = [
            lax.ppermute(value, "row", [(i, i ^ (2 * mask)) for i in range(row_count)])
            for mask in range(1, chips)
        ]
        return [value, *far]

    def send_chunks(chunks):
        return [
            lax.ppermute(
                chunks[turn], "col", [(i, (i + turn + 1) % col_count) for i in range(col_count)]
            )
            for turn in range(col_count - 1)
        ]

    def reduced(target, chunks, arrived):
        total = chunks[-1]
        for part in arrived:
            total = total + part.astype(F32)
        return rhs[target] - total

    def to_halves(value):
        kept = lax.dynamic_slice_in_dim(value, core * half, half, 1)
        other = swap(lax.dynamic_slice_in_dim(value, (1 - core) * half, half, 1))
        return jnp.where(
            core == 0,
            jnp.concatenate([kept, other], axis=0),
            jnp.concatenate([other, kept], axis=0),
        )

    def from_halves(value):
        kept = lax.dynamic_slice_in_dim(value, core * rows, rows, 0)
        other = swap(lax.dynamic_slice_in_dim(value, (1 - core) * rows, rows, 0))
        return jnp.where(
            core == 0,
            jnp.concatenate([kept, other], axis=1),
            jnp.concatenate([other, kept], axis=1),
        )

    diag_other = swap(diag_inv)
    chunks = panel_products(turns, l_panel, x_solved, [0], width)
    arrived = send_chunks(chunks[0])
    if steps > 1:
        chunks += panel_products(turns, l_panel, x_solved, range(1, steps), width)
    l_inner, diag_other = lax.optimization_barrier((l_inner, diag_other))
    inner_other = swap(l_inner)
    pending = [to_halves(reduced(0, chunks[0], arrived))]
    for target in range(1, steps):
        sent, arrived = lax.optimization_barrier((chunks[target][:-1], arrived))
        arrived = send_chunks(sent)
        pending.append(to_halves(reduced(target, chunks[target], arrived)))
    results = []
    resid_low = pending[0].astype(BF16)
    for target in range(steps):
        last = target + 1 == steps
        matrix = load_rows(place, diag_inv, diag_other, target)
        current = apply_rows(place, matrix, gather(resid_low), None, (F32,) if last else (F32, BF16))
        results.append(from_halves(current[0]))
        if last:
            break
        shards = gather(current[1])
        for follower in range(target + 1, steps):
            index = inner_index(follower, target)
            matrix = load_rows(place, l_inner, inner_other, index)
            following = follower == target + 1
            updated = apply_rows(
                place, matrix, shards, pending[follower], (BF16,) if following else (F32,)
            )
            if following:
                resid_low = updated[0]
            else:
                pending[follower] = updated[0]
    return jnp.stack(results, axis=0)


def solution(mesh):
    in_specs = (
        P(None, "row", "col"),
        P(None, "row", "col"),
        P("col", None),
        P(None, "row", None),
        P(None, "row", None),
    )
    out_specs = P(None, "row", "col")
    body = functools.partial(local, row_count=mesh.shape["row"], col_count=mesh.shape["col"])
    return jax.shard_map(body, mesh=mesh, in_specs=in_specs, out_specs=out_specs, check_vma=False)
```

time: 296 us -> 151 us (0.51)
  waiting for transfers between devices: 240 us -> 38.7 us
  starting transfers between devices: 0.3 us -> 50.4 us
  Pallas kernels: 0 us -> 42.6 us
  matrix products: 39.2 us -> 0 us
  between operations: 13.5 us -> 0.58 us
  local copies, waits for them, and re-layouts: 1.32 us -> 13.9 us
    all_gather x7 -> x0, waiting for transfers between devices: 160 us -> none  [the longest x4 95.1 us: local(): lax.all_gather(resid_low, 'row', axis=0, tiled=True)]
    reduce_scatter x1 -> x0, waiting for transfers between devices: 79.6 us -> none  [local(): shares = lax.psum_scatter(products, 'col', scatter_dimension=2, tiled=True)]
    ppermute x0 -> x43, starting transfers between devices: none -> 50.4 us  [the longest x21 26.8 us: gather(): lax.ppermute(value, 'row', [(i, i ^ 2 * mask) for i in range(row_count)])]
    pallas_call x0 -> x22, Pallas kernels: none -> 42.6 us  [the longest x2 15.8 us: panel_products(): pl.pallas_call(functools.partial(product_kernel, len(targets), count), gr...]
    dot_general x11 -> x0, matrix products: 39.2 us -> none  [the longest x1 15.1 us: local(): jnp.dot(l_panel.reshape(step_count * local_rows, solved_count), x_solved,...]
    ppermute x0 -> x43, waiting for transfers between devices: none -> 38.7 us  [the longest x12 19.6 us: send_chunks(): lax.ppermute(chunks[turn], 'col', [(i, (i + turn + 1) % col_count) for i...]
    unnamed x4 -> x26, local copies, waits for them, and re-layouts: 0.01 us -> 12.3 us
  transfers between devices with their start and end apart: 8 -> 43, of which waited for: 8 -> 15; matrix products, arithmetic and copies ran while one was open for 2% -> 3% of each run, Pallas kernels for 0% -> 27%
where the time goes in v2:
time: 151 us
  starting transfers between devices  50.4 us (33%)
  Pallas kernels  42.6 us (28%)
  waiting for transfers between devices  38.7 us (26%)
  local copies, waits for them, and re-layouts  13.9 us (9%)
  other arithmetic  4.74 us (3%)
    ppermute x21, starting transfers between devices, gather(): lax.ppermute(value, 'row', [(i, i ^ 2 * mask) for i in range(row_count)])  26.8 us
    ppermute x12, starting transfers between devices, send_chunks(): lax.ppermute(chunks[turn], 'col', [(i, (i + turn + 1) % col_count) for i...  21.9 us
    ppermute x12, waiting for transfers between devices, send_chunks(): lax.ppermute(chunks[turn], 'col', [(i, (i + turn + 1) % col_count) for i...  19.6 us
    pallas_call x2, Pallas kernels, panel_products(): pl.pallas_call(functools.partial(product_kernel, len(targets), count), gr...  15.8 us
    pallas_call x10, Pallas kernels, load_rows(): pl.pallas_call(functools.partial(load_kernel, index), in_specs=[SMEM, ANY...  14.3 us
    pallas_call x10, Pallas kernels, apply_rows(): pl.pallas_call(functools.partial(apply_kernel, len(shards), int(pending i...  12.5 us
    unnamed x26, local copies, waits for them, and re-layouts  12.3 us
    ppermute x21, waiting for transfers between devices, gather(): lax.ppermute(value, 'row', [(i, i ^ 2 * mask) for i in range(row_count)])  10.8 us
  transfers between devices with their start and end apart: 43, of which 15 were waited for; matrix products, arithmetic and copies ran while one was open for 3% of the time, Pallas kernels for 27%

profile of v2, /device:TPU:0, one launch (start us, length us, event | category | flops | bytes accessed | tf_op | source)
XLA Modules:
  0.0 150.9 jit_solution(2022563351827910558)
XLA Ops:
  0.5 7.0 %collective-permute-done.other_ref = bf16[4,256,2048]{2,1,0:T(8,128)(2,1)S(1)} collective-permute-done((bf16[4,256,2048]{2,1,0:T(8,128)(2,1)}, bf16[4,256,2048]{2,1,0:T(8,128)(2,1)S(1)}, u32[]{:S(2)}, u32[]{:S(2)}) %collective-permute-start) | collective-permute-done | bytes 4194336 | tf_op jit(solution)/shard_map/ppermute | solution.py:137
  7.5 2.1 %copy-done.4 = bf16[4,256,2048]{2,1,0:T(8,128)(2,1)} copy-done((bf16[4,256,2048]{2,1,0:T(8,128)(2,1)}, bf16[4,256,2048]{2,1,0:T(8,128)(2,1)S(1)}, u32[]{:S(2)}) %copy-start.4) | copy-done | bytes 4194328
  9.9 3.4 %copy-done = bf16[4,256,4096]{2,1,0:T(8,128)(2,1)S(1)} copy-done((bf16[4,256,4096]{2,1,0:T(8,128)(2,1)S(1)}, bf16[4,256,4096]{2,1,0:T(8,128)(2,1)}, u32[]{:S(2)}) %copy-start) | copy-done | bytes 8388632
  13.3 6.2 %shard_map.56 = (bf16[256,256]{1,0:T(8,128)(2,1)S(1)}, bf16[256,256]{1,0:T(8,128)(2,1)S(1)}, bf16[256,256]{1,0:T(8,128)(2,1)S(1)}, f32[256,256]{1,0:T(8,128)S(1)}) custom-call(s32[4]{0:T(128)S(1)} %and_select_fusion.place_ref, bf16[4,256,4096]{2,1,0:T(8,128)(2,1)S(1)} %copy-done, bf16[4096,1024]{1,0:T(8,128)(2,1)} %refs_3_.1), custom_call_target="tpu_custom_call" | custom-call | flops 2147483648 | bytes 10485760 | tf_op jit(solution)/shard_map/pallas_call | solution.py:37
  19.4 2.8 %collective-permute-start.1 = (bf16[256,256]{1,0:T(8,128)(2,1)S(1)}, bf16[256,256]{1,0:T(8,128)(2,1)S(1)}, u32[]{:S(2)}, u32[]{:S(2)}) collective-permute-start(bf16[256,256]{1,0:T(8,128)(2,1)S(1)} %get-tuple-element.40), channel_id=1, source_target_pairs={{0,1},{1,2},{2,3},{3,0},{4,5},{5,6},{6,7},{7,4},{8,9},{9,10},{10,1... | collective-permute-start | bytes 393224 | tf_op jit(solution)/shard_map/ppermute | solution.py:148
  22.2 2.6 %collective-permute-start.2 = (bf16[256,256]{1,0:T(8,128)(2,1)S(1)}, bf16[256,256]{1,0:T(8,128)(2,1)S(1)}, u32[]{:S(2)}, u32[]{:S(2)}) collective-permute-start(bf16[256,256]{1,0:T(8,128)(2,1)S(1)} %get-tuple-element.41), channel_id=1, source_target_pairs={{0,2},{1,3},{2,0},{3,1},{4,6},{5,7},{6,4},{7,5},{8,10},{9,11},{10,... | collective-permute-start | bytes 393224 | tf_op jit(solution)/shard_map/ppermute | solution.py:148
  24.8 1.3 collective-permute-start.3
  26.2 9.6 %shard_map.60 = (bf16[256,256]{1,0:T(8,128)(2,1)S(1)}, bf16[256,256]{1,0:T(8,128)(2,1)S(1)}, bf16[256,256]{1,0:T(8,128)(2,1)S(1)}, f32[256,256]{1,0:T(8,128)S(1)...) custom-call(s32[4]{0:T(128)S(1)} %and_select_fusion.place_ref, ...), custom_call_target="tpu_custom_call" | custom-call | flops 6442450944 | bytes 14680064 | tf_op jit(solution)/shard_map/pallas_call | solution.py:37
  35.8 1.5 collective-permute-start.13
  37.3 1.6 %collective-permute-start.14 = (bf16[256,256]{1,0:T(8,128)(2,1)S(1)}, bf16[256,256]{1,0:T(8,128)(2,1)S(1)}, u32[]{:S(2)}, u32[]{:S(2)}) collective-permute-start(bf16[256,256]{1,0:T(8,128)(2,1)S(1)} %get-tuple-element.51), channel_id=1, source_target_pairs={{0,2},{1,3},{2,0},{3,1},{4,6},{5,7},{6,4},{7,5},{8,10},{9,11},{10,... | collective-permute-start | bytes 393224 | tf_op jit(solution)/shard_map/ppermute | solution.py:148
  38.9 0.8 collective-permute-start.15
  39.7 4.4 %collective-permute-done.13 = bf16[256,256]{1,0:T(8,128)(2,1)S(1)} collective-permute-done((bf16[256,256]{1,0:T(8,128)(2,1)S(1)}, bf16[256,256]{1,0:T(8,128)(2,1)S(1)}, u32[]{:S(2)}, u32[]{:S(2)}) %collective-permute-start.13) | collective-permute-done | bytes 131104 | tf_op jit(solution)/shard_map/ppermute | solution.py:148
  44.1 4.2 %collective-permute-done.14 = bf16[256,256]{1,0:T(8,128)(2,1)S(1)} collective-permute-done((bf16[256,256]{1,0:T(8,128)(2,1)S(1)}, bf16[256,256]{1,0:T(8,128)(2,1)S(1)}, u32[]{:S(2)}, u32[]{:S(2)}) %collective-permute-start.14) | collective-permute-done | bytes 131104 | tf_op jit(solution)/shard_map/ppermute | solution.py:148
  48.3 3.3 %collective-permute-start.24 = (bf16[256,256]{1,0:T(8,128)(2,1)S(1)}, bf16[256,256]{1,0:T(8,128)(2,1)S(1)}, u32[]{:S(2)}, u32[]{:S(2)}) collective-permute-start(bf16[256,256]{1,0:T(8,128)(2,1)S(1)} %get-tuple-element.59), channel_id=1, source_target_pairs={{0,1},{1,2},{2,3},{3,0},{4,5},{5,6},{6,7},{7,4},{8,9},{9,10},{10,1... | collective-permute-start | bytes 393224 | tf_op jit(solution)/shard_map/ppermute | solution.py:148
  52.3 1.6 %collective-permute-start.26 = (bf16[256,256]{1,0:T(8,128)(2,1)S(1)}, bf16[256,256]{1,0:T(8,128)(2,1)S(1)}, u32[]{:S(2)}, u32[]{:S(2)}) collective-permute-start(bf16[256,256]{1,0:T(8,128)(2,1)S(1)} %get-tuple-element.61), channel_id=1, source_target_pairs={{0,3},{1,0},{2,1},{3,2},{4,7},{5,4},{6,5},{7,6},{8,11},{9,8},{10,9... | collective-permute-start | bytes 393224 | tf_op jit(solution)/shard_map/ppermute | solution.py:148
  53.9 1.0 bitcast_subtract_fusion.3
  55.1 1.4 collective-permute-done.24
  56.4 4.7 %collective-permute-done.25 = bf16[256,256]{1,0:T(8,128)(2,1)S(1)} collective-permute-done((bf16[256,256]{1,0:T(8,128)(2,1)S(1)}, bf16[256,256]{1,0:T(8,128)(2,1)S(1)}, u32[]{:S(2)}, u32[]{:S(2)}) %collective-permute-start.25) | collective-permute-done | bytes 131104 | tf_op jit(solution)/shard_map/ppermute | solution.py:148
  61.1 3.3 %collective-permute-start.35 = (bf16[256,256]{1,0:T(8,128)(2,1)S(1)}, bf16[256,256]{1,0:T(8,128)(2,1)S(1)}, u32[]{:S(2)}, u32[]{:S(2)}) collective-permute-start(bf16[256,256]{1,0:T(8,128)(2,1)S(1)} %get-tuple-element.68), channel_id=1, source_target_pairs={{0,1},{1,2},{2,3},{3,0},{4,5},{5,6},{6,7},{7,4},{8,9},{9,10},{10,1... | collective-permute-start | bytes 393224 | tf_op jit(solution)/shard_map/ppermute | solution.py:148
  64.4 2.2 %collective-permute-start.36 = (bf16[256,256]{1,0:T(8,128)(2,1)S(1)}, bf16[256,256]{1,0:T(8,128)(2,1)S(1)}, u32[]{:S(2)}, u32[]{:S(2)}) collective-permute-start(bf16[256,256]{1,0:T(8,128)(2,1)S(1)} %get-tuple-element.69), channel_id=1, source_target_pairs={{0,2},{1,3},{2,0},{3,1},{4,6},{5,7},{6,4},{7,5},{8,10},{9,11},{10,... | collective-permute-start | bytes 393224 | tf_op jit(solution)/shard_map/ppermute | solution.py:148
  66.9 1.6 %collective-permute-start.5 = (bf16[512,128]{1,0:T(8,128)(2,1)S(1)}, bf16[512,128]{1,0:T(8,128)(2,1)S(1)}, u32[]{:S(2)}, u32[]{:S(2)}) collective-permute-start(bf16[512,128]{1,0:T(8,128)(2,1)S(1)} %fusion.refs_0_), channel_id=1, source_target_pairs={{0,8},{4,12},{8,0},{12,4},{16,24},{20,28},{24,16},{28,20},{1,9},{5... | collective-permute-start | bytes 393224 | tf_op jit(solution)/shard_map/ppermute | solution.py:141
  68.4 2.1 %collective-permute-done.35 = bf16[256,256]{1,0:T(8,128)(2,1)S(1)} collective-permute-done((bf16[256,256]{1,0:T(8,128)(2,1)S(1)}, bf16[256,256]{1,0:T(8,128)(2,1)S(1)}, u32[]{:S(2)}, u32[]{:S(2)}) %collective-permute-start.35) | collective-permute-done | bytes 131104 | tf_op jit(solution)/shard_map/ppermute | solution.py:148
  70.5 1.5 %collective-permute-start.6 = (bf16[512,128]{1,0:T(8,128)(2,1)S(1)}, bf16[512,128]{1,0:T(8,128)(2,1)S(1)}, u32[]{:S(2)}, u32[]{:S(2)}) collective-permute-start(bf16[512,128]{1,0:T(8,128)(2,1)S(1)} %fusion.refs_0_), channel_id=1, source_target_pairs={{0,16},{4,20},{8,24},{12,28},{16,0},{20,4},{24,8},{28,12},{1,17},{... | collective-permute-start | bytes 393224 | tf_op jit(solution)/shard_map/ppermute | solution.py:141
  72.0 2.9 %collective-permute-done.36 = bf16[256,256]{1,0:T(8,128)(2,1)S(1)} collective-permute-done((bf16[256,256]{1,0:T(8,128)(2,1)S(1)}, bf16[256,256]{1,0:T(8,128)(2,1)S(1)}, u32[]{:S(2)}, u32[]{:S(2)}) %collective-permute-start.36) | collective-permute-done | bytes 131104 | tf_op jit(solution)/shard_map/ppermute | solution.py:148
  74.9 2.4 %collective-permute-start.7 = (bf16[512,128]{1,0:T(8,128)(2,1)S(1)}, bf16[512,128]{1,0:T(8,128)(2,1)S(1)}, u32[]{:S(2)}, u32[]{:S(2)}) collective-permute-start(bf16[512,128]{1,0:T(8,128)(2,1)S(1)} %fusion.refs_0_), channel_id=1, source_target_pairs={{0,24},{4,28},{8,16},{12,20},{16,8},{20,12},{24,0},{28,4},{1,25},{... | collective-permute-start | bytes 393224 | tf_op jit(solution)/shard_map/ppermute | solution.py:141
  77.3 1.3 bitcast_subtract_fusion
  78.8 2.3 %copy-done.5 = bf16[4,256,2048]{2,1,0:T(8,128)(2,1)S(1)} copy-done((bf16[4,256,2048]{2,1,0:T(8,128)(2,1)S(1)}, bf16[4,256,2048]{2,1,0:T(8,128)(2,1)}, u32[]{:S(2)}) %copy-start.5) | copy-done | bytes 4194328
  81.9 1.3 shard_map.57
  83.9 1.5 %collective-permute-start.11 = (bf16[512,128]{1,0:T(8,128)(2,1)S(1)}, bf16[512,128]{1,0:T(8,128)(2,1)S(1)}, u32[]{:S(2)}, u32[]{:S(2)}) collective-permute-start(bf16[512,128]{1,0:T(8,128)(2,1)S(1)} %get-tuple-element.45.refs_0_), channel_id=1, source_target_pairs={{0,16},{4,20},{8,24},{12,28},{16,0},{20,4},{24,8},{28,12},{1,17},{... | collective-permute-start | bytes 393224 | tf_op jit(solution)/shard_map/ppermute | solution.py:141
  85.4 1.2 collective-permute-start.12
  87.4 1.9 %shard_map.59.matrix_ref = bf16[512,2048]{1,0:T(8,128)(2,1)S(1)} custom-call(s32[6]{0:T(128)S(1)} %pad_add_fusion.place_ref, bf16[6,256,2048]{2,1,0:T(8,128)(2,1)S(1)} %bitcast.23, bf16[6,256,2048]{2,1,0:T(8,128)(2,1)} %collective-permute-done.9.other_ref), custom_call_target="tpu_custom_call" | custom-call | bytes 4194304 | tf_op jit(solution)/shard_map/pallas_call | solution.py:78
  89.6 2.9 %collective-permute-done.11.refs_2_ = bf16[512,128]{1,0:T(8,128)(2,1)S(1)} collective-permute-done((bf16[512,128]{1,0:T(8,128)(2,1)S(1)}, bf16[512,128]{1,0:T(8,128)(2,1)S(1)}, u32[]{:S(2)}, u32[]{:S(2)}) %collective-permute-start.11) | collective-permute-done | bytes 131104 | tf_op jit(solution)/shard_map/ppermute | solution.py:141
  92.5 1.3 shard_map.61.refs_0_
  93.7 1.6 %collective-permute-start.17 = (bf16[512,128]{1,0:T(8,128)(2,1)S(1)}, bf16[512,128]{1,0:T(8,128)(2,1)S(1)}, u32[]{:S(2)}, u32[]{:S(2)}) collective-permute-start(bf16[512,128]{1,0:T(8,128)(2,1)S(1)} %shard_map.61.refs_0_), channel_id=1, source_target_pairs={{0,8},{4,12},{8,0},{12,4},{16,24},{20,28},{24,16},{28,20},{1,9},{5... | collective-permute-start | bytes 393224 | tf_op jit(solution)/shard_map/ppermute | solution.py:141
  95.8 1.5 collective-permute-start.19
  98.0 2.3 %copy-done.2 = bf16[4,256,2048]{2,1,0:T(8,128)(2,1)S(1)} copy-done((bf16[4,256,2048]{2,1,0:T(8,128)(2,1)S(1)}, bf16[4,256,2048]{2,1,0:T(8,128)(2,1)}, u32[]{:S(2)}) %copy-start.2) | copy-done | bytes 4194328
  100.3 2.2 %copy-done.6 = bf16[4,256,2048]{2,1,0:T(8,128)(2,1)S(1)} copy-done((bf16[4,256,2048]{2,1,0:T(8,128)(2,1)S(1)}, bf16[4,256,2048]{2,1,0:T(8,128)(2,1)}, u32[]{:S(2)}) %copy-start.6) | copy-done | bytes 4194328
  103.3 1.2 shard_map.62
  104.5 1.6 %collective-permute-start.21 = (bf16[512,128]{1,0:T(8,128)(2,1)S(1)}, bf16[512,128]{1,0:T(8,128)(2,1)S(1)}, u32[]{:S(2)}, u32[]{:S(2)}) collective-permute-start(bf16[512,128]{1,0:T(8,128)(2,1)S(1)} %get-tuple-element.54.refs_0_), channel_id=1, source_target_pairs={{0,8},{4,12},{8,0},{12,4},{16,24},{20,28},{24,16},{28,20},{1,9},{5... | collective-permute-start | bytes 393224 | tf_op jit(solution)/shard_map/ppermute | solution.py:141
  106.6 1.5 collective-permute-start.23
  108.1 1.2 maximum_select_fusion.4
  109.3 1.9 %shard_map.65.matrix_ref = bf16[512,2048]{1,0:T(8,128)(2,1)S(1)} custom-call(s32[6]{0:T(128)S(1)} %pad_add_fusion.place_ref, bf16[6,256,2048]{2,1,0:T(8,128)(2,1)S(1)} %bitcast.25, bf16[6,256,2048]{2,1,0:T(8,128)(2,1)} %collective-permute-done.9.other_ref), custom_call_target="tpu_custom_call" | custom-call | bytes 4194304 | tf_op jit(solution)/shard_map/pallas_call | solution.py:78
  111.2 2.2 %shard_map.64.matrix_ref = bf16[512,2048]{1,0:T(8,128)(2,1)S(1)} custom-call(s32[6]{0:T(128)S(1)} %pad_add_fusion.place_ref, bf16[6,256,2048]{2,1,0:T(8,128)(2,1)S(1)} %bitcast.25, bf16[6,256,2048]{2,1,0:T(8,128)(2,1)} %collective-permute-done.9.other_ref), custom_call_target="tpu_custom_call" | custom-call | bytes 4194304 | tf_op jit(solution)/shard_map/pallas_call | solution.py:78
  113.4 1.3 shard_map.66.refs_4_
  114.7 1.3 shard_map.67.refs_0_
  115.9 1.6 %collective-permute-start.28 = (bf16[512,128]{1,0:T(8,128)(2,1)S(1)}, bf16[512,128]{1,0:T(8,128)(2,1)S(1)}, u32[]{:S(2)}, u32[]{:S(2)}) collective-permute-start(bf16[512,128]{1,0:T(8,128)(2,1)S(1)} %shard_map.67.refs_0_), channel_id=1, source_target_pairs={{0,8},{4,12},{8,0},{12,4},{16,24},{20,28},{24,16},{28,20},{1,9},{5... | collective-permute-start | bytes 393224 | tf_op jit(solution)/shard_map/ppermute | solution.py:141
  118.0 1.5 collective-permute-start.30
  121.4 3.6 %collective-permute-done.29.refs_2_ = bf16[512,128]{1,0:T(8,128)(2,1)S(1)} collective-permute-done((bf16[512,128]{1,0:T(8,128)(2,1)S(1)}, bf16[512,128]{1,0:T(8,128)(2,1)S(1)}, u32[]{:S(2)}, u32[]{:S(2)}) %collective-permute-start.29) | collective-permute-done | bytes 131104 | tf_op jit(solution)/shard_map/ppermute | solution.py:141
  125.1 1.3 shard_map.68
  127.1 1.1 collective-permute-start.33
  128.3 1.6 %collective-permute-start.34 = (bf16[512,128]{1,0:T(8,128)(2,1)S(1)}, bf16[512,128]{1,0:T(8,128)(2,1)S(1)}, u32[]{:S(2)}, u32[]{:S(2)}) collective-permute-start(bf16[512,128]{1,0:T(8,128)(2,1)S(1)} %get-tuple-element.63.refs_0_), channel_id=1, source_target_pairs={{0,24},{4,28},{8,16},{12,20},{16,8},{20,12},{24,0},{28,4},{1,25},{... | collective-permute-start | bytes 393224 | tf_op jit(solution)/shard_map/ppermute | solution.py:141
  129.9 1.9 %shard_map.72.matrix_ref = bf16[512,2048]{1,0:T(8,128)(2,1)S(1)} custom-call(s32[6]{0:T(128)S(1)} %pad_add_fusion.place_ref, bf16[6,256,2048]{2,1,0:T(8,128)(2,1)S(1)} %bitcast.25, bf16[6,256,2048]{2,1,0:T(8,128)(2,1)} %collective-permute-done.9.other_ref), custom_call_target="tpu_custom_call" | custom-call | bytes 4194304 | tf_op jit(solution)/shard_map/pallas_call | solution.py:78
  131.8 1.9 %shard_map.71.matrix_ref = bf16[512,2048]{1,0:T(8,128)(2,1)S(1)} custom-call(s32[6]{0:T(128)S(1)} %pad_add_fusion.place_ref, bf16[6,256,2048]{2,1,0:T(8,128)(2,1)S(1)} %bitcast.25, bf16[6,256,2048]{2,1,0:T(8,128)(2,1)} %collective-permute-done.9.other_ref), custom_call_target="tpu_custom_call" | custom-call | bytes 4194304 | tf_op jit(solution)/shard_map/pallas_call | solution.py:78
  133.6 1.9 %shard_map.70.matrix_ref = bf16[512,2048]{1,0:T(8,128)(2,1)S(1)} custom-call(s32[6]{0:T(128)S(1)} %pad_add_fusion.place_ref, bf16[6,256,2048]{2,1,0:T(8,128)(2,1)S(1)} %bitcast.25, bf16[6,256,2048]{2,1,0:T(8,128)(2,1)} %collective-permute-done.9.other_ref), custom_call_target="tpu_custom_call" | custom-call | bytes 4194304 | tf_op jit(solution)/shard_map/pallas_call | solution.py:78
  135.5 1.3 shard_map.73.refs_4_
  136.8 1.3 shard_map.74.refs_4_
  138.1 1.3 shard_map.75.refs_0_
  140.1 1.1 collective-permute-start.40
  141.2 1.6 %collective-permute-start.41 = (bf16[512,128]{1,0:T(8,128)(2,1)S(1)}, bf16[512,128]{1,0:T(8,128)(2,1)S(1)}, u32[]{:S(2)}, u32[]{:S(2)}) collective-permute-start(bf16[512,128]{1,0:T(8,128)(2,1)S(1)} %shard_map.75.refs_0_), channel_id=1, source_target_pairs={{0,24},{4,28},{8,16},{12,20},{16,8},{20,12},{24,0},{28,4},{1,25},{... | collective-permute-start | bytes 393224 | tf_op jit(solution)/shard_map/ppermute | solution.py:141
  143.6 0.8 collective-permute-done.39.refs_1_
  145.1 2.0 %collective-permute-done.41.refs_3_ = bf16[512,128]{1,0:T(8,128)(2,1)S(1)} collective-permute-done((bf16[512,128]{1,0:T(8,128)(2,1)S(1)}, bf16[512,128]{1,0:T(8,128)(2,1)S(1)}, u32[]{:S(2)}, u32[]{:S(2)}) %collective-permute-start.41) | collective-permute-done | bytes 131104 | tf_op jit(solution)/shard_map/ppermute | solution.py:141
  147.1 1.2 shard_map.76
  148.5 1.3 collective-permute-done.42
  149.8 1.0 pad_maximum_fusion
  (93 shorter events, 12.6 us)
Async XLA Ops:
  0.0 7.4 %collective-permute-start = (bf16[4,256,2048]{2,1,0:T(8,128)(2,1)}, bf16[4,256,2048]{2,1,0:T(8,128)(2,1)S(1)}, u32[]{:S(2)}, u32[]{:S(2)}) collective-permute-start(bf16[4,256,2048]{2,1,0:T(8,128)(2,1)} %own_ref.10), channel_id=1, source_target_pairs={{0,4},{4,0},{8,12},{12,8},{16,20},{20,16},{24,28},{28,24},{1,5},{5... | collective-permute-start | bytes 12582920 | tf_op jit(solution)/shard_map/ppermute | solution.py:137
  7.5 2.1 %copy-start.4 = (bf16[4,256,2048]{2,1,0:T(8,128)(2,1)}, bf16[4,256,2048]{2,1,0:T(8,128)(2,1)S(1)}, u32[]{:S(2)}) copy-start(bf16[4,256,2048]{2,1,0:T(8,128)(2,1)S(1)} %collective-permute-done.other_ref) | copy-start | bytes 12582916
  9.5 77.9 %collective-permute-start.9 = (bf16[6,256,2048]{2,1,0:T(8,128)(2,1)}, bf16[6,256,2048]{2,1,0:T(8,128)(2,1)}, u32[]{:S(2)}, u32[]{:S(2)}) collective-permute-start(bf16[6,256,2048]{2,1,0:T(8,128)(2,1)} %own_ref.13), channel_id=1, source_target_pairs={{0,4},{4,0},{8,12},{12,8},{16,20},{20,16},{24,28},{28,24},{1,5},{5... | collective-permute-start | bytes 18874376 | tf_op jit(solution)/shard_map/ppermute | solution.py:137
  9.9 3.4 %copy-start = (bf16[4,256,4096]{2,1,0:T(8,128)(2,1)S(1)}, bf16[4,256,4096]{2,1,0:T(8,128)(2,1)}, u32[]{:S(2)}) copy-start(bf16[4,256,4096]{2,1,0:T(8,128)(2,1)} %refs_2_.1) | copy-start | bytes 25165828
  19.4 16.3 %collective-permute-start.1 = (bf16[256,256]{1,0:T(8,128)(2,1)S(1)}, bf16[256,256]{1,0:T(8,128)(2,1)S(1)}, u32[]{:S(2)}, u32[]{:S(2)}) collective-permute-start(bf16[256,256]{1,0:T(8,128)(2,1)S(1)} %get-tuple-element.40), channel_id=1, source_target_pairs={{0,1},{1,2},{2,3},{3,0},{4,5},{5,6},{6,7},{7,4},{8,9},{9,10},{10,1... | collective-permute-start | bytes 393224 | tf_op jit(solution)/shard_map/ppermute | solution.py:148
  22.2 13.6 %collective-permute-start.2 = (bf16[256,256]{1,0:T(8,128)(2,1)S(1)}, bf16[256,256]{1,0:T(8,128)(2,1)S(1)}, u32[]{:S(2)}, u32[]{:S(2)}) collective-permute-start(bf16[256,256]{1,0:T(8,128)(2,1)S(1)} %get-tuple-element.41), channel_id=1, source_target_pairs={{0,2},{1,3},{2,0},{3,1},{4,6},{5,7},{6,4},{7,5},{8,10},{9,11},{10,... | collective-permute-start | bytes 393224 | tf_op jit(solution)/shard_map/ppermute | solution.py:148
  24.8 11.0 %collective-permute-start.3 = (bf16[256,256]{1,0:T(8,128)(2,1)S(1)}, bf16[256,256]{1,0:T(8,128)(2,1)S(1)}, u32[]{:S(2)}, u32[]{:S(2)}) collective-permute-start(bf16[256,256]{1,0:T(8,128)(2,1)S(1)} %get-tuple-element.42), channel_id=1, source_target_pairs={{0,3},{1,0},{2,1},{3,2},{4,7},{5,4},{6,5},{7,6},{8,11},{9,8},{10,9... | collective-permute-start | bytes 393224 | tf_op jit(solution)/shard_map/ppermute | solution.py:148
  35.8 8.3 %collective-permute-start.13 = (bf16[256,256]{1,0:T(8,128)(2,1)S(1)}, bf16[256,256]{1,0:T(8,128)(2,1)S(1)}, u32[]{:S(2)}, u32[]{:S(2)}) collective-permute-start(bf16[256,256]{1,0:T(8,128)(2,1)S(1)} %get-tuple-element.50), channel_id=1, source_target_pairs={{0,1},{1,2},{2,3},{3,0},{4,5},{5,6},{6,7},{7,4},{8,9},{9,10},{10,1... | collective-permute-start | bytes 393224 | tf_op jit(solution)/shard_map/ppermute | solution.py:148
  37.3 11.0 %collective-permute-start.14 = (bf16[256,256]{1,0:T(8,128)(2,1)S(1)}, bf16[256,256]{1,0:T(8,128)(2,1)S(1)}, u32[]{:S(2)}, u32[]{:S(2)}) collective-permute-start(bf16[256,256]{1,0:T(8,128)(2,1)S(1)} %get-tuple-element.51), channel_id=1, source_target_pairs={{0,2},{1,3},{2,0},{3,1},{4,6},{5,7},{6,4},{7,5},{8,10},{9,11},{10,... | collective-permute-start | bytes 393224 | tf_op jit(solution)/shard_map/ppermute | solution.py:148
  38.9 9.4 %collective-permute-start.15 = (bf16[256,256]{1,0:T(8,128)(2,1)S(1)}, bf16[256,256]{1,0:T(8,128)(2,1)S(1)}, u32[]{:S(2)}, u32[]{:S(2)}) collective-permute-start(bf16[256,256]{1,0:T(8,128)(2,1)S(1)} %get-tuple-element.52), channel_id=1, source_target_pairs={{0,3},{1,0},{2,1},{3,2},{4,7},{5,4},{6,5},{7,6},{8,11},{9,8},{10,9... | collective-permute-start | bytes 393224 | tf_op jit(solution)/shard_map/ppermute | solution.py:148
  48.3 8.1 %collective-permute-start.24 = (bf16[256,256]{1,0:T(8,128)(2,1)S(1)}, bf16[256,256]{1,0:T(8,128)(2,1)S(1)}, u32[]{:S(2)}, u32[]{:S(2)}) collective-permute-start(bf16[256,256]{1,0:T(8,128)(2,1)S(1)} %get-tuple-element.59), channel_id=1, source_target_pairs={{0,1},{1,2},{2,3},{3,0},{4,5},{5,6},{6,7},{7,4},{8,9},{9,10},{10,1... | collective-permute-start | bytes 393224 | tf_op jit(solution)/shard_map/ppermute | solution.py:148
  51.6 9.6 %collective-permute-start.25 = (bf16[256,256]{1,0:T(8,128)(2,1)S(1)}, bf16[256,256]{1,0:T(8,128)(2,1)S(1)}, u32[]{:S(2)}, u32[]{:S(2)}) collective-permute-start(bf16[256,256]{1,0:T(8,128)(2,1)S(1)} %get-tuple-element.60), channel_id=1, source_target_pairs={{0,2},{1,3},{2,0},{3,1},{4,6},{5,7},{6,4},{7,5},{8,10},{9,11},{10,... | collective-permute-start | bytes 393224 | tf_op jit(solution)/shard_map/ppermute | solution.py:148
  52.3 8.8 %collective-permute-start.26 = (bf16[256,256]{1,0:T(8,128)(2,1)S(1)}, bf16[256,256]{1,0:T(8,128)(2,1)S(1)}, u32[]{:S(2)}, u32[]{:S(2)}) collective-permute-start(bf16[256,256]{1,0:T(8,128)(2,1)S(1)} %get-tuple-element.61), channel_id=1, source_target_pairs={{0,3},{1,0},{2,1},{3,2},{4,7},{5,4},{6,5},{7,6},{8,11},{9,8},{10,9... | collective-permute-start | bytes 393224 | tf_op jit(solution)/shard_map/ppermute | solution.py:148
  55.0 11.9 %collective-permute-start.4 = (bf16[256,128]{1,0:T(8,128)(2,1)S(1)}, bf16[256,128]{1,0:T(8,128)(2,1)S(1)}, u32[]{:S(2)}, u32[]{:S(2)}) collective-permute-start(bf16[256,128]{1,0:T(8,128)(2,1)S(1)} %get-tuple-element.89), channel_id=1, source_target_pairs={{0,4},{4,0},{8,12},{12,8},{16,20},{20,16},{24,28},{28,24},{1,5},{5... | collective-permute-start | bytes 196616 | tf_op jit(solution)/shard_map/ppermute | solution.py:137
  61.1 9.4 %collective-permute-start.35 = (bf16[256,256]{1,0:T(8,128)(2,1)S(1)}, bf16[256,256]{1,0:T(8,128)(2,1)S(1)}, u32[]{:S(2)}, u32[]{:S(2)}) collective-permute-start(bf16[256,256]{1,0:T(8,128)(2,1)S(1)} %get-tuple-element.68), channel_id=1, source_target_pairs={{0,1},{1,2},{2,3},{3,0},{4,5},{5,6},{6,7},{7,4},{8,9},{9,10},{10,1... | collective-permute-start | bytes 393224 | tf_op jit(solution)/shard_map/ppermute | solution.py:148
  64.4 10.5 %collective-permute-start.36 = (bf16[256,256]{1,0:T(8,128)(2,1)S(1)}, bf16[256,256]{1,0:T(8,128)(2,1)S(1)}, u32[]{:S(2)}, u32[]{:S(2)}) collective-permute-start(bf16[256,256]{1,0:T(8,128)(2,1)S(1)} %get-tuple-element.69), channel_id=1, source_target_pairs={{0,2},{1,3},{2,0},{3,1},{4,6},{5,7},{6,4},{7,5},{8,10},{9,11},{10,... | collective-permute-start | bytes 393224 | tf_op jit(solution)/shard_map/ppermute | solution.py:148
  66.6 10.7 %collective-permute-start.37 = (bf16[256,256]{1,0:T(8,128)(2,1)S(1)}, bf16[256,256]{1,0:T(8,128)(2,1)S(1)}, u32[]{:S(2)}, u32[]{:S(2)}) collective-permute-start(bf16[256,256]{1,0:T(8,128)(2,1)S(1)} %get-tuple-element.70), channel_id=1, source_target_pairs={{0,3},{1,0},{2,1},{3,2},{4,7},{5,4},{6,5},{7,6},{8,11},{9,8},{10,9... | collective-permute-start | bytes 393224 | tf_op jit(solution)/shard_map/ppermute | solution.py:148
  66.9 11.9 %copy-start.1 = (bf16[4,256,2048]{2,1,0:T(8,128)(2,1)S(1)}, bf16[4,256,2048]{2,1,0:T(8,128)(2,1)}, u32[]{:S(2)}) copy-start(bf16[4,256,2048]{2,1,0:T(8,128)(2,1)} %own_ref.10) | copy-start | bytes 12582916
  66.9 15.0 %collective-permute-start.5 = (bf16[512,128]{1,0:T(8,128)(2,1)S(1)}, bf16[512,128]{1,0:T(8,128)(2,1)S(1)}, u32[]{:S(2)}, u32[]{:S(2)}) collective-permute-start(bf16[512,128]{1,0:T(8,128)(2,1)S(1)} %fusion.refs_0_), channel_id=1, source_target_pairs={{0,8},{4,12},{8,0},{12,4},{16,24},{20,28},{24,16},{28,20},{1,9},{5... | collective-permute-start | bytes 393224 | tf_op jit(solution)/shard_map/ppermute | solution.py:141
  70.5 11.4 %collective-permute-start.6 = (bf16[512,128]{1,0:T(8,128)(2,1)S(1)}, bf16[512,128]{1,0:T(8,128)(2,1)S(1)}, u32[]{:S(2)}, u32[]{:S(2)}) collective-permute-start(bf16[512,128]{1,0:T(8,128)(2,1)S(1)} %fusion.refs_0_), channel_id=1, source_target_pairs={{0,16},{4,20},{8,24},{12,28},{16,0},{20,4},{24,8},{28,12},{1,17},{... | collective-permute-start | bytes 393224 | tf_op jit(solution)/shard_map/ppermute | solution.py:141
  74.9 7.0 %collective-permute-start.7 = (bf16[512,128]{1,0:T(8,128)(2,1)S(1)}, bf16[512,128]{1,0:T(8,128)(2,1)S(1)}, u32[]{:S(2)}, u32[]{:S(2)}) collective-permute-start(bf16[512,128]{1,0:T(8,128)(2,1)S(1)} %fusion.refs_0_), channel_id=1, source_target_pairs={{0,24},{4,28},{8,16},{12,20},{16,8},{20,12},{24,0},{28,4},{1,25},{... | collective-permute-start | bytes 393224 | tf_op jit(solution)/shard_map/ppermute | solution.py:141
  78.7 8.7 %slice-start = ((s8[6291456]{0:T(1024)(128)(4,1)}), s8[4194304]{0:T(1024)(128)(4,1)S(1)}, s32[]{:S(2)}) async-start(s8[6291456]{0:T(1024)(128)(4,1)} %bitcast.22), calls=%async_computation | async-start | bytes 8388608
  78.7 8.7 %slice-start.1 = ((s8[6291456]{0:T(1024)(128)(4,1)}), s8[2097152]{0:T(1024)(128)(4,1)S(1)}, s32[]{:S(2)}) async-start(s8[6291456]{0:T(1024)(128)(4,1)} %bitcast.22), calls=%async_computation.1 | async-start | bytes 4194304
  78.7 8.7 %collective-permute-start.16 = (f32[256,128]{1,0:T(8,128)S(1)}, f32[256,128]{1,0:T(8,128)S(1)}, u32[]{:S(2)}, u32[]{:S(2)}) collective-permute-start(f32[256,128]{1,0:T(8,128)S(1)} %get-tuple-element.87), channel_id=1, source_target_pairs={{0,4},{4,0},{8,12},{12,8},{16,20},{20,16},{24,28},{28,24},{1,5},{5... | collective-permute-start | bytes 393224 | tf_op jit(solution)/shard_map/ppermute | solution.py:137
  78.8 2.3 %copy-start.5 = (bf16[4,256,2048]{2,1,0:T(8,128)(2,1)S(1)}, bf16[4,256,2048]{2,1,0:T(8,128)(2,1)}, u32[]{:S(2)}) copy-start(bf16[4,256,2048]{2,1,0:T(8,128)(2,1)} %copy-done.4) | copy-start | bytes 12582916
  83.1 6.4 %collective-permute-start.10 = (bf16[512,128]{1,0:T(8,128)(2,1)S(1)}, bf16[512,128]{1,0:T(8,128)(2,1)S(1)}, u32[]{:S(2)}, u32[]{:S(2)}) collective-permute-start(bf16[512,128]{1,0:T(8,128)(2,1)S(1)} %get-tuple-element.45.refs_0_), channel_id=1, source_target_pairs={{0,8},{4,12},{8,0},{12,4},{16,24},{20,28},{24,16},{28,20},{1,9},{5... | collective-permute-start | bytes 393224 | tf_op jit(solution)/shard_map/ppermute | solution.py:141
  83.9 8.5 %collective-permute-start.11 = (bf16[512,128]{1,0:T(8,128)(2,1)S(1)}, bf16[512,128]{1,0:T(8,128)(2,1)S(1)}, u32[]{:S(2)}, u32[]{:S(2)}) collective-permute-start(bf16[512,128]{1,0:T(8,128)(2,1)S(1)} %get-tuple-element.45.refs_0_), channel_id=1, source_target_pairs={{0,16},{4,20},{8,24},{12,28},{16,0},{20,4},{24,8},{28,12},{1,17},{... | collective-permute-start | bytes 393224 | tf_op jit(solution)/shard_map/ppermute | solution.py:141
  85.4 7.0 %collective-permute-start.12 = (bf16[512,128]{1,0:T(8,128)(2,1)S(1)}, bf16[512,128]{1,0:T(8,128)(2,1)S(1)}, u32[]{:S(2)}, u32[]{:S(2)}) collective-permute-start(bf16[512,128]{1,0:T(8,128)(2,1)S(1)} %get-tuple-element.45.refs_0_), channel_id=1, source_target_pairs={{0,24},{4,28},{8,16},{12,20},{16,8},{20,12},{24,0},{28,4},{1,25},{... | collective-permute-start | bytes 393224 | tf_op jit(solution)/shard_map/ppermute | solution.py:141
  87.4 20.7 %collective-permute-start.27 = (f32[256,128]{1,0:T(8,128)}, f32[256,128]{1,0:T(8,128)}, u32[]{:S(2)}, u32[]{:S(2)}) collective-permute-start(f32[256,128]{1,0:T(8,128)} %get-tuple-element.85), channel_id=1, source_target_pairs={{0,4},{4,0},{8,12},{12,8},{16,20},{20,16},{24,28},{28,24},{1,5},{5... | collective-permute-start | bytes 393224 | tf_op jit(solution)/shard_map/ppermute | solution.py:137
  93.7 9.5 %collective-permute-start.17 = (bf16[512,128]{1,0:T(8,128)(2,1)S(1)}, bf16[512,128]{1,0:T(8,128)(2,1)S(1)}, u32[]{:S(2)}, u32[]{:S(2)}) collective-permute-start(bf16[512,128]{1,0:T(8,128)(2,1)S(1)} %shard_map.61.refs_0_), channel_id=1, source_target_pairs={{0,8},{4,12},{8,0},{12,4},{16,24},{20,28},{24,16},{28,20},{1,9},{5... | collective-permute-start | bytes 393224 | tf_op jit(solution)/shard_map/ppermute | solution.py:141
  95.3 8.0 %collective-permute-start.18 = (bf16[512,128]{1,0:T(8,128)(2,1)S(1)}, bf16[512,128]{1,0:T(8,128)(2,1)S(1)}, u32[]{:S(2)}, u32[]{:S(2)}) collective-permute-start(bf16[512,128]{1,0:T(8,128)(2,1)S(1)} %shard_map.61.refs_0_), channel_id=1, source_target_pairs={{0,16},{4,20},{8,24},{12,28},{16,0},{20,4},{24,8},{28,12},{1,17},{... | collective-permute-start | bytes 393224 | tf_op jit(solution)/shard_map/ppermute | solution.py:141
  95.8 7.5 %collective-permute-start.19 = (bf16[512,128]{1,0:T(8,128)(2,1)S(1)}, bf16[512,128]{1,0:T(8,128)(2,1)S(1)}, u32[]{:S(2)}, u32[]{:S(2)}) collective-permute-start(bf16[512,128]{1,0:T(8,128)(2,1)S(1)} %shard_map.61.refs_0_), channel_id=1, source_target_pairs={{0,24},{4,28},{8,16},{12,20},{16,8},{20,12},{24,0},{28,4},{1,25},{... | collective-permute-start | bytes 393224 | tf_op jit(solution)/shard_map/ppermute | solution.py:141
  98.0 10.1 %collective-permute-start.38 = (f32[256,128]{1,0:T(8,128)}, f32[256,128]{1,0:T(8,128)}, u32[]{:S(2)}, u32[]{:S(2)}) collective-permute-start(f32[256,128]{1,0:T(8,128)} %get-tuple-element.83), channel_id=1, source_target_pairs={{0,4},{4,0},{8,12},{12,8},{16,20},{20,16},{24,28},{28,24},{1,5},{5... | collective-permute-start | bytes 393224 | tf_op jit(solution)/shard_map/ppermute | solution.py:137
  98.0 11.3 %slice-start.2 = ((s8[6291456]{0:T(1024)(128)(4,1)}), s8[2097152]{0:T(1024)(128)(4,1)S(1)}, s32[]{:S(2)}) async-start(s8[6291456]{0:T(1024)(128)(4,1)} %bitcast.24), calls=%async_computation.2 | async-start | bytes 4194304
  98.0 2.3 %copy-start.2 = (bf16[4,256,2048]{2,1,0:T(8,128)(2,1)S(1)}, bf16[4,256,2048]{2,1,0:T(8,128)(2,1)}, u32[]{:S(2)}) copy-start(bf16[4,256,2048]{2,1,0:T(8,128)(2,1)} %own_ref.10) | copy-start | bytes 12582916
  100.3 2.2 %copy-start.6 = (bf16[4,256,2048]{2,1,0:T(8,128)(2,1)S(1)}, bf16[4,256,2048]{2,1,0:T(8,128)(2,1)}, u32[]{:S(2)}) copy-start(bf16[4,256,2048]{2,1,0:T(8,128)(2,1)} %copy-done.4) | copy-start | bytes 12582916
  102.5 6.7 %slice-start.3 = ((s8[6291456]{0:T(1024)(128)(4,1)}), s8[4194304]{0:T(1024)(128)(4,1)S(1)}, s32[]{:S(2)}) async-start(s8[6291456]{0:T(1024)(128)(4,1)} %bitcast.24), calls=%async_computation.3 | async-start | bytes 8388608
  103.2 4.9 %copy-start.8 = (f32[256,128]{1,0:T(8,128)S(1)}, f32[256,128]{1,0:T(8,128)}, u32[]{:S(2)}) copy-start(f32[256,128]{1,0:T(8,128)} %get-tuple-element.82) | copy-start | bytes 393220
  104.5 10.1 %collective-permute-start.21 = (bf16[512,128]{1,0:T(8,128)(2,1)S(1)}, bf16[512,128]{1,0:T(8,128)(2,1)S(1)}, u32[]{:S(2)}, u32[]{:S(2)}) collective-permute-start(bf16[512,128]{1,0:T(8,128)(2,1)S(1)} %get-tuple-element.54.refs_0_), channel_id=1, source_target_pairs={{0,8},{4,12},{8,0},{12,4},{16,24},{20,28},{24,16},{28,20},{1,9},{5... | collective-permute-start | bytes 393224 | tf_op jit(solution)/shard_map/ppermute | solution.py:141
  106.1 8.5 %collective-permute-start.22 = (bf16[512,128]{1,0:T(8,128)(2,1)S(1)}, bf16[512,128]{1,0:T(8,128)(2,1)S(1)}, u32[]{:S(2)}, u32[]{:S(2)}) collective-permute-start(bf16[512,128]{1,0:T(8,128)(2,1)S(1)} %get-tuple-element.54.refs_0_), channel_id=1, source_target_pairs={{0,16},{4,20},{8,24},{12,28},{16,0},{20,4},{24,8},{28,12},{1,17},{... | collective-permute-start | bytes 393224 | tf_op jit(solution)/shard_map/ppermute | solution.py:141
  106.6 8.0 %collective-permute-start.23 = (bf16[512,128]{1,0:T(8,128)(2,1)S(1)}, bf16[512,128]{1,0:T(8,128)(2,1)S(1)}, u32[]{:S(2)}, u32[]{:S(2)}) collective-permute-start(bf16[512,128]{1,0:T(8,128)(2,1)S(1)} %get-tuple-element.54.refs_0_), channel_id=1, source_target_pairs={{0,24},{4,28},{8,16},{12,20},{16,8},{20,12},{24,0},{28,4},{1,25},{... | collective-permute-start | bytes 393224 | tf_op jit(solution)/shard_map/ppermute | solution.py:141
  111.2 8.4 %copy-start.7 = (bf16[4,256,2048]{2,1,0:T(8,128)(2,1)S(1)}, bf16[4,256,2048]{2,1,0:T(8,128)(2,1)}, u32[]{:S(2)}) copy-start(bf16[4,256,2048]{2,1,0:T(8,128)(2,1)} %copy-done.4) | copy-start | bytes 12582916
  113.3 6.2 %copy-start.3 = (bf16[4,256,2048]{2,1,0:T(8,128)(2,1)S(1)}, bf16[4,256,2048]{2,1,0:T(8,128)(2,1)}, u32[]{:S(2)}) copy-start(bf16[4,256,2048]{2,1,0:T(8,128)(2,1)} %own_ref.10) | copy-start | bytes 12582916
  115.9 5.5 %collective-permute-start.28 = (bf16[512,128]{1,0:T(8,128)(2,1)S(1)}, bf16[512,128]{1,0:T(8,128)(2,1)S(1)}, u32[]{:S(2)}, u32[]{:S(2)}) collective-permute-start(bf16[512,128]{1,0:T(8,128)(2,1)S(1)} %shard_map.67.refs_0_), channel_id=1, source_target_pairs={{0,8},{4,12},{8,0},{12,4},{16,24},{20,28},{24,16},{28,20},{1,9},{5... | collective-permute-start | bytes 393224 | tf_op jit(solution)/shard_map/ppermute | solution.py:141
  117.5 7.6 %collective-permute-start.29 = (bf16[512,128]{1,0:T(8,128)(2,1)S(1)}, bf16[512,128]{1,0:T(8,128)(2,1)S(1)}, u32[]{:S(2)}, u32[]{:S(2)}) collective-permute-start(bf16[512,128]{1,0:T(8,128)(2,1)S(1)} %shard_map.67.refs_0_), channel_id=1, source_target_pairs={{0,16},{4,20},{8,24},{12,28},{16,0},{20,4},{24,8},{28,12},{1,17},{... | collective-permute-start | bytes 393224 | tf_op jit(solution)/shard_map/ppermute | solution.py:141
  118.0 7.1 %collective-permute-start.30 = (bf16[512,128]{1,0:T(8,128)(2,1)S(1)}, bf16[512,128]{1,0:T(8,128)(2,1)S(1)}, u32[]{:S(2)}, u32[]{:S(2)}) collective-permute-start(bf16[512,128]{1,0:T(8,128)(2,1)S(1)} %shard_map.67.refs_0_), channel_id=1, source_target_pairs={{0,24},{4,28},{8,16},{12,20},{16,8},{20,12},{24,0},{28,4},{1,25},{... | collective-permute-start | bytes 393224 | tf_op jit(solution)/shard_map/ppermute | solution.py:141
  119.5 10.4 %collective-permute-start.8 = (f32[256,128]{1,0:T(8,128)S(1)}, f32[256,128]{1,0:T(8,128)S(1)}, u32[]{:S(2)}, u32[]{:S(2)}) collective-permute-start(f32[256,128]{1,0:T(8,128)S(1)} %get-tuple-element.75), channel_id=1, source_target_pairs={{0,4},{4,0},{8,12},{12,8},{16,20},{20,16},{24,28},{28,24},{1,5},{5... | collective-permute-start | bytes 393224 | tf_op jit(solution)/shard_map/ppermute | solution.py:137
  126.3 11.7 %collective-permute-start.32 = (bf16[512,128]{1,0:T(8,128)(2,1)S(1)}, bf16[512,128]{1,0:T(8,128)(2,1)S(1)}, u32[]{:S(2)}, u32[]{:S(2)}) collective-permute-start(bf16[512,128]{1,0:T(8,128)(2,1)S(1)} %get-tuple-element.63.refs_0_), channel_id=1, source_target_pairs={{0,8},{4,12},{8,0},{12,4},{16,24},{20,28},{24,16},{28,20},{1,9},{5... | collective-permute-start | bytes 393224 | tf_op jit(solution)/shard_map/ppermute | solution.py:141
  127.1 10.9 %collective-permute-start.33 = (bf16[512,128]{1,0:T(8,128)(2,1)S(1)}, bf16[512,128]{1,0:T(8,128)(2,1)S(1)}, u32[]{:S(2)}, u32[]{:S(2)}) collective-permute-start(bf16[512,128]{1,0:T(8,128)(2,1)S(1)} %get-tuple-element.63.refs_0_), channel_id=1, source_target_pairs={{0,16},{4,20},{8,24},{12,28},{16,0},{20,4},{24,8},{28,12},{1,17},{... | collective-permute-start | bytes 393224 | tf_op jit(solution)/shard_map/ppermute | solution.py:141
  128.3 9.8 %collective-permute-start.34 = (bf16[512,128]{1,0:T(8,128)(2,1)S(1)}, bf16[512,128]{1,0:T(8,128)(2,1)S(1)}, u32[]{:S(2)}, u32[]{:S(2)}) collective-permute-start(bf16[512,128]{1,0:T(8,128)(2,1)S(1)} %get-tuple-element.63.refs_0_), channel_id=1, source_target_pairs={{0,24},{4,28},{8,16},{12,20},{16,8},{20,12},{24,0},{28,4},{1,25},{... | collective-permute-start | bytes 393224 | tf_op jit(solution)/shard_map/ppermute | solution.py:141
  139.3 5.0 %collective-permute-start.39 = (bf16[512,128]{1,0:T(8,128)(2,1)S(1)}, bf16[512,128]{1,0:T(8,128)(2,1)S(1)}, u32[]{:S(2)}, u32[]{:S(2)}) collective-permute-start(bf16[512,128]{1,0:T(8,128)(2,1)S(1)} %shard_map.75.refs_0_), channel_id=1, source_target_pairs={{0,8},{4,12},{8,0},{12,4},{16,24},{20,28},{24,16},{28,20},{1,9},{5... | collective-permute-start | bytes 393224 | tf_op jit(solution)/shard_map/ppermute | solution.py:141
  140.1 5.0 %collective-permute-start.40 = (bf16[512,128]{1,0:T(8,128)(2,1)S(1)}, bf16[512,128]{1,0:T(8,128)(2,1)S(1)}, u32[]{:S(2)}, u32[]{:S(2)}) collective-permute-start(bf16[512,128]{1,0:T(8,128)(2,1)S(1)} %shard_map.75.refs_0_), channel_id=1, source_target_pairs={{0,16},{4,20},{8,24},{12,28},{16,0},{20,4},{24,8},{28,12},{1,17},{... | collective-permute-start | bytes 393224 | tf_op jit(solution)/shard_map/ppermute | solution.py:141
  141.2 5.9 %collective-permute-start.41 = (bf16[512,128]{1,0:T(8,128)(2,1)S(1)}, bf16[512,128]{1,0:T(8,128)(2,1)S(1)}, u32[]{:S(2)}, u32[]{:S(2)}) collective-permute-start(bf16[512,128]{1,0:T(8,128)(2,1)S(1)} %shard_map.75.refs_0_), channel_id=1, source_target_pairs={{0,24},{4,28},{8,16},{12,20},{16,8},{20,12},{24,0},{28,4},{1,25},{... | collective-permute-start | bytes 393224 | tf_op jit(solution)/shard_map/ppermute | solution.py:141
  142.9 5.6 %collective-permute-start.20 = (f32[256,128]{1,0:T(8,128)S(1)}, f32[256,128]{1,0:T(8,128)S(1)}, u32[]{:S(2)}, u32[]{:S(2)}) collective-permute-start(f32[256,128]{1,0:T(8,128)S(1)} %get-tuple-element.77), channel_id=1, source_target_pairs={{0,4},{4,0},{8,12},{12,8},{16,20},{20,16},{24,28},{28,24},{1,5},{5... | collective-permute-start | bytes 393224 | tf_op jit(solution)/shard_map/ppermute | solution.py:137
  143.0 5.5 %collective-permute-start.31 = (f32[256,128]{1,0:T(8,128)S(1)}, f32[256,128]{1,0:T(8,128)S(1)}, u32[]{:S(2)}, u32[]{:S(2)}) collective-permute-start(f32[256,128]{1,0:T(8,128)S(1)} %get-tuple-element.79), channel_id=1, source_target_pairs={{0,4},{4,0},{8,12},{12,8},{16,20},{20,16},{24,28},{28,24},{1,5},{5... | collective-permute-start | bytes 393224 | tf_op jit(solution)/shard_map/ppermute | solution.py:137
  148.4 1.4 collective-permute-start.42

commit v3 on v0

v3 whole, which is shorter than its diff:
```python
import functools

import jax
import jax.numpy as jnp
from jax import lax
from jax.experimental import pallas as pl
from jax.experimental.pallas import tpu as pltpu
from jax.sharding import PartitionSpec as P

F32, BF16 = jnp.float32, jnp.bfloat16
VMEM = pl.BlockSpec(memory_space=pltpu.VMEM)
HBM = pl.BlockSpec(memory_space=pltpu.HBM)
SMALL = pl.CostEstimate(flops=1024, bytes_accessed=1024, transcendentals=0)


def inner_index(target, earlier):
    return target * (target - 1) // 2 + earlier


def params(mebibytes):
    return pltpu.CompilerParams(vmem_limit_bytes=mebibytes << 20)


def work(rows, depth, columns):
    return pl.CostEstimate(
        flops=2 * rows * depth * columns,
        bytes_accessed=2 * (rows + columns) * depth,
        transcendentals=0,
    )


def accumulate(total, piece, part, there=slice(None)):
    if piece == 0:
        total[:, there] = part
    else:
        total[:, there] += part


def first_kernel(shifts, pieces, l_ref, x_ref, *refs):
    count = len(shifts)
    outs, (l_buf, x_buf, total, l_sems, x_sems) = refs[:count], refs[count:]
    deep = x_ref.shape[0] // pieces
    width = x_ref.shape[1] // count
    mine = lax.axis_index("col")
    l_copies, x_copies = [], []
    for piece in range(pieces):
        cut = pl.ds(piece * deep, deep)
        l_copies.append(
            pltpu.make_async_copy(l_ref.at[0, :, cut], l_buf.at[piece], l_sems.at[piece])
        )
        x_copies.append(pltpu.make_async_copy(x_ref.at[cut], x_buf.at[piece], x_sems.at[piece]))
    for piece in range(pieces):
        l_copies[piece].start()
        x_copies[piece].start()
    for piece in range(pieces):
        l_copies[piece].wait()
        x_copies[piece].wait()
        accumulate(
            total, piece, jnp.dot(l_buf[piece], x_buf[piece], preferred_element_type=F32)
        )
    for shift, out in zip(shifts, outs):
        begin = pl.multiple_of(lax.rem(mine + shift, count) * width, width)
        out[...] = total[:, pl.ds(begin, width)].astype(out.dtype)


def second_kernel(shifts, pieces, flight, l_ref, x_ref, *refs):
    count = len(shifts)
    rows, depth = l_ref.shape[1:]
    blocks = l_ref.shape[0] - 1
    outs, refs = refs[: blocks * count], refs[blocks * count :]
    l_buf, x_buf, total, sent, kept, l_sems, x_sems, out_sems = refs
    deep = depth // pieces
    width = x_ref.shape[1] // count
    mine = lax.axis_index("col")
    copies = []
    for piece in range(pieces):
        cut = pl.ds(piece * deep, deep)
        copies.append(
            [
                pltpu.make_async_copy(
                    l_ref.at[block + 1, :, cut],
                    l_buf.at[piece, pl.ds(block * rows, rows)],
                    l_sems.at[piece, block],
                )
                for block in range(blocks)
            ]
            + [pltpu.make_async_copy(x_ref.at[cut], x_buf.at[piece], x_sems.at[piece])]
        )
    for row in copies[:flight]:
        for copy in row:
            copy.start()
    for piece in range(pieces):
        for copy in copies[piece]:
            copy.wait()
        if piece + flight < pieces:
            for copy in copies[piece + flight]:
                copy.start()
        accumulate(
            total, piece, jnp.dot(l_buf[piece], x_buf[piece], preferred_element_type=F32)
        )
    copies = []
    for block in range(blocks):
        for k, shift in enumerate(shifts):
            begin = pl.multiple_of(lax.rem(mine + shift, count) * width, width)
            found = total[block * rows : (block + 1) * rows, pl.ds(begin, width)]
            held = sent.at[block, k] if shift else kept.at[block]
            held[...] = found.astype(held.dtype)
            copy = pltpu.make_async_copy(held, outs[block * count + k], out_sems.at[block, k])
            copy.start()
            copies.append(copy)
    for copy in copies:
        copy.wait()


def load_kernel(indices, *refs):
    count = len(refs) // 2
    ins, outs, sems = refs[:count], refs[count:-1], refs[-1]
    copies = [
        pltpu.make_async_copy(ref.at[index], out.at[place], sems.at[k, place])
        for k, (ref, out) in enumerate(zip(ins, outs))
        for place, index in enumerate(indices)
    ]
    for copy in copies:
        copy.start()
    for copy in copies:
        copy.wait()


def load(arrays, indices):
    shapes = [
        jax.ShapeDtypeStruct((len(indices), *array.shape[1:]), array.dtype) for array in arrays
    ]
    return pl.pallas_call(
        functools.partial(load_kernel, tuple(indices)),
        in_specs=[HBM] * len(arrays),
        out_specs=[VMEM] * len(arrays),
        out_shape=shapes,
        scratch_shapes=[pltpu.SemaphoreType.DMA((len(arrays), len(indices)))],
        compiler_params=params(16),
        cost_estimate=SMALL,
    )(*arrays)


def reduce_kernel(parts, rhs_ref, own_ref, *refs):
    arrived, refs = refs[:parts], refs[parts:]
    taken, (kept_ref, other_ref) = refs[:-2], refs[-2:]
    total = rhs_ref[...] - own_ref[...]
    for ref in arrived:
        total -= ref[...].astype(F32)
    half = total.shape[1] // 2
    first = lax.rem(lax.axis_index("row"), 2) == 0
    kept = jnp.where(first, total[:, :half], total[:, half:])
    other = jnp.where(first, total[:, half:], total[:, :half])
    for k in range(0, len(taken), 2):
        kept -= taken[k][...]
        other -= taken[k + 1][...]
    kept_ref[...] = kept.astype(kept_ref.dtype)
    other_ref[...] = other.astype(other_ref.dtype)


def reduce_rows(rhs, target, own, arrived, taken, dtype):
    _, rows, width = rhs.shape
    taken = [part for pair in taken for part in pair]
    return pl.pallas_call(
        functools.partial(reduce_kernel, len(arrived)),
        grid=(1,),
        in_specs=[pl.BlockSpec((None, rows, width), lambda i: (target, 0, 0))]
        + [VMEM] * (1 + len(arrived) + len(taken)),
        out_specs=[VMEM, VMEM],
        out_shape=[jax.ShapeDtypeStruct((rows, width // 2), dtype)] * 2,
        compiler_params=params(8),
        cost_estimate=SMALL,
    )(rhs, own, *arrived, *taken)


def apply_kernel(index, parts, pairs, exact, full, own_ref, other_ref, *refs):
    shards, refs = refs[:parts], refs[parts:]
    held, outs = refs[: 2 * pairs], list(refs[2 * pairs :])
    me = lax.axis_index("row")
    core, chip = lax.rem(me, 2), me // 2
    rows = own_ref.shape[1]
    high, width = shards[0].shape
    low_ref = outs.pop()
    full_ref = outs.pop() if full else None
    total = jnp.zeros((high, width), F32)
    for mask, shard in enumerate(shards):
        cut = pl.ds(pl.multiple_of((chip ^ mask) * high, high), high)
        both = jnp.concatenate([own_ref[index, :, cut], other_ref[index, :, cut]], axis=0)
        total += jnp.dot(both, shard[...], preferred_element_type=F32)
        if full:
            full_ref[cut, :] = shard[...]
    for half, place in ((0, core), (1, 1 - core)):
        found = total[half * rows : (half + 1) * rows]
        if pairs:
            found = held[half][...] - found
        if exact:
            outs[half][...] = found
        there = pl.ds(pl.multiple_of(place * rows, rows), rows)
        low_ref[there, :] = found.astype(BF16)


def apply_rows(matrices, index, shards, held, exact, full):
    _, rows, depth = matrices[0].shape
    high, width = shards[0].shape
    operands = [*matrices, *shards, *held]
    shapes = [jax.ShapeDtypeStruct((rows, width), F32)] * (2 * exact)
    shapes += [jax.ShapeDtypeStruct((depth, width), BF16)] * full
    shapes.append(jax.ShapeDtypeStruct((high, width), BF16))
    return pl.pallas_call(
        functools.partial(apply_kernel, index, len(shards), len(held) // 2, exact, full),
        in_specs=[VMEM] * len(operands),
        out_specs=[VMEM] * len(shapes),
        out_shape=shapes,
        compiler_params=params(8),
        cost_estimate=SMALL,
    )(*operands)


def rows_kernel(places, matrix_ref, kept_ref, other_ref, *outs):
    for k, place in enumerate(places):
        for ref, out in zip((kept_ref, other_ref), outs[2 * k : 2 * k + 2]):
            out[...] = jnp.dot(matrix_ref[place], ref[...], preferred_element_type=F32)


def own_rows(matrices, places, kept, other):
    _, rows, _ = matrices.shape
    found = pl.pallas_call(
        functools.partial(rows_kernel, places),
        in_specs=[VMEM] * 3,
        out_specs=[VMEM] * (2 * len(places)),
        out_shape=[jax.ShapeDtypeStruct((rows, kept.shape[1]), F32)] * (2 * len(places)),
        compiler_params=params(8),
        cost_estimate=SMALL,
    )(matrices, kept, other)
    return [found[2 * k : 2 * k + 2] for k in range(len(places))]


def after(value, token):
    return lax.optimization_barrier((value, token))[0]


def local(rhs, l_panel, x_solved, diag_inv, l_inner, row_count, col_count):
    steps, rows, depth = l_panel.shape
    width = rhs.shape[2]
    total = x_solved.shape[1]
    chips = row_count // 2
    core = lax.axis_index("row") % 2
    pieces = 4
    shifts = sorted(range(1, col_count), key=lambda s: (abs(2 * s - col_count), s)) + [0]
    near = [inner_index(target, target - 1) for target in range(1, steps)]
    far = [inner_index(target, earlier) for target in range(2, steps) for earlier in range(target - 1)]
    chunk_shapes = [jax.ShapeDtypeStruct((rows, width), BF16 if s else F32) for s in shifts]

    def swap(value):
        return lax.ppermute(value, "row", [(i, i ^ 1) for i in range(row_count)])

    def gather(value):
        others = [
            lax.ppermute(value, "row", [(i, i ^ (2 * mask)) for i in range(row_count)])
            for mask in range(1, chips)
        ]
        return [value, *others]

    def send_chunks(chunks):
        return [
            lax.ppermute(chunk, "col", [(i, (i + s) % col_count) for i in range(col_count)])
            for s, chunk in zip(shifts[:-1], chunks)
        ]

    def by_core(kept, other, axis):
        return jnp.where(
            core == 0,
            jnp.concatenate([kept, other], axis=axis),
            jnp.concatenate([other, kept], axis=axis),
        )

    diag_other, inner_other = swap(diag_inv), swap(l_inner)
    first = pl.pallas_call(
        functools.partial(first_kernel, shifts, 8),
        in_specs=[HBM, HBM],
        out_specs=[VMEM] * col_count,
        out_shape=chunk_shapes,
        scratch_shapes=[
            pltpu.VMEM((8, rows, depth // 8), BF16),
            pltpu.VMEM((8, depth // 8, total), BF16),
            pltpu.VMEM((rows, total), F32),
            pltpu.SemaphoreType.DMA((8,)),
            pltpu.SemaphoreType.DMA((8,)),
        ],
        compiler_params=params(56),
        cost_estimate=work(rows, depth, total),
    )(l_panel, x_solved)
    chunks = [first]
    arrived = {0: send_chunks(first[:-1])}
    found = pl.pallas_call(
        functools.partial(second_kernel, shifts, pieces, 2),
        in_specs=[HBM, HBM],
        out_specs=[HBM] * ((steps - 1) * col_count),
        out_shape=chunk_shapes * (steps - 1),
        scratch_shapes=[
            pltpu.VMEM((pieces, rows * (steps - 1), depth // pieces), BF16),
            pltpu.VMEM((pieces, depth // pieces, total), BF16),
            pltpu.VMEM((rows * (steps - 1), total), F32),
            pltpu.VMEM((steps - 1, col_count - 1, rows, width), BF16),
            pltpu.VMEM((steps - 1, rows, width), F32),
            pltpu.SemaphoreType.DMA((pieces, steps - 1)),
            pltpu.SemaphoreType.DMA((pieces,)),
            pltpu.SemaphoreType.DMA((steps - 1, col_count)),
        ],
        compiler_params=params(56),
        cost_estimate=work(rows * (steps - 1), depth, total),
    )(l_panel, after(x_solved, first[0]))
    chunks += [found[i * col_count : (i + 1) * col_count] for i in range(steps - 1)]
    taken = {target: [] for target in range(steps)}

    def reduced(target, token, dtype):
        own = after(chunks[target][-1], token)
        kept, other = reduce_rows(rhs, target, own, arrived[target], taken[target], dtype)
        return kept, swap(other)

    resid_low = by_core(*reduced(0, found[0], BF16), 0)
    results = []
    for target in range(steps):
        last = target + 1 == steps
        shards = gather(resid_low)
        if target == 0:
            arrived[1] = send_chunks(after(chunks[1][:-1], resid_low))
            diag = load((after(diag_inv, resid_low), diag_other), range(steps))
        kept, other, solved_low = apply_rows(diag, target, shards, [], True, False)
        results.append((kept, other))
        if last:
            break
        shards = gather(solved_low)
        if target + 2 < steps:
            arrived[target + 2] = send_chunks(after(chunks[target + 2][:-1], solved_low))
        if target == 0:
            inner = load((after(l_inner, solved_low), inner_other), near)
        held = reduced(target + 1, solved_low, F32)
        *full, resid_low = apply_rows(inner, target, shards, held, False, target + 2 < steps)
        if full:
            followers = range(target + 2, steps)
            places = [far.index(inner_index(follower, target)) for follower in followers]
            whole = after(full[0], resid_low)
            if target == 0:
                (far_own,) = load((after(l_inner, resid_low),), far)
            for follower, pair in zip(followers, own_rows(far_own, places, whole, swap(whole))):
                taken[follower].append(pair)
    before = jnp.stack([other for _, other in results[:-1]])
    swapped = swap(after(before, resid_low))
    others = [swapped[k] for k in range(steps - 1)] + [swap(results[-1][1])]
    return jnp.stack([by_core(kept, other, 1) for (kept, _), other in zip(results, others)], axis=0)


def solution(mesh):
    in_specs = (
        P(None, "row", "col"),
        P(None, "row", "col"),
        P("col", None),
        P(None, "row", None),
        P(None, "row", None),
    )
    out_specs = P(None, "row", "col")
    body = functools.partial(local, row_count=mesh.shape["row"], col_count=mesh.shape["col"])
    return jax.shard_map(body, mesh=mesh, in_specs=in_specs, out_specs=out_specs, check_vma=False)
```

time: 296 us -> 115 us (0.39)
  waiting for transfers between devices: 240 us -> 36.9 us
  starting transfers between devices: 0.3 us -> 43.9 us
  matrix products: 39.2 us -> 0 us
  Pallas kernels: 0 us -> 29.6 us
  between operations: 13.5 us -> 0.44 us
    all_gather x7 -> x0, waiting for transfers between devices: 160 us -> none  [the longest x4 95.1 us: local(): lax.all_gather(resid_low, 'row', axis=0, tiled=True)]
    reduce_scatter x1 -> x0, waiting for transfers between devices: 79.6 us -> none  [local(): shares = lax.psum_scatter(products, 'col', scatter_dimension=2, tiled=True)]
    ppermute x0 -> x43, starting transfers between devices: none -> 43.9 us  [the longest x21 25.5 us: gather(): lax.ppermute(value, 'row', [(i, i ^ 2 * mask) for i in range(row_count)])]
    dot_general x11 -> x0, matrix products: 39.2 us -> none  [the longest x1 15.1 us: local(): jnp.dot(l_panel.reshape(step_count * local_rows, solved_count), x_solved,...]
    ppermute x0 -> x43, waiting for transfers between devices: none -> 36.9 us  [the longest x21 31.6 us: gather(): lax.ppermute(value, 'row', [(i, i ^ 2 * mask) for i in range(row_count)])]
    pallas_call x0 -> x18, Pallas kernels: none -> 29.6 us  [the longest x1 11 us: local(): pl.pallas_call(functools.partial(second_kernel, shifts, pieces, 2), in_sp...]
  transfers between devices with their start and end apart: 8 -> 43, of which waited for: 8 -> 18; matrix products, arithmetic and copies ran while one was open for 2% -> 0% of each run, Pallas kernels for 0% -> 24%
where the time goes in v3:
time: 115 us
  starting transfers between devices  43.9 us (38%)
  waiting for transfers between devices  36.9 us (32%)
  Pallas kernels  29.6 us (26%)
  local copies, waits for them, and re-layouts  2.45 us (2%)
  other arithmetic  1.2 us (1%)
    ppermute x21, waiting for transfers between devices, gather(): lax.ppermute(value, 'row', [(i, i ^ 2 * mask) for i in range(row_count)])  31.6 us
    ppermute x21, starting transfers between devices, gather(): lax.ppermute(value, 'row', [(i, i ^ 2 * mask) for i in range(row_count)])  25.5 us
    ppermute x12, starting transfers between devices, send_chunks(): lax.ppermute(chunk, 'col', [(i, (i + s) % col_count) for i in range(col_c...  17.4 us
    pallas_call x1, Pallas kernels, local(): pl.pallas_call(functools.partial(second_kernel, shifts, pieces, 2), in_sp...  11 us
    pallas_call x7, Pallas kernels, apply_rows(): pl.pallas_call(functools.partial(apply_kernel, index, len(shards), len(he...  5.75 us
    pallas_call x1, Pallas kernels, local(): pl.pallas_call(functools.partial(first_kernel, shifts, 8), in_specs=[HBM,...  5.56 us
    pallas_call x3, Pallas kernels, load(): pl.pallas_call(functools.partial(load_kernel, tuple(indices)), in_specs=[...  5.03 us
    ppermute x12, waiting for transfers between devices, send_chunks(): lax.ppermute(chunk, 'col', [(i, (i + s) % col_count) for i in range(col_c...  2.71 us
  transfers between devices with their start and end apart: 43, of which 18 were waited for; matrix products, arithmetic and copies ran while one was open for 0% of the time, Pallas kernels for 24%

profile of v3, /device:TPU:0, one launch (start us, length us, event | category | flops | bytes accessed | tf_op | source)
XLA Modules:
  0.0 114.5 jit_solution(16704281861583235426)
XLA Ops:
  0.0 0.5 collective-permute-start.8
  0.5 5.6 %shard_map.55 = (bf16[256,256]{1,0:T(8,128)(2,1)}, bf16[256,256]{1,0:T(8,128)(2,1)}, bf16[256,256]{1,0:T(8,128)(2,1)}, f32[256,256]{1,0:T(8,128)}) custom-call(bf16[4,256,4096]{2,1,0:T(8,128)(2,1)} %l_ref.3, bf16[4096,1024]{1,0:T(8,128)(2,1)} %x_ref.2), custom_call_target="tpu_custom_call" | custom-call | flops 2147483648 | bytes 10485760 | tf_op jit(solution)/shard_map/pallas_call | solution.py:278
  6.1 4.1 %collective-permute-start = (bf16[256,256]{1,0:T(8,128)(2,1)}, bf16[256,256]{1,0:T(8,128)(2,1)S(1)}, u32[]{:S(2)}, u32[]{:S(2)}) collective-permute-start(bf16[256,256]{1,0:T(8,128)(2,1)} %get-tuple-element.75), channel_id=1, source_target_pairs={{0,2},{1,3},{2,0},{3,1},{4,6},{5,7},{6,4},{7,5},{8,10},{9,11},{10,... | collective-permute-start | bytes 393224 | tf_op jit(solution)/shard_map/ppermute | solution.py:266
  10.2 1.6 %collective-permute-start.1 = (bf16[256,256]{1,0:T(8,128)(2,1)}, bf16[256,256]{1,0:T(8,128)(2,1)S(1)}, u32[]{:S(2)}, u32[]{:S(2)}) collective-permute-start(bf16[256,256]{1,0:T(8,128)(2,1)} %get-tuple-element.79), channel_id=1, source_target_pairs={{0,1},{1,2},{2,3},{3,0},{4,5},{5,6},{6,7},{7,4},{8,9},{9,10},{10,1... | collective-permute-start | bytes 393224 | tf_op jit(solution)/shard_map/ppermute | solution.py:266
  11.8 2.2 %collective-permute-start.2 = (bf16[256,256]{1,0:T(8,128)(2,1)}, bf16[256,256]{1,0:T(8,128)(2,1)S(1)}, u32[]{:S(2)}, u32[]{:S(2)}) collective-permute-start(bf16[256,256]{1,0:T(8,128)(2,1)} %get-tuple-element.80), channel_id=1, source_target_pairs={{0,3},{1,0},{2,1},{3,2},{4,7},{5,4},{6,5},{7,6},{8,11},{9,8},{10,9... | collective-permute-start | bytes 393224 | tf_op jit(solution)/shard_map/ppermute | solution.py:266
  14.0 11.0 %shard_map.56 = (bf16[256,256]{1,0:T(8,128)(2,1)}, bf16[256,256]{1,0:T(8,128)(2,1)}, bf16[256,256]{1,0:T(8,128)(2,1)}, f32[256,256]{1,0:T(8,128)}, bf16[256,256]...) custom-call(bf16[4,256,4096]{2,1,0:T(8,128)(2,1)} %l_ref.3, ...), custom_call_target="tpu_custom_call" | custom-call | flops 6442450944 | bytes 14680064 | tf_op jit(solution)/shard_map/pallas_call | solution.py:295
  25.3 1.2 %collective-permute-done.3 = bf16[256,128]{1,0:T(8,128)(2,1)S(1)} collective-permute-done((bf16[256,128]{1,0:T(8,128)(2,1)S(1)}, bf16[256,128]{1,0:T(8,128)(2,1)S(1)}, u32[]{:S(2)}, u32[]{:S(2)}) %collective-permute-start.3) | collective-permute-done | bytes 65568 | tf_op jit(solution)/shard_map/ppermute | solution.py:255
  26.5 1.6 %collective-permute-start.5 = (bf16[512,128]{1,0:T(8,128)(2,1)S(1)}, bf16[512,128]{1,0:T(8,128)(2,1)S(1)}, u32[]{:S(2)}, u32[]{:S(2)}) collective-permute-start(bf16[512,128]{1,0:T(8,128)(2,1)S(1)} %maximum_select_fusion.4.refs_0_), channel_id=1, source_target_pairs={{0,8},{4,12},{8,0},{12,4},{16,24},{20,28},{24,16},{28,20},{1,9},{5... | collective-permute-start | bytes 393224 | tf_op jit(solution)/shard_map/ppermute | solution.py:259
  28.1 1.5 %collective-permute-start.6 = (bf16[512,128]{1,0:T(8,128)(2,1)S(1)}, bf16[512,128]{1,0:T(8,128)(2,1)S(1)}, u32[]{:S(2)}, u32[]{:S(2)}) collective-permute-start(bf16[512,128]{1,0:T(8,128)(2,1)S(1)} %maximum_select_fusion.4.refs_0_), channel_id=1, source_target_pairs={{0,16},{4,20},{8,24},{12,28},{16,0},{20,4},{24,8},{28,12},{1,17},{... | collective-permute-start | bytes 393224 | tf_op jit(solution)/shard_map/ppermute | solution.py:259
  29.6 0.5 collective-permute-start.7
  30.1 2.4 %collective-permute-done.5.refs_1_ = bf16[512,128]{1,0:T(8,128)(2,1)S(1)} collective-permute-done((bf16[512,128]{1,0:T(8,128)(2,1)S(1)}, bf16[512,128]{1,0:T(8,128)(2,1)S(1)}, u32[]{:S(2)}, u32[]{:S(2)}) %collective-permute-start.5) | collective-permute-done | bytes 131104 | tf_op jit(solution)/shard_map/ppermute | solution.py:259
  32.6 3.6 %collective-permute-done.6.refs_2_ = bf16[512,128]{1,0:T(8,128)(2,1)S(1)} collective-permute-done((bf16[512,128]{1,0:T(8,128)(2,1)S(1)}, bf16[512,128]{1,0:T(8,128)(2,1)S(1)}, u32[]{:S(2)}, u32[]{:S(2)}) %collective-permute-start.6) | collective-permute-done | bytes 131104 | tf_op jit(solution)/shard_map/ppermute | solution.py:259
  36.2 3.8 %collective-permute-start.14 = (bf16[256,256]{1,0:T(8,128)(2,1)}, bf16[256,256]{1,0:T(8,128)(2,1)S(1)}, u32[]{:S(2)}, u32[]{:S(2)}) collective-permute-start(bf16[256,256]{1,0:T(8,128)(2,1)} %get-tuple-element.98), channel_id=1, source_target_pairs={{0,3},{1,0},{2,1},{3,2},{4,7},{5,4},{6,5},{7,6},{8,11},{9,8},{10,9... | collective-permute-start | bytes 393224 | tf_op jit(solution)/shard_map/ppermute | solution.py:266
  40.0 2.2 %copy-done.1 = bf16[4,256,2048]{2,1,0:T(8,128)(2,1)S(1)} copy-done((bf16[4,256,2048]{2,1,0:T(8,128)(2,1)S(1)}, bf16[4,256,2048]{2,1,0:T(8,128)(2,1)}, u32[]{:S(2)}) %copy-start.1) | copy-done | bytes 4194328
  42.2 2.7 %shard_map.58 = (bf16[4,256,2048]{2,1,0:T(8,128)(2,1)S(1)}, bf16[4,256,2048]{2,1,0:T(8,128)(2,1)S(1)}) custom-call(bf16[4,256,2048]{2,1,0:T(8,128)(2,1)S(1)} %copy-done.1, bf16[4,256,2048]{2,1,0:T(8,128)(2,1)} %collective-permute-done.4.refs_1_), custom_call_target="tpu_custom_call" | custom-call | flops 1024 | bytes 1024 | tf_op jit(solution)/shard_map/pallas_call | solution.py:133
  44.9 0.7 shard_map.59
  45.7 0.2 copy-done.4
  46.0 1.6 %collective-permute-start.10 = (bf16[512,128]{1,0:T(8,128)(2,1)S(1)}, bf16[512,128]{1,0:T(8,128)(2,1)S(1)}, u32[]{:S(2)}, u32[]{:S(2)}) collective-permute-start(bf16[512,128]{1,0:T(8,128)(2,1)S(1)} %get-tuple-element.88.refs_0_), channel_id=1, source_target_pairs={{0,16},{4,20},{8,24},{12,28},{16,0},{20,4},{24,8},{28,12},{1,17},{... | collective-permute-start | bytes 393224 | tf_op jit(solution)/shard_map/ppermute | solution.py:259
  47.6 1.9 %collective-permute-start.9 = (bf16[512,128]{1,0:T(8,128)(2,1)S(1)}, bf16[512,128]{1,0:T(8,128)(2,1)S(1)}, u32[]{:S(2)}, u32[]{:S(2)}) collective-permute-start(bf16[512,128]{1,0:T(8,128)(2,1)S(1)} %get-tuple-element.88.refs_0_), channel_id=1, source_target_pairs={{0,8},{4,12},{8,0},{12,4},{16,24},{20,28},{24,16},{28,20},{1,9},{5... | collective-permute-start | bytes 393224 | tf_op jit(solution)/shard_map/ppermute | solution.py:259
  49.6 2.1 %shard_map.60 = (bf16[3,256,2048]{2,1,0:T(8,128)(2,1)S(1)}, bf16[3,256,2048]{2,1,0:T(8,128)(2,1)S(1)}) custom-call(bf16[6,256,2048]{2,1,0:T(8,128)(2,1)S(1)} %bitcast.9, bf16[6,256,2048]{2,1,0:T(8,128)(2,1)} %collective-permute-done.8.refs_1_), custom_call_target="tpu_custom_call" | custom-call | flops 1024 | bytes 1024 | tf_op jit(solution)/shard_map/pallas_call | solution.py:133
  51.7 2.8 %collective-permute-done.10.refs_2_ = bf16[512,128]{1,0:T(8,128)(2,1)S(1)} collective-permute-done((bf16[512,128]{1,0:T(8,128)(2,1)S(1)}, bf16[512,128]{1,0:T(8,128)(2,1)S(1)}, u32[]{:S(2)}, u32[]{:S(2)}) %collective-permute-start.10) | collective-permute-done | bytes 131104 | tf_op jit(solution)/shard_map/ppermute | solution.py:259
  54.6 0.3 collective-permute-done.11.refs_3_
  54.9 1.1 collective-permute-done.9.refs_1_
  56.0 0.8 shard_map.62
  56.8 0.4 collective-permute-start.16
  57.2 1.7 %collective-permute-start.17 = (bf16[512,128]{1,0:T(8,128)(2,1)S(1)}, bf16[512,128]{1,0:T(8,128)(2,1)S(1)}, u32[]{:S(2)}, u32[]{:S(2)}) collective-permute-start(bf16[512,128]{1,0:T(8,128)(2,1)S(1)} %get-tuple-element.101.refs_0_), channel_id=1, source_target_pairs={{0,16},{4,20},{8,24},{12,28},{16,0},{20,4},{24,8},{28,12},{1,17},{... | collective-permute-start | bytes 393224 | tf_op jit(solution)/shard_map/ppermute | solution.py:259
  58.9 1.4 %collective-permute-start.18 = (bf16[512,128]{1,0:T(8,128)(2,1)S(1)}, bf16[512,128]{1,0:T(8,128)(2,1)S(1)}, u32[]{:S(2)}, u32[]{:S(2)}) collective-permute-start(bf16[512,128]{1,0:T(8,128)(2,1)S(1)} %get-tuple-element.101.refs_0_), channel_id=1, source_target_pairs={{0,24},{4,28},{8,16},{12,20},{16,8},{20,12},{24,0},{28,4},{1,25},{... | collective-permute-start | bytes 393224 | tf_op jit(solution)/shard_map/ppermute | solution.py:259
  60.4 2.8 %collective-permute-done.16.refs_1_ = bf16[512,128]{1,0:T(8,128)(2,1)S(1)} collective-permute-done((bf16[512,128]{1,0:T(8,128)(2,1)S(1)}, bf16[512,128]{1,0:T(8,128)(2,1)S(1)}, u32[]{:S(2)}, u32[]{:S(2)}) %collective-permute-start.16) | collective-permute-done | bytes 131104 | tf_op jit(solution)/shard_map/ppermute | solution.py:259
  63.2 0.3 collective-permute-start.23
  63.4 1.4 %collective-permute-done.17.refs_2_ = bf16[512,128]{1,0:T(8,128)(2,1)S(1)} collective-permute-done((bf16[512,128]{1,0:T(8,128)(2,1)S(1)}, bf16[512,128]{1,0:T(8,128)(2,1)S(1)}, u32[]{:S(2)}, u32[]{:S(2)}) %collective-permute-start.17) | collective-permute-done | bytes 131104 | tf_op jit(solution)/shard_map/ppermute | solution.py:259
  64.9 2.1 %collective-permute-start.24 = (bf16[256,256]{1,0:T(8,128)(2,1)S(1)}, bf16[256,256]{1,0:T(8,128)(2,1)S(1)}, u32[]{:S(2)}, u32[]{:S(2)}) collective-permute-start(bf16[256,256]{1,0:T(8,128)(2,1)S(1)} %copy-done.9), channel_id=1, source_target_pairs={{0,3},{1,0},{2,1},{3,2},{4,7},{5,4},{6,5},{7,6},{8,11},{9,8},{10,9... | collective-permute-start | bytes 393224 | tf_op jit(solution)/shard_map/ppermute | solution.py:266
  67.0 0.2 shard_map.64.matrix_ref
  67.3 0.7 shard_map.63
  68.0 1.5 %collective-permute-start.19 = (bf16[512,128]{1,0:T(8,128)(2,1)S(1)}, bf16[512,128]{1,0:T(8,128)(2,1)S(1)}, u32[]{:S(2)}, u32[]{:S(2)}) collective-permute-start(bf16[512,128]{1,0:T(8,128)(2,1)S(1)} %get-tuple-element.103.refs_0_), channel_id=1, source_target_pairs={{0,8},{4,12},{8,0},{12,4},{16,24},{20,28},{24,16},{28,20},{1,9},{5... | collective-permute-start | bytes 393224 | tf_op jit(solution)/shard_map/ppermute | solution.py:259
  69.5 1.5 %collective-permute-start.20 = (bf16[512,128]{1,0:T(8,128)(2,1)S(1)}, bf16[512,128]{1,0:T(8,128)(2,1)S(1)}, u32[]{:S(2)}, u32[]{:S(2)}) collective-permute-start(bf16[512,128]{1,0:T(8,128)(2,1)S(1)} %get-tuple-element.103.refs_0_), channel_id=1, source_target_pairs={{0,16},{4,20},{8,24},{12,28},{16,0},{20,4},{24,8},{28,12},{1,17},{... | collective-permute-start | bytes 393224 | tf_op jit(solution)/shard_map/ppermute | solution.py:259
  71.0 1.2 %shard_map.65 = (f32[256,128]{1,0:T(8,128)S(1)}, f32[256,128]{1,0:T(8,128)S(1)}, f32[256,128]{1,0:T(8,128)S(1)}, f32[256,128]{1,0:T(8,128)S(1)}) custom-call(bf16[3,256,2048]{2,1,0:T(8,128)(2,1)S(1)} %shard_map.64.matrix_ref, bf16[2048,128]{1,0:T(8,128)(2,1)S(1)} %get-tuple-element.113.kept_ref, bf16[2048,128]{1,0:T(8,128)(2,1)S(1)} %collective-permute-done.25.other_ref), custom_call_target="tpu_custom_call" | custom-call | flops 1024 | bytes 1024 | tf_op jit(solution)/shard_map/pallas_call | solution.py:227
  72.3 2.1 %collective-permute-start.21 = (bf16[512,128]{1,0:T(8,128)(2,1)S(1)}, bf16[512,128]{1,0:T(8,128)(2,1)S(1)}, u32[]{:S(2)}, u32[]{:S(2)}) collective-permute-start(bf16[512,128]{1,0:T(8,128)(2,1)S(1)} %get-tuple-element.103.refs_0_), channel_id=1, source_target_pairs={{0,24},{4,28},{8,16},{12,20},{16,8},{20,12},{24,0},{28,4},{1,25},{... | collective-permute-start | bytes 393224 | tf_op jit(solution)/shard_map/ppermute | solution.py:259
  74.3 0.2 collective-permute-done.24.refs_2_
  74.7 3.5 %collective-permute-done.21.refs_3_ = bf16[512,128]{1,0:T(8,128)(2,1)S(1)} collective-permute-done((bf16[512,128]{1,0:T(8,128)(2,1)S(1)}, bf16[512,128]{1,0:T(8,128)(2,1)S(1)}, u32[]{:S(2)}, u32[]{:S(2)}) %collective-permute-start.21) | collective-permute-done | bytes 131104 | tf_op jit(solution)/shard_map/ppermute | solution.py:259
  78.2 0.8 shard_map.67
  79.0 1.1 collective-permute-start.27
  80.2 1.5 %collective-permute-start.28 = (bf16[512,128]{1,0:T(8,128)(2,1)S(1)}, bf16[512,128]{1,0:T(8,128)(2,1)S(1)}, u32[]{:S(2)}, u32[]{:S(2)}) collective-permute-start(bf16[512,128]{1,0:T(8,128)(2,1)S(1)} %get-tuple-element.118.refs_0_), channel_id=1, source_target_pairs={{0,16},{4,20},{8,24},{12,28},{16,0},{20,4},{24,8},{28,12},{1,17},{... | collective-permute-start | bytes 393224 | tf_op jit(solution)/shard_map/ppermute | solution.py:259
  81.7 0.9 collective-permute-start.29
  82.6 0.7 collective-permute-start.33
  83.3 2.1 %collective-permute-done.27.refs_1_ = bf16[512,128]{1,0:T(8,128)(2,1)S(1)} collective-permute-done((bf16[512,128]{1,0:T(8,128)(2,1)S(1)}, bf16[512,128]{1,0:T(8,128)(2,1)S(1)}, u32[]{:S(2)}, u32[]{:S(2)}) %collective-permute-start.27) | collective-permute-done | bytes 131104 | tf_op jit(solution)/shard_map/ppermute | solution.py:259
  85.4 0.9 collective-permute-start.34
  86.3 1.3 %collective-permute-done.28.refs_2_ = bf16[512,128]{1,0:T(8,128)(2,1)S(1)} collective-permute-done((bf16[512,128]{1,0:T(8,128)(2,1)S(1)}, bf16[512,128]{1,0:T(8,128)(2,1)S(1)}, u32[]{:S(2)}, u32[]{:S(2)}) %collective-permute-start.28) | collective-permute-done | bytes 131104 | tf_op jit(solution)/shard_map/ppermute | solution.py:259
  87.6 1.7 %collective-permute-start.35 = (bf16[256,256]{1,0:T(8,128)(2,1)S(1)}, bf16[256,256]{1,0:T(8,128)(2,1)S(1)}, u32[]{:S(2)}, u32[]{:S(2)}) collective-permute-start(bf16[256,256]{1,0:T(8,128)(2,1)S(1)} %copy-done.6), channel_id=1, source_target_pairs={{0,3},{1,0},{2,1},{3,2},{4,7},{5,4},{6,5},{7,6},{8,11},{9,8},{10,9... | collective-permute-start | bytes 393224 | tf_op jit(solution)/shard_map/ppermute | solution.py:266
  89.2 0.7 shard_map.68
  90.0 1.1 collective-permute-start.30
  91.1 1.5 %collective-permute-start.31 = (bf16[512,128]{1,0:T(8,128)(2,1)S(1)}, bf16[512,128]{1,0:T(8,128)(2,1)S(1)}, u32[]{:S(2)}, u32[]{:S(2)}) collective-permute-start(bf16[512,128]{1,0:T(8,128)(2,1)S(1)} %get-tuple-element.120.refs_0_), channel_id=1, source_target_pairs={{0,16},{4,20},{8,24},{12,28},{16,0},{20,4},{24,8},{28,12},{1,17},{... | collective-permute-start | bytes 393224 | tf_op jit(solution)/shard_map/ppermute | solution.py:259
  92.6 0.7 shard_map.69
  93.3 1.3 %collective-permute-done.33.refs_0_ = bf16[256,256]{1,0:T(8,128)(2,1)S(1)} collective-permute-done((bf16[256,256]{1,0:T(8,128)(2,1)S(1)}, bf16[256,256]{1,0:T(8,128)(2,1)S(1)}, u32[]{:S(2)}, u32[]{:S(2)}) %collective-permute-start.33) | collective-permute-done | bytes 131104 | tf_op jit(solution)/shard_map/ppermute | solution.py:266
  94.6 1.2 %collective-permute-done.35.refs_2_ = bf16[256,256]{1,0:T(8,128)(2,1)S(1)} collective-permute-done((bf16[256,256]{1,0:T(8,128)(2,1)S(1)}, bf16[256,256]{1,0:T(8,128)(2,1)S(1)}, u32[]{:S(2)}, u32[]{:S(2)}) %collective-permute-start.35) | collective-permute-done | bytes 131104 | tf_op jit(solution)/shard_map/ppermute | solution.py:266
  96.1 4.4 %collective-permute-done.32.refs_3_ = bf16[512,128]{1,0:T(8,128)(2,1)S(1)} collective-permute-done((bf16[512,128]{1,0:T(8,128)(2,1)S(1)}, bf16[512,128]{1,0:T(8,128)(2,1)S(1)}, u32[]{:S(2)}, u32[]{:S(2)}) %collective-permute-start.32) | collective-permute-done | bytes 131104 | tf_op jit(solution)/shard_map/ppermute | solution.py:259
  100.5 0.7 shard_map.71.refs_0_
  101.3 0.9 collective-permute-start.39
  102.2 0.1 collective-permute-start.40
  102.3 2.5 %collective-permute-start.41 = (bf16[512,128]{1,0:T(8,128)(2,1)S(1)}, bf16[512,128]{1,0:T(8,128)(2,1)S(1)}, u32[]{:S(2)}, u32[]{:S(2)}) collective-permute-start(bf16[512,128]{1,0:T(8,128)(2,1)S(1)} %shard_map.71.refs_0_), channel_id=1, source_target_pairs={{0,24},{4,28},{8,16},{12,20},{16,8},{20,12},{24,0},{28,4},{1,25},{... | collective-permute-start | bytes 393224 | tf_op jit(solution)/shard_map/ppermute | solution.py:259
  104.9 2.8 %collective-permute-done.39.refs_1_ = bf16[512,128]{1,0:T(8,128)(2,1)S(1)} collective-permute-done((bf16[512,128]{1,0:T(8,128)(2,1)S(1)}, bf16[512,128]{1,0:T(8,128)(2,1)S(1)}, u32[]{:S(2)}, u32[]{:S(2)}) %collective-permute-start.39) | collective-permute-done | bytes 131104 | tf_op jit(solution)/shard_map/ppermute | solution.py:259
  107.7 2.9 %collective-permute-done.40.refs_2_ = bf16[512,128]{1,0:T(8,128)(2,1)S(1)} collective-permute-done((bf16[512,128]{1,0:T(8,128)(2,1)S(1)}, bf16[512,128]{1,0:T(8,128)(2,1)S(1)}, u32[]{:S(2)}, u32[]{:S(2)}) %collective-permute-start.40) | collective-permute-done | bytes 131104 | tf_op jit(solution)/shard_map/ppermute | solution.py:259
  110.6 1.4 %shard_map.72 = (f32[256,128]{1,0:T(8,128)S(1)}, f32[256,128]{1,0:T(8,128)S(1)}, bf16[512,128]{1,0:T(8,128)(2,1)}) custom-call(bf16[4,256,2048]{2,1,0:T(8,128)(2,1)S(1)} %get-tuple-element.84.own_ref, bf16[4,256,2048]{2,1,0:T(8,128)(2,1)S(1)} %get-tuple-element.85.other_ref, bf16[512,128]{1,0:T(8,128)(2,1)S(1)} %shard_map.71.refs_0_, ...), custom_call_target="tpu_custom_call" | custom-call | flops 1024 | bytes 1024 | tf_op jit(solution)/shard_map/pallas_call | solution.py:209
  112.0 1.3 %collective-permute-done.42 = f32[256,128]{1,0:T(8,128)S(1)} collective-permute-done((f32[256,128]{1,0:T(8,128)S(1)}, f32[256,128]{1,0:T(8,128)S(1)}, u32[]{:S(2)}, u32[]{:S(2)}) %collective-permute-start.42) | collective-permute-done | bytes 131104 | tf_op jit(solution)/shard_map/ppermute | solution.py:255
  113.5 1.0 pad_maximum_fusion
  (76 shorter events, 1.3 us)
Async XLA Ops:
  0.0 49.6 %collective-permute-start.8 = (bf16[6,256,2048]{2,1,0:T(8,128)(2,1)}, bf16[6,256,2048]{2,1,0:T(8,128)(2,1)}, u32[]{:S(2)}, u32[]{:S(2)}) collective-permute-start(bf16[6,256,2048]{2,1,0:T(8,128)(2,1)} %refs_0_.2), channel_id=1, source_target_pairs={{0,4},{4,0},{8,12},{12,8},{16,20},{20,16},{24,28},{28,24},{1,5},{5... | collective-permute-start | bytes 18874376 | tf_op jit(solution)/shard_map/ppermute | solution.py:255
  0.5 35.7 %collective-permute-start.4 = (bf16[4,256,2048]{2,1,0:T(8,128)(2,1)}, bf16[4,256,2048]{2,1,0:T(8,128)(2,1)}, u32[]{:S(2)}, u32[]{:S(2)}) collective-permute-start(bf16[4,256,2048]{2,1,0:T(8,128)(2,1)} %refs_0_), channel_id=1, source_target_pairs={{0,4},{4,0},{8,12},{12,8},{16,20},{20,16},{24,28},{28,24},{1,5},{5... | collective-permute-start | bytes 12582920 | tf_op jit(solution)/shard_map/ppermute | solution.py:255
  6.1 19.0 %collective-permute-start = (bf16[256,256]{1,0:T(8,128)(2,1)}, bf16[256,256]{1,0:T(8,128)(2,1)S(1)}, u32[]{:S(2)}, u32[]{:S(2)}) collective-permute-start(bf16[256,256]{1,0:T(8,128)(2,1)} %get-tuple-element.75), channel_id=1, source_target_pairs={{0,2},{1,3},{2,0},{3,1},{4,6},{5,7},{6,4},{7,5},{8,10},{9,11},{10,... | collective-permute-start | bytes 393224 | tf_op jit(solution)/shard_map/ppermute | solution.py:266
  10.2 14.9 %collective-permute-start.1 = (bf16[256,256]{1,0:T(8,128)(2,1)}, bf16[256,256]{1,0:T(8,128)(2,1)S(1)}, u32[]{:S(2)}, u32[]{:S(2)}) collective-permute-start(bf16[256,256]{1,0:T(8,128)(2,1)} %get-tuple-element.79), channel_id=1, source_target_pairs={{0,1},{1,2},{2,3},{3,0},{4,5},{5,6},{6,7},{7,4},{8,9},{9,10},{10,1... | collective-permute-start | bytes 393224 | tf_op jit(solution)/shard_map/ppermute | solution.py:266
  11.8 13.3 %copy-start = (f32[4,256,256]{2,1,0:T(8,128)S(1)}, f32[4,256,256]{2,1,0:T(8,128)}, u32[]{:S(2)}) copy-start(f32[4,256,256]{2,1,0:T(8,128)} %rhs_ref.7) | copy-start | bytes 3145732
  11.8 13.3 %copy-start.5 = (f32[256,256]{1,0:T(8,128)S(1)}, f32[256,256]{1,0:T(8,128)}, u32[]{:S(2)}) copy-start(f32[256,256]{1,0:T(8,128)} %get-tuple-element.78.own_ref) | copy-start | bytes 786436
  11.8 13.3 %collective-permute-start.2 = (bf16[256,256]{1,0:T(8,128)(2,1)}, bf16[256,256]{1,0:T(8,128)(2,1)S(1)}, u32[]{:S(2)}, u32[]{:S(2)}) collective-permute-start(bf16[256,256]{1,0:T(8,128)(2,1)} %get-tuple-element.80), channel_id=1, source_target_pairs={{0,3},{1,0},{2,1},{3,2},{4,7},{5,4},{6,5},{7,6},{8,11},{9,8},{10,9... | collective-permute-start | bytes 393224 | tf_op jit(solution)/shard_map/ppermute | solution.py:266
  25.2 1.3 %collective-permute-start.3 = (bf16[256,128]{1,0:T(8,128)(2,1)S(1)}, bf16[256,128]{1,0:T(8,128)(2,1)S(1)}, u32[]{:S(2)}, u32[]{:S(2)}) collective-permute-start(bf16[256,128]{1,0:T(8,128)(2,1)S(1)} %get-tuple-element.82), channel_id=1, source_target_pairs={{0,4},{4,0},{8,12},{12,8},{16,20},{20,16},{24,28},{28,24},{1,5},{5... | collective-permute-start | bytes 196616 | tf_op jit(solution)/shard_map/ppermute | solution.py:255
  26.5 6.0 %collective-permute-start.5 = (bf16[512,128]{1,0:T(8,128)(2,1)S(1)}, bf16[512,128]{1,0:T(8,128)(2,1)S(1)}, u32[]{:S(2)}, u32[]{:S(2)}) collective-permute-start(bf16[512,128]{1,0:T(8,128)(2,1)S(1)} %maximum_select_fusion.4.refs_0_), channel_id=1, source_target_pairs={{0,8},{4,12},{8,0},{12,4},{16,24},{20,28},{24,16},{28,20},{1,9},{5... | collective-permute-start | bytes 393224 | tf_op jit(solution)/shard_map/ppermute | solution.py:259
  28.1 8.1 %collective-permute-start.6 = (bf16[512,128]{1,0:T(8,128)(2,1)S(1)}, bf16[512,128]{1,0:T(8,128)(2,1)S(1)}, u32[]{:S(2)}, u32[]{:S(2)}) collective-permute-start(bf16[512,128]{1,0:T(8,128)(2,1)S(1)} %maximum_select_fusion.4.refs_0_), channel_id=1, source_target_pairs={{0,16},{4,20},{8,24},{12,28},{16,0},{20,4},{24,8},{28,12},{1,17},{... | collective-permute-start | bytes 393224 | tf_op jit(solution)/shard_map/ppermute | solution.py:259
  29.6 15.3 %collective-permute-start.7 = (bf16[512,128]{1,0:T(8,128)(2,1)S(1)}, bf16[512,128]{1,0:T(8,128)(2,1)S(1)}, u32[]{:S(2)}, u32[]{:S(2)}) collective-permute-start(bf16[512,128]{1,0:T(8,128)(2,1)S(1)} %maximum_select_fusion.4.refs_0_), channel_id=1, source_target_pairs={{0,24},{4,28},{8,16},{12,20},{16,8},{20,12},{24,0},{28,4},{1,25},{... | collective-permute-start | bytes 393224 | tf_op jit(solution)/shard_map/ppermute | solution.py:259
  32.5 13.1 %collective-permute-start.12 = (bf16[256,256]{1,0:T(8,128)(2,1)}, bf16[256,256]{1,0:T(8,128)(2,1)S(1)}, u32[]{:S(2)}, u32[]{:S(2)}) collective-permute-start(bf16[256,256]{1,0:T(8,128)(2,1)} %get-tuple-element.96), channel_id=1, source_target_pairs={{0,2},{1,3},{2,0},{3,1},{4,6},{5,7},{6,4},{7,5},{8,10},{9,11},{10,... | collective-permute-start | bytes 393224 | tf_op jit(solution)/shard_map/ppermute | solution.py:266
  36.2 9.5 %collective-permute-start.13 = (bf16[256,256]{1,0:T(8,128)(2,1)}, bf16[256,256]{1,0:T(8,128)(2,1)S(1)}, u32[]{:S(2)}, u32[]{:S(2)}) collective-permute-start(bf16[256,256]{1,0:T(8,128)(2,1)} %get-tuple-element.97), channel_id=1, source_target_pairs={{0,1},{1,2},{2,3},{3,0},{4,5},{5,6},{6,7},{7,4},{8,9},{9,10},{10,1... | collective-permute-start | bytes 393224 | tf_op jit(solution)/shard_map/ppermute | solution.py:266
  36.2 9.5 %collective-permute-start.14 = (bf16[256,256]{1,0:T(8,128)(2,1)}, bf16[256,256]{1,0:T(8,128)(2,1)S(1)}, u32[]{:S(2)}, u32[]{:S(2)}) collective-permute-start(bf16[256,256]{1,0:T(8,128)(2,1)} %get-tuple-element.98), channel_id=1, source_target_pairs={{0,3},{1,0},{2,1},{3,2},{4,7},{5,4},{6,5},{7,6},{8,11},{9,8},{10,9... | collective-permute-start | bytes 393224 | tf_op jit(solution)/shard_map/ppermute | solution.py:266
  40.0 2.2 %copy-start.1 = (bf16[4,256,2048]{2,1,0:T(8,128)(2,1)S(1)}, bf16[4,256,2048]{2,1,0:T(8,128)(2,1)}, u32[]{:S(2)}) copy-start(bf16[4,256,2048]{2,1,0:T(8,128)(2,1)} %refs_0_) | copy-start | bytes 12582916
  42.2 7.4 %slice-start = ((s8[6291456]{0:T(1024)(128)(4,1)}), s8[4194304]{0:T(1024)(128)(4,1)S(1)}, s32[]{:S(2)}) async-start(s8[6291456]{0:T(1024)(128)(4,1)} %bitcast.8), calls=%async_computation | async-start | bytes 8388608
  44.9 1.0 copy-start.4
  44.9 4.7 %slice-start.1 = ((s8[6291456]{0:T(1024)(128)(4,1)}), s8[2097152]{0:T(1024)(128)(4,1)S(1)}, s32[]{:S(2)}) async-start(s8[6291456]{0:T(1024)(128)(4,1)} %bitcast.8), calls=%async_computation.1 | async-start | bytes 4194304
  45.9 5.8 %collective-permute-start.15 = (f32[256,128]{1,0:T(8,128)S(1)}, f32[256,128]{1,0:T(8,128)S(1)}, u32[]{:S(2)}, u32[]{:S(2)}) collective-permute-start(f32[256,128]{1,0:T(8,128)S(1)} %get-tuple-element.100), channel_id=1, source_target_pairs={{0,4},{4,0},{8,12},{12,8},{16,20},{20,16},{24,28},{28,24},{1,5},{5... | collective-permute-start | bytes 393224 | tf_op jit(solution)/shard_map/ppermute | solution.py:255
  46.0 8.6 %collective-permute-start.10 = (bf16[512,128]{1,0:T(8,128)(2,1)S(1)}, bf16[512,128]{1,0:T(8,128)(2,1)S(1)}, u32[]{:S(2)}, u32[]{:S(2)}) collective-permute-start(bf16[512,128]{1,0:T(8,128)(2,1)S(1)} %get-tuple-element.88.refs_0_), channel_id=1, source_target_pairs={{0,16},{4,20},{8,24},{12,28},{16,0},{20,4},{24,8},{28,12},{1,17},{... | collective-permute-start | bytes 393224 | tf_op jit(solution)/shard_map/ppermute | solution.py:259
  47.6 7.3 %collective-permute-start.11 = (bf16[512,128]{1,0:T(8,128)(2,1)S(1)}, bf16[512,128]{1,0:T(8,128)(2,1)S(1)}, u32[]{:S(2)}, u32[]{:S(2)}) collective-permute-start(bf16[512,128]{1,0:T(8,128)(2,1)S(1)} %get-tuple-element.88.refs_0_), channel_id=1, source_target_pairs={{0,24},{4,28},{8,16},{12,20},{16,8},{20,12},{24,0},{28,4},{1,25},{... | collective-permute-start | bytes 393224 | tf_op jit(solution)/shard_map/ppermute | solution.py:259
  47.6 8.3 %collective-permute-start.9 = (bf16[512,128]{1,0:T(8,128)(2,1)S(1)}, bf16[512,128]{1,0:T(8,128)(2,1)S(1)}, u32[]{:S(2)}, u32[]{:S(2)}) collective-permute-start(bf16[512,128]{1,0:T(8,128)(2,1)S(1)} %get-tuple-element.88.refs_0_), channel_id=1, source_target_pairs={{0,8},{4,12},{8,0},{12,4},{16,24},{20,28},{24,16},{28,20},{1,9},{5... | collective-permute-start | bytes 393224 | tf_op jit(solution)/shard_map/ppermute | solution.py:259
  51.7 8.7 %copy-start.11 = (bf16[256,256]{1,0:T(8,128)(2,1)S(1)}, bf16[256,256]{1,0:T(8,128)(2,1)}, u32[]{:S(2)}) copy-start(bf16[256,256]{1,0:T(8,128)(2,1)} %get-tuple-element.109) | copy-start | bytes 393220
  51.7 11.5 %copy-start.10 = (bf16[256,256]{1,0:T(8,128)(2,1)S(1)}, bf16[256,256]{1,0:T(8,128)(2,1)}, u32[]{:S(2)}) copy-start(bf16[256,256]{1,0:T(8,128)(2,1)} %get-tuple-element.110) | copy-start | bytes 393220
  51.7 13.1 %copy-start.9 = (bf16[256,256]{1,0:T(8,128)(2,1)S(1)}, bf16[256,256]{1,0:T(8,128)(2,1)}, u32[]{:S(2)}) copy-start(bf16[256,256]{1,0:T(8,128)(2,1)} %get-tuple-element.111) | copy-start | bytes 393220
  56.7 12.8 %collective-permute-start.25 = (bf16[2048,128]{1,0:T(8,128)(2,1)S(1)}, bf16[2048,128]{1,0:T(8,128)(2,1)S(1)}, u32[]{:S(2)}, u32[]{:S(2)}) collective-permute-start(bf16[2048,128]{1,0:T(8,128)(2,1)S(1)} %get-tuple-element.113.kept_ref), channel_id=1, source_target_pairs={{0,4},{4,0},{8,12},{12,8},{16,20},{20,16},{24,28},{28,24},{1,5},{5... | collective-permute-start | bytes 1572872 | tf_op jit(solution)/shard_map/ppermute | solution.py:255
  56.8 6.4 %collective-permute-start.16 = (bf16[512,128]{1,0:T(8,128)(2,1)S(1)}, bf16[512,128]{1,0:T(8,128)(2,1)S(1)}, u32[]{:S(2)}, u32[]{:S(2)}) collective-permute-start(bf16[512,128]{1,0:T(8,128)(2,1)S(1)} %get-tuple-element.101.refs_0_), channel_id=1, source_target_pairs={{0,8},{4,12},{8,0},{12,4},{16,24},{20,28},{24,16},{28,20},{1,9},{5... | collective-permute-start | bytes 393224 | tf_op jit(solution)/shard_map/ppermute | solution.py:259
  57.2 7.6 %collective-permute-start.17 = (bf16[512,128]{1,0:T(8,128)(2,1)S(1)}, bf16[512,128]{1,0:T(8,128)(2,1)S(1)}, u32[]{:S(2)}, u32[]{:S(2)}) collective-permute-start(bf16[512,128]{1,0:T(8,128)(2,1)S(1)} %get-tuple-element.101.refs_0_), channel_id=1, source_target_pairs={{0,16},{4,20},{8,24},{12,28},{16,0},{20,4},{24,8},{28,12},{1,17},{... | collective-permute-start | bytes 393224 | tf_op jit(solution)/shard_map/ppermute | solution.py:259
  58.9 8.3 %collective-permute-start.18 = (bf16[512,128]{1,0:T(8,128)(2,1)S(1)}, bf16[512,128]{1,0:T(8,128)(2,1)S(1)}, u32[]{:S(2)}, u32[]{:S(2)}) collective-permute-start(bf16[512,128]{1,0:T(8,128)(2,1)S(1)} %get-tuple-element.101.refs_0_), channel_id=1, source_target_pairs={{0,24},{4,28},{8,16},{12,20},{16,8},{20,12},{24,0},{28,4},{1,25},{... | collective-permute-start | bytes 393224 | tf_op jit(solution)/shard_map/ppermute | solution.py:259
  60.4 11.9 %collective-permute-start.22 = (bf16[256,256]{1,0:T(8,128)(2,1)S(1)}, bf16[256,256]{1,0:T(8,128)(2,1)S(1)}, u32[]{:S(2)}, u32[]{:S(2)}) collective-permute-start(bf16[256,256]{1,0:T(8,128)(2,1)S(1)} %copy-done.11), channel_id=1, source_target_pairs={{0,2},{1,3},{2,0},{3,1},{4,6},{5,7},{6,4},{7,5},{8,10},{9,11},{10,... | collective-permute-start | bytes 393224 | tf_op jit(solution)/shard_map/ppermute | solution.py:266
  63.2 11.2 %collective-permute-start.23 = (bf16[256,256]{1,0:T(8,128)(2,1)S(1)}, bf16[256,256]{1,0:T(8,128)(2,1)S(1)}, u32[]{:S(2)}, u32[]{:S(2)}) collective-permute-start(bf16[256,256]{1,0:T(8,128)(2,1)S(1)} %copy-done.10), channel_id=1, source_target_pairs={{0,1},{1,2},{2,3},{3,0},{4,5},{5,6},{6,7},{7,4},{8,9},{9,10},{10,1... | collective-permute-start | bytes 393224 | tf_op jit(solution)/shard_map/ppermute | solution.py:266
  64.9 9.6 %collective-permute-start.24 = (bf16[256,256]{1,0:T(8,128)(2,1)S(1)}, bf16[256,256]{1,0:T(8,128)(2,1)S(1)}, u32[]{:S(2)}, u32[]{:S(2)}) collective-permute-start(bf16[256,256]{1,0:T(8,128)(2,1)S(1)} %copy-done.9), channel_id=1, source_target_pairs={{0,3},{1,0},{2,1},{3,2},{4,7},{5,4},{6,5},{7,6},{8,11},{9,8},{10,9... | collective-permute-start | bytes 393224 | tf_op jit(solution)/shard_map/ppermute | solution.py:266
  68.0 6.5 %copy-start.3 = (f32[256,256]{1,0:T(8,128)S(1)}, f32[256,256]{1,0:T(8,128)}, u32[]{:S(2)}) copy-start(f32[256,256]{1,0:T(8,128)} %get-tuple-element.105.own_ref) | copy-start | bytes 786436
  68.0 6.7 %collective-permute-start.19 = (bf16[512,128]{1,0:T(8,128)(2,1)S(1)}, bf16[512,128]{1,0:T(8,128)(2,1)S(1)}, u32[]{:S(2)}, u32[]{:S(2)}) collective-permute-start(bf16[512,128]{1,0:T(8,128)(2,1)S(1)} %get-tuple-element.103.refs_0_), channel_id=1, source_target_pairs={{0,8},{4,12},{8,0},{12,4},{16,24},{20,28},{24,16},{28,20},{1,9},{5... | collective-permute-start | bytes 393224 | tf_op jit(solution)/shard_map/ppermute | solution.py:259
  69.5 5.2 %collective-permute-start.20 = (bf16[512,128]{1,0:T(8,128)(2,1)S(1)}, bf16[512,128]{1,0:T(8,128)(2,1)S(1)}, u32[]{:S(2)}, u32[]{:S(2)}) collective-permute-start(bf16[512,128]{1,0:T(8,128)(2,1)S(1)} %get-tuple-element.103.refs_0_), channel_id=1, source_target_pairs={{0,16},{4,20},{8,24},{12,28},{16,0},{20,4},{24,8},{28,12},{1,17},{... | collective-permute-start | bytes 393224 | tf_op jit(solution)/shard_map/ppermute | solution.py:259
  72.3 5.9 %collective-permute-start.21 = (bf16[512,128]{1,0:T(8,128)(2,1)S(1)}, bf16[512,128]{1,0:T(8,128)(2,1)S(1)}, u32[]{:S(2)}, u32[]{:S(2)}) collective-permute-start(bf16[512,128]{1,0:T(8,128)(2,1)S(1)} %get-tuple-element.103.refs_0_), channel_id=1, source_target_pairs={{0,24},{4,28},{8,16},{12,20},{16,8},{20,12},{24,0},{28,4},{1,25},{... | collective-permute-start | bytes 393224 | tf_op jit(solution)/shard_map/ppermute | solution.py:259
  74.5 8.1 %copy-start.8 = (bf16[256,256]{1,0:T(8,128)(2,1)S(1)}, bf16[256,256]{1,0:T(8,128)(2,1)}, u32[]{:S(2)}) copy-start(bf16[256,256]{1,0:T(8,128)(2,1)} %get-tuple-element.126) | copy-start | bytes 393220
  74.5 10.9 %copy-start.7 = (bf16[256,256]{1,0:T(8,128)(2,1)S(1)}, bf16[256,256]{1,0:T(8,128)(2,1)}, u32[]{:S(2)}) copy-start(bf16[256,256]{1,0:T(8,128)(2,1)} %get-tuple-element.127) | copy-start | bytes 393220
  74.5 13.1 %copy-start.6 = (bf16[256,256]{1,0:T(8,128)(2,1)S(1)}, bf16[256,256]{1,0:T(8,128)(2,1)}, u32[]{:S(2)}) copy-start(bf16[256,256]{1,0:T(8,128)(2,1)} %get-tuple-element.128) | copy-start | bytes 393220
  74.6 3.6 %collective-permute-start.26 = (f32[256,128]{1,0:T(8,128)S(1)}, f32[256,128]{1,0:T(8,128)S(1)}, u32[]{:S(2)}, u32[]{:S(2)}) collective-permute-start(f32[256,128]{1,0:T(8,128)S(1)} %get-tuple-element.117), channel_id=1, source_target_pairs={{0,4},{4,0},{8,12},{12,8},{16,20},{20,16},{24,28},{28,24},{1,5},{5... | collective-permute-start | bytes 393224 | tf_op jit(solution)/shard_map/ppermute | solution.py:255
  79.0 12.1 %collective-permute-start.36 = (bf16[2048,128]{1,0:T(8,128)(2,1)S(1)}, bf16[2048,128]{1,0:T(8,128)(2,1)S(1)}, u32[]{:S(2)}, u32[]{:S(2)}) collective-permute-start(bf16[2048,128]{1,0:T(8,128)(2,1)S(1)} %get-tuple-element.131.kept_ref), channel_id=1, source_target_pairs={{0,4},{4,0},{8,12},{12,8},{16,20},{20,16},{24,28},{28,24},{1,5},{5... | collective-permute-start | bytes 1572872 | tf_op jit(solution)/shard_map/ppermute | solution.py:255
  79.0 6.4 %collective-permute-start.27 = (bf16[512,128]{1,0:T(8,128)(2,1)S(1)}, bf16[512,128]{1,0:T(8,128)(2,1)S(1)}, u32[]{:S(2)}, u32[]{:S(2)}) collective-permute-start(bf16[512,128]{1,0:T(8,128)(2,1)S(1)} %get-tuple-element.118.refs_0_), channel_id=1, source_target_pairs={{0,8},{4,12},{8,0},{12,4},{16,24},{20,28},{24,16},{28,20},{1,9},{5... | collective-permute-start | bytes 393224 | tf_op jit(solution)/shard_map/ppermute | solution.py:259
  80.2 7.4 %collective-permute-start.28 = (bf16[512,128]{1,0:T(8,128)(2,1)S(1)}, bf16[512,128]{1,0:T(8,128)(2,1)S(1)}, u32[]{:S(2)}, u32[]{:S(2)}) collective-permute-start(bf16[512,128]{1,0:T(8,128)(2,1)S(1)} %get-tuple-element.118.refs_0_), channel_id=1, source_target_pairs={{0,16},{4,20},{8,24},{12,28},{16,0},{20,4},{24,8},{28,12},{1,17},{... | collective-permute-start | bytes 393224 | tf_op jit(solution)/shard_map/ppermute | solution.py:259
  81.7 7.6 %collective-permute-start.29 = (bf16[512,128]{1,0:T(8,128)(2,1)S(1)}, bf16[512,128]{1,0:T(8,128)(2,1)S(1)}, u32[]{:S(2)}, u32[]{:S(2)}) collective-permute-start(bf16[512,128]{1,0:T(8,128)(2,1)S(1)} %get-tuple-element.118.refs_0_), channel_id=1, source_target_pairs={{0,24},{4,28},{8,16},{12,20},{16,8},{20,12},{24,0},{28,4},{1,25},{... | collective-permute-start | bytes 393224 | tf_op jit(solution)/shard_map/ppermute | solution.py:259
  82.6 12.0 %collective-permute-start.33 = (bf16[256,256]{1,0:T(8,128)(2,1)S(1)}, bf16[256,256]{1,0:T(8,128)(2,1)S(1)}, u32[]{:S(2)}, u32[]{:S(2)}) collective-permute-start(bf16[256,256]{1,0:T(8,128)(2,1)S(1)} %copy-done.8), channel_id=1, source_target_pairs={{0,2},{1,3},{2,0},{3,1},{4,6},{5,7},{6,4},{7,5},{8,10},{9,11},{10,... | collective-permute-start | bytes 393224 | tf_op jit(solution)/shard_map/ppermute | solution.py:266
  85.4 9.2 %collective-permute-start.34 = (bf16[256,256]{1,0:T(8,128)(2,1)S(1)}, bf16[256,256]{1,0:T(8,128)(2,1)S(1)}, u32[]{:S(2)}, u32[]{:S(2)}) collective-permute-start(bf16[256,256]{1,0:T(8,128)(2,1)S(1)} %copy-done.7), channel_id=1, source_target_pairs={{0,1},{1,2},{2,3},{3,0},{4,5},{5,6},{6,7},{7,4},{8,9},{9,10},{10,1... | collective-permute-start | bytes 393224 | tf_op jit(solution)/shard_map/ppermute | solution.py:266
  87.6 8.3 %collective-permute-start.35 = (bf16[256,256]{1,0:T(8,128)(2,1)S(1)}, bf16[256,256]{1,0:T(8,128)(2,1)S(1)}, u32[]{:S(2)}, u32[]{:S(2)}) collective-permute-start(bf16[256,256]{1,0:T(8,128)(2,1)S(1)} %copy-done.6), channel_id=1, source_target_pairs={{0,3},{1,0},{2,1},{3,2},{4,7},{5,4},{6,5},{7,6},{8,11},{9,8},{10,9... | collective-permute-start | bytes 393224 | tf_op jit(solution)/shard_map/ppermute | solution.py:266
  90.0 5.9 %copy-start.2 = (f32[256,256]{1,0:T(8,128)S(1)}, f32[256,256]{1,0:T(8,128)}, u32[]{:S(2)}) copy-start(f32[256,256]{1,0:T(8,128)} %get-tuple-element.122.own_ref) | copy-start | bytes 786436
  90.0 6.1 %collective-permute-start.30 = (bf16[512,128]{1,0:T(8,128)(2,1)S(1)}, bf16[512,128]{1,0:T(8,128)(2,1)S(1)}, u32[]{:S(2)}, u32[]{:S(2)}) collective-permute-start(bf16[512,128]{1,0:T(8,128)(2,1)S(1)} %get-tuple-element.120.refs_0_), channel_id=1, source_target_pairs={{0,8},{4,12},{8,0},{12,4},{16,24},{20,28},{24,16},{28,20},{1,9},{5... | collective-permute-start | bytes 393224 | tf_op jit(solution)/shard_map/ppermute | solution.py:259
  91.1 5.0 %collective-permute-start.31 = (bf16[512,128]{1,0:T(8,128)(2,1)S(1)}, bf16[512,128]{1,0:T(8,128)(2,1)S(1)}, u32[]{:S(2)}, u32[]{:S(2)}) collective-permute-start(bf16[512,128]{1,0:T(8,128)(2,1)S(1)} %get-tuple-element.120.refs_0_), channel_id=1, source_target_pairs={{0,16},{4,20},{8,24},{12,28},{16,0},{20,4},{24,8},{28,12},{1,17},{... | collective-permute-start | bytes 393224 | tf_op jit(solution)/shard_map/ppermute | solution.py:259
  94.6 5.9 %collective-permute-start.32 = (bf16[512,128]{1,0:T(8,128)(2,1)S(1)}, bf16[512,128]{1,0:T(8,128)(2,1)S(1)}, u32[]{:S(2)}, u32[]{:S(2)}) collective-permute-start(bf16[512,128]{1,0:T(8,128)(2,1)S(1)} %get-tuple-element.120.refs_0_), channel_id=1, source_target_pairs={{0,24},{4,28},{8,16},{12,20},{16,8},{20,12},{24,0},{28,4},{1,25},{... | collective-permute-start | bytes 393224 | tf_op jit(solution)/shard_map/ppermute | solution.py:259
  95.9 4.6 %collective-permute-start.37 = (f32[256,128]{1,0:T(8,128)S(1)}, f32[256,128]{1,0:T(8,128)S(1)}, u32[]{:S(2)}, u32[]{:S(2)}) collective-permute-start(f32[256,128]{1,0:T(8,128)S(1)} %get-tuple-element.135), channel_id=1, source_target_pairs={{0,4},{4,0},{8,12},{12,8},{16,20},{20,16},{24,28},{28,24},{1,5},{5... | collective-permute-start | bytes 393224 | tf_op jit(solution)/shard_map/ppermute | solution.py:255
  101.2 12.1 %collective-permute-start.38 = (f32[3,256,128]{2,1,0:T(8,128)S(1)}, f32[3,256,128]{2,1,0:T(8,128)S(1)}, u32[]{:S(2)}, u32[]{:S(2)}) collective-permute-start(f32[3,256,128]{2,1,0:T(8,128)S(1)} %pad_maximum_fusion.1), channel_id=1, source_target_pairs={{0,4},{4,0},{8,12},{12,8},{16,20},{20,16},{24,28},{28,24},{1,5},{5... | collective-permute-start | bytes 1179656 | tf_op jit(solution)/shard_map/ppermute | solution.py:255
  101.3 6.4 %collective-permute-start.39 = (bf16[512,128]{1,0:T(8,128)(2,1)S(1)}, bf16[512,128]{1,0:T(8,128)(2,1)S(1)}, u32[]{:S(2)}, u32[]{:S(2)}) collective-permute-start(bf16[512,128]{1,0:T(8,128)(2,1)S(1)} %shard_map.71.refs_0_), channel_id=1, source_target_pairs={{0,8},{4,12},{8,0},{12,4},{16,24},{20,28},{24,16},{28,20},{1,9},{5... | collective-permute-start | bytes 393224 | tf_op jit(solution)/shard_map/ppermute | solution.py:259
  102.2 8.4 %collective-permute-start.40 = (bf16[512,128]{1,0:T(8,128)(2,1)S(1)}, bf16[512,128]{1,0:T(8,128)(2,1)S(1)}, u32[]{:S(2)}, u32[]{:S(2)}) collective-permute-start(bf16[512,128]{1,0:T(8,128)(2,1)S(1)} %shard_map.71.refs_0_), channel_id=1, source_target_pairs={{0,16},{4,20},{8,24},{12,28},{16,0},{20,4},{24,8},{28,12},{1,17},{... | collective-permute-start | bytes 393224 | tf_op jit(solution)/shard_map/ppermute | solution.py:259
  102.3 8.3 %collective-permute-start.41 = (bf16[512,128]{1,0:T(8,128)(2,1)S(1)}, bf16[512,128]{1,0:T(8,128)(2,1)S(1)}, u32[]{:S(2)}, u32[]{:S(2)}) collective-permute-start(bf16[512,128]{1,0:T(8,128)(2,1)S(1)} %shard_map.71.refs_0_), channel_id=1, source_target_pairs={{0,24},{4,28},{8,16},{12,20},{16,8},{20,12},{24,0},{28,4},{1,25},{... | collective-permute-start | bytes 393224 | tf_op jit(solution)/shard_map/ppermute | solution.py:259
  112.0 1.3 %collective-permute-start.42 = (f32[256,128]{1,0:T(8,128)S(1)}, f32[256,128]{1,0:T(8,128)S(1)}, u32[]{:S(2)}, u32[]{:S(2)}) collective-permute-start(f32[256,128]{1,0:T(8,128)S(1)} %get-tuple-element.140), channel_id=1, source_target_pairs={{0,4},{4,0},{8,12},{12,8},{16,20},{20,16},{24,28},{28,24},{1,5},{5... | collective-permute-start | bytes 393224 | tf_op jit(solution)/shard_map/ppermute | solution.py:255

commit v4 on v3

--- a/solution.py
+++ b/solution.py
@@ -19,6 +19,10 @@
 
 def params(mebibytes):
     return pltpu.CompilerParams(vmem_limit_bytes=mebibytes << 20)
+
+
+def in_hbm(array):
+    return pltpu.with_memory_space_constraint(array, pltpu.HBM)
 
 
 def work(rows, depth, columns):
@@ -63,12 +67,12 @@
         out[...] = total[:, pl.ds(begin, width)].astype(out.dtype)
 
 
-def second_kernel(shifts, pieces, flight, l_ref, x_ref, *refs):
+def later_kernel(shifts, pieces, flight, l_ref, x_ref, *refs):
     count = len(shifts)
     rows, depth = l_ref.shape[1:]
     blocks = l_ref.shape[0] - 1
-    outs, refs = refs[: blocks * count], refs[blocks * count :]
-    l_buf, x_buf, total, sent, kept, l_sems, x_sems, out_sems = refs
+    outs, refs = refs[: count + 2 * (blocks - 1)], refs[count + 2 * (blocks - 1) :]
+    l_buf, x_buf, total, low, exact, l_sems, x_sems, out_sems = refs
     deep = depth // pieces
     width = x_ref.shape[1] // count
     mine = lax.axis_index("col")
@@ -99,25 +103,55 @@
             total, piece, jnp.dot(l_buf[piece], x_buf[piece], preferred_element_type=F32)
         )
     copies = []
-    for block in range(blocks):
-        for k, shift in enumerate(shifts):
-            begin = pl.multiple_of(lax.rem(mine + shift, count) * width, width)
-            found = total[block * rows : (block + 1) * rows, pl.ds(begin, width)]
-            held = sent.at[block, k] if shift else kept.at[block]
-            held[...] = found.astype(held.dtype)
-            copy = pltpu.make_async_copy(held, outs[block * count + k], out_sems.at[block, k])
-            copy.start()
-            copies.append(copy)
+
+    def found(block, chunk):
+        begin = pl.multiple_of(chunk * width, width)
+        return total[block * rows : (block + 1) * rows, pl.ds(begin, width)]
+
+    def send_out(held, out):
+        copy = pltpu.make_async_copy(held, out, out_sems.at[len(copies)])
+        copy.start()
+        copies.append(copy)
+
+    for k, shift in enumerate(shifts):
+        held = low.at[0, k] if shift else exact.at[0, 0]
+        held[...] = found(0, lax.rem(mine + shift, count)).astype(held.dtype)
+        send_out(held, outs[k])
+    for block in range(1, blocks):
+        for slot in range(count):
+            held = (low if slot % 2 else exact).at[block, slot // 2]
+            held[...] = found(block, mine ^ slot).astype(held.dtype)
+        place = count + 2 * (block - 1)
+        send_out(low.at[block, pl.ds(0, count // 2)], outs[place])
+        send_out(exact.at[block], outs[place + 1])
     for copy in copies:
         copy.wait()
 
 
-def load_kernel(indices, *refs):
-    count = len(refs) // 2
+def combine_kernel(exact_ref, arrived_ref, low_out, exact_out):
+    for k in range(exact_ref.shape[0]):
+        out = low_out if k % 2 else exact_out
+        out[k // 2] = (exact_ref[k] + arrived_ref[k].astype(F32)).astype(out.dtype)
+
+
+def combine(exact, arrived):
+    count, rows, width = exact.shape
+    return pl.pallas_call(
+        combine_kernel,
+        in_specs=[VMEM] * 2,
+        out_specs=[VMEM] * 2,
+        out_shape=[pltpu.VMEM((count // 2, rows, width), dtype) for dtype in (BF16, F32)],
+        compiler_params=params(8),
+        cost_estimate=SMALL,
+    )(exact, arrived)
+
+
+def load_kernel(stacks, *refs):
+    count = len(stacks)
     ins, outs, sems = refs[:count], refs[count:-1], refs[-1]
     copies = [
-        pltpu.make_async_copy(ref.at[index], out.at[place], sems.at[k, place])
-        for k, (ref, out) in enumerate(zip(ins, outs))
+        pltpu.make_async_copy(ins[k].at[index], outs[k].at[place], sems.at[k, place])
+        for k, indices in enumerate(stacks)
         for place, index in enumerate(indices)
     ]
     for copy in copies:
@@ -126,27 +160,27 @@
         copy.wait()
 
 
-def load(arrays, indices):
-    shapes = [
-        jax.ShapeDtypeStruct((len(indices), *array.shape[1:]), array.dtype) for array in arrays
-    ]
+def load(*stacks):
+    picks = tuple(tuple(indices) for _, indices in stacks)
     return pl.pallas_call(
-        functools.partial(load_kernel, tuple(indices)),
-        in_specs=[HBM] * len(arrays),
-        out_specs=[VMEM] * len(arrays),
-        out_shape=shapes,
-        scratch_shapes=[pltpu.SemaphoreType.DMA((len(arrays), len(indices)))],
-        compiler_params=params(16),
+        functools.partial(load_kernel, picks),
+        in_specs=[HBM] * len(stacks),
+        out_specs=[VMEM] * len(stacks),
+        out_shape=[
+            pltpu.VMEM((len(indices), *array.shape[1:]), array.dtype) for array, indices in stacks
+        ],
+        scratch_shapes=[pltpu.SemaphoreType.DMA((len(stacks), max(map(len, picks))))],
+        compiler_params=params(8),
         cost_estimate=SMALL,
-    )(*arrays)
+    )(*[array for array, _ in stacks])
 
 
 def reduce_kernel(parts, rhs_ref, own_ref, *refs):
     arrived, refs = refs[:parts], refs[parts:]
     taken, (kept_ref, other_ref) = refs[:-2], refs[-2:]
-    total = rhs_ref[...] - own_ref[...]
+    total = rhs_ref[...] - own_ref[...].reshape(rhs_ref.shape)
     for ref in arrived:
-        total -= ref[...].astype(F32)
+        total -= ref[...].reshape(rhs_ref.shape).astype(F32)
     half = total.shape[1] // 2
     first = lax.rem(lax.axis_index("row"), 2) == 0
     kept = jnp.where(first, total[:, :half], total[:, half:])
@@ -173,14 +207,14 @@
     )(rhs, own, *arrived, *taken)
 
 
-def apply_kernel(index, parts, pairs, exact, full, own_ref, other_ref, *refs):
+def apply_kernel(index, parts, pairs, exact, full, low, own_ref, other_ref, *refs):
     shards, refs = refs[:parts], refs[parts:]
     held, outs = refs[: 2 * pairs], list(refs[2 * pairs :])
     me = lax.axis_index("row")
     core, chip = lax.rem(me, 2), me // 2
     rows = own_ref.shape[1]
     high, width = shards[0].shape
-    low_ref = outs.pop()
+    low_ref = outs.pop() if low else None
     full_ref = outs.pop() if full else None
     total = jnp.zeros((high, width), F32)
     for mask, shard in enumerate(shards):
@@ -195,19 +229,20 @@
             found = held[half][...] - found
         if exact:
             outs[half][...] = found
-        there = pl.ds(pl.multiple_of(place * rows, rows), rows)
-        low_ref[there, :] = found.astype(BF16)
-
-
-def apply_rows(matrices, index, shards, held, exact, full):
+        if low:
+            there = pl.ds(pl.multiple_of(place * rows, rows), rows)
+            low_ref[there, :] = found.astype(BF16)
+
+
+def apply_rows(matrices, index, shards, held, exact, full, low):
     _, rows, depth = matrices[0].shape
     high, width = shards[0].shape
     operands = [*matrices, *shards, *held]
-    shapes = [jax.ShapeDtypeStruct((rows, width), F32)] * (2 * exact)
-    shapes += [jax.ShapeDtypeStruct((depth, width), BF16)] * full
-    shapes.append(jax.ShapeDtypeStruct((high, width), BF16))
+    shapes = [pltpu.VMEM((rows, width), F32)] * (2 * exact)
+    shapes += [pltpu.VMEM((depth, width), BF16)] * full
+    shapes += [pltpu.VMEM((high, width), BF16)] * low
     return pl.pallas_call(
-        functools.partial(apply_kernel, index, len(shards), len(held) // 2, exact, full),
+        functools.partial(apply_kernel, index, len(shards), len(held) // 2, exact, full, low),
         in_specs=[VMEM] * len(operands),
         out_specs=[VMEM] * len(shapes),
         out_shape=shapes,
@@ -254,18 +289,15 @@
     def swap(value):
         return lax.ppermute(value, "row", [(i, i ^ 1) for i in range(row_count)])
 
-    def gather(value):
+    def gather(value, token=None):
+        late = value if token is None else after(value, token)
         others = [
-            lax.ppermute(value, "row", [(i, i ^ (2 * mask)) for i in range(row_count)])
+            lax.ppermute(
+                late if mask == 1 else value, "row", [(i, i ^ (2 * mask)) for i in range(row_count)]
+            )
             for mask in range(1, chips)
         ]
         return [value, *others]
-
-    def send_chunks(chunks):
-        return [
-            lax.ppermute(chunk, "col", [(i, (i + s) % col_count) for i in range(col_count)])
-            for s, chunk in zip(shifts[:-1], chunks)
-        ]
 
     def by_core(kept, other, axis):
         return jnp.where(
@@ -287,68 +319,122 @@
             pltpu.SemaphoreType.DMA((8,)),
             pltpu.SemaphoreType.DMA((8,)),
         ],
-        compiler_params=params(56),
+        compiler_params=params(16),
         cost_estimate=work(rows, depth, total),
-    )(l_panel, x_solved)
-    chunks = [first]
-    arrived = {0: send_chunks(first[:-1])}
+    )(in_hbm(l_panel), in_hbm(x_solved))
+    chunks, arrived = {0: first}, {target: [] for target in range(steps)}
+
+    def send(target, which, token):
+        arrived[target] += [
+            lax.ppermute(
+                after(chunks[target][k], token),
+                "col",
+                [(i, (i + shifts[k]) % col_count) for i in range(col_count)],
+            )
+            for k in which
+        ]
+
+    ahead, behind = range(1), range(1, col_count - 1)
+    send(0, range(col_count - 1), first[0])
+
+    blocks = steps - 1
+    shapes = list(chunk_shapes)
+    for _ in range(blocks - 1):
+        shapes += [jax.ShapeDtypeStruct((col_count // 2, rows, width), t) for t in (BF16, F32)]
     found = pl.pallas_call(
-        functools.partial(second_kernel, shifts, pieces, 2),
-        in_specs=[HBM, HBM],
-        out_specs=[HBM] * ((steps - 1) * col_count),
-        out_shape=chunk_shapes * (steps - 1),
+        functools.partial(later_kernel, shifts, pieces, 2),
+        in_specs=[HBM] * 2,
+        out_specs=[HBM] * len(shapes),
+        out_shape=[pltpu.HBM(shape.shape, shape.dtype) for shape in shapes],
         scratch_shapes=[
-            pltpu.VMEM((pieces, rows * (steps - 1), depth // pieces), BF16),
+            pltpu.VMEM((pieces, rows * blocks, depth // pieces), BF16),
             pltpu.VMEM((pieces, depth // pieces, total), BF16),
-            pltpu.VMEM((rows * (steps - 1), total), F32),
-            pltpu.VMEM((steps - 1, col_count - 1, rows, width), BF16),
-            pltpu.VMEM((steps - 1, rows, width), F32),
-            pltpu.SemaphoreType.DMA((pieces, steps - 1)),
+            pltpu.VMEM((rows * blocks, total), F32),
+            pltpu.VMEM((blocks, col_count - 1, rows, width), BF16),
+            pltpu.VMEM((blocks, col_count // 2, rows, width), F32),
+            pltpu.SemaphoreType.DMA((pieces, blocks)),
             pltpu.SemaphoreType.DMA((pieces,)),
-            pltpu.SemaphoreType.DMA((steps - 1, col_count)),
+            pltpu.SemaphoreType.DMA((len(shapes),)),
         ],
-        compiler_params=params(56),
-        cost_estimate=work(rows * (steps - 1), depth, total),
-    )(l_panel, after(x_solved, first[0]))
-    chunks += [found[i * col_count : (i + 1) * col_count] for i in range(steps - 1)]
+        compiler_params=params(60),
+        cost_estimate=work(rows * blocks, depth, total),
+    )(in_hbm(l_panel), in_hbm(after(x_solved, first[0])))
+    chunks[1], found = found[:col_count], found[col_count:]
+    halves = {target: found[2 * target - 4 : 2 * target - 2] for target in range(2, steps)}
+
+    def halve(target, stage, token):
+        low, exact = halves[target]
+        if stage:
+            arrived_low = arrived[target]
+            low, exact = combine(after(exact, token), arrived_low)
+        else:
+            low = after(low, token)
+        pairs = [(i, i ^ (1 << stage)) for i in range(col_count)]
+        halves[target] = (low, exact)
+        arrived[target] = lax.ppermute(low, "col", pairs)
+
     taken = {target: [] for target in range(steps)}
 
     def reduced(target, token, dtype):
-        own = after(chunks[target][-1], token)
-        kept, other = reduce_rows(rhs, target, own, arrived[target], taken[target], dtype)
-        return kept, swap(other)
-
-    resid_low = by_core(*reduced(0, found[0], BF16), 0)
-    results = []
+        if target in chunks:
+            own, parts = chunks[target][-1], arrived[target]
+        else:
+            own, parts = halves[target][1], [arrived[target]]
+        return reduce_rows(rhs, target, after(own, token), parts, taken[target], dtype)
+
+    kept, other = reduced(0, (chunks[1][0], diag_other), BF16)
+    send(1, ahead, other)
+    resid_low = by_core(kept, swap(other), 0)
+    results, wholes = [], {}
+    stages = (col_count - 1).bit_length()
     for target in range(steps):
         last = target + 1 == steps
         shards = gather(resid_low)
         if target == 0:
-            arrived[1] = send_chunks(after(chunks[1][:-1], resid_low))
-            diag = load((after(diag_inv, resid_low), diag_other), range(steps))
-        kept, other, solved_low = apply_rows(diag, target, shards, [], True, False)
+            later = in_hbm(after(diag_inv, resid_low))
+            diag = {0: load((later, [0]), (in_hbm(diag_other), [0]))}
+            send(1, behind, (resid_low, inner_other, diag[0]))
+        elif not last:
+            for stage in range(1, stages):
+                halve(target + 1, stage, resid_low)
+        else:
+            before = jnp.stack([other for _, other in results])
+            swapped = swap(after(before, resid_low))
+            parts = [by_core(kept, swapped[k], 1) for k, (kept, _) in enumerate(results)]
+            solved = jnp.stack([*parts, jnp.zeros_like(parts[0])])
+            shards, solved = lax.optimization_barrier((shards, solved))
+        kept, other, *low = apply_rows(diag[target], 0, shards, [], True, False, not last)
         results.append((kept, other))
         if last:
             break
-        shards = gather(solved_low)
+        (solved_low,) = low
+        shards = gather(solved_low, arrived[1][0] if target == 0 else None)
+        if target == 0:
+            inner = load((in_hbm(after(l_inner, solved_low)), near), (in_hbm(inner_other), near))
+            token = (solved_low, inner)
+        elif target == 1:
+            (far_own,) = load((in_hbm(after(l_inner, solved_low)), far))
+            token = solved_low
+        else:
+            token = solved_low
         if target + 2 < steps:
-            arrived[target + 2] = send_chunks(after(chunks[target + 2][:-1], solved_low))
-        if target == 0:
-            inner = load((after(l_inner, solved_low), inner_other), near)
-        held = reduced(target + 1, solved_low, F32)
-        *full, resid_low = apply_rows(inner, target, shards, held, False, target + 2 < steps)
+            halve(target + 2, 0, token)
+        for earlier in list(wholes):
+            followers = range(earlier + 2, steps)
+            places = [far.index(inner_index(follower, earlier)) for follower in followers]
+            for follower, pair in zip(followers, own_rows(far_own, places, *wholes.pop(earlier))):
+                taken[follower].append(pair)
+        kept, other = reduced(target + 1, token, F32)
+        later = in_hbm(after(diag_inv, other))
+        diag[target + 1] = load((later, [target + 1]), (in_hbm(diag_other), [target + 1]))
+        held = (kept, swap(other))
+        shards, diag[target + 1] = lax.optimization_barrier((shards, diag[target + 1]))
+        *full, resid_low = apply_rows(inner, target, shards, held, False, target + 2 < steps, True)
         if full:
-            followers = range(target + 2, steps)
-            places = [far.index(inner_index(follower, target)) for follower in followers]
             whole = after(full[0], resid_low)
-            if target == 0:
-                (far_own,) = load((after(l_inner, resid_low),), far)
-            for follower, pair in zip(followers, own_rows(far_own, places, whole, swap(whole))):
-                taken[follower].append(pair)
-    before = jnp.stack([other for _, other in results[:-1]])
-    swapped = swap(after(before, resid_low))
-    others = [swapped[k] for k in range(steps - 1)] + [swap(results[-1][1])]
-    return jnp.stack([by_core(kept, other, 1) for (kept, _), other in zip(results, others)], axis=0)
+            wholes[target] = (whole, swap(whole))
+    kept, other = results[-1]
+    return lax.dynamic_update_slice(solved, by_core(kept, swap(other), 1)[None], (steps - 1, 0, 0))
 
 
 def solution(mesh):

time: 115 us -> 100 us (0.87)
  waiting for transfers between devices: 36.9 us -> 18.6 us
  Pallas kernels: 29.6 us -> 34.1 us
  local copies, waits for them, and re-layouts: 2.45 us -> 0.14 us
    ppermute x33 -> x31, waiting for transfers between devices: 34.3 us -> 16 us  [the longest x4 8.26 us: halve(): arrived[target] = lax.ppermute(low, 'col', pairs)]
    pallas_call x4 -> x9, Pallas kernels: 16.1 us -> 22.1 us  [the longest x1 11 us: local(): pl.pallas_call(functools.partial(later_kernel, shifts, pieces, 2), in_spe...]
    unnamed x28 -> x16, local copies, waits for them, and re-layouts: 2.42 us -> 0.04 us
    ppermute x33 -> x31, starting transfers between devices: 42.9 us -> 42.7 us  [the longest x21 25.4 us: gather(): lax.ppermute(late if mask == 1 else value, 'row', [(i, i ^ 2 * mask) for...]
  transfers between devices with their start and end apart: 43 -> 41, of which waited for: 18 -> 12; matrix products, arithmetic and copies ran while one was open for 0% -> 1% of each run, Pallas kernels for 24% -> 31%
where the time goes in v4:
time: 100 us; the launch traced here: 99.9 us
  starting transfers between devices  44.7 us (45%)
  Pallas kernels  34.1 us (34%)
  waiting for transfers between devices  18.6 us (19%)
  other arithmetic  1.99 us (2%)
    ppermute x21, starting transfers between devices, gather(): lax.ppermute(late if mask == 1 else value, 'row', [(i, i ^ 2 * mask) for...  25.4 us
    pallas_call x1, Pallas kernels, local(): pl.pallas_call(functools.partial(later_kernel, shifts, pieces, 2), in_spe...  11 us
    pallas_call x6, Pallas kernels, load(): pl.pallas_call(functools.partial(load_kernel, picks), in_specs=[HBM] * le...  11 us
    ppermute x6, starting transfers between devices, send(): lax.ppermute(after(chunks[target][k], token), 'col', [(i, (i + shifts[k])...  10.2 us
    ppermute x4, waiting for transfers between devices, halve(): arrived[target] = lax.ppermute(low, 'col', pairs)  8.26 us
    ppermute x4, starting transfers between devices, halve(): arrived[target] = lax.ppermute(low, 'col', pairs)  7.16 us
    ppermute x21, waiting for transfers between devices, gather(): lax.ppermute(late if mask == 1 else value, 'row', [(i, i ^ 2 * mask) for...  6.44 us
    pallas_call x7, Pallas kernels, apply_rows(): pl.pallas_call(functools.partial(apply_kernel, index, len(shards), len(he...  5.09 us
  transfers between devices with their start and end apart: 41, of which 12 were waited for; matrix products, arithmetic and copies ran while one was open for 1% of the time, Pallas kernels for 31%

profile of v4, /device:TPU:0, one launch (start us, length us, event | category | flops | bytes accessed | tf_op | source)
XLA Modules:
  0.0 99.9 jit_solution(9640024221702605207)
XLA Ops:
  0.0 0.5 collective-permute-start.8
  0.5 4.7 %shard_map.55 = (bf16[256,256]{1,0:T(8,128)(2,1)S(1)}, bf16[256,256]{1,0:T(8,128)(2,1)S(1)}, bf16[256,256]{1,0:T(8,128)(2,1)S(1)}, f32[256,256]{1,0:T(8,128)S(1)}) custom-call(bf16[4,256,4096]{2,1,0:T(8,128)(2,1)} %l_ref.3, bf16[4096,1024]{1,0:T(8,128)(2,1)} %x_ref.2), custom_call_target="tpu_custom_call" | custom-call | flops 2147483648 | bytes 10485760 | tf_op jit(solution)/shard_map/pallas_call | solution.py:310
  5.3 3.1 %collective-permute-start.2 = (bf16[256,256]{1,0:T(8,128)(2,1)S(1)}, bf16[256,256]{1,0:T(8,128)(2,1)S(1)}, u32[]{:S(2)}, u32[]{:S(2)}) collective-permute-start(bf16[256,256]{1,0:T(8,128)(2,1)S(1)} %get-tuple-element.115), channel_id=1, source_target_pairs={{0,1},{1,2},{2,3},{3,0},{4,5},{5,6},{6,7},{7,4},{8,9},{9,10},{10,1... | collective-permute-start | bytes 393224 | tf_op jit(solution)/shard_map/ppermute | solution.py:329
  8.3 2.1 %collective-permute-start.3 = (bf16[256,256]{1,0:T(8,128)(2,1)S(1)}, bf16[256,256]{1,0:T(8,128)(2,1)S(1)}, u32[]{:S(2)}, u32[]{:S(2)}) collective-permute-start(bf16[256,256]{1,0:T(8,128)(2,1)S(1)} %get-tuple-element.117), channel_id=1, source_target_pairs={{0,3},{1,0},{2,1},{3,2},{4,7},{5,4},{6,5},{7,6},{8,11},{9,8},{10,9... | collective-permute-start | bytes 393224 | tf_op jit(solution)/shard_map/ppermute | solution.py:329
  10.4 0.9 collective-permute-start.1
  11.4 11.0 %shard_map.56 = (bf16[256,256]{1,0:T(8,128)(2,1)}, bf16[256,256]{1,0:T(8,128)(2,1)}, bf16[256,256]{1,0:T(8,128)(2,1)}, f32[256,256]{1,0:T(8,128)}, bf16[2,256,25...) custom-call(bf16[4,256,4096]{2,1,0:T(8,128)(2,1)} %l_ref.3, ...), custom_call_target="tpu_custom_call" | custom-call | flops 6442450944 | bytes 14680064 | tf_op jit(solution)/shard_map/pallas_call | solution.py:344
  22.6 1.2 %collective-permute-done.4 = bf16[256,128]{1,0:T(8,128)(2,1)S(1)} collective-permute-done((bf16[256,128]{1,0:T(8,128)(2,1)S(1)}, bf16[256,128]{1,0:T(8,128)(2,1)S(1)}, u32[]{:S(2)}, u32[]{:S(2)}) %collective-permute-start.4) | collective-permute-done | bytes 65568 | tf_op jit(solution)/shard_map/ppermute | solution.py:290
  23.9 1.6 %collective-permute-start.5 = (bf16[512,128]{1,0:T(8,128)(2,1)S(1)}, bf16[512,128]{1,0:T(8,128)(2,1)S(1)}, u32[]{:S(2)}, u32[]{:S(2)}) collective-permute-start(bf16[512,128]{1,0:T(8,128)(2,1)S(1)} %maximum_select_fusion.4.refs_0_), channel_id=1, source_target_pairs={{0,8},{4,12},{8,0},{12,4},{16,24},{20,28},{24,16},{28,20},{1,9},{5... | collective-permute-start | bytes 393224 | tf_op jit(solution)/shard_map/ppermute | solution.py:295
  25.5 1.5 %collective-permute-start.6 = (bf16[512,128]{1,0:T(8,128)(2,1)S(1)}, bf16[512,128]{1,0:T(8,128)(2,1)S(1)}, u32[]{:S(2)}, u32[]{:S(2)}) collective-permute-start(bf16[512,128]{1,0:T(8,128)(2,1)S(1)} %maximum_select_fusion.4.refs_0_), channel_id=1, source_target_pairs={{0,16},{4,20},{8,24},{12,28},{16,0},{20,4},{24,8},{28,12},{1,17},{... | collective-permute-start | bytes 393224 | tf_op jit(solution)/shard_map/ppermute | solution.py:295
  27.0 0.5 collective-permute-start.7
  27.5 2.0 %collective-permute-start.9 = (bf16[256,256]{1,0:T(8,128)(2,1)}, bf16[256,256]{1,0:T(8,128)(2,1)S(1)}, u32[]{:S(2)}, u32[]{:S(2)}) collective-permute-start(bf16[256,256]{1,0:T(8,128)(2,1)} %get-tuple-element.127), channel_id=1, source_target_pairs={{0,2},{1,3},{2,0},{3,1},{4,6},{5,7},{6,4},{7,5},{8,10},{9,11},{10,... | collective-permute-start | bytes 393224 | tf_op jit(solution)/shard_map/ppermute | solution.py:329
  29.4 1.6 %shard_map.58 = (bf16[1,256,2048]{2,1,0:T(8,128)(2,1)S(1)}, bf16[1,256,2048]{2,1,0:T(8,128)(2,1)S(1)}) custom-call(bf16[4,256,2048]{2,1,0:T(8,128)(2,1)} %refs_0_.5, bf16[4,256,2048]{2,1,0:T(8,128)(2,1)} %collective-permute-done.refs_1_), custom_call_target="tpu_custom_call" | custom-call | flops 1024 | bytes 1024 | tf_op jit(solution)/shard_map/pallas_call | solution.py:165
  31.0 2.0 %collective-permute-start.14 = (bf16[256,256]{1,0:T(8,128)(2,1)S(1)}, bf16[256,256]{1,0:T(8,128)(2,1)S(1)}, u32[]{:S(2)}, u32[]{:S(2)}) collective-permute-start(bf16[256,256]{1,0:T(8,128)(2,1)S(1)} %copy-done.7), channel_id=1, source_target_pairs={{0,3},{1,0},{2,1},{3,2},{4,7},{5,4},{6,5},{7,6},{8,11},{9,8},{10,9... | collective-permute-start | bytes 393224 | tf_op jit(solution)/shard_map/ppermute | solution.py:329
  33.1 0.5 collective-permute-done.6.refs_2_
  33.6 0.7 shard_map.59
  34.3 1.6 %collective-permute-start.11 = (bf16[512,128]{1,0:T(8,128)(2,1)S(1)}, bf16[512,128]{1,0:T(8,128)(2,1)S(1)}, u32[]{:S(2)}, u32[]{:S(2)}) collective-permute-start(bf16[512,128]{1,0:T(8,128)(2,1)S(1)} %get-tuple-element.141.refs_0_), channel_id=1, source_target_pairs={{0,16},{4,20},{8,24},{12,28},{16,0},{20,4},{24,8},{28,12},{1,17},{... | collective-permute-start | bytes 393224 | tf_op jit(solution)/shard_map/ppermute | solution.py:295
  35.9 1.2 %collective-permute-start.12 = (bf16[512,128]{1,0:T(8,128)(2,1)S(1)}, bf16[512,128]{1,0:T(8,128)(2,1)S(1)}, u32[]{:S(2)}, u32[]{:S(2)}) collective-permute-start(bf16[512,128]{1,0:T(8,128)(2,1)S(1)} %get-tuple-element.141.refs_0_), channel_id=1, source_target_pairs={{0,24},{4,28},{8,16},{12,20},{16,8},{20,12},{24,0},{28,4},{1,25},{... | collective-permute-start | bytes 393224 | tf_op jit(solution)/shard_map/ppermute | solution.py:295
  37.1 1.2 %collective-permute-done.9.refs_0_ = bf16[256,256]{1,0:T(8,128)(2,1)S(1)} collective-permute-done((bf16[256,256]{1,0:T(8,128)(2,1)}, bf16[256,256]{1,0:T(8,128)(2,1)S(1)}, u32[]{:S(2)}, u32[]{:S(2)}) %collective-permute-start.9) | collective-permute-done | bytes 131104 | tf_op jit(solution)/shard_map/ppermute | solution.py:329
  38.3 1.5 %collective-permute-start.10 = (bf16[512,128]{1,0:T(8,128)(2,1)S(1)}, bf16[512,128]{1,0:T(8,128)(2,1)S(1)}, u32[]{:S(2)}, u32[]{:S(2)}) collective-permute-start(bf16[512,128]{1,0:T(8,128)(2,1)S(1)} %get-tuple-element.141.refs_0_), channel_id=1, source_target_pairs={{0,8},{4,12},{8,0},{12,4},{16,24},{20,28},{24,16},{28,20},{1,9},{5... | collective-permute-start | bytes 393224 | tf_op jit(solution)/shard_map/ppermute | solution.py:295
  39.8 2.9 %shard_map.60 = (bf16[3,256,2048]{2,1,0:T(8,128)(2,1)S(1)}, bf16[3,256,2048]{2,1,0:T(8,128)(2,1)S(1)}) custom-call(bf16[6,256,2048]{2,1,0:T(8,128)(2,1)} %refs_0_.3, bf16[6,256,2048]{2,1,0:T(8,128)(2,1)} %collective-permute-done.8.refs_1_), custom_call_target="tpu_custom_call" | custom-call | flops 1024 | bytes 1024 | tf_op jit(solution)/shard_map/pallas_call | solution.py:165
  42.8 1.6 %shard_map.62 = (bf16[1,256,2048]{2,1,0:T(8,128)(2,1)S(1)}, bf16[1,256,2048]{2,1,0:T(8,128)(2,1)S(1)}) custom-call(bf16[4,256,2048]{2,1,0:T(8,128)(2,1)} %refs_0_.5, bf16[4,256,2048]{2,1,0:T(8,128)(2,1)} %collective-permute-done.refs_1_), custom_call_target="tpu_custom_call" | custom-call | flops 1024 | bytes 1024 | tf_op jit(solution)/shard_map/pallas_call | solution.py:165
  44.5 0.8 shard_map.63
  45.2 0.6 collective-permute-start.24
  45.8 0.7 collective-permute-start.22
  46.5 0.7 collective-permute-start.16
  47.2 1.4 %collective-permute-start.17 = (bf16[512,128]{1,0:T(8,128)(2,1)S(1)}, bf16[512,128]{1,0:T(8,128)(2,1)S(1)}, u32[]{:S(2)}, u32[]{:S(2)}) collective-permute-start(bf16[512,128]{1,0:T(8,128)(2,1)S(1)} %get-tuple-element.146.refs_0_), channel_id=1, source_target_pairs={{0,16},{4,20},{8,24},{12,28},{16,0},{20,4},{24,8},{28,12},{1,17},{... | collective-permute-start | bytes 393224 | tf_op jit(solution)/shard_map/ppermute | solution.py:295
  48.6 1.4 %collective-permute-start.18 = (bf16[512,128]{1,0:T(8,128)(2,1)S(1)}, bf16[512,128]{1,0:T(8,128)(2,1)S(1)}, u32[]{:S(2)}, u32[]{:S(2)}) collective-permute-start(bf16[512,128]{1,0:T(8,128)(2,1)S(1)} %get-tuple-element.146.refs_0_), channel_id=1, source_target_pairs={{0,24},{4,28},{8,16},{12,20},{16,8},{20,12},{24,0},{28,4},{1,25},{... | collective-permute-start | bytes 393224 | tf_op jit(solution)/shard_map/ppermute | solution.py:295
  50.0 4.1 %collective-permute-done.22.arrived_ref = bf16[2,256,256]{2,1,0:T(8,128)(2,1)S(1)} collective-permute-done((bf16[2,256,256]{2,1,0:T(8,128)(2,1)S(1)}, bf16[2,256,256]{2,1,0:T(8,128)(2,1)S(1)}, u32[]{:S(2)}, u32[]{:S(2)}) %collective-permute-start.22) | collective-permute-done | bytes 262176 | tf_op jit(solution)/shard_map/ppermute | solution.py:374
  54.1 2.3 %collective-permute-start.23 = (bf16[1,256,256]{2,1,0:T(8,128)(2,1)S(1)}, bf16[1,256,256]{2,1,0:T(8,128)(2,1)S(1)}, u32[]{:S(2)}, u32[]{:S(2)}) collective-permute-start(bf16[1,256,256]{2,1,0:T(8,128)(2,1)S(1)} %get-tuple-element.154), channel_id=1, source_target_pairs={{0,2},{1,3},{2,0},{3,1},{4,6},{5,7},{6,4},{7,5},{8,10},{9,11},{10,... | collective-permute-start | bytes 393224 | tf_op jit(solution)/shard_map/ppermute | solution.py:374
  56.5 0.7 shard_map.64
  57.2 0.7 collective-permute-start.19
  58.0 1.4 %collective-permute-start.20 = (bf16[512,128]{1,0:T(8,128)(2,1)S(1)}, bf16[512,128]{1,0:T(8,128)(2,1)S(1)}, u32[]{:S(2)}, u32[]{:S(2)}) collective-permute-start(bf16[512,128]{1,0:T(8,128)(2,1)S(1)} %get-tuple-element.165.refs_0_), channel_id=1, source_target_pairs={{0,16},{4,20},{8,24},{12,28},{16,0},{20,4},{24,8},{28,12},{1,17},{... | collective-permute-start | bytes 393224 | tf_op jit(solution)/shard_map/ppermute | solution.py:295
  59.3 1.4 %collective-permute-start.21 = (bf16[512,128]{1,0:T(8,128)(2,1)S(1)}, bf16[512,128]{1,0:T(8,128)(2,1)S(1)}, u32[]{:S(2)}, u32[]{:S(2)}) collective-permute-start(bf16[512,128]{1,0:T(8,128)(2,1)S(1)} %get-tuple-element.165.refs_0_), channel_id=1, source_target_pairs={{0,24},{4,28},{8,16},{12,20},{16,8},{20,12},{24,0},{28,4},{1,25},{... | collective-permute-start | bytes 393224 | tf_op jit(solution)/shard_map/ppermute | solution.py:295
  60.8 1.9 %shard_map.66.matrix_ref = bf16[3,256,2048]{2,1,0:T(8,128)(2,1)S(1)} custom-call(bf16[6,256,2048]{2,1,0:T(8,128)(2,1)} %refs_0_.3), custom_call_target="tpu_custom_call" | custom-call | flops 1024 | bytes 1024 | tf_op jit(solution)/shard_map/pallas_call | solution.py:165
  62.7 1.2 %shard_map.67 = (f32[256,128]{1,0:T(8,128)S(1)}, f32[256,128]{1,0:T(8,128)S(1)}, f32[256,128]{1,0:T(8,128)S(1)}, f32[256,128]{1,0:T(8,128)S(1)}) custom-call(bf16[3,256,2048]{2,1,0:T(8,128)(2,1)S(1)} %shard_map.66.matrix_ref, bf16[2048,128]{1,0:T(8,128)(2,1)S(1)} %get-tuple-element.156.kept_ref, bf16[2048,128]{1,0:T(8,128)(2,1)S(1)} %collective-permute-done.24.other_ref), custom_call_target="tpu_custom_call" | custom-call | flops 1024 | bytes 1024 | tf_op jit(solution)/shard_map/pallas_call | solution.py:262
  64.1 1.6 %shard_map.69 = (bf16[1,256,2048]{2,1,0:T(8,128)(2,1)S(1)}, bf16[1,256,2048]{2,1,0:T(8,128)(2,1)S(1)}) custom-call(bf16[4,256,2048]{2,1,0:T(8,128)(2,1)} %refs_0_.5, bf16[4,256,2048]{2,1,0:T(8,128)(2,1)} %collective-permute-done.refs_1_), custom_call_target="tpu_custom_call" | custom-call | flops 1024 | bytes 1024 | tf_op jit(solution)/shard_map/pallas_call | solution.py:165
  65.7 0.1 collective-permute-done.21.refs_3_
  65.8 0.8 shard_map.70
  66.5 0.5 collective-permute-start.34
  67.0 1.7 %collective-permute-start.32 = (bf16[2,256,256]{2,1,0:T(8,128)(2,1)S(1)}, bf16[2,256,256]{2,1,0:T(8,128)(2,1)S(1)}, u32[]{:S(2)}, u32[]{:S(2)}) collective-permute-start(bf16[2,256,256]{2,1,0:T(8,128)(2,1)S(1)} %copy-done.4), channel_id=1, source_target_pairs={{0,1},{1,0},{2,3},{3,2},{4,5},{5,4},{6,7},{7,6},{8,9},{9,8},{10,11... | collective-permute-start | bytes 786440 | tf_op jit(solution)/shard_map/ppermute | solution.py:374
  68.8 0.9 collective-permute-start.26
  69.6 1.2 %collective-permute-start.27 = (bf16[512,128]{1,0:T(8,128)(2,1)S(1)}, bf16[512,128]{1,0:T(8,128)(2,1)S(1)}, u32[]{:S(2)}, u32[]{:S(2)}) collective-permute-start(bf16[512,128]{1,0:T(8,128)(2,1)S(1)} %get-tuple-element.170.refs_0_), channel_id=1, source_target_pairs={{0,16},{4,20},{8,24},{12,28},{16,0},{20,4},{24,8},{28,12},{1,17},{... | collective-permute-start | bytes 393224 | tf_op jit(solution)/shard_map/ppermute | solution.py:295
  70.8 1.4 %collective-permute-start.28 = (bf16[512,128]{1,0:T(8,128)(2,1)S(1)}, bf16[512,128]{1,0:T(8,128)(2,1)S(1)}, u32[]{:S(2)}, u32[]{:S(2)}) collective-permute-start(bf16[512,128]{1,0:T(8,128)(2,1)S(1)} %get-tuple-element.170.refs_0_), channel_id=1, source_target_pairs={{0,24},{4,28},{8,16},{12,20},{16,8},{20,12},{24,0},{28,4},{1,25},{... | collective-permute-start | bytes 393224 | tf_op jit(solution)/shard_map/ppermute | solution.py:295
  72.3 3.1 %collective-permute-done.32.arrived_ref = bf16[2,256,256]{2,1,0:T(8,128)(2,1)S(1)} collective-permute-done((bf16[2,256,256]{2,1,0:T(8,128)(2,1)S(1)}, bf16[2,256,256]{2,1,0:T(8,128)(2,1)S(1)}, u32[]{:S(2)}, u32[]{:S(2)}) %collective-permute-start.32) | collective-permute-done | bytes 262176 | tf_op jit(solution)/shard_map/ppermute | solution.py:374
  75.4 2.3 %collective-permute-start.33 = (bf16[1,256,256]{2,1,0:T(8,128)(2,1)S(1)}, bf16[1,256,256]{2,1,0:T(8,128)(2,1)S(1)}, u32[]{:S(2)}, u32[]{:S(2)}) collective-permute-start(bf16[1,256,256]{2,1,0:T(8,128)(2,1)S(1)} %get-tuple-element.178), channel_id=1, source_target_pairs={{0,2},{1,3},{2,0},{3,1},{4,6},{5,7},{6,4},{7,5},{8,10},{9,11},{10,... | collective-permute-start | bytes 393224 | tf_op jit(solution)/shard_map/ppermute | solution.py:374
  77.7 0.7 shard_map.71
  78.5 0.9 collective-permute-start.29
  79.4 1.5 %collective-permute-start.30 = (bf16[512,128]{1,0:T(8,128)(2,1)S(1)}, bf16[512,128]{1,0:T(8,128)(2,1)S(1)}, u32[]{:S(2)}, u32[]{:S(2)}) collective-permute-start(bf16[512,128]{1,0:T(8,128)(2,1)S(1)} %get-tuple-element.188.refs_0_), channel_id=1, source_target_pairs={{0,16},{4,20},{8,24},{12,28},{16,0},{20,4},{24,8},{28,12},{1,17},{... | collective-permute-start | bytes 393224 | tf_op jit(solution)/shard_map/ppermute | solution.py:295
  80.9 1.1 %collective-permute-start.31 = (bf16[512,128]{1,0:T(8,128)(2,1)S(1)}, bf16[512,128]{1,0:T(8,128)(2,1)S(1)}, u32[]{:S(2)}, u32[]{:S(2)}) collective-permute-start(bf16[512,128]{1,0:T(8,128)(2,1)S(1)} %get-tuple-element.188.refs_0_), channel_id=1, source_target_pairs={{0,24},{4,28},{8,16},{12,20},{16,8},{20,12},{24,0},{28,4},{1,25},{... | collective-permute-start | bytes 393224 | tf_op jit(solution)/shard_map/ppermute | solution.py:295
  82.0 0.7 shard_map.73
  82.7 1.1 %collective-permute-done.33.refs_0_ = bf16[1,256,256]{2,1,0:T(8,128)(2,1)S(1)} collective-permute-done((bf16[1,256,256]{2,1,0:T(8,128)(2,1)S(1)}, bf16[1,256,256]{2,1,0:T(8,128)(2,1)S(1)}, u32[]{:S(2)}, u32[]{:S(2)}) %collective-permute-start.33) | collective-permute-done | bytes 131104 | tf_op jit(solution)/shard_map/ppermute | solution.py:374
  84.0 1.6 %shard_map.75 = (bf16[1,256,2048]{2,1,0:T(8,128)(2,1)S(1)}, bf16[1,256,2048]{2,1,0:T(8,128)(2,1)S(1)}) custom-call(bf16[4,256,2048]{2,1,0:T(8,128)(2,1)} %refs_0_.5, bf16[4,256,2048]{2,1,0:T(8,128)(2,1)} %collective-permute-done.refs_1_), custom_call_target="tpu_custom_call" | custom-call | flops 1024 | bytes 1024 | tf_op jit(solution)/shard_map/pallas_call | solution.py:165
  85.6 1.5 %collective-permute-done.30.refs_2_ = bf16[512,128]{1,0:T(8,128)(2,1)S(1)} collective-permute-done((bf16[512,128]{1,0:T(8,128)(2,1)S(1)}, bf16[512,128]{1,0:T(8,128)(2,1)S(1)}, u32[]{:S(2)}, u32[]{:S(2)}) %collective-permute-start.30) | collective-permute-done | bytes 131104 | tf_op jit(solution)/shard_map/ppermute | solution.py:295
  87.0 0.7 shard_map.76.refs_0_
  87.9 0.8 collective-permute-start.36
  88.7 1.2 %collective-permute-start.37 = (bf16[512,128]{1,0:T(8,128)(2,1)S(1)}, bf16[512,128]{1,0:T(8,128)(2,1)S(1)}, u32[]{:S(2)}, u32[]{:S(2)}) collective-permute-start(bf16[512,128]{1,0:T(8,128)(2,1)S(1)} %shard_map.76.refs_0_), channel_id=1, source_target_pairs={{0,16},{4,20},{8,24},{12,28},{16,0},{20,4},{24,8},{28,12},{1,17},{... | collective-permute-start | bytes 393224 | tf_op jit(solution)/shard_map/ppermute | solution.py:295
  89.9 1.5 %collective-permute-start.38 = (bf16[512,128]{1,0:T(8,128)(2,1)S(1)}, bf16[512,128]{1,0:T(8,128)(2,1)S(1)}, u32[]{:S(2)}, u32[]{:S(2)}) collective-permute-start(bf16[512,128]{1,0:T(8,128)(2,1)S(1)} %shard_map.76.refs_0_), channel_id=1, source_target_pairs={{0,24},{4,28},{8,16},{12,20},{16,8},{20,12},{24,0},{28,4},{1,25},{... | collective-permute-start | bytes 393224 | tf_op jit(solution)/shard_map/ppermute | solution.py:295
  91.5 1.1 %maximum_maximum_fusion = f32[4,256,256]{2,1,0:T(8,128)} fusion(f32[1,256,256]{2,1,0:T(8,128)S(1)} %maximum_select_fusion.2, f32[1,256,256]{2,1,0:T(8,128)S(1)} %get-tuple-element.213, f32[1,256,256]{2,1,0:T(8,128)S(1)} %get-tuple-element.212, f32[4]{0:T(128)S(1)} %pad.7.clone), kind=kLoop, calls=%fused_computation | loop fusion | flops 786432 | bytes 1835024 | tf_op jit(solution)/shard_map/stack | solution.py:404
  92.7 1.6 %collective-permute-done.36.refs_1_ = bf16[512,128]{1,0:T(8,128)(2,1)S(1)} collective-permute-done((bf16[512,128]{1,0:T(8,128)(2,1)S(1)}, bf16[512,128]{1,0:T(8,128)(2,1)S(1)}, u32[]{:S(2)}, u32[]{:S(2)}) %collective-permute-start.36) | collective-permute-done | bytes 131104 | tf_op jit(solution)/shard_map/ppermute | solution.py:295
  94.2 0.4 collective-permute-done.37.refs_2_
  94.7 2.4 %collective-permute-done.38.refs_3_ = bf16[512,128]{1,0:T(8,128)(2,1)S(1)} collective-permute-done((bf16[512,128]{1,0:T(8,128)(2,1)S(1)}, bf16[512,128]{1,0:T(8,128)(2,1)S(1)}, u32[]{:S(2)}, u32[]{:S(2)}) %collective-permute-start.38) | collective-permute-done | bytes 131104 | tf_op jit(solution)/shard_map/ppermute | solution.py:295
  97.0 0.7 shard_map.77
  97.8 1.3 %collective-permute-done.40 = f32[256,128]{1,0:T(8,128)S(1)} collective-permute-done((f32[256,128]{1,0:T(8,128)S(1)}, f32[256,128]{1,0:T(8,128)S(1)}, u32[]{:S(2)}, u32[]{:S(2)}) %collective-permute-start.40) | collective-permute-done | bytes 131104 | tf_op jit(solution)/shard_map/ppermute | solution.py:290
  99.2 0.7 fusion
  (65 shorter events, 1.3 us)
Async XLA Ops:
  0.0 31.0 %collective-permute-start.8 = (bf16[6,256,2048]{2,1,0:T(8,128)(2,1)}, bf16[6,256,2048]{2,1,0:T(8,128)(2,1)}, u32[]{:S(2)}, u32[]{:S(2)}) collective-permute-start(bf16[6,256,2048]{2,1,0:T(8,128)(2,1)} %refs_0_.3), channel_id=1, source_target_pairs={{0,4},{4,0},{8,12},{12,8},{16,20},{20,16},{24,28},{28,24},{1,5},{5... | collective-permute-start | bytes 18874376 | tf_op jit(solution)/shard_map/ppermute | solution.py:290
  0.5 21.9 %collective-permute-start = (bf16[4,256,2048]{2,1,0:T(8,128)(2,1)}, bf16[4,256,2048]{2,1,0:T(8,128)(2,1)}, u32[]{:S(2)}, u32[]{:S(2)}) collective-permute-start(bf16[4,256,2048]{2,1,0:T(8,128)(2,1)} %refs_0_.5), channel_id=1, source_target_pairs={{0,4},{4,0},{8,12},{12,8},{16,20},{20,16},{24,28},{28,24},{1,5},{5... | collective-permute-start | bytes 12582920 | tf_op jit(solution)/shard_map/ppermute | solution.py:290
  5.3 17.1 %collective-permute-start.2 = (bf16[256,256]{1,0:T(8,128)(2,1)S(1)}, bf16[256,256]{1,0:T(8,128)(2,1)S(1)}, u32[]{:S(2)}, u32[]{:S(2)}) collective-permute-start(bf16[256,256]{1,0:T(8,128)(2,1)S(1)} %get-tuple-element.115), channel_id=1, source_target_pairs={{0,1},{1,2},{2,3},{3,0},{4,5},{5,6},{6,7},{7,4},{8,9},{9,10},{10,1... | collective-permute-start | bytes 393224 | tf_op jit(solution)/shard_map/ppermute | solution.py:329
  8.3 14.1 %copy-start = (f32[4,256,256]{2,1,0:T(8,128)S(1)}, f32[4,256,256]{2,1,0:T(8,128)}, u32[]{:S(2)}) copy-start(f32[4,256,256]{2,1,0:T(8,128)} %rhs_ref.7) | copy-start | bytes 3145732
  8.3 14.1 %collective-permute-start.3 = (bf16[256,256]{1,0:T(8,128)(2,1)S(1)}, bf16[256,256]{1,0:T(8,128)(2,1)S(1)}, u32[]{:S(2)}, u32[]{:S(2)}) collective-permute-start(bf16[256,256]{1,0:T(8,128)(2,1)S(1)} %get-tuple-element.117), channel_id=1, source_target_pairs={{0,3},{1,0},{2,1},{3,2},{4,7},{5,4},{6,5},{7,6},{8,11},{9,8},{10,9... | collective-permute-start | bytes 393224 | tf_op jit(solution)/shard_map/ppermute | solution.py:329
  10.4 12.0 %collective-permute-start.1 = (bf16[256,256]{1,0:T(8,128)(2,1)S(1)}, bf16[256,256]{1,0:T(8,128)(2,1)S(1)}, u32[]{:S(2)}, u32[]{:S(2)}) collective-permute-start(bf16[256,256]{1,0:T(8,128)(2,1)S(1)} %get-tuple-element.113), channel_id=1, source_target_pairs={{0,2},{1,3},{2,0},{3,1},{4,6},{5,7},{6,4},{7,5},{8,10},{9,11},{10,... | collective-permute-start | bytes 393224 | tf_op jit(solution)/shard_map/ppermute | solution.py:329
  22.5 1.3 %collective-permute-start.4 = (bf16[256,128]{1,0:T(8,128)(2,1)S(1)}, bf16[256,128]{1,0:T(8,128)(2,1)S(1)}, u32[]{:S(2)}, u32[]{:S(2)}) collective-permute-start(bf16[256,128]{1,0:T(8,128)(2,1)S(1)} %get-tuple-element.119), channel_id=1, source_target_pairs={{0,4},{4,0},{8,12},{12,8},{16,20},{20,16},{24,28},{28,24},{1,5},{5... | collective-permute-start | bytes 196616 | tf_op jit(solution)/shard_map/ppermute | solution.py:290
  23.9 7.1 %copy-start.7 = (bf16[256,256]{1,0:T(8,128)(2,1)S(1)}, bf16[256,256]{1,0:T(8,128)(2,1)}, u32[]{:S(2)}) copy-start(bf16[256,256]{1,0:T(8,128)(2,1)} %get-tuple-element.134) | copy-start | bytes 393220
  23.9 9.1 %copy-start.6 = (bf16[256,256]{1,0:T(8,128)(2,1)S(1)}, bf16[256,256]{1,0:T(8,128)(2,1)}, u32[]{:S(2)}) copy-start(bf16[256,256]{1,0:T(8,128)(2,1)} %get-tuple-element.132) | copy-start | bytes 393220
  23.9 9.1 %collective-permute-start.5 = (bf16[512,128]{1,0:T(8,128)(2,1)S(1)}, bf16[512,128]{1,0:T(8,128)(2,1)S(1)}, u32[]{:S(2)}, u32[]{:S(2)}) collective-permute-start(bf16[512,128]{1,0:T(8,128)(2,1)S(1)} %maximum_select_fusion.4.refs_0_), channel_id=1, source_target_pairs={{0,8},{4,12},{8,0},{12,4},{16,24},{20,28},{24,16},{28,20},{1,9},{5... | collective-permute-start | bytes 393224 | tf_op jit(solution)/shard_map/ppermute | solution.py:295
  25.5 8.1 %collective-permute-start.6 = (bf16[512,128]{1,0:T(8,128)(2,1)S(1)}, bf16[512,128]{1,0:T(8,128)(2,1)S(1)}, u32[]{:S(2)}, u32[]{:S(2)}) collective-permute-start(bf16[512,128]{1,0:T(8,128)(2,1)S(1)} %maximum_select_fusion.4.refs_0_), channel_id=1, source_target_pairs={{0,16},{4,20},{8,24},{12,28},{16,0},{20,4},{24,8},{28,12},{1,17},{... | collective-permute-start | bytes 393224 | tf_op jit(solution)/shard_map/ppermute | solution.py:295
  27.0 6.6 %collective-permute-start.7 = (bf16[512,128]{1,0:T(8,128)(2,1)S(1)}, bf16[512,128]{1,0:T(8,128)(2,1)S(1)}, u32[]{:S(2)}, u32[]{:S(2)}) collective-permute-start(bf16[512,128]{1,0:T(8,128)(2,1)S(1)} %maximum_select_fusion.4.refs_0_), channel_id=1, source_target_pairs={{0,24},{4,28},{8,16},{12,20},{16,8},{20,12},{24,0},{28,4},{1,25},{... | collective-permute-start | bytes 393224 | tf_op jit(solution)/shard_map/ppermute | solution.py:295
  27.5 10.8 %collective-permute-start.9 = (bf16[256,256]{1,0:T(8,128)(2,1)}, bf16[256,256]{1,0:T(8,128)(2,1)S(1)}, u32[]{:S(2)}, u32[]{:S(2)}) collective-permute-start(bf16[256,256]{1,0:T(8,128)(2,1)} %get-tuple-element.127), channel_id=1, source_target_pairs={{0,2},{1,3},{2,0},{3,1},{4,6},{5,7},{6,4},{7,5},{8,10},{9,11},{10,... | collective-permute-start | bytes 393224 | tf_op jit(solution)/shard_map/ppermute | solution.py:329
  31.0 11.6 %collective-permute-start.14 = (bf16[256,256]{1,0:T(8,128)(2,1)S(1)}, bf16[256,256]{1,0:T(8,128)(2,1)S(1)}, u32[]{:S(2)}, u32[]{:S(2)}) collective-permute-start(bf16[256,256]{1,0:T(8,128)(2,1)S(1)} %copy-done.7), channel_id=1, source_target_pairs={{0,3},{1,0},{2,1},{3,2},{4,7},{5,4},{6,5},{7,6},{8,11},{9,8},{10,9... | collective-permute-start | bytes 393224 | tf_op jit(solution)/shard_map/ppermute | solution.py:329
  33.0 9.6 %collective-permute-start.13 = (bf16[256,256]{1,0:T(8,128)(2,1)S(1)}, bf16[256,256]{1,0:T(8,128)(2,1)S(1)}, u32[]{:S(2)}, u32[]{:S(2)}) collective-permute-start(bf16[256,256]{1,0:T(8,128)(2,1)S(1)} %copy-done.6), channel_id=1, source_target_pairs={{0,1},{1,2},{2,3},{3,0},{4,5},{5,6},{6,7},{7,4},{8,9},{9,10},{10,1... | collective-permute-start | bytes 393224 | tf_op jit(solution)/shard_map/ppermute | solution.py:329
  34.3 8.4 %copy-start.3 = (f32[256,256]{1,0:T(8,128)S(1)}, f32[256,256]{1,0:T(8,128)}, u32[]{:S(2)}) copy-start(f32[256,256]{1,0:T(8,128)} %get-tuple-element.130.own_ref) | copy-start | bytes 786436
  34.3 10.1 %collective-permute-start.11 = (bf16[512,128]{1,0:T(8,128)(2,1)S(1)}, bf16[512,128]{1,0:T(8,128)(2,1)S(1)}, u32[]{:S(2)}, u32[]{:S(2)}) collective-permute-start(bf16[512,128]{1,0:T(8,128)(2,1)S(1)} %get-tuple-element.141.refs_0_), channel_id=1, source_target_pairs={{0,16},{4,20},{8,24},{12,28},{16,0},{20,4},{24,8},{28,12},{1,17},{... | collective-permute-start | bytes 393224 | tf_op jit(solution)/shard_map/ppermute | solution.py:295
  35.9 8.6 %collective-permute-start.12 = (bf16[512,128]{1,0:T(8,128)(2,1)S(1)}, bf16[512,128]{1,0:T(8,128)(2,1)S(1)}, u32[]{:S(2)}, u32[]{:S(2)}) collective-permute-start(bf16[512,128]{1,0:T(8,128)(2,1)S(1)} %get-tuple-element.141.refs_0_), channel_id=1, source_target_pairs={{0,24},{4,28},{8,16},{12,20},{16,8},{20,12},{24,0},{28,4},{1,25},{... | collective-permute-start | bytes 393224 | tf_op jit(solution)/shard_map/ppermute | solution.py:295
  38.3 6.1 %collective-permute-start.10 = (bf16[512,128]{1,0:T(8,128)(2,1)S(1)}, bf16[512,128]{1,0:T(8,128)(2,1)S(1)}, u32[]{:S(2)}, u32[]{:S(2)}) collective-permute-start(bf16[512,128]{1,0:T(8,128)(2,1)S(1)} %get-tuple-element.141.refs_0_), channel_id=1, source_target_pairs={{0,8},{4,12},{8,0},{12,4},{16,24},{20,28},{24,16},{28,20},{1,9},{5... | collective-permute-start | bytes 393224 | tf_op jit(solution)/shard_map/ppermute | solution.py:295
  42.7 1.7 %collective-permute-start.15 = (f32[256,128]{1,0:T(8,128)S(1)}, f32[256,128]{1,0:T(8,128)S(1)}, u32[]{:S(2)}, u32[]{:S(2)}) collective-permute-start(f32[256,128]{1,0:T(8,128)S(1)} %get-tuple-element.135), channel_id=1, source_target_pairs={{0,4},{4,0},{8,12},{12,8},{16,20},{20,16},{24,28},{28,24},{1,5},{5... | collective-permute-start | bytes 393224 | tf_op jit(solution)/shard_map/ppermute | solution.py:290
  44.4 1.4 %copy-start.5 = (bf16[2,256,256]{2,1,0:T(8,128)(2,1)S(1)}, bf16[2,256,256]{2,1,0:T(8,128)(2,1)}, u32[]{:S(2)}) copy-start(bf16[2,256,256]{2,1,0:T(8,128)(2,1)} %get-tuple-element.151) | copy-start | bytes 786436
  44.4 9.7 %copy-start.2 = (f32[2,256,256]{2,1,0:T(8,128)S(1)}, f32[2,256,256]{2,1,0:T(8,128)}, u32[]{:S(2)}) copy-start(f32[2,256,256]{2,1,0:T(8,128)} %get-tuple-element.149.exact_ref) | copy-start | bytes 1572868
  45.2 17.4 %collective-permute-start.24 = (bf16[2048,128]{1,0:T(8,128)(2,1)S(1)}, bf16[2048,128]{1,0:T(8,128)(2,1)S(1)}, u32[]{:S(2)}, u32[]{:S(2)}) collective-permute-start(bf16[2048,128]{1,0:T(8,128)(2,1)S(1)} %get-tuple-element.156.kept_ref), channel_id=1, source_target_pairs={{0,4},{4,0},{8,12},{12,8},{16,20},{20,16},{24,28},{28,24},{1,5},{5... | collective-permute-start | bytes 1572872 | tf_op jit(solution)/shard_map/ppermute | solution.py:290
  45.8 8.3 %collective-permute-start.22 = (bf16[2,256,256]{2,1,0:T(8,128)(2,1)S(1)}, bf16[2,256,256]{2,1,0:T(8,128)(2,1)S(1)}, u32[]{:S(2)}, u32[]{:S(2)}) collective-permute-start(bf16[2,256,256]{2,1,0:T(8,128)(2,1)S(1)} %copy-done.5), channel_id=1, source_target_pairs={{0,1},{1,0},{2,3},{3,2},{4,5},{5,4},{6,7},{7,6},{8,9},{9,8},{10,11... | collective-permute-start | bytes 786440 | tf_op jit(solution)/shard_map/ppermute | solution.py:374
  46.5 10.0 %collective-permute-start.16 = (bf16[512,128]{1,0:T(8,128)(2,1)S(1)}, bf16[512,128]{1,0:T(8,128)(2,1)S(1)}, u32[]{:S(2)}, u32[]{:S(2)}) collective-permute-start(bf16[512,128]{1,0:T(8,128)(2,1)S(1)} %get-tuple-element.146.refs_0_), channel_id=1, source_target_pairs={{0,8},{4,12},{8,0},{12,4},{16,24},{20,28},{24,16},{28,20},{1,9},{5... | collective-permute-start | bytes 393224 | tf_op jit(solution)/shard_map/ppermute | solution.py:295
  47.2 9.3 %collective-permute-start.17 = (bf16[512,128]{1,0:T(8,128)(2,1)S(1)}, bf16[512,128]{1,0:T(8,128)(2,1)S(1)}, u32[]{:S(2)}, u32[]{:S(2)}) collective-permute-start(bf16[512,128]{1,0:T(8,128)(2,1)S(1)} %get-tuple-element.146.refs_0_), channel_id=1, source_target_pairs={{0,16},{4,20},{8,24},{12,28},{16,0},{20,4},{24,8},{28,12},{1,17},{... | collective-permute-start | bytes 393224 | tf_op jit(solution)/shard_map/ppermute | solution.py:295
  48.6 7.9 %collective-permute-start.18 = (bf16[512,128]{1,0:T(8,128)(2,1)S(1)}, bf16[512,128]{1,0:T(8,128)(2,1)S(1)}, u32[]{:S(2)}, u32[]{:S(2)}) collective-permute-start(bf16[512,128]{1,0:T(8,128)(2,1)S(1)} %get-tuple-element.146.refs_0_), channel_id=1, source_target_pairs={{0,24},{4,28},{8,16},{12,20},{16,8},{20,12},{24,0},{28,4},{1,25},{... | collective-permute-start | bytes 393224 | tf_op jit(solution)/shard_map/ppermute | solution.py:295
  54.1 9.8 %collective-permute-start.23 = (bf16[1,256,256]{2,1,0:T(8,128)(2,1)S(1)}, bf16[1,256,256]{2,1,0:T(8,128)(2,1)S(1)}, u32[]{:S(2)}, u32[]{:S(2)}) collective-permute-start(bf16[1,256,256]{2,1,0:T(8,128)(2,1)S(1)} %get-tuple-element.154), channel_id=1, source_target_pairs={{0,2},{1,3},{2,0},{3,1},{4,6},{5,7},{6,4},{7,5},{8,10},{9,11},{10,... | collective-permute-start | bytes 393224 | tf_op jit(solution)/shard_map/ppermute | solution.py:374
  57.2 8.4 %collective-permute-start.19 = (bf16[512,128]{1,0:T(8,128)(2,1)S(1)}, bf16[512,128]{1,0:T(8,128)(2,1)S(1)}, u32[]{:S(2)}, u32[]{:S(2)}) collective-permute-start(bf16[512,128]{1,0:T(8,128)(2,1)S(1)} %get-tuple-element.165.refs_0_), channel_id=1, source_target_pairs={{0,8},{4,12},{8,0},{12,4},{16,24},{20,28},{24,16},{28,20},{1,9},{5... | collective-permute-start | bytes 393224 | tf_op jit(solution)/shard_map/ppermute | solution.py:295
  58.0 7.7 %collective-permute-start.20 = (bf16[512,128]{1,0:T(8,128)(2,1)S(1)}, bf16[512,128]{1,0:T(8,128)(2,1)S(1)}, u32[]{:S(2)}, u32[]{:S(2)}) collective-permute-start(bf16[512,128]{1,0:T(8,128)(2,1)S(1)} %get-tuple-element.165.refs_0_), channel_id=1, source_target_pairs={{0,16},{4,20},{8,24},{12,28},{16,0},{20,4},{24,8},{28,12},{1,17},{... | collective-permute-start | bytes 393224 | tf_op jit(solution)/shard_map/ppermute | solution.py:295
  59.3 6.4 %collective-permute-start.21 = (bf16[512,128]{1,0:T(8,128)(2,1)S(1)}, bf16[512,128]{1,0:T(8,128)(2,1)S(1)}, u32[]{:S(2)}, u32[]{:S(2)}) collective-permute-start(bf16[512,128]{1,0:T(8,128)(2,1)S(1)} %get-tuple-element.165.refs_0_), channel_id=1, source_target_pairs={{0,24},{4,28},{8,16},{12,20},{16,8},{20,12},{24,0},{28,4},{1,25},{... | collective-permute-start | bytes 393224 | tf_op jit(solution)/shard_map/ppermute | solution.py:295
  64.0 1.8 %collective-permute-start.25 = (f32[256,128]{1,0:T(8,128)S(1)}, f32[256,128]{1,0:T(8,128)S(1)}, u32[]{:S(2)}, u32[]{:S(2)}) collective-permute-start(f32[256,128]{1,0:T(8,128)S(1)} %get-tuple-element.159), channel_id=1, source_target_pairs={{0,4},{4,0},{8,12},{12,8},{16,20},{20,16},{24,28},{28,24},{1,5},{5... | collective-permute-start | bytes 393224 | tf_op jit(solution)/shard_map/ppermute | solution.py:290
  65.6 1.4 %copy-start.4 = (bf16[2,256,256]{2,1,0:T(8,128)(2,1)S(1)}, bf16[2,256,256]{2,1,0:T(8,128)(2,1)}, u32[]{:S(2)}) copy-start(bf16[2,256,256]{2,1,0:T(8,128)(2,1)} %get-tuple-element.175) | copy-start | bytes 786436
  65.6 9.7 %copy-start.1 = (f32[2,256,256]{2,1,0:T(8,128)S(1)}, f32[2,256,256]{2,1,0:T(8,128)}, u32[]{:S(2)}) copy-start(f32[2,256,256]{2,1,0:T(8,128)} %get-tuple-element.173.exact_ref) | copy-start | bytes 1572868
  66.5 15.5 %collective-permute-start.34 = (bf16[2048,128]{1,0:T(8,128)(2,1)S(1)}, bf16[2048,128]{1,0:T(8,128)(2,1)S(1)}, u32[]{:S(2)}, u32[]{:S(2)}) collective-permute-start(bf16[2048,128]{1,0:T(8,128)(2,1)S(1)} %get-tuple-element.181.kept_ref), channel_id=1, source_target_pairs={{0,4},{4,0},{8,12},{12,8},{16,20},{20,16},{24,28},{28,24},{1,5},{5... | collective-permute-start | bytes 1572872 | tf_op jit(solution)/shard_map/ppermute | solution.py:290
  67.0 8.3 %collective-permute-start.32 = (bf16[2,256,256]{2,1,0:T(8,128)(2,1)S(1)}, bf16[2,256,256]{2,1,0:T(8,128)(2,1)S(1)}, u32[]{:S(2)}, u32[]{:S(2)}) collective-permute-start(bf16[2,256,256]{2,1,0:T(8,128)(2,1)S(1)} %copy-done.4), channel_id=1, source_target_pairs={{0,1},{1,0},{2,3},{3,2},{4,5},{5,4},{6,7},{7,6},{8,9},{9,8},{10,11... | collective-permute-start | bytes 786440 | tf_op jit(solution)/shard_map/ppermute | solution.py:374
  68.8 9.0 %collective-permute-start.26 = (bf16[512,128]{1,0:T(8,128)(2,1)S(1)}, bf16[512,128]{1,0:T(8,128)(2,1)S(1)}, u32[]{:S(2)}, u32[]{:S(2)}) collective-permute-start(bf16[512,128]{1,0:T(8,128)(2,1)S(1)} %get-tuple-element.170.refs_0_), channel_id=1, source_target_pairs={{0,8},{4,12},{8,0},{12,4},{16,24},{20,28},{24,16},{28,20},{1,9},{5... | collective-permute-start | bytes 393224 | tf_op jit(solution)/shard_map/ppermute | solution.py:295
  69.6 8.1 %collective-permute-start.27 = (bf16[512,128]{1,0:T(8,128)(2,1)S(1)}, bf16[512,128]{1,0:T(8,128)(2,1)S(1)}, u32[]{:S(2)}, u32[]{:S(2)}) collective-permute-start(bf16[512,128]{1,0:T(8,128)(2,1)S(1)} %get-tuple-element.170.refs_0_), channel_id=1, source_target_pairs={{0,16},{4,20},{8,24},{12,28},{16,0},{20,4},{24,8},{28,12},{1,17},{... | collective-permute-start | bytes 393224 | tf_op jit(solution)/shard_map/ppermute | solution.py:295
  70.8 6.9 %collective-permute-start.28 = (bf16[512,128]{1,0:T(8,128)(2,1)S(1)}, bf16[512,128]{1,0:T(8,128)(2,1)S(1)}, u32[]{:S(2)}, u32[]{:S(2)}) collective-permute-start(bf16[512,128]{1,0:T(8,128)(2,1)S(1)} %get-tuple-element.170.refs_0_), channel_id=1, source_target_pairs={{0,24},{4,28},{8,16},{12,20},{16,8},{20,12},{24,0},{28,4},{1,25},{... | collective-permute-start | bytes 393224 | tf_op jit(solution)/shard_map/ppermute | solution.py:295
  75.4 8.4 %collective-permute-start.33 = (bf16[1,256,256]{2,1,0:T(8,128)(2,1)S(1)}, bf16[1,256,256]{2,1,0:T(8,128)(2,1)S(1)}, u32[]{:S(2)}, u32[]{:S(2)}) collective-permute-start(bf16[1,256,256]{2,1,0:T(8,128)(2,1)S(1)} %get-tuple-element.178), channel_id=1, source_target_pairs={{0,2},{1,3},{2,0},{3,1},{4,6},{5,7},{6,4},{7,5},{8,10},{9,11},{10,... | collective-permute-start | bytes 393224 | tf_op jit(solution)/shard_map/ppermute | solution.py:374
  78.5 7.1 %collective-permute-start.29 = (bf16[512,128]{1,0:T(8,128)(2,1)S(1)}, bf16[512,128]{1,0:T(8,128)(2,1)S(1)}, u32[]{:S(2)}, u32[]{:S(2)}) collective-permute-start(bf16[512,128]{1,0:T(8,128)(2,1)S(1)} %get-tuple-element.188.refs_0_), channel_id=1, source_target_pairs={{0,8},{4,12},{8,0},{12,4},{16,24},{20,28},{24,16},{28,20},{1,9},{5... | collective-permute-start | bytes 393224 | tf_op jit(solution)/shard_map/ppermute | solution.py:295
  79.4 7.7 %collective-permute-start.30 = (bf16[512,128]{1,0:T(8,128)(2,1)S(1)}, bf16[512,128]{1,0:T(8,128)(2,1)S(1)}, u32[]{:S(2)}, u32[]{:S(2)}) collective-permute-start(bf16[512,128]{1,0:T(8,128)(2,1)S(1)} %get-tuple-element.188.refs_0_), channel_id=1, source_target_pairs={{0,16},{4,20},{8,24},{12,28},{16,0},{20,4},{24,8},{28,12},{1,17},{... | collective-permute-start | bytes 393224 | tf_op jit(solution)/shard_map/ppermute | solution.py:295
  80.9 6.2 %collective-permute-start.31 = (bf16[512,128]{1,0:T(8,128)(2,1)S(1)}, bf16[512,128]{1,0:T(8,128)(2,1)S(1)}, u32[]{:S(2)}, u32[]{:S(2)}) collective-permute-start(bf16[512,128]{1,0:T(8,128)(2,1)S(1)} %get-tuple-element.188.refs_0_), channel_id=1, source_target_pairs={{0,24},{4,28},{8,16},{12,20},{16,8},{20,12},{24,0},{28,4},{1,25},{... | collective-permute-start | bytes 393224 | tf_op jit(solution)/shard_map/ppermute | solution.py:295
  83.9 3.2 %collective-permute-start.35 = (f32[256,128]{1,0:T(8,128)S(1)}, f32[256,128]{1,0:T(8,128)S(1)}, u32[]{:S(2)}, u32[]{:S(2)}) collective-permute-start(f32[256,128]{1,0:T(8,128)S(1)} %get-tuple-element.184), channel_id=1, source_target_pairs={{0,4},{4,0},{8,12},{12,8},{16,20},{20,16},{24,28},{28,24},{1,5},{5... | collective-permute-start | bytes 393224 | tf_op jit(solution)/shard_map/ppermute | solution.py:290
  87.8 3.7 %collective-permute-start.39 = (f32[3,256,128]{2,1,0:T(8,128)S(1)}, f32[3,256,128]{2,1,0:T(8,128)S(1)}, u32[]{:S(2)}, u32[]{:S(2)}) collective-permute-start(f32[3,256,128]{2,1,0:T(8,128)S(1)} %pad_maximum_fusion), channel_id=1, source_target_pairs={{0,4},{4,0},{8,12},{12,8},{16,20},{20,16},{24,28},{28,24},{1,5},{5... | collective-permute-start | bytes 1179656 | tf_op jit(solution)/shard_map/ppermute | solution.py:290
  87.9 6.3 %collective-permute-start.36 = (bf16[512,128]{1,0:T(8,128)(2,1)S(1)}, bf16[512,128]{1,0:T(8,128)(2,1)S(1)}, u32[]{:S(2)}, u32[]{:S(2)}) collective-permute-start(bf16[512,128]{1,0:T(8,128)(2,1)S(1)} %shard_map.76.refs_0_), channel_id=1, source_target_pairs={{0,8},{4,12},{8,0},{12,4},{16,24},{20,28},{24,16},{28,20},{1,9},{5... | collective-permute-start | bytes 393224 | tf_op jit(solution)/shard_map/ppermute | solution.py:295
  88.7 6.0 %collective-permute-start.37 = (bf16[512,128]{1,0:T(8,128)(2,1)S(1)}, bf16[512,128]{1,0:T(8,128)(2,1)S(1)}, u32[]{:S(2)}, u32[]{:S(2)}) collective-permute-start(bf16[512,128]{1,0:T(8,128)(2,1)S(1)} %shard_map.76.refs_0_), channel_id=1, source_target_pairs={{0,16},{4,20},{8,24},{12,28},{16,0},{20,4},{24,8},{28,12},{1,17},{... | collective-permute-start | bytes 393224 | tf_op jit(solution)/shard_map/ppermute | solution.py:295
  89.9 7.2 %collective-permute-start.38 = (bf16[512,128]{1,0:T(8,128)(2,1)S(1)}, bf16[512,128]{1,0:T(8,128)(2,1)S(1)}, u32[]{:S(2)}, u32[]{:S(2)}) collective-permute-start(bf16[512,128]{1,0:T(8,128)(2,1)S(1)} %shard_map.76.refs_0_), channel_id=1, source_target_pairs={{0,24},{4,28},{8,16},{12,20},{16,8},{20,12},{24,0},{28,4},{1,25},{... | collective-permute-start | bytes 393224 | tf_op jit(solution)/shard_map/ppermute | solution.py:295
  97.8 1.4 %collective-permute-start.40 = (f32[256,128]{1,0:T(8,128)S(1)}, f32[256,128]{1,0:T(8,128)S(1)}, u32[]{:S(2)}, u32[]{:S(2)}) collective-permute-start(f32[256,128]{1,0:T(8,128)S(1)} %get-tuple-element.208), channel_id=1, source_target_pairs={{0,4},{4,0},{8,12},{12,8},{16,20},{20,16},{24,28},{28,24},{1,5},{5... | collective-permute-start | bytes 393224 | tf_op jit(solution)/shard_map/ppermute | solution.py:290

commit v5 on v4

v5 whole, which is shorter than its diff:
```python
import functools

import jax
import jax.numpy as jnp
from jax import lax
from jax.experimental import pallas as pl
from jax.experimental.pallas import tpu as pltpu
from jax.sharding import PartitionSpec as P

F32, BF16 = jnp.float32, jnp.bfloat16
VMEM = pl.BlockSpec(memory_space=pltpu.VMEM)
HBM = pl.BlockSpec(memory_space=pltpu.HBM)
SMALL = pl.CostEstimate(flops=1024, bytes_accessed=1024, transcendentals=0)


def inner_index(target, earlier):
    return target * (target - 1) // 2 + earlier


def params(mebibytes):
    return pltpu.CompilerParams(vmem_limit_bytes=mebibytes << 20)


def in_hbm(array):
    return pltpu.with_memory_space_constraint(array, pltpu.HBM)


def work(rows, depth, columns):
    return pl.CostEstimate(
        flops=2 * rows * depth * columns,
        bytes_accessed=2 * (rows + columns) * depth,
        transcendentals=0,
    )


def accumulate(total, piece, part, there=slice(None)):
    if piece == 0:
        total[:, there] = part
    else:
        total[:, there] += part


def first_kernel(shifts, pieces, l_ref, x_ref, *refs):
    count = len(shifts)
    outs, (l_buf, x_buf, total, l_sems, x_sems) = refs[:count], refs[count:]
    deep = x_ref.shape[0] // pieces
    width = x_ref.shape[1] // count
    mine = lax.axis_index("col")
    l_copies, x_copies = [], []
    for piece in range(pieces):
        cut = pl.ds(piece * deep, deep)
        l_copies.append(
            pltpu.make_async_copy(l_ref.at[0, :, cut], l_buf.at[piece], l_sems.at[piece])
        )
        x_copies.append(pltpu.make_async_copy(x_ref.at[cut], x_buf.at[piece], x_sems.at[piece]))
    for piece in range(pieces):
        l_copies[piece].start()
        x_copies[piece].start()
    for piece in range(pieces):
        l_copies[piece].wait()
        x_copies[piece].wait()
        accumulate(
            total, piece, jnp.dot(l_buf[piece], x_buf[piece], preferred_element_type=F32)
        )
    for shift, out in zip(shifts, outs):
        begin = pl.multiple_of(lax.rem(mine + shift, count) * width, width)
        out[...] = total[:, pl.ds(begin, width)].astype(out.dtype)


def later_kernel(count, pieces, flight, l_ref, x_ref, *refs):
    rows, depth = l_ref.shape[1:]
    blocks = l_ref.shape[0] - 1
    outs, refs = refs[: 2 * blocks], refs[2 * blocks :]
    l_buf, x_buf, total, low, exact, l_sems, x_sems, out_sems = refs
    deep = depth // pieces
    width = x_ref.shape[1] // count
    mine = lax.axis_index("col")
    copies = []
    for piece in range(pieces):
        cut = pl.ds(piece * deep, deep)
        copies.append(
            [
                pltpu.make_async_copy(
                    l_ref.at[block + 1, :, cut],
                    l_buf.at[piece, pl.ds(block * rows, rows)],
                    l_sems.at[piece, block],
                )
                for block in range(blocks)
            ]
            + [pltpu.make_async_copy(x_ref.at[cut], x_buf.at[piece], x_sems.at[piece])]
        )
    for row in copies[:flight]:
        for copy in row:
            copy.start()
    for piece in range(pieces):
        for copy in copies[piece]:
            copy.wait()
        if piece + flight < pieces:
            for copy in copies[piece + flight]:
                copy.start()
        accumulate(
            total, piece, jnp.dot(l_buf[piece], x_buf[piece], preferred_element_type=F32)
        )
    copies = []

    def found(block, chunk):
        begin = pl.multiple_of(chunk * width, width)
        return total[block * rows : (block + 1) * rows, pl.ds(begin, width)]

    def send_out(held, out):
        copy = pltpu.make_async_copy(held, out, out_sems.at[len(copies)])
        copy.start()
        copies.append(copy)

    for block in range(blocks):
        for slot in range(count):
            held = (low if slot % 2 else exact).at[block, slot // 2]
            held[...] = found(block, mine ^ slot).astype(held.dtype)
        send_out(low.at[block], outs[2 * block])
        send_out(exact.at[block], outs[2 * block + 1])
    for copy in copies:
        copy.wait()


def combine_kernel(exact_ref, arrived_ref, low_out, exact_out):
    for k in range(exact_ref.shape[0]):
        out = low_out if k % 2 else exact_out
        out[k // 2] = (exact_ref[k] + arrived_ref[k].astype(F32)).astype(out.dtype)


def combine(exact, arrived):
    count, rows, width = exact.shape
    return pl.pallas_call(
        combine_kernel,
        in_specs=[VMEM] * 2,
        out_specs=[VMEM] * 2,
        out_shape=[pltpu.VMEM((count // 2, rows, width), dtype) for dtype in (BF16, F32)],
        compiler_params=params(8),
        cost_estimate=SMALL,
    )(exact, arrived)


def load_kernel(indices, *refs):
    count = len(indices)
    ins, outs, sems = refs[:count], refs[count:-1], refs[-1]
    copies = [
        pltpu.make_async_copy(ref.at[index], out, sems.at[k])
        for k, (ref, out, index) in enumerate(zip(ins, outs, indices))
    ]
    for copy in copies:
        copy.start()
    for copy in copies:
        copy.wait()


def load(token, *picks):
    indices = tuple(index for _, _, index in picks for _ in range(2))
    arrays = [in_hbm(array) for own, other, _ in picks for array in (after(own, token), other)]
    found = pl.pallas_call(
        functools.partial(load_kernel, indices),
        in_specs=[HBM] * len(arrays),
        out_specs=[VMEM] * len(arrays),
        out_shape=[pltpu.VMEM(array.shape[1:], array.dtype) for array in arrays],
        scratch_shapes=[pltpu.SemaphoreType.DMA((len(arrays),))],
        compiler_params=params(8),
        cost_estimate=SMALL,
    )(*arrays)
    return [tuple(found[2 * k : 2 * k + 2]) for k in range(len(picks))]


def reduce_kernel(rhs_ref, own_ref, *refs):
    arrived, (kept_ref, other_ref) = refs[:-2], refs[-2:]
    total = rhs_ref[...] - own_ref[...].reshape(rhs_ref.shape)
    for ref in arrived:
        total -= ref[...].reshape(rhs_ref.shape).astype(F32)
    half = total.shape[1] // 2
    first = lax.rem(lax.axis_index("row"), 2) == 0
    kept_ref[...] = jnp.where(first, total[:, :half], total[:, half:]).astype(kept_ref.dtype)
    other_ref[...] = jnp.where(first, total[:, half:], total[:, :half]).astype(other_ref.dtype)


def reduce_rows(rhs, target, own, arrived, dtype):
    _, rows, width = rhs.shape
    return pl.pallas_call(
        reduce_kernel,
        grid=(1,),
        in_specs=[pl.BlockSpec((None, rows, width), lambda i: (target, 0, 0))]
        + [VMEM] * (1 + len(arrived)),
        out_specs=[VMEM, VMEM],
        out_shape=[jax.ShapeDtypeStruct((rows, width // 2), dtype)] * 2,
        compiler_params=params(8),
        cost_estimate=SMALL,
    )(rhs, own, *arrived)


def apply_kernel(masks, pairs, sign, exact, low, own_ref, other_ref, *refs):
    shards, refs = refs[: len(masks)], refs[len(masks) :]
    held, outs = refs[: 2 * pairs], refs[2 * pairs :]
    me = lax.axis_index("row")
    core, chip = lax.rem(me, 2), me // 2
    rows = own_ref.shape[0]
    high, width = shards[0].shape
    total = jnp.zeros((high, width), F32)
    for mask, shard in zip(masks, shards):
        cut = pl.ds(pl.multiple_of((chip ^ mask) * high, high), high)
        both = jnp.concatenate([own_ref[:, cut], other_ref[:, cut]], axis=0)
        total += jnp.dot(both, shard[...], preferred_element_type=F32)
    for half, place in ((0, core), (1, 1 - core)):
        found = total[half * rows : (half + 1) * rows]
        if pairs:
            base = held[half][...]
            for pair in range(1, pairs):
                base -= held[2 * pair + half][...]
            found = base + found if sign > 0 else base - found
        if exact:
            outs[half][...] = found
        if low:
            there = pl.ds(pl.multiple_of(place * rows, rows), rows)
            outs[-1][there, :] = found.astype(BF16)


def apply_rows(matrix, shards, held, sign, exact, low):
    masks = tuple(shards)
    rows = matrix[0].shape[0]
    high, width = shards[masks[0]].shape
    operands = [*matrix, *shards.values(), *(part for pair in held for part in pair)]
    shapes = [pltpu.VMEM((rows, width), F32)] * (2 * exact)
    shapes += [pltpu.VMEM((high, width), BF16)] * low
    return pl.pallas_call(
        functools.partial(apply_kernel, masks, len(held), sign, exact, low),
        in_specs=[VMEM] * len(operands),
        out_specs=[VMEM] * len(shapes),
        out_shape=shapes,
        compiler_params=params(8),
        cost_estimate=SMALL,
    )(*operands)


def rows_kernel(masks, matrix_ref, *refs):
    shards, out_ref = refs[:-1], refs[-1]
    chip = lax.axis_index("row") // 2
    high, width = shards[0].shape
    total = jnp.zeros(out_ref.shape, F32)
    for mask, shard in zip(masks, shards):
        cut = pl.ds(pl.multiple_of((chip ^ mask) * high, high), high)
        total += jnp.dot(matrix_ref[:, cut], shard[...], preferred_element_type=F32)
    out_ref[...] = total


def last_rows(matrix, shards):
    masks = tuple(shards)

    def rows_of(part):
        shape = (part.shape[0], shards[0].shape[1])
        return pl.pallas_call(
            functools.partial(rows_kernel, masks),
            in_specs=[VMEM] * (1 + len(masks)),
            out_specs=VMEM,
            out_shape=pltpu.VMEM(shape, F32),
            compiler_params=params(8),
            cost_estimate=SMALL,
        )(part, *shards.values())

    other = rows_of(matrix[1])
    return rows_of(after(matrix[0], other)), other


def after(value, token):
    return lax.optimization_barrier((value, token))[0]


def local(rhs, l_panel, x_solved, diag_inv, l_inner, row_count, col_count):
    steps, rows, depth = l_panel.shape
    width = rhs.shape[2]
    total = x_solved.shape[1]
    chips = row_count // 2
    core = lax.axis_index("row") % 2
    pieces = 4
    shifts = sorted(range(1, col_count), key=lambda s: (abs(2 * s - col_count), s)) + [0]
    chunk_shapes = [jax.ShapeDtypeStruct((rows, width), BF16 if s else F32) for s in shifts]

    def swap(value):
        return lax.ppermute(value, "row", [(i, i ^ 1) for i in range(row_count)])

    def gather(value, token=None):
        late = value if token is None else after(value, token)
        shards = {0: value}
        for mask in range(1, chips):
            pairs = [(i, i ^ (2 * mask)) for i in range(row_count)]
            shards[mask] = lax.ppermute(late if mask == 1 else value, "row", pairs)
        return shards

    def by_core(kept, other, axis):
        return jnp.where(
            core == 0,
            jnp.concatenate([kept, other], axis=axis),
            jnp.concatenate([other, kept], axis=axis),
        )

    diag_other, inner_other = swap(diag_inv), swap(l_inner)
    first = pl.pallas_call(
        functools.partial(first_kernel, shifts, 8),
        in_specs=[HBM, HBM],
        out_specs=[VMEM] * col_count,
        out_shape=chunk_shapes,
        scratch_shapes=[
            pltpu.VMEM((8, rows, depth // 8), BF16),
            pltpu.VMEM((8, depth // 8, total), BF16),
            pltpu.VMEM((rows, total), F32),
            pltpu.SemaphoreType.DMA((8,)),
            pltpu.SemaphoreType.DMA((8,)),
        ],
        compiler_params=params(16),
        cost_estimate=work(rows, depth, total),
    )(in_hbm(l_panel), in_hbm(x_solved))
    chunks, arrived = {0: first}, {target: [] for target in range(steps)}

    def send(target, which, token):
        arrived[target] += [
            lax.ppermute(
                after(chunks[target][k], token),
                "col",
                [(i, (i + shifts[k]) % col_count) for i in range(col_count)],
            )
            for k in which
        ]

    send(0, [*range(1, col_count - 1), 0], first[0])

    blocks = steps - 1
    shapes = []
    for _ in range(blocks):
        shapes += [jax.ShapeDtypeStruct((col_count // 2, rows, width), t) for t in (BF16, F32)]
    found = pl.pallas_call(
        functools.partial(later_kernel, col_count, pieces, 2),
        in_specs=[HBM] * 2,
        out_specs=[HBM] * len(shapes),
        out_shape=[pltpu.HBM(shape.shape, shape.dtype) for shape in shapes],
        scratch_shapes=[
            pltpu.VMEM((pieces, rows * blocks, depth // pieces), BF16),
            pltpu.VMEM((pieces, depth // pieces, total), BF16),
            pltpu.VMEM((rows * blocks, total), F32),
            pltpu.VMEM((blocks, col_count // 2, rows, width), BF16),
            pltpu.VMEM((blocks, col_count // 2, rows, width), F32),
            pltpu.SemaphoreType.DMA((pieces, blocks)),
            pltpu.SemaphoreType.DMA((pieces,)),
            pltpu.SemaphoreType.DMA((len(shapes),)),
        ],
        compiler_params=params(60),
        cost_estimate=work(rows * blocks, depth, total),
    )(in_hbm(l_panel), in_hbm(after(x_solved, first[0])))
    halves = {target: found[2 * target - 2 : 2 * target] for target in range(1, steps)}

    def halve(target, stage, token):
        low, exact = halves[target]
        if stage:
            arrived_low = arrived[target]
            low, exact = combine(after(exact, token), arrived_low)
        else:
            low = after(low, token)
        pairs = [(i, i ^ (1 << stage)) for i in range(col_count)]
        halves[target] = (low, exact)
        arrived[target] = lax.ppermute(low, "col", pairs)


    def reduced(target, token, dtype):
        if target in chunks:
            own, parts = chunks[target][-1], arrived[target]
        else:
            own, parts = halves[target][1], [arrived[target]]
        return reduce_rows(rhs, target, after(own, token), parts, dtype)

    kept, other = reduced(0, (found[0], diag_other), BF16)
    halve(1, 0, other)
    resid_low = by_core(kept, swap(other), 0)
    results, solved_shards = [], {}
    products = {target: [] for target in range(steps)}
    stages = (col_count - 1).bit_length()
    diag_pick = [(diag_inv, diag_other, target) for target in range(steps)]
    inner_pick = [(l_inner, inner_other, index) for index in range(l_inner.shape[0])]
    near_matrix = {}
    for target in range(steps):
        last = target + 1 == steps
        shards = gather(resid_low)
        if target == 0:
            diag_matrix, near_matrix[0] = load(resid_low, diag_pick[0], inner_pick[0])
            for stage in range(1, stages):
                halve(1, stage, diag_matrix)
        elif not last:
            diag_matrix, near_matrix[target] = load(
                resid_low, diag_pick[target], inner_pick[inner_index(target + 1, target)]
            )
            if target > 1:
                halve(target + 1, 0, resid_low)
            for stage in range(1, stages):
                halve(target + 1, stage, (resid_low, diag_matrix))
        else:
            (diag_matrix,) = load(resid_low, diag_pick[target])
            before = jnp.stack([other for _, other in results])
            swapped = swap(after(before, resid_low))
            parts = [by_core(kept, swapped[k], 1) for k, (kept, _) in enumerate(results)]
            solved = jnp.stack([*parts, jnp.zeros_like(parts[0])])
            shards[0], solved, diag_matrix = lax.optimization_barrier((shards[0], solved, diag_matrix))
        if last:
            kept, other = last_rows(diag_matrix, shards)
        else:
            kept, other, *low = apply_rows(diag_matrix, shards, [], 1, True, True)
        results.append((kept, other))
        if last:
            break
        (solved_low,) = low
        shards = gather(solved_low)
        solved_shards[target] = shards
        token = solved_low
        if target == 0:
            pass
        if target == 0:
            halve(target + 2, 0, token)
        kept, other = reduced(target + 1, token, F32)
        held = [(kept, swap(other))]
        if target:
            earlier = range(target)
            loaded = load(solved_low, *[inner_pick[inner_index(target + 1, k)] for k in earlier])
            for k, matrix in zip(earlier, loaded):
                held.append(apply_rows(matrix, solved_shards[k], [], 1, True, False))
        (resid_low,) = apply_rows(near_matrix[target], shards, held, -1, False, True)
    kept, other = results[-1]
    return lax.dynamic_update_slice(solved, by_core(kept, swap(other), 1)[None], (steps - 1, 0, 0))


def solution(mesh):
    in_specs = (
        P(None, "row", "col"),
        P(None, "row", "col"),
        P("col", None),
        P(None, "row", None),
        P(None, "row", None),
    )
    out_specs = P(None, "row", "col")
    body = functools.partial(local, row_count=mesh.shape["row"], col_count=mesh.shape["col"])
    return jax.shard_map(body, mesh=mesh, in_specs=in_specs, out_specs=out_specs, check_vma=False)
```

time: 100 us -> 94.6 us (0.946)
  waiting for transfers between devices: 18.6 us -> 15 us
  starting transfers between devices: 44.7 us -> 41.5 us
  Pallas kernels: 34.1 us -> 35.4 us
    ppermute x6 -> x3, starting transfers between devices: 10.2 us -> 6.12 us  [send(): lax.ppermute(after(chunks[target][k], token), 'col', [(i, (i + shifts[k])...]
    ppermute x4 -> x6, waiting for transfers between devices: 8.26 us -> 5.44 us  [halve(): arrived[target] = lax.ppermute(low, 'col', pairs)]
    ppermute x21, waiting for transfers between devices: 6.44 us -> 8.66 us  [gather(): shards[mask] = lax.ppermute(late if mask == 1 else value, 'row', pairs)]
    ppermute x4 -> x6, starting transfers between devices: 7.16 us -> 9.28 us  [halve(): arrived[target] = lax.ppermute(low, 'col', pairs)]
    ppermute x10 -> x8, waiting for transfers between devices: 2.58 us -> 0.93 us  [swap(): return lax.ppermute(value, 'row', [(i, i ^ 1) for i in range(row_count)])]
    ppermute x6 -> x3, waiting for transfers between devices: 1.27 us -> 0.01 us  [send(): lax.ppermute(after(chunks[target][k], token), 'col', [(i, (i + shifts[k])...]
    pallas_call x20 -> x22, Pallas kernels: 29.3 us -> 30.5 us  [the longest x6 11.9 us: load(): pl.pallas_call(functools.partial(load_kernel, indices), in_specs=[HBM] *...]
  transfers between devices with their start and end apart: 41 -> 38, of which waited for: 12 -> 13; matrix products, arithmetic and copies ran while one was open for 1% -> 1% of each run, Pallas kernels for 31% -> 36%
where the time goes in v5:
time: 94.6 us; the launch traced here: 94.4 us
  starting transfers between devices  41.5 us (44%)
  Pallas kernels  35.4 us (37%)
  waiting for transfers between devices  15 us (16%)
  other arithmetic  1.97 us (2%)
    ppermute x21, starting transfers between devices, gather(): shards[mask] = lax.ppermute(late if mask == 1 else value, 'row', pairs)  24.7 us
    pallas_call x6, Pallas kernels, load(): pl.pallas_call(functools.partial(load_kernel, indices), in_specs=[HBM] *...  11.9 us
    pallas_call x1, Pallas kernels, local(): pl.pallas_call(functools.partial(later_kernel, col_count, pieces, 2), in_...  11.1 us
    ppermute x6, starting transfers between devices, halve(): arrived[target] = lax.ppermute(low, 'col', pairs)  9.28 us
    ppermute x21, waiting for transfers between devices, gather(): shards[mask] = lax.ppermute(late if mask == 1 else value, 'row', pairs)  8.66 us
    pallas_call x9, Pallas kernels, apply_rows(): pl.pallas_call(functools.partial(apply_kernel, masks, len(held), sign, ex...  6.4 us
    ppermute x3, starting transfers between devices, send(): lax.ppermute(after(chunks[target][k], token), 'col', [(i, (i + shifts[k])...  6.12 us
    ppermute x6, waiting for transfers between devices, halve(): arrived[target] = lax.ppermute(low, 'col', pairs)  5.44 us
  transfers between devices with their start and end apart: 38, of which 13 were waited for; matrix products, arithmetic and copies ran while one was open for 1% of the time, Pallas kernels for 36%

profile of v5, /device:TPU:0, one launch (start us, length us, event | category | flops | bytes accessed | tf_op | source)
XLA Modules:
  0.0 94.4 jit_solution(15429322115485449165)
XLA Ops:
  0.0 0.5 collective-permute-start.5
  0.5 4.7 %shard_map.55 = (bf16[256,256]{1,0:T(8,128)(2,1)S(1)}, bf16[256,256]{1,0:T(8,128)(2,1)S(1)}, bf16[256,256]{1,0:T(8,128)(2,1)S(1)}, f32[256,256]{1,0:T(8,128)S(1)}) custom-call(bf16[4,256,4096]{2,1,0:T(8,128)(2,1)} %l_ref.3, bf16[4096,1024]{1,0:T(8,128)(2,1)} %x_ref.2), custom_call_target="tpu_custom_call" | custom-call | flops 2147483648 | bytes 10485760 | tf_op jit(solution)/shard_map/pallas_call | solution.py:301
  5.3 3.1 %collective-permute-start.1 = (bf16[256,256]{1,0:T(8,128)(2,1)S(1)}, bf16[256,256]{1,0:T(8,128)(2,1)S(1)}, u32[]{:S(2)}, u32[]{:S(2)}) collective-permute-start(bf16[256,256]{1,0:T(8,128)(2,1)S(1)} %get-tuple-element.99), channel_id=1, source_target_pairs={{0,1},{1,2},{2,3},{3,0},{4,5},{5,6},{6,7},{7,4},{8,9},{9,10},{10,1... | collective-permute-start | bytes 393224 | tf_op jit(solution)/shard_map/ppermute | solution.py:320
  8.3 2.1 %collective-permute-start.2 = (bf16[256,256]{1,0:T(8,128)(2,1)S(1)}, bf16[256,256]{1,0:T(8,128)(2,1)S(1)}, u32[]{:S(2)}, u32[]{:S(2)}) collective-permute-start(bf16[256,256]{1,0:T(8,128)(2,1)S(1)} %get-tuple-element.101), channel_id=1, source_target_pairs={{0,3},{1,0},{2,1},{3,2},{4,7},{5,4},{6,5},{7,6},{8,11},{9,8},{10,9... | collective-permute-start | bytes 393224 | tf_op jit(solution)/shard_map/ppermute | solution.py:320
  10.4 0.9 collective-permute-start.3
  11.4 11.1 %shard_map.56 = (bf16[2,256,256]{2,1,0:T(8,128)(2,1)}, f32[2,256,256]{2,1,0:T(8,128)}, bf16[2,256,256]{2,1,0:T(8,128)(2,1)}, f32[2,256,256]{2,1,0:T(8,128)}, bf1...) custom-call(bf16[4,256,4096]{2,1,0:T(8,128)(2,1)} %l_ref.3, bf16[4096,1024]{1,0:T(8,128)(2,1)} %x_ref.2), custom_call_target="tpu_custom_call" | custom-call | flops 6442450944 | bytes 14680064 | tf_op jit(solution)/shard_map/pallas_call | solution.py:334
  22.7 1.6 %collective-permute-start.12 = (bf16[2,256,256]{2,1,0:T(8,128)(2,1)}, bf16[2,256,256]{2,1,0:T(8,128)(2,1)S(1)}, u32[]{:S(2)}, u32[]{:S(2)}) collective-permute-start(bf16[2,256,256]{2,1,0:T(8,128)(2,1)} %get-tuple-element.114), channel_id=1, source_target_pairs={{0,1},{1,0},{2,3},{3,2},{4,5},{5,4},{6,7},{7,6},{8,9},{9,8},{10,11... | collective-permute-start | bytes 786440 | tf_op jit(solution)/shard_map/ppermute | solution.py:363
  24.4 1.6 %collective-permute-start.6 = (bf16[512,128]{1,0:T(8,128)(2,1)S(1)}, bf16[512,128]{1,0:T(8,128)(2,1)S(1)}, u32[]{:S(2)}, u32[]{:S(2)}) collective-permute-start(bf16[512,128]{1,0:T(8,128)(2,1)S(1)} %maximum_select_fusion.4.refs_0_), channel_id=1, source_target_pairs={{0,8},{4,12},{8,0},{12,4},{16,24},{20,28},{24,16},{28,20},{1,9},{5... | collective-permute-start | bytes 393224 | tf_op jit(solution)/shard_map/ppermute | solution.py:290
  26.0 1.5 %collective-permute-start.7 = (bf16[512,128]{1,0:T(8,128)(2,1)S(1)}, bf16[512,128]{1,0:T(8,128)(2,1)S(1)}, u32[]{:S(2)}, u32[]{:S(2)}) collective-permute-start(bf16[512,128]{1,0:T(8,128)(2,1)S(1)} %maximum_select_fusion.4.refs_0_), channel_id=1, source_target_pairs={{0,16},{4,20},{8,24},{12,28},{16,0},{20,4},{24,8},{28,12},{1,17},{... | collective-permute-start | bytes 393224 | tf_op jit(solution)/shard_map/ppermute | solution.py:290
  27.5 0.5 collective-permute-start.8
  28.0 2.2 %shard_map.58 = (bf16[256,2048]{1,0:T(8,128)(2,1)S(1)}, bf16[256,2048]{1,0:T(8,128)(2,1)S(1)}, bf16[256,2048]{1,0:T(8,128)(2,1)S(1)}, bf16[256,2048]{1,0:T(8,128)(2,1)S(1)}) custom-call(bf16[4,256,2048]{2,1,0:T(8,128)(2,1)} %refs_0_.5, bf16[4,256,2048]{2,1,0:T(8,128)(2,1)} %collective-permute-done.refs_1_, bf16[6,256,2048]{2,1,0:T(8,128)(2,1)} %refs_2_.3, ...), custom_call_target="tpu_custom_call" | custom-call | flops 1024 | bytes 1024 | tf_op jit(solution)/shard_map/pallas_call | solution.py:159
  30.2 1.5 %collective-permute-done.12.arrived_ref = bf16[2,256,256]{2,1,0:T(8,128)(2,1)S(1)} collective-permute-done((bf16[2,256,256]{2,1,0:T(8,128)(2,1)}, bf16[2,256,256]{2,1,0:T(8,128)(2,1)S(1)}, u32[]{:S(2)}, u32[]{:S(2)}) %collective-permute-start.12) | collective-permute-done | bytes 262176 | tf_op jit(solution)/shard_map/ppermute | solution.py:363
  31.7 2.1 %collective-permute-start.13 = (bf16[1,256,256]{2,1,0:T(8,128)(2,1)S(1)}, bf16[1,256,256]{2,1,0:T(8,128)(2,1)S(1)}, u32[]{:S(2)}, u32[]{:S(2)}) collective-permute-start(bf16[1,256,256]{2,1,0:T(8,128)(2,1)S(1)} %get-tuple-element.117), channel_id=1, source_target_pairs={{0,2},{1,3},{2,0},{3,1},{4,6},{5,7},{6,4},{7,5},{8,10},{9,11},{10,... | collective-permute-start | bytes 393224 | tf_op jit(solution)/shard_map/ppermute | solution.py:363
  34.1 0.7 shard_map.59
  34.8 1.2 %collective-permute-start.21 = (bf16[2,256,256]{2,1,0:T(8,128)(2,1)S(1)}, bf16[2,256,256]{2,1,0:T(8,128)(2,1)S(1)}, u32[]{:S(2)}, u32[]{:S(2)}) collective-permute-start(bf16[2,256,256]{2,1,0:T(8,128)(2,1)S(1)} %copy-done.5), channel_id=1, source_target_pairs={{0,1},{1,0},{2,3},{3,2},{4,5},{5,4},{6,7},{7,6},{8,9},{9,8},{10,11... | collective-permute-start | bytes 786440 | tf_op jit(solution)/shard_map/ppermute | solution.py:363
  36.0 1.2 %collective-permute-start.9 = (bf16[512,128]{1,0:T(8,128)(2,1)S(1)}, bf16[512,128]{1,0:T(8,128)(2,1)S(1)}, u32[]{:S(2)}, u32[]{:S(2)}) collective-permute-start(bf16[512,128]{1,0:T(8,128)(2,1)S(1)} %get-tuple-element.111.refs_0_), channel_id=1, source_target_pairs={{0,8},{4,12},{8,0},{12,4},{16,24},{20,28},{24,16},{28,20},{1,9},{5... | collective-permute-start | bytes 393224 | tf_op jit(solution)/shard_map/ppermute | solution.py:290
  37.3 0.8 collective-permute-start.10
  38.1 1.4 %collective-permute-start.11 = (bf16[512,128]{1,0:T(8,128)(2,1)S(1)}, bf16[512,128]{1,0:T(8,128)(2,1)S(1)}, u32[]{:S(2)}, u32[]{:S(2)}) collective-permute-start(bf16[512,128]{1,0:T(8,128)(2,1)S(1)} %get-tuple-element.111.refs_0_), channel_id=1, source_target_pairs={{0,24},{4,28},{8,16},{12,20},{16,8},{20,12},{24,0},{28,4},{1,25},{... | collective-permute-start | bytes 393224 | tf_op jit(solution)/shard_map/ppermute | solution.py:290
  39.5 1.1 %collective-permute-done.13.refs_0_ = bf16[1,256,256]{2,1,0:T(8,128)(2,1)S(1)} collective-permute-done((bf16[1,256,256]{2,1,0:T(8,128)(2,1)S(1)}, bf16[1,256,256]{2,1,0:T(8,128)(2,1)S(1)}, u32[]{:S(2)}, u32[]{:S(2)}) %collective-permute-start.13) | collective-permute-done | bytes 131104 | tf_op jit(solution)/shard_map/ppermute | solution.py:363
  40.8 1.4 %collective-permute-done.9.refs_1_ = bf16[512,128]{1,0:T(8,128)(2,1)S(1)} collective-permute-done((bf16[512,128]{1,0:T(8,128)(2,1)S(1)}, bf16[512,128]{1,0:T(8,128)(2,1)S(1)}, u32[]{:S(2)}, u32[]{:S(2)}) %collective-permute-start.9) | collective-permute-done | bytes 131104 | tf_op jit(solution)/shard_map/ppermute | solution.py:290
  42.2 2.4 %collective-permute-done.10.refs_2_ = bf16[512,128]{1,0:T(8,128)(2,1)S(1)} collective-permute-done((bf16[512,128]{1,0:T(8,128)(2,1)S(1)}, bf16[512,128]{1,0:T(8,128)(2,1)S(1)}, u32[]{:S(2)}, u32[]{:S(2)}) %collective-permute-start.10) | collective-permute-done | bytes 131104 | tf_op jit(solution)/shard_map/ppermute | solution.py:290
  44.6 0.7 shard_map.62.refs_0_
  45.3 1.1 %collective-permute-start.15 = (bf16[512,128]{1,0:T(8,128)(2,1)S(1)}, bf16[512,128]{1,0:T(8,128)(2,1)S(1)}, u32[]{:S(2)}, u32[]{:S(2)}) collective-permute-start(bf16[512,128]{1,0:T(8,128)(2,1)S(1)} %shard_map.62.refs_0_), channel_id=1, source_target_pairs={{0,8},{4,12},{8,0},{12,4},{16,24},{20,28},{24,16},{28,20},{1,9},{5... | collective-permute-start | bytes 393224 | tf_op jit(solution)/shard_map/ppermute | solution.py:290
  46.4 0.7 collective-permute-start.16
  47.2 1.7 %collective-permute-start.17 = (bf16[512,128]{1,0:T(8,128)(2,1)S(1)}, bf16[512,128]{1,0:T(8,128)(2,1)S(1)}, u32[]{:S(2)}, u32[]{:S(2)}) collective-permute-start(bf16[512,128]{1,0:T(8,128)(2,1)S(1)} %shard_map.62.refs_0_), channel_id=1, source_target_pairs={{0,24},{4,28},{8,16},{12,20},{16,8},{20,12},{24,0},{28,4},{1,25},{... | collective-permute-start | bytes 393224 | tf_op jit(solution)/shard_map/ppermute | solution.py:290
  48.8 2.2 %shard_map.63 = (bf16[256,2048]{1,0:T(8,128)(2,1)S(1)}, bf16[256,2048]{1,0:T(8,128)(2,1)S(1)}, bf16[256,2048]{1,0:T(8,128)(2,1)S(1)}, bf16[256,2048]{1,0:T(8,128)(2,1)S(1)}) custom-call(bf16[4,256,2048]{2,1,0:T(8,128)(2,1)} %refs_0_.5, bf16[4,256,2048]{2,1,0:T(8,128)(2,1)} %collective-permute-done.refs_1_, bf16[6,256,2048]{2,1,0:T(8,128)(2,1)} %refs_2_.3, ...), custom_call_target="tpu_custom_call" | custom-call | flops 1024 | bytes 1024 | tf_op jit(solution)/shard_map/pallas_call | solution.py:159
  51.1 1.9 %collective-permute-start.22 = (bf16[1,256,256]{2,1,0:T(8,128)(2,1)S(1)}, bf16[1,256,256]{2,1,0:T(8,128)(2,1)S(1)}, u32[]{:S(2)}, u32[]{:S(2)}) collective-permute-start(bf16[1,256,256]{2,1,0:T(8,128)(2,1)S(1)} %get-tuple-element.133), channel_id=1, source_target_pairs={{0,2},{1,3},{2,0},{3,1},{4,6},{5,7},{6,4},{7,5},{8,10},{9,11},{10,... | collective-permute-start | bytes 393224 | tf_op jit(solution)/shard_map/ppermute | solution.py:363
  53.0 0.5 collective-permute-done.16.refs_2_
  53.5 0.7 shard_map.64
  54.2 1.0 %collective-permute-start.18 = (bf16[512,128]{1,0:T(8,128)(2,1)S(1)}, bf16[512,128]{1,0:T(8,128)(2,1)S(1)}, u32[]{:S(2)}, u32[]{:S(2)}) collective-permute-start(bf16[512,128]{1,0:T(8,128)(2,1)S(1)} %get-tuple-element.126.refs_0_), channel_id=1, source_target_pairs={{0,8},{4,12},{8,0},{12,4},{16,24},{20,28},{24,16},{28,20},{1,9},{5... | collective-permute-start | bytes 393224 | tf_op jit(solution)/shard_map/ppermute | solution.py:290
  55.2 0.9 collective-permute-start.19
  56.1 1.7 %collective-permute-start.20 = (bf16[512,128]{1,0:T(8,128)(2,1)S(1)}, bf16[512,128]{1,0:T(8,128)(2,1)S(1)}, u32[]{:S(2)}, u32[]{:S(2)}) collective-permute-start(bf16[512,128]{1,0:T(8,128)(2,1)S(1)} %get-tuple-element.126.refs_0_), channel_id=1, source_target_pairs={{0,24},{4,28},{8,16},{12,20},{16,8},{20,12},{24,0},{28,4},{1,25},{... | collective-permute-start | bytes 393224 | tf_op jit(solution)/shard_map/ppermute | solution.py:290
  57.8 0.7 collective-permute-done.22.refs_0_
  58.6 1.6 %shard_map.67 = (bf16[256,2048]{1,0:T(8,128)(2,1)S(1)}, bf16[256,2048]{1,0:T(8,128)(2,1)S(1)}) custom-call(bf16[6,256,2048]{2,1,0:T(8,128)(2,1)} %refs_2_.3, bf16[6,256,2048]{2,1,0:T(8,128)(2,1)} %collective-permute-done.5.refs_3_.refs_1_), custom_call_target="tpu_custom_call" | custom-call | flops 1024 | bytes 1024 | tf_op jit(solution)/shard_map/pallas_call | solution.py:159
  60.2 0.7 shard_map.68
  60.9 1.0 %collective-permute-done.20.refs_3_ = bf16[512,128]{1,0:T(8,128)(2,1)S(1)} collective-permute-done((bf16[512,128]{1,0:T(8,128)(2,1)S(1)}, bf16[512,128]{1,0:T(8,128)(2,1)S(1)}, u32[]{:S(2)}, u32[]{:S(2)}) %collective-permute-start.20) | collective-permute-done | bytes 131104 | tf_op jit(solution)/shard_map/ppermute | solution.py:290
  61.9 0.7 shard_map.69.refs_0_
  62.7 1.5 %collective-permute-start.30 = (bf16[2,256,256]{2,1,0:T(8,128)(2,1)S(1)}, bf16[2,256,256]{2,1,0:T(8,128)(2,1)S(1)}, u32[]{:S(2)}, u32[]{:S(2)}) collective-permute-start(bf16[2,256,256]{2,1,0:T(8,128)(2,1)S(1)} %copy-done.4), channel_id=1, source_target_pairs={{0,1},{1,0},{2,3},{3,2},{4,5},{5,4},{6,7},{7,6},{8,9},{9,8},{10,11... | collective-permute-start | bytes 786440 | tf_op jit(solution)/shard_map/ppermute | solution.py:363
  64.2 0.5 collective-permute-start.24
  64.7 0.8 collective-permute-start.25
  65.5 2.1 %collective-permute-start.26 = (bf16[512,128]{1,0:T(8,128)(2,1)S(1)}, bf16[512,128]{1,0:T(8,128)(2,1)S(1)}, u32[]{:S(2)}, u32[]{:S(2)}) collective-permute-start(bf16[512,128]{1,0:T(8,128)(2,1)S(1)} %shard_map.69.refs_0_), channel_id=1, source_target_pairs={{0,24},{4,28},{8,16},{12,20},{16,8},{20,12},{24,0},{28,4},{1,25},{... | collective-permute-start | bytes 393224 | tf_op jit(solution)/shard_map/ppermute | solution.py:290
  67.7 2.2 %shard_map.70 = (bf16[256,2048]{1,0:T(8,128)(2,1)S(1)}, bf16[256,2048]{1,0:T(8,128)(2,1)S(1)}, bf16[256,2048]{1,0:T(8,128)(2,1)S(1)}, bf16[256,2048]{1,0:T(8,128)(2,1)S(1)}) custom-call(bf16[4,256,2048]{2,1,0:T(8,128)(2,1)} %refs_0_.5, bf16[4,256,2048]{2,1,0:T(8,128)(2,1)} %collective-permute-done.refs_1_, bf16[6,256,2048]{2,1,0:T(8,128)(2,1)} %refs_2_.3, ...), custom_call_target="tpu_custom_call" | custom-call | flops 1024 | bytes 1024 | tf_op jit(solution)/shard_map/pallas_call | solution.py:159
  69.9 0.6 collective-permute-done.30.arrived_ref
  70.5 1.0 %collective-permute-start.31 = (bf16[1,256,256]{2,1,0:T(8,128)(2,1)S(1)}, bf16[1,256,256]{2,1,0:T(8,128)(2,1)S(1)}, u32[]{:S(2)}, u32[]{:S(2)}) collective-permute-start(bf16[1,256,256]{2,1,0:T(8,128)(2,1)S(1)} %get-tuple-element.154), channel_id=1, source_target_pairs={{0,2},{1,3},{2,0},{3,1},{4,6},{5,7},{6,4},{7,5},{8,10},{9,11},{10,... | collective-permute-start | bytes 393224 | tf_op jit(solution)/shard_map/ppermute | solution.py:363
  71.7 0.7 shard_map.71
  72.4 1.6 %collective-permute-start.27 = (bf16[512,128]{1,0:T(8,128)(2,1)S(1)}, bf16[512,128]{1,0:T(8,128)(2,1)S(1)}, u32[]{:S(2)}, u32[]{:S(2)}) collective-permute-start(bf16[512,128]{1,0:T(8,128)(2,1)S(1)} %get-tuple-element.147.refs_0_), channel_id=1, source_target_pairs={{0,8},{4,12},{8,0},{12,4},{16,24},{20,28},{24,16},{28,20},{1,9},{5... | collective-permute-start | bytes 393224 | tf_op jit(solution)/shard_map/ppermute | solution.py:290
  74.0 0.9 collective-permute-start.28
  74.9 1.1 %collective-permute-start.29 = (bf16[512,128]{1,0:T(8,128)(2,1)S(1)}, bf16[512,128]{1,0:T(8,128)(2,1)S(1)}, u32[]{:S(2)}, u32[]{:S(2)}) collective-permute-start(bf16[512,128]{1,0:T(8,128)(2,1)S(1)} %get-tuple-element.147.refs_0_), channel_id=1, source_target_pairs={{0,24},{4,28},{8,16},{12,20},{16,8},{20,12},{24,0},{28,4},{1,25},{... | collective-permute-start | bytes 393224 | tf_op jit(solution)/shard_map/ppermute | solution.py:290
  76.0 1.6 %collective-permute-done.31.refs_0_ = bf16[1,256,256]{2,1,0:T(8,128)(2,1)S(1)} collective-permute-done((bf16[1,256,256]{2,1,0:T(8,128)(2,1)S(1)}, bf16[1,256,256]{2,1,0:T(8,128)(2,1)S(1)}, u32[]{:S(2)}, u32[]{:S(2)}) %collective-permute-start.31) | collective-permute-done | bytes 131104 | tf_op jit(solution)/shard_map/ppermute | solution.py:363
  77.7 2.2 %shard_map.74 = (bf16[256,2048]{1,0:T(8,128)(2,1)S(1)}, bf16[256,2048]{1,0:T(8,128)(2,1)S(1)}, bf16[256,2048]{1,0:T(8,128)(2,1)S(1)}, bf16[256,2048]{1,0:T(8,128)(2,1)S(1)}) custom-call(bf16[6,256,2048]{2,1,0:T(8,128)(2,1)} %refs_2_.3, bf16[6,256,2048]{2,1,0:T(8,128)(2,1)} %collective-permute-done.5.refs_3_.refs_1_, bf16[6,256,2048]{2,1,0:T(8,128)(2,1)} %refs_2_.3, ...), custom_call_target="tpu_custom_call" | custom-call | flops 1024 | bytes 1024 | tf_op jit(solution)/shard_map/pallas_call | solution.py:159
  79.9 0.7 shard_map.75
  80.6 0.7 shard_map.76
  81.4 0.7 shard_map.77.refs_0_
  82.1 0.6 collective-permute-start.33
  82.8 1.2 %collective-permute-start.34 = (bf16[512,128]{1,0:T(8,128)(2,1)S(1)}, bf16[512,128]{1,0:T(8,128)(2,1)S(1)}, u32[]{:S(2)}, u32[]{:S(2)}) collective-permute-start(bf16[512,128]{1,0:T(8,128)(2,1)S(1)} %shard_map.77.refs_0_), channel_id=1, source_target_pairs={{0,8},{4,12},{8,0},{12,4},{16,24},{20,28},{24,16},{28,20},{1,9},{5... | collective-permute-start | bytes 393224 | tf_op jit(solution)/shard_map/ppermute | solution.py:290
  83.9 0.9 collective-permute-start.35
  84.8 1.4 %collective-permute-start.36 = (bf16[512,128]{1,0:T(8,128)(2,1)S(1)}, bf16[512,128]{1,0:T(8,128)(2,1)S(1)}, u32[]{:S(2)}, u32[]{:S(2)}) collective-permute-start(bf16[512,128]{1,0:T(8,128)(2,1)S(1)} %shard_map.77.refs_0_), channel_id=1, source_target_pairs={{0,24},{4,28},{8,16},{12,20},{16,8},{20,12},{24,0},{28,4},{1,25},{... | collective-permute-start | bytes 393224 | tf_op jit(solution)/shard_map/ppermute | solution.py:290
  86.3 1.6 %shard_map.78 = (bf16[256,2048]{1,0:T(8,128)(2,1)S(1)}, bf16[256,2048]{1,0:T(8,128)(2,1)S(1)}) custom-call(bf16[4,256,2048]{2,1,0:T(8,128)(2,1)} %refs_0_.5, bf16[4,256,2048]{2,1,0:T(8,128)(2,1)} %collective-permute-done.refs_1_), custom_call_target="tpu_custom_call" | custom-call | flops 1024 | bytes 1024 | tf_op jit(solution)/shard_map/pallas_call | solution.py:159
  87.9 1.1 %maximum_maximum_fusion = f32[4,256,256]{2,1,0:T(8,128)} fusion(f32[1,256,256]{2,1,0:T(8,128)S(1)} %maximum_select_fusion.2, f32[1,256,256]{2,1,0:T(8,128)S(1)} %get-tuple-element.185, f32[1,256,256]{2,1,0:T(8,128)S(1)} %get-tuple-element.184, f32[4]{0:T(128)S(1)} %pad.7.clone), kind=kLoop, calls=%fused_computation | loop fusion | flops 786432 | bytes 1835024 | tf_op jit(solution)/shard_map/stack | solution.py:402
  89.1 2.8 %collective-permute-done.35.refs_2_ = bf16[512,128]{1,0:T(8,128)(2,1)S(1)} collective-permute-done((bf16[512,128]{1,0:T(8,128)(2,1)S(1)}, bf16[512,128]{1,0:T(8,128)(2,1)S(1)}, u32[]{:S(2)}, u32[]{:S(2)}) %collective-permute-start.35) | collective-permute-done | bytes 131104 | tf_op jit(solution)/shard_map/ppermute | solution.py:290
  91.9 0.4 shard_map.79
  92.4 0.4 shard_map.80
  92.8 0.9 collective-permute-done.37
  93.7 0.7 fusion
  (58 shorter events, 1.6 us)
Async XLA Ops:
  0.0 28.0 %collective-permute-start.5 = (bf16[6,256,2048]{2,1,0:T(8,128)(2,1)}, bf16[6,256,2048]{2,1,0:T(8,128)(2,1)}, u32[]{:S(2)}, u32[]{:S(2)}) collective-permute-start(bf16[6,256,2048]{2,1,0:T(8,128)(2,1)} %refs_2_.3), channel_id=1, source_target_pairs={{0,4},{4,0},{8,12},{12,8},{16,20},{20,16},{24,28},{28,24},{1,5},{5... | collective-permute-start | bytes 18874376 | tf_op jit(solution)/shard_map/ppermute | solution.py:283
  0.5 22.0 %collective-permute-start = (bf16[4,256,2048]{2,1,0:T(8,128)(2,1)}, bf16[4,256,2048]{2,1,0:T(8,128)(2,1)}, u32[]{:S(2)}, u32[]{:S(2)}) collective-permute-start(bf16[4,256,2048]{2,1,0:T(8,128)(2,1)} %refs_0_.5), channel_id=1, source_target_pairs={{0,4},{4,0},{8,12},{12,8},{16,20},{20,16},{24,28},{28,24},{1,5},{5... | collective-permute-start | bytes 12582920 | tf_op jit(solution)/shard_map/ppermute | solution.py:283
  5.3 17.2 %collective-permute-start.1 = (bf16[256,256]{1,0:T(8,128)(2,1)S(1)}, bf16[256,256]{1,0:T(8,128)(2,1)S(1)}, u32[]{:S(2)}, u32[]{:S(2)}) collective-permute-start(bf16[256,256]{1,0:T(8,128)(2,1)S(1)} %get-tuple-element.99), channel_id=1, source_target_pairs={{0,1},{1,2},{2,3},{3,0},{4,5},{5,6},{6,7},{7,4},{8,9},{9,10},{10,1... | collective-permute-start | bytes 393224 | tf_op jit(solution)/shard_map/ppermute | solution.py:320
  8.3 14.2 %copy-start = (f32[4,256,256]{2,1,0:T(8,128)S(1)}, f32[4,256,256]{2,1,0:T(8,128)}, u32[]{:S(2)}) copy-start(f32[4,256,256]{2,1,0:T(8,128)} %rhs_ref.7) | copy-start | bytes 3145732
  8.3 14.2 %collective-permute-start.2 = (bf16[256,256]{1,0:T(8,128)(2,1)S(1)}, bf16[256,256]{1,0:T(8,128)(2,1)S(1)}, u32[]{:S(2)}, u32[]{:S(2)}) collective-permute-start(bf16[256,256]{1,0:T(8,128)(2,1)S(1)} %get-tuple-element.101), channel_id=1, source_target_pairs={{0,3},{1,0},{2,1},{3,2},{4,7},{5,4},{6,5},{7,6},{8,11},{9,8},{10,9... | collective-permute-start | bytes 393224 | tf_op jit(solution)/shard_map/ppermute | solution.py:320
  10.4 12.1 %collective-permute-start.3 = (bf16[256,256]{1,0:T(8,128)(2,1)S(1)}, bf16[256,256]{1,0:T(8,128)(2,1)S(1)}, u32[]{:S(2)}, u32[]{:S(2)}) collective-permute-start(bf16[256,256]{1,0:T(8,128)(2,1)S(1)} %get-tuple-element.102), channel_id=1, source_target_pairs={{0,2},{1,3},{2,0},{3,1},{4,6},{5,7},{6,4},{7,5},{8,10},{9,11},{10,... | collective-permute-start | bytes 393224 | tf_op jit(solution)/shard_map/ppermute | solution.py:320
  22.6 1.7 %collective-permute-start.4 = (bf16[256,128]{1,0:T(8,128)(2,1)S(1)}, bf16[256,128]{1,0:T(8,128)(2,1)S(1)}, u32[]{:S(2)}, u32[]{:S(2)}) collective-permute-start(bf16[256,128]{1,0:T(8,128)(2,1)S(1)} %get-tuple-element.104), channel_id=1, source_target_pairs={{0,4},{4,0},{8,12},{12,8},{16,20},{20,16},{24,28},{28,24},{1,5},{5... | collective-permute-start | bytes 196616 | tf_op jit(solution)/shard_map/ppermute | solution.py:283
  22.7 8.9 %collective-permute-start.12 = (bf16[2,256,256]{2,1,0:T(8,128)(2,1)}, bf16[2,256,256]{2,1,0:T(8,128)(2,1)S(1)}, u32[]{:S(2)}, u32[]{:S(2)}) collective-permute-start(bf16[2,256,256]{2,1,0:T(8,128)(2,1)} %get-tuple-element.114), channel_id=1, source_target_pairs={{0,1},{1,0},{2,3},{3,2},{4,5},{5,4},{6,7},{7,6},{8,9},{9,8},{10,11... | collective-permute-start | bytes 786440 | tf_op jit(solution)/shard_map/ppermute | solution.py:363
  24.4 7.3 %copy-start.3 = (f32[2,256,256]{2,1,0:T(8,128)S(1)}, f32[2,256,256]{2,1,0:T(8,128)}, u32[]{:S(2)}) copy-start(f32[2,256,256]{2,1,0:T(8,128)} %get-tuple-element.113.exact_ref) | copy-start | bytes 1572868
  24.4 10.4 %copy-start.5 = (bf16[2,256,256]{2,1,0:T(8,128)(2,1)S(1)}, bf16[2,256,256]{2,1,0:T(8,128)(2,1)}, u32[]{:S(2)}) copy-start(bf16[2,256,256]{2,1,0:T(8,128)(2,1)} %get-tuple-element.130) | copy-start | bytes 786436
  24.4 9.3 %collective-permute-start.6 = (bf16[512,128]{1,0:T(8,128)(2,1)S(1)}, bf16[512,128]{1,0:T(8,128)(2,1)S(1)}, u32[]{:S(2)}, u32[]{:S(2)}) collective-permute-start(bf16[512,128]{1,0:T(8,128)(2,1)S(1)} %maximum_select_fusion.4.refs_0_), channel_id=1, source_target_pairs={{0,8},{4,12},{8,0},{12,4},{16,24},{20,28},{24,16},{28,20},{1,9},{5... | collective-permute-start | bytes 393224 | tf_op jit(solution)/shard_map/ppermute | solution.py:290
  26.0 8.1 %collective-permute-start.7 = (bf16[512,128]{1,0:T(8,128)(2,1)S(1)}, bf16[512,128]{1,0:T(8,128)(2,1)S(1)}, u32[]{:S(2)}, u32[]{:S(2)}) collective-permute-start(bf16[512,128]{1,0:T(8,128)(2,1)S(1)} %maximum_select_fusion.4.refs_0_), channel_id=1, source_target_pairs={{0,16},{4,20},{8,24},{12,28},{16,0},{20,4},{24,8},{28,12},{1,17},{... | collective-permute-start | bytes 393224 | tf_op jit(solution)/shard_map/ppermute | solution.py:290
  27.5 6.6 %collective-permute-start.8 = (bf16[512,128]{1,0:T(8,128)(2,1)S(1)}, bf16[512,128]{1,0:T(8,128)(2,1)S(1)}, u32[]{:S(2)}, u32[]{:S(2)}) collective-permute-start(bf16[512,128]{1,0:T(8,128)(2,1)S(1)} %maximum_select_fusion.4.refs_0_), channel_id=1, source_target_pairs={{0,24},{4,28},{8,16},{12,20},{16,8},{20,12},{24,0},{28,4},{1,25},{... | collective-permute-start | bytes 393224 | tf_op jit(solution)/shard_map/ppermute | solution.py:290
  31.7 8.9 %collective-permute-start.13 = (bf16[1,256,256]{2,1,0:T(8,128)(2,1)S(1)}, bf16[1,256,256]{2,1,0:T(8,128)(2,1)S(1)}, u32[]{:S(2)}, u32[]{:S(2)}) collective-permute-start(bf16[1,256,256]{2,1,0:T(8,128)(2,1)S(1)} %get-tuple-element.117), channel_id=1, source_target_pairs={{0,2},{1,3},{2,0},{3,1},{4,6},{5,7},{6,4},{7,5},{8,10},{9,11},{10,... | collective-permute-start | bytes 393224 | tf_op jit(solution)/shard_map/ppermute | solution.py:363
  34.8 16.3 %collective-permute-start.21 = (bf16[2,256,256]{2,1,0:T(8,128)(2,1)S(1)}, bf16[2,256,256]{2,1,0:T(8,128)(2,1)S(1)}, u32[]{:S(2)}, u32[]{:S(2)}) collective-permute-start(bf16[2,256,256]{2,1,0:T(8,128)(2,1)S(1)} %copy-done.5), channel_id=1, source_target_pairs={{0,1},{1,0},{2,3},{3,2},{4,5},{5,4},{6,7},{7,6},{8,9},{9,8},{10,11... | collective-permute-start | bytes 786440 | tf_op jit(solution)/shard_map/ppermute | solution.py:363
  36.0 6.2 %collective-permute-start.9 = (bf16[512,128]{1,0:T(8,128)(2,1)S(1)}, bf16[512,128]{1,0:T(8,128)(2,1)S(1)}, u32[]{:S(2)}, u32[]{:S(2)}) collective-permute-start(bf16[512,128]{1,0:T(8,128)(2,1)S(1)} %get-tuple-element.111.refs_0_), channel_id=1, source_target_pairs={{0,8},{4,12},{8,0},{12,4},{16,24},{20,28},{24,16},{28,20},{1,9},{5... | collective-permute-start | bytes 393224 | tf_op jit(solution)/shard_map/ppermute | solution.py:290
  37.3 7.3 %collective-permute-start.10 = (bf16[512,128]{1,0:T(8,128)(2,1)S(1)}, bf16[512,128]{1,0:T(8,128)(2,1)S(1)}, u32[]{:S(2)}, u32[]{:S(2)}) collective-permute-start(bf16[512,128]{1,0:T(8,128)(2,1)S(1)} %get-tuple-element.111.refs_0_), channel_id=1, source_target_pairs={{0,16},{4,20},{8,24},{12,28},{16,0},{20,4},{24,8},{28,12},{1,17},{... | collective-permute-start | bytes 393224 | tf_op jit(solution)/shard_map/ppermute | solution.py:290
  38.1 6.5 %collective-permute-start.11 = (bf16[512,128]{1,0:T(8,128)(2,1)S(1)}, bf16[512,128]{1,0:T(8,128)(2,1)S(1)}, u32[]{:S(2)}, u32[]{:S(2)}) collective-permute-start(bf16[512,128]{1,0:T(8,128)(2,1)S(1)} %get-tuple-element.111.refs_0_), channel_id=1, source_target_pairs={{0,24},{4,28},{8,16},{12,20},{16,8},{20,12},{24,0},{28,4},{1,25},{... | collective-permute-start | bytes 393224 | tf_op jit(solution)/shard_map/ppermute | solution.py:290
  40.7 3.9 %collective-permute-start.14 = (f32[256,128]{1,0:T(8,128)S(1)}, f32[256,128]{1,0:T(8,128)S(1)}, u32[]{:S(2)}, u32[]{:S(2)}) collective-permute-start(f32[256,128]{1,0:T(8,128)S(1)} %get-tuple-element.119), channel_id=1, source_target_pairs={{0,4},{4,0},{8,12},{12,8},{16,20},{20,16},{24,28},{28,24},{1,5},{5... | collective-permute-start | bytes 393224 | tf_op jit(solution)/shard_map/ppermute | solution.py:283
  45.3 5.8 %copy-start.2 = (f32[2,256,256]{2,1,0:T(8,128)S(1)}, f32[2,256,256]{2,1,0:T(8,128)}, u32[]{:S(2)}) copy-start(f32[2,256,256]{2,1,0:T(8,128)} %get-tuple-element.128.exact_ref) | copy-start | bytes 1572868
  45.3 7.7 %collective-permute-start.15 = (bf16[512,128]{1,0:T(8,128)(2,1)S(1)}, bf16[512,128]{1,0:T(8,128)(2,1)S(1)}, u32[]{:S(2)}, u32[]{:S(2)}) collective-permute-start(bf16[512,128]{1,0:T(8,128)(2,1)S(1)} %shard_map.62.refs_0_), channel_id=1, source_target_pairs={{0,8},{4,12},{8,0},{12,4},{16,24},{20,28},{24,16},{28,20},{1,9},{5... | collective-permute-start | bytes 393224 | tf_op jit(solution)/shard_map/ppermute | solution.py:290
  46.4 7.1 %collective-permute-start.16 = (bf16[512,128]{1,0:T(8,128)(2,1)S(1)}, bf16[512,128]{1,0:T(8,128)(2,1)S(1)}, u32[]{:S(2)}, u32[]{:S(2)}) collective-permute-start(bf16[512,128]{1,0:T(8,128)(2,1)S(1)} %shard_map.62.refs_0_), channel_id=1, source_target_pairs={{0,16},{4,20},{8,24},{12,28},{16,0},{20,4},{24,8},{28,12},{1,17},{... | collective-permute-start | bytes 393224 | tf_op jit(solution)/shard_map/ppermute | solution.py:290
  47.2 6.3 %collective-permute-start.17 = (bf16[512,128]{1,0:T(8,128)(2,1)S(1)}, bf16[512,128]{1,0:T(8,128)(2,1)S(1)}, u32[]{:S(2)}, u32[]{:S(2)}) collective-permute-start(bf16[512,128]{1,0:T(8,128)(2,1)S(1)} %shard_map.62.refs_0_), channel_id=1, source_target_pairs={{0,24},{4,28},{8,16},{12,20},{16,8},{20,12},{24,0},{28,4},{1,25},{... | collective-permute-start | bytes 393224 | tf_op jit(solution)/shard_map/ppermute | solution.py:290
  51.1 7.3 %collective-permute-start.22 = (bf16[1,256,256]{2,1,0:T(8,128)(2,1)S(1)}, bf16[1,256,256]{2,1,0:T(8,128)(2,1)S(1)}, u32[]{:S(2)}, u32[]{:S(2)}) collective-permute-start(bf16[1,256,256]{2,1,0:T(8,128)(2,1)S(1)} %get-tuple-element.133), channel_id=1, source_target_pairs={{0,2},{1,3},{2,0},{3,1},{4,6},{5,7},{6,4},{7,5},{8,10},{9,11},{10,... | collective-permute-start | bytes 393224 | tf_op jit(solution)/shard_map/ppermute | solution.py:363
  54.2 6.7 %collective-permute-start.18 = (bf16[512,128]{1,0:T(8,128)(2,1)S(1)}, bf16[512,128]{1,0:T(8,128)(2,1)S(1)}, u32[]{:S(2)}, u32[]{:S(2)}) collective-permute-start(bf16[512,128]{1,0:T(8,128)(2,1)S(1)} %get-tuple-element.126.refs_0_), channel_id=1, source_target_pairs={{0,8},{4,12},{8,0},{12,4},{16,24},{20,28},{24,16},{28,20},{1,9},{5... | collective-permute-start | bytes 393224 | tf_op jit(solution)/shard_map/ppermute | solution.py:290
  55.2 5.7 %collective-permute-start.19 = (bf16[512,128]{1,0:T(8,128)(2,1)S(1)}, bf16[512,128]{1,0:T(8,128)(2,1)S(1)}, u32[]{:S(2)}, u32[]{:S(2)}) collective-permute-start(bf16[512,128]{1,0:T(8,128)(2,1)S(1)} %get-tuple-element.126.refs_0_), channel_id=1, source_target_pairs={{0,16},{4,20},{8,24},{12,28},{16,0},{20,4},{24,8},{28,12},{1,17},{... | collective-permute-start | bytes 393224 | tf_op jit(solution)/shard_map/ppermute | solution.py:290
  56.1 5.9 %collective-permute-start.20 = (bf16[512,128]{1,0:T(8,128)(2,1)S(1)}, bf16[512,128]{1,0:T(8,128)(2,1)S(1)}, u32[]{:S(2)}, u32[]{:S(2)}) collective-permute-start(bf16[512,128]{1,0:T(8,128)(2,1)S(1)} %get-tuple-element.126.refs_0_), channel_id=1, source_target_pairs={{0,24},{4,28},{8,16},{12,20},{16,8},{20,12},{24,0},{28,4},{1,25},{... | collective-permute-start | bytes 393224 | tf_op jit(solution)/shard_map/ppermute | solution.py:290
  58.5 4.1 %copy-start.4 = (bf16[2,256,256]{2,1,0:T(8,128)(2,1)S(1)}, bf16[2,256,256]{2,1,0:T(8,128)(2,1)}, u32[]{:S(2)}) copy-start(bf16[2,256,256]{2,1,0:T(8,128)(2,1)} %get-tuple-element.151) | copy-start | bytes 786436
  58.5 3.4 %collective-permute-start.23 = (f32[256,128]{1,0:T(8,128)S(1)}, f32[256,128]{1,0:T(8,128)S(1)}, u32[]{:S(2)}, u32[]{:S(2)}) collective-permute-start(f32[256,128]{1,0:T(8,128)S(1)} %get-tuple-element.135), channel_id=1, source_target_pairs={{0,4},{4,0},{8,12},{12,8},{16,20},{20,16},{24,28},{28,24},{1,5},{5... | collective-permute-start | bytes 393224 | tf_op jit(solution)/shard_map/ppermute | solution.py:283
  62.7 7.8 %copy-start.1 = (f32[2,256,256]{2,1,0:T(8,128)S(1)}, f32[2,256,256]{2,1,0:T(8,128)}, u32[]{:S(2)}) copy-start(f32[2,256,256]{2,1,0:T(8,128)} %get-tuple-element.149.exact_ref) | copy-start | bytes 1572868
  62.7 7.8 %collective-permute-start.30 = (bf16[2,256,256]{2,1,0:T(8,128)(2,1)S(1)}, bf16[2,256,256]{2,1,0:T(8,128)(2,1)S(1)}, u32[]{:S(2)}, u32[]{:S(2)}) collective-permute-start(bf16[2,256,256]{2,1,0:T(8,128)(2,1)S(1)} %copy-done.4), channel_id=1, source_target_pairs={{0,1},{1,0},{2,3},{3,2},{4,5},{5,4},{6,7},{7,6},{8,9},{9,8},{10,11... | collective-permute-start | bytes 786440 | tf_op jit(solution)/shard_map/ppermute | solution.py:363
  64.2 7.3 %collective-permute-start.24 = (bf16[512,128]{1,0:T(8,128)(2,1)S(1)}, bf16[512,128]{1,0:T(8,128)(2,1)S(1)}, u32[]{:S(2)}, u32[]{:S(2)}) collective-permute-start(bf16[512,128]{1,0:T(8,128)(2,1)S(1)} %shard_map.69.refs_0_), channel_id=1, source_target_pairs={{0,8},{4,12},{8,0},{12,4},{16,24},{20,28},{24,16},{28,20},{1,9},{5... | collective-permute-start | bytes 393224 | tf_op jit(solution)/shard_map/ppermute | solution.py:290
  64.7 6.8 %collective-permute-start.25 = (bf16[512,128]{1,0:T(8,128)(2,1)S(1)}, bf16[512,128]{1,0:T(8,128)(2,1)S(1)}, u32[]{:S(2)}, u32[]{:S(2)}) collective-permute-start(bf16[512,128]{1,0:T(8,128)(2,1)S(1)} %shard_map.69.refs_0_), channel_id=1, source_target_pairs={{0,16},{4,20},{8,24},{12,28},{16,0},{20,4},{24,8},{28,12},{1,17},{... | collective-permute-start | bytes 393224 | tf_op jit(solution)/shard_map/ppermute | solution.py:290
  65.5 6.2 %collective-permute-start.26 = (bf16[512,128]{1,0:T(8,128)(2,1)S(1)}, bf16[512,128]{1,0:T(8,128)(2,1)S(1)}, u32[]{:S(2)}, u32[]{:S(2)}) collective-permute-start(bf16[512,128]{1,0:T(8,128)(2,1)S(1)} %shard_map.69.refs_0_), channel_id=1, source_target_pairs={{0,24},{4,28},{8,16},{12,20},{16,8},{20,12},{24,0},{28,4},{1,25},{... | collective-permute-start | bytes 393224 | tf_op jit(solution)/shard_map/ppermute | solution.py:290
  70.5 7.1 %collective-permute-start.31 = (bf16[1,256,256]{2,1,0:T(8,128)(2,1)S(1)}, bf16[1,256,256]{2,1,0:T(8,128)(2,1)S(1)}, u32[]{:S(2)}, u32[]{:S(2)}) collective-permute-start(bf16[1,256,256]{2,1,0:T(8,128)(2,1)S(1)} %get-tuple-element.154), channel_id=1, source_target_pairs={{0,2},{1,3},{2,0},{3,1},{4,6},{5,7},{6,4},{7,5},{8,10},{9,11},{10,... | collective-permute-start | bytes 393224 | tf_op jit(solution)/shard_map/ppermute | solution.py:363
  72.4 9.0 %collective-permute-start.27 = (bf16[512,128]{1,0:T(8,128)(2,1)S(1)}, bf16[512,128]{1,0:T(8,128)(2,1)S(1)}, u32[]{:S(2)}, u32[]{:S(2)}) collective-permute-start(bf16[512,128]{1,0:T(8,128)(2,1)S(1)} %get-tuple-element.147.refs_0_), channel_id=1, source_target_pairs={{0,8},{4,12},{8,0},{12,4},{16,24},{20,28},{24,16},{28,20},{1,9},{5... | collective-permute-start | bytes 393224 | tf_op jit(solution)/shard_map/ppermute | solution.py:290
  74.0 7.4 %collective-permute-start.28 = (bf16[512,128]{1,0:T(8,128)(2,1)S(1)}, bf16[512,128]{1,0:T(8,128)(2,1)S(1)}, u32[]{:S(2)}, u32[]{:S(2)}) collective-permute-start(bf16[512,128]{1,0:T(8,128)(2,1)S(1)} %get-tuple-element.147.refs_0_), channel_id=1, source_target_pairs={{0,16},{4,20},{8,24},{12,28},{16,0},{20,4},{24,8},{28,12},{1,17},{... | collective-permute-start | bytes 393224 | tf_op jit(solution)/shard_map/ppermute | solution.py:290
  74.9 6.5 %collective-permute-start.29 = (bf16[512,128]{1,0:T(8,128)(2,1)S(1)}, bf16[512,128]{1,0:T(8,128)(2,1)S(1)}, u32[]{:S(2)}, u32[]{:S(2)}) collective-permute-start(bf16[512,128]{1,0:T(8,128)(2,1)S(1)} %get-tuple-element.147.refs_0_), channel_id=1, source_target_pairs={{0,24},{4,28},{8,16},{12,20},{16,8},{20,12},{24,0},{28,4},{1,25},{... | collective-permute-start | bytes 393224 | tf_op jit(solution)/shard_map/ppermute | solution.py:290
  77.6 3.8 %collective-permute-start.32 = (f32[256,128]{1,0:T(8,128)S(1)}, f32[256,128]{1,0:T(8,128)S(1)}, u32[]{:S(2)}, u32[]{:S(2)}) collective-permute-start(f32[256,128]{1,0:T(8,128)S(1)} %get-tuple-element.156), channel_id=1, source_target_pairs={{0,4},{4,0},{8,12},{12,8},{16,20},{20,16},{24,28},{28,24},{1,5},{5... | collective-permute-start | bytes 393224 | tf_op jit(solution)/shard_map/ppermute | solution.py:283
  82.1 5.7 %collective-permute-start.33 = (f32[3,256,128]{2,1,0:T(8,128)S(1)}, f32[3,256,128]{2,1,0:T(8,128)S(1)}, u32[]{:S(2)}, u32[]{:S(2)}) collective-permute-start(f32[3,256,128]{2,1,0:T(8,128)S(1)} %pad_maximum_fusion), channel_id=1, source_target_pairs={{0,4},{4,0},{8,12},{12,8},{16,20},{20,16},{24,28},{28,24},{1,5},{5... | collective-permute-start | bytes 1179656 | tf_op jit(solution)/shard_map/ppermute | solution.py:283
  82.8 6.3 %collective-permute-start.34 = (bf16[512,128]{1,0:T(8,128)(2,1)S(1)}, bf16[512,128]{1,0:T(8,128)(2,1)S(1)}, u32[]{:S(2)}, u32[]{:S(2)}) collective-permute-start(bf16[512,128]{1,0:T(8,128)(2,1)S(1)} %shard_map.77.refs_0_), channel_id=1, source_target_pairs={{0,8},{4,12},{8,0},{12,4},{16,24},{20,28},{24,16},{28,20},{1,9},{5... | collective-permute-start | bytes 393224 | tf_op jit(solution)/shard_map/ppermute | solution.py:290
  83.9 8.0 %collective-permute-start.35 = (bf16[512,128]{1,0:T(8,128)(2,1)S(1)}, bf16[512,128]{1,0:T(8,128)(2,1)S(1)}, u32[]{:S(2)}, u32[]{:S(2)}) collective-permute-start(bf16[512,128]{1,0:T(8,128)(2,1)S(1)} %shard_map.77.refs_0_), channel_id=1, source_target_pairs={{0,16},{4,20},{8,24},{12,28},{16,0},{20,4},{24,8},{28,12},{1,17},{... | collective-permute-start | bytes 393224 | tf_op jit(solution)/shard_map/ppermute | solution.py:290
  84.8 7.0 %collective-permute-start.36 = (bf16[512,128]{1,0:T(8,128)(2,1)S(1)}, bf16[512,128]{1,0:T(8,128)(2,1)S(1)}, u32[]{:S(2)}, u32[]{:S(2)}) collective-permute-start(bf16[512,128]{1,0:T(8,128)(2,1)S(1)} %shard_map.77.refs_0_), channel_id=1, source_target_pairs={{0,24},{4,28},{8,16},{12,20},{16,8},{20,12},{24,0},{28,4},{1,25},{... | collective-permute-start | bytes 393224 | tf_op jit(solution)/shard_map/ppermute | solution.py:290
  92.3 1.4 %collective-permute-start.37 = (f32[256,128]{1,0:T(8,128)S(1)}, f32[256,128]{1,0:T(8,128)S(1)}, u32[]{:S(2)}, u32[]{:S(2)}) collective-permute-start(f32[256,128]{1,0:T(8,128)S(1)} %shard_map.79), channel_id=1, source_target_pairs={{0,4},{4,0},{8,12},{12,8},{16,20},{20,16},{24,28},{28,24},{1,5},{5... | collective-permute-start | bytes 393224 | tf_op jit(solution)/shard_map/ppermute | solution.py:283

commit v6 on v5

--- a/solution.py
+++ b/solution.py
@@ -282,11 +282,13 @@
     def swap(value):
         return lax.ppermute(value, "row", [(i, i ^ 1) for i in range(row_count)])
 
-    def gather(value, token=None):
+    def gather(value, token=None, lower=False):
         late = value if token is None else after(value, token)
         shards = {0: value}
         for mask in range(1, chips):
             pairs = [(i, i ^ (2 * mask)) for i in range(row_count)]
+            if lower and mask == chips - 1:
+                pairs = [(i, j) for i, j in pairs if i < j]
             shards[mask] = lax.ppermute(late if mask == 1 else value, "row", pairs)
         return shards
 
@@ -381,7 +383,7 @@
     near_matrix = {}
     for target in range(steps):
         last = target + 1 == steps
-        shards = gather(resid_low)
+        shards = gather(resid_low, lower=last)
         if target == 0:
             diag_matrix, near_matrix[0] = load(resid_low, diag_pick[0], inner_pick[0])
             for stage in range(1, stages):

time: 94.6 us -> 93.8 us (level)
  waiting for transfers between devices: 15 us -> 12.2 us
  starting transfers between devices: 41.5 us -> 43.4 us
    ppermute x21, waiting for transfers between devices: 8.66 us -> 5.84 us  [gather(): shards[mask] = lax.ppermute(late if mask == 1 else value, 'row', pairs)]
    ppermute x21, starting transfers between devices: 24.7 us -> 26.6 us  [gather(): shards[mask] = lax.ppermute(late if mask == 1 else value, 'row', pairs)]
  transfers between devices with their start and end apart: 38 -> 38, of which waited for: 13 -> 12; matrix products, arithmetic and copies ran while one was open for 1% -> 1% of each run, Pallas kernels for 36% -> 36%
where the time goes in v6:
time: 93.8 us; the launch traced here: 93.6 us
  starting transfers between devices  43.4 us (46%)
  Pallas kernels  35.4 us (38%)
  waiting for transfers between devices  12.2 us (13%)
  other arithmetic  1.97 us (2%)
    ppermute x21, starting transfers between devices, gather(): shards[mask] = lax.ppermute(late if mask == 1 else value, 'row', pairs)  26.6 us
    pallas_call x6, Pallas kernels, load(): pl.pallas_call(functools.partial(load_kernel, indices), in_specs=[HBM] *...  12 us
    pallas_call x1, Pallas kernels, local(): pl.pallas_call(functools.partial(later_kernel, col_count, pieces, 2), in_...  11.1 us
    ppermute x6, starting transfers between devices, halve(): arrived[target] = lax.ppermute(low, 'col', pairs)  9.28 us
    pallas_call x9, Pallas kernels, apply_rows(): pl.pallas_call(functools.partial(apply_kernel, masks, len(held), sign, ex...  6.4 us
    ppermute x3, starting transfers between devices, send(): lax.ppermute(after(chunks[target][k], token), 'col', [(i, (i + shifts[k])...  6.12 us
    ppermute x21, waiting for transfers between devices, gather(): shards[mask] = lax.ppermute(late if mask == 1 else value, 'row', pairs)  5.84 us
    ppermute x6, waiting for transfers between devices, halve(): arrived[target] = lax.ppermute(low, 'col', pairs)  5.44 us
  transfers between devices with their start and end apart: 38, of which 12 were waited for; matrix products, arithmetic and copies ran while one was open for 1% of the time, Pallas kernels for 36%

profile of v6, /device:TPU:0, one launch (start us, length us, event | category | flops | bytes accessed | tf_op | source)
XLA Modules:
  0.0 93.6 jit_solution(14753126689591397658)
XLA Ops:
  0.0 0.5 collective-permute-start.5
  0.5 4.7 %shard_map.55 = (bf16[256,256]{1,0:T(8,128)(2,1)S(1)}, bf16[256,256]{1,0:T(8,128)(2,1)S(1)}, bf16[256,256]{1,0:T(8,128)(2,1)S(1)}, f32[256,256]{1,0:T(8,128)S(1)}) custom-call(bf16[4,256,4096]{2,1,0:T(8,128)(2,1)} %l_ref.3, bf16[4096,1024]{1,0:T(8,128)(2,1)} %x_ref.2), custom_call_target="tpu_custom_call" | custom-call | flops 2147483648 | bytes 10485760 | tf_op jit(solution)/shard_map/pallas_call | solution.py:303
  5.3 3.1 %collective-permute-start.1 = (bf16[256,256]{1,0:T(8,128)(2,1)S(1)}, bf16[256,256]{1,0:T(8,128)(2,1)S(1)}, u32[]{:S(2)}, u32[]{:S(2)}) collective-permute-start(bf16[256,256]{1,0:T(8,128)(2,1)S(1)} %get-tuple-element.99), channel_id=1, source_target_pairs={{0,1},{1,2},{2,3},{3,0},{4,5},{5,6},{6,7},{7,4},{8,9},{9,10},{10,1... | collective-permute-start | bytes 393224 | tf_op jit(solution)/shard_map/ppermute | solution.py:322
  8.3 2.1 %collective-permute-start.2 = (bf16[256,256]{1,0:T(8,128)(2,1)S(1)}, bf16[256,256]{1,0:T(8,128)(2,1)S(1)}, u32[]{:S(2)}, u32[]{:S(2)}) collective-permute-start(bf16[256,256]{1,0:T(8,128)(2,1)S(1)} %get-tuple-element.101), channel_id=1, source_target_pairs={{0,3},{1,0},{2,1},{3,2},{4,7},{5,4},{6,5},{7,6},{8,11},{9,8},{10,9... | collective-permute-start | bytes 393224 | tf_op jit(solution)/shard_map/ppermute | solution.py:322
  10.4 0.9 %collective-permute-start.3 = (bf16[256,256]{1,0:T(8,128)(2,1)S(1)}, bf16[256,256]{1,0:T(8,128)(2,1)S(1)}, u32[]{:S(2)}, u32[]{:S(2)}) collective-permute-start(bf16[256,256]{1,0:T(8,128)(2,1)S(1)} %get-tuple-element.102), channel_id=1, source_target_pairs={{0,2},{1,3},{2,0},{3,1},{4,6},{5,7},{6,4},{7,5},{8,10},{9,11},{10,... | collective-permute-start | bytes 393224 | tf_op jit(solution)/shard_map/ppermute | solution.py:322
  11.4 11.1 %shard_map.56 = (bf16[2,256,256]{2,1,0:T(8,128)(2,1)}, f32[2,256,256]{2,1,0:T(8,128)}, bf16[2,256,256]{2,1,0:T(8,128)(2,1)}, f32[2,256,256]{2,1,0:T(8,128)}, bf1...) custom-call(bf16[4,256,4096]{2,1,0:T(8,128)(2,1)} %l_ref.3, bf16[4096,1024]{1,0:T(8,128)(2,1)} %x_ref.2), custom_call_target="tpu_custom_call" | custom-call | flops 6442450944 | bytes 14680064 | tf_op jit(solution)/shard_map/pallas_call | solution.py:336
  22.7 1.6 %collective-permute-start.12 = (bf16[2,256,256]{2,1,0:T(8,128)(2,1)}, bf16[2,256,256]{2,1,0:T(8,128)(2,1)S(1)}, u32[]{:S(2)}, u32[]{:S(2)}) collective-permute-start(bf16[2,256,256]{2,1,0:T(8,128)(2,1)} %get-tuple-element.114), channel_id=1, source_target_pairs={{0,1},{1,0},{2,3},{3,2},{4,5},{5,4},{6,7},{7,6},{8,9},{9,8},{10,11... | collective-permute-start | bytes 786440 | tf_op jit(solution)/shard_map/ppermute | solution.py:365
  24.4 1.6 %collective-permute-start.6 = (bf16[512,128]{1,0:T(8,128)(2,1)S(1)}, bf16[512,128]{1,0:T(8,128)(2,1)S(1)}, u32[]{:S(2)}, u32[]{:S(2)}) collective-permute-start(bf16[512,128]{1,0:T(8,128)(2,1)S(1)} %maximum_select_fusion.4.refs_0_), channel_id=1, source_target_pairs={{0,8},{4,12},{8,0},{12,4},{16,24},{20,28},{24,16},{28,20},{1,9},{5... | collective-permute-start | bytes 393224 | tf_op jit(solution)/shard_map/ppermute | solution.py:292
  26.0 1.5 %collective-permute-start.7 = (bf16[512,128]{1,0:T(8,128)(2,1)S(1)}, bf16[512,128]{1,0:T(8,128)(2,1)S(1)}, u32[]{:S(2)}, u32[]{:S(2)}) collective-permute-start(bf16[512,128]{1,0:T(8,128)(2,1)S(1)} %maximum_select_fusion.4.refs_0_), channel_id=1, source_target_pairs={{0,16},{4,20},{8,24},{12,28},{16,0},{20,4},{24,8},{28,12},{1,17},{... | collective-permute-start | bytes 393224 | tf_op jit(solution)/shard_map/ppermute | solution.py:292
  27.5 0.5 collective-permute-start.8
  28.0 2.2 %shard_map.58 = (bf16[256,2048]{1,0:T(8,128)(2,1)S(1)}, bf16[256,2048]{1,0:T(8,128)(2,1)S(1)}, bf16[256,2048]{1,0:T(8,128)(2,1)S(1)}, bf16[256,2048]{1,0:T(8,128)(2,1)S(1)}) custom-call(bf16[4,256,2048]{2,1,0:T(8,128)(2,1)} %refs_0_.5, bf16[4,256,2048]{2,1,0:T(8,128)(2,1)} %collective-permute-done.refs_1_, bf16[6,256,2048]{2,1,0:T(8,128)(2,1)} %refs_2_.3, ...), custom_call_target="tpu_custom_call" | custom-call | flops 1024 | bytes 1024 | tf_op jit(solution)/shard_map/pallas_call | solution.py:159
  30.2 1.5 %collective-permute-done.12.arrived_ref = bf16[2,256,256]{2,1,0:T(8,128)(2,1)S(1)} collective-permute-done((bf16[2,256,256]{2,1,0:T(8,128)(2,1)}, bf16[2,256,256]{2,1,0:T(8,128)(2,1)S(1)}, u32[]{:S(2)}, u32[]{:S(2)}) %collective-permute-start.12) | collective-permute-done | bytes 262176 | tf_op jit(solution)/shard_map/ppermute | solution.py:365
  31.7 2.1 %collective-permute-start.13 = (bf16[1,256,256]{2,1,0:T(8,128)(2,1)S(1)}, bf16[1,256,256]{2,1,0:T(8,128)(2,1)S(1)}, u32[]{:S(2)}, u32[]{:S(2)}) collective-permute-start(bf16[1,256,256]{2,1,0:T(8,128)(2,1)S(1)} %get-tuple-element.117), channel_id=1, source_target_pairs={{0,2},{1,3},{2,0},{3,1},{4,6},{5,7},{6,4},{7,5},{8,10},{9,11},{10,... | collective-permute-start | bytes 393224 | tf_op jit(solution)/shard_map/ppermute | solution.py:365
  33.8 0.3 collective-permute-done.7.refs_2_
  34.1 0.7 shard_map.59
  34.8 1.2 %collective-permute-start.21 = (bf16[2,256,256]{2,1,0:T(8,128)(2,1)S(1)}, bf16[2,256,256]{2,1,0:T(8,128)(2,1)S(1)}, u32[]{:S(2)}, u32[]{:S(2)}) collective-permute-start(bf16[2,256,256]{2,1,0:T(8,128)(2,1)S(1)} %copy-done.5), channel_id=1, source_target_pairs={{0,1},{1,0},{2,3},{3,2},{4,5},{5,4},{6,7},{7,6},{8,9},{9,8},{10,11... | collective-permute-start | bytes 786440 | tf_op jit(solution)/shard_map/ppermute | solution.py:365
  36.0 1.2 %collective-permute-start.9 = (bf16[512,128]{1,0:T(8,128)(2,1)S(1)}, bf16[512,128]{1,0:T(8,128)(2,1)S(1)}, u32[]{:S(2)}, u32[]{:S(2)}) collective-permute-start(bf16[512,128]{1,0:T(8,128)(2,1)S(1)} %get-tuple-element.111.refs_0_), channel_id=1, source_target_pairs={{0,8},{4,12},{8,0},{12,4},{16,24},{20,28},{24,16},{28,20},{1,9},{5... | collective-permute-start | bytes 393224 | tf_op jit(solution)/shard_map/ppermute | solution.py:292
  37.3 0.8 collective-permute-start.10
  38.1 1.4 %collective-permute-start.11 = (bf16[512,128]{1,0:T(8,128)(2,1)S(1)}, bf16[512,128]{1,0:T(8,128)(2,1)S(1)}, u32[]{:S(2)}, u32[]{:S(2)}) collective-permute-start(bf16[512,128]{1,0:T(8,128)(2,1)S(1)} %get-tuple-element.111.refs_0_), channel_id=1, source_target_pairs={{0,24},{4,28},{8,16},{12,20},{16,8},{20,12},{24,0},{28,4},{1,25},{... | collective-permute-start | bytes 393224 | tf_op jit(solution)/shard_map/ppermute | solution.py:292
  39.5 1.1 %collective-permute-done.13.refs_0_ = bf16[1,256,256]{2,1,0:T(8,128)(2,1)S(1)} collective-permute-done((bf16[1,256,256]{2,1,0:T(8,128)(2,1)S(1)}, bf16[1,256,256]{2,1,0:T(8,128)(2,1)S(1)}, u32[]{:S(2)}, u32[]{:S(2)}) %collective-permute-start.13) | collective-permute-done | bytes 131104 | tf_op jit(solution)/shard_map/ppermute | solution.py:365
  40.8 1.4 %collective-permute-done.9.refs_1_ = bf16[512,128]{1,0:T(8,128)(2,1)S(1)} collective-permute-done((bf16[512,128]{1,0:T(8,128)(2,1)S(1)}, bf16[512,128]{1,0:T(8,128)(2,1)S(1)}, u32[]{:S(2)}, u32[]{:S(2)}) %collective-permute-start.9) | collective-permute-done | bytes 131104 | tf_op jit(solution)/shard_map/ppermute | solution.py:292
  42.2 2.4 %collective-permute-done.10.refs_2_ = bf16[512,128]{1,0:T(8,128)(2,1)S(1)} collective-permute-done((bf16[512,128]{1,0:T(8,128)(2,1)S(1)}, bf16[512,128]{1,0:T(8,128)(2,1)S(1)}, u32[]{:S(2)}, u32[]{:S(2)}) %collective-permute-start.10) | collective-permute-done | bytes 131104 | tf_op jit(solution)/shard_map/ppermute | solution.py:292
  44.6 0.7 shard_map.62.refs_0_
  45.3 1.1 %collective-permute-start.15 = (bf16[512,128]{1,0:T(8,128)(2,1)S(1)}, bf16[512,128]{1,0:T(8,128)(2,1)S(1)}, u32[]{:S(2)}, u32[]{:S(2)}) collective-permute-start(bf16[512,128]{1,0:T(8,128)(2,1)S(1)} %shard_map.62.refs_0_), channel_id=1, source_target_pairs={{0,8},{4,12},{8,0},{12,4},{16,24},{20,28},{24,16},{28,20},{1,9},{5... | collective-permute-start | bytes 393224 | tf_op jit(solution)/shard_map/ppermute | solution.py:292
  46.4 0.7 collective-permute-start.16
  47.2 1.7 %collective-permute-start.17 = (bf16[512,128]{1,0:T(8,128)(2,1)S(1)}, bf16[512,128]{1,0:T(8,128)(2,1)S(1)}, u32[]{:S(2)}, u32[]{:S(2)}) collective-permute-start(bf16[512,128]{1,0:T(8,128)(2,1)S(1)} %shard_map.62.refs_0_), channel_id=1, source_target_pairs={{0,24},{4,28},{8,16},{12,20},{16,8},{20,12},{24,0},{28,4},{1,25},{... | collective-permute-start | bytes 393224 | tf_op jit(solution)/shard_map/ppermute | solution.py:292
  48.8 2.2 %shard_map.63 = (bf16[256,2048]{1,0:T(8,128)(2,1)S(1)}, bf16[256,2048]{1,0:T(8,128)(2,1)S(1)}, bf16[256,2048]{1,0:T(8,128)(2,1)S(1)}, bf16[256,2048]{1,0:T(8,128)(2,1)S(1)}) custom-call(bf16[4,256,2048]{2,1,0:T(8,128)(2,1)} %refs_0_.5, bf16[4,256,2048]{2,1,0:T(8,128)(2,1)} %collective-permute-done.refs_1_, bf16[6,256,2048]{2,1,0:T(8,128)(2,1)} %refs_2_.3, ...), custom_call_target="tpu_custom_call" | custom-call | flops 1024 | bytes 1024 | tf_op jit(solution)/shard_map/pallas_call | solution.py:159
  51.1 1.9 %collective-permute-start.22 = (bf16[1,256,256]{2,1,0:T(8,128)(2,1)S(1)}, bf16[1,256,256]{2,1,0:T(8,128)(2,1)S(1)}, u32[]{:S(2)}, u32[]{:S(2)}) collective-permute-start(bf16[1,256,256]{2,1,0:T(8,128)(2,1)S(1)} %get-tuple-element.133), channel_id=1, source_target_pairs={{0,2},{1,3},{2,0},{3,1},{4,6},{5,7},{6,4},{7,5},{8,10},{9,11},{10,... | collective-permute-start | bytes 393224 | tf_op jit(solution)/shard_map/ppermute | solution.py:365
  53.0 0.5 collective-permute-done.16.refs_2_
  53.5 0.7 shard_map.64
  54.2 1.0 %collective-permute-start.18 = (bf16[512,128]{1,0:T(8,128)(2,1)S(1)}, bf16[512,128]{1,0:T(8,128)(2,1)S(1)}, u32[]{:S(2)}, u32[]{:S(2)}) collective-permute-start(bf16[512,128]{1,0:T(8,128)(2,1)S(1)} %get-tuple-element.126.refs_0_), channel_id=1, source_target_pairs={{0,8},{4,12},{8,0},{12,4},{16,24},{20,28},{24,16},{28,20},{1,9},{5... | collective-permute-start | bytes 393224 | tf_op jit(solution)/shard_map/ppermute | solution.py:292
  55.2 0.9 collective-permute-start.19
  56.1 1.7 %collective-permute-start.20 = (bf16[512,128]{1,0:T(8,128)(2,1)S(1)}, bf16[512,128]{1,0:T(8,128)(2,1)S(1)}, u32[]{:S(2)}, u32[]{:S(2)}) collective-permute-start(bf16[512,128]{1,0:T(8,128)(2,1)S(1)} %get-tuple-element.126.refs_0_), channel_id=1, source_target_pairs={{0,24},{4,28},{8,16},{12,20},{16,8},{20,12},{24,0},{28,4},{1,25},{... | collective-permute-start | bytes 393224 | tf_op jit(solution)/shard_map/ppermute | solution.py:292
  57.8 0.7 collective-permute-done.22.refs_0_
  58.6 1.6 %shard_map.67 = (bf16[256,2048]{1,0:T(8,128)(2,1)S(1)}, bf16[256,2048]{1,0:T(8,128)(2,1)S(1)}) custom-call(bf16[6,256,2048]{2,1,0:T(8,128)(2,1)} %refs_2_.3, bf16[6,256,2048]{2,1,0:T(8,128)(2,1)} %collective-permute-done.5.refs_3_.refs_1_), custom_call_target="tpu_custom_call" | custom-call | flops 1024 | bytes 1024 | tf_op jit(solution)/shard_map/pallas_call | solution.py:159
  60.2 0.7 shard_map.68
  60.9 1.0 %collective-permute-done.20.refs_3_ = bf16[512,128]{1,0:T(8,128)(2,1)S(1)} collective-permute-done((bf16[512,128]{1,0:T(8,128)(2,1)S(1)}, bf16[512,128]{1,0:T(8,128)(2,1)S(1)}, u32[]{:S(2)}, u32[]{:S(2)}) %collective-permute-start.20) | collective-permute-done | bytes 131104 | tf_op jit(solution)/shard_map/ppermute | solution.py:292
  61.9 0.7 shard_map.69.refs_0_
  62.7 1.5 %collective-permute-start.30 = (bf16[2,256,256]{2,1,0:T(8,128)(2,1)S(1)}, bf16[2,256,256]{2,1,0:T(8,128)(2,1)S(1)}, u32[]{:S(2)}, u32[]{:S(2)}) collective-permute-start(bf16[2,256,256]{2,1,0:T(8,128)(2,1)S(1)} %copy-done.4), channel_id=1, source_target_pairs={{0,1},{1,0},{2,3},{3,2},{4,5},{5,4},{6,7},{7,6},{8,9},{9,8},{10,11... | collective-permute-start | bytes 786440 | tf_op jit(solution)/shard_map/ppermute | solution.py:365
  64.2 0.5 collective-permute-start.24
  64.7 0.8 collective-permute-start.25
  65.5 2.1 %collective-permute-start.26 = (bf16[512,128]{1,0:T(8,128)(2,1)S(1)}, bf16[512,128]{1,0:T(8,128)(2,1)S(1)}, u32[]{:S(2)}, u32[]{:S(2)}) collective-permute-start(bf16[512,128]{1,0:T(8,128)(2,1)S(1)} %shard_map.69.refs_0_), channel_id=1, source_target_pairs={{0,24},{4,28},{8,16},{12,20},{16,8},{20,12},{24,0},{28,4},{1,25},{... | collective-permute-start | bytes 393224 | tf_op jit(solution)/shard_map/ppermute | solution.py:292
  67.7 2.2 %shard_map.70 = (bf16[256,2048]{1,0:T(8,128)(2,1)S(1)}, bf16[256,2048]{1,0:T(8,128)(2,1)S(1)}, bf16[256,2048]{1,0:T(8,128)(2,1)S(1)}, bf16[256,2048]{1,0:T(8,128)(2,1)S(1)}) custom-call(bf16[4,256,2048]{2,1,0:T(8,128)(2,1)} %refs_0_.5, bf16[4,256,2048]{2,1,0:T(8,128)(2,1)} %collective-permute-done.refs_1_, bf16[6,256,2048]{2,1,0:T(8,128)(2,1)} %refs_2_.3, ...), custom_call_target="tpu_custom_call" | custom-call | flops 1024 | bytes 1024 | tf_op jit(solution)/shard_map/pallas_call | solution.py:159
  69.9 0.6 collective-permute-done.30.arrived_ref
  70.5 1.0 %collective-permute-start.31 = (bf16[1,256,256]{2,1,0:T(8,128)(2,1)S(1)}, bf16[1,256,256]{2,1,0:T(8,128)(2,1)S(1)}, u32[]{:S(2)}, u32[]{:S(2)}) collective-permute-start(bf16[1,256,256]{2,1,0:T(8,128)(2,1)S(1)} %get-tuple-element.154), channel_id=1, source_target_pairs={{0,2},{1,3},{2,0},{3,1},{4,6},{5,7},{6,4},{7,5},{8,10},{9,11},{10,... | collective-permute-start | bytes 393224 | tf_op jit(solution)/shard_map/ppermute | solution.py:365
  71.7 0.7 shard_map.71
  72.4 1.6 %collective-permute-start.27 = (bf16[512,128]{1,0:T(8,128)(2,1)S(1)}, bf16[512,128]{1,0:T(8,128)(2,1)S(1)}, u32[]{:S(2)}, u32[]{:S(2)}) collective-permute-start(bf16[512,128]{1,0:T(8,128)(2,1)S(1)} %get-tuple-element.147.refs_0_), channel_id=1, source_target_pairs={{0,8},{4,12},{8,0},{12,4},{16,24},{20,28},{24,16},{28,20},{1,9},{5... | collective-permute-start | bytes 393224 | tf_op jit(solution)/shard_map/ppermute | solution.py:292
  74.0 0.9 collective-permute-start.28
  74.9 1.1 %collective-permute-start.29 = (bf16[512,128]{1,0:T(8,128)(2,1)S(1)}, bf16[512,128]{1,0:T(8,128)(2,1)S(1)}, u32[]{:S(2)}, u32[]{:S(2)}) collective-permute-start(bf16[512,128]{1,0:T(8,128)(2,1)S(1)} %get-tuple-element.147.refs_0_), channel_id=1, source_target_pairs={{0,24},{4,28},{8,16},{12,20},{16,8},{20,12},{24,0},{28,4},{1,25},{... | collective-permute-start | bytes 393224 | tf_op jit(solution)/shard_map/ppermute | solution.py:292
  76.0 1.6 %collective-permute-done.31.refs_0_ = bf16[1,256,256]{2,1,0:T(8,128)(2,1)S(1)} collective-permute-done((bf16[1,256,256]{2,1,0:T(8,128)(2,1)S(1)}, bf16[1,256,256]{2,1,0:T(8,128)(2,1)S(1)}, u32[]{:S(2)}, u32[]{:S(2)}) %collective-permute-start.31) | collective-permute-done | bytes 131104 | tf_op jit(solution)/shard_map/ppermute | solution.py:365
  77.7 2.2 %shard_map.74 = (bf16[256,2048]{1,0:T(8,128)(2,1)S(1)}, bf16[256,2048]{1,0:T(8,128)(2,1)S(1)}, bf16[256,2048]{1,0:T(8,128)(2,1)S(1)}, bf16[256,2048]{1,0:T(8,128)(2,1)S(1)}) custom-call(bf16[6,256,2048]{2,1,0:T(8,128)(2,1)} %refs_2_.3, bf16[6,256,2048]{2,1,0:T(8,128)(2,1)} %collective-permute-done.5.refs_3_.refs_1_, bf16[6,256,2048]{2,1,0:T(8,128)(2,1)} %refs_2_.3, ...), custom_call_target="tpu_custom_call" | custom-call | flops 1024 | bytes 1024 | tf_op jit(solution)/shard_map/pallas_call | solution.py:159
  79.9 0.7 shard_map.75
  80.6 0.7 shard_map.76
  81.4 0.7 shard_map.77.refs_0_
  82.1 0.6 collective-permute-start.33
  82.8 1.2 %collective-permute-start.34 = (bf16[512,128]{1,0:T(8,128)(2,1)S(1)}, bf16[512,128]{1,0:T(8,128)(2,1)S(1)}, u32[]{:S(2)}, u32[]{:S(2)}) collective-permute-start(bf16[512,128]{1,0:T(8,128)(2,1)S(1)} %shard_map.77.refs_0_), channel_id=1, source_target_pairs={{0,8},{4,12},{8,0},{12,4},{16,24},{20,28},{24,16},{28,20},{1,9},{5... | collective-permute-start | bytes 393224 | tf_op jit(solution)/shard_map/ppermute | solution.py:292
  83.9 0.9 collective-permute-start.35
  84.8 3.3 %collective-permute-start.36 = (bf16[512,128]{1,0:T(8,128)(2,1)S(1)}, bf16[512,128]{1,0:T(8,128)(2,1)S(1)}, u32[]{:S(2)}, u32[]{:S(2)}) collective-permute-start(bf16[512,128]{1,0:T(8,128)(2,1)S(1)} %shard_map.77.refs_0_), channel_id=1, source_target_pairs={{0,24},{4,28},{8,16},{12,20},{1,25},{5,29},{9,17},{13,21},{2,26},{... | collective-permute-start | bytes 393224 | tf_op jit(solution)/shard_map/ppermute | solution.py:292
  88.2 1.6 %shard_map.78 = (bf16[256,2048]{1,0:T(8,128)(2,1)S(1)}, bf16[256,2048]{1,0:T(8,128)(2,1)S(1)}) custom-call(bf16[4,256,2048]{2,1,0:T(8,128)(2,1)} %refs_0_.5, bf16[4,256,2048]{2,1,0:T(8,128)(2,1)} %collective-permute-done.refs_1_), custom_call_target="tpu_custom_call" | custom-call | flops 1024 | bytes 1024 | tf_op jit(solution)/shard_map/pallas_call | solution.py:159
  89.9 1.1 %maximum_maximum_fusion = f32[4,256,256]{2,1,0:T(8,128)} fusion(f32[1,256,256]{2,1,0:T(8,128)S(1)} %maximum_select_fusion.2, f32[1,256,256]{2,1,0:T(8,128)S(1)} %get-tuple-element.185, f32[1,256,256]{2,1,0:T(8,128)S(1)} %get-tuple-element.184, f32[4]{0:T(128)S(1)} %pad.7.clone), kind=kLoop, calls=%fused_computation | loop fusion | flops 786432 | bytes 1835024 | tf_op jit(solution)/shard_map/stack | solution.py:404
  91.0 0.4 shard_map.79
  91.5 0.4 shard_map.80
  91.9 0.9 collective-permute-done.37
  92.8 0.7 fusion
  (58 shorter events, 1.3 us)
Async XLA Ops:
  0.0 28.0 %collective-permute-start.5 = (bf16[6,256,2048]{2,1,0:T(8,128)(2,1)}, bf16[6,256,2048]{2,1,0:T(8,128)(2,1)}, u32[]{:S(2)}, u32[]{:S(2)}) collective-permute-start(bf16[6,256,2048]{2,1,0:T(8,128)(2,1)} %refs_2_.3), channel_id=1, source_target_pairs={{0,4},{4,0},{8,12},{12,8},{16,20},{20,16},{24,28},{28,24},{1,5},{5... | collective-permute-start | bytes 18874376 | tf_op jit(solution)/shard_map/ppermute | solution.py:283
  0.5 22.0 %collective-permute-start = (bf16[4,256,2048]{2,1,0:T(8,128)(2,1)}, bf16[4,256,2048]{2,1,0:T(8,128)(2,1)}, u32[]{:S(2)}, u32[]{:S(2)}) collective-permute-start(bf16[4,256,2048]{2,1,0:T(8,128)(2,1)} %refs_0_.5), channel_id=1, source_target_pairs={{0,4},{4,0},{8,12},{12,8},{16,20},{20,16},{24,28},{28,24},{1,5},{5... | collective-permute-start | bytes 12582920 | tf_op jit(solution)/shard_map/ppermute | solution.py:283
  5.3 17.2 %collective-permute-start.1 = (bf16[256,256]{1,0:T(8,128)(2,1)S(1)}, bf16[256,256]{1,0:T(8,128)(2,1)S(1)}, u32[]{:S(2)}, u32[]{:S(2)}) collective-permute-start(bf16[256,256]{1,0:T(8,128)(2,1)S(1)} %get-tuple-element.99), channel_id=1, source_target_pairs={{0,1},{1,2},{2,3},{3,0},{4,5},{5,6},{6,7},{7,4},{8,9},{9,10},{10,1... | collective-permute-start | bytes 393224 | tf_op jit(solution)/shard_map/ppermute | solution.py:322
  8.3 14.2 %copy-start = (f32[4,256,256]{2,1,0:T(8,128)S(1)}, f32[4,256,256]{2,1,0:T(8,128)}, u32[]{:S(2)}) copy-start(f32[4,256,256]{2,1,0:T(8,128)} %rhs_ref.7) | copy-start | bytes 3145732
  8.3 14.2 %collective-permute-start.2 = (bf16[256,256]{1,0:T(8,128)(2,1)S(1)}, bf16[256,256]{1,0:T(8,128)(2,1)S(1)}, u32[]{:S(2)}, u32[]{:S(2)}) collective-permute-start(bf16[256,256]{1,0:T(8,128)(2,1)S(1)} %get-tuple-element.101), channel_id=1, source_target_pairs={{0,3},{1,0},{2,1},{3,2},{4,7},{5,4},{6,5},{7,6},{8,11},{9,8},{10,9... | collective-permute-start | bytes 393224 | tf_op jit(solution)/shard_map/ppermute | solution.py:322
  10.4 12.1 %collective-permute-start.3 = (bf16[256,256]{1,0:T(8,128)(2,1)S(1)}, bf16[256,256]{1,0:T(8,128)(2,1)S(1)}, u32[]{:S(2)}, u32[]{:S(2)}) collective-permute-start(bf16[256,256]{1,0:T(8,128)(2,1)S(1)} %get-tuple-element.102), channel_id=1, source_target_pairs={{0,2},{1,3},{2,0},{3,1},{4,6},{5,7},{6,4},{7,5},{8,10},{9,11},{10,... | collective-permute-start | bytes 393224 | tf_op jit(solution)/shard_map/ppermute | solution.py:322
  22.6 1.7 %collective-permute-start.4 = (bf16[256,128]{1,0:T(8,128)(2,1)S(1)}, bf16[256,128]{1,0:T(8,128)(2,1)S(1)}, u32[]{:S(2)}, u32[]{:S(2)}) collective-permute-start(bf16[256,128]{1,0:T(8,128)(2,1)S(1)} %get-tuple-element.104), channel_id=1, source_target_pairs={{0,4},{4,0},{8,12},{12,8},{16,20},{20,16},{24,28},{28,24},{1,5},{5... | collective-permute-start | bytes 196616 | tf_op jit(solution)/shard_map/ppermute | solution.py:283
  22.7 8.9 %collective-permute-start.12 = (bf16[2,256,256]{2,1,0:T(8,128)(2,1)}, bf16[2,256,256]{2,1,0:T(8,128)(2,1)S(1)}, u32[]{:S(2)}, u32[]{:S(2)}) collective-permute-start(bf16[2,256,256]{2,1,0:T(8,128)(2,1)} %get-tuple-element.114), channel_id=1, source_target_pairs={{0,1},{1,0},{2,3},{3,2},{4,5},{5,4},{6,7},{7,6},{8,9},{9,8},{10,11... | collective-permute-start | bytes 786440 | tf_op jit(solution)/shard_map/ppermute | solution.py:365
  24.4 7.3 %copy-start.3 = (f32[2,256,256]{2,1,0:T(8,128)S(1)}, f32[2,256,256]{2,1,0:T(8,128)}, u32[]{:S(2)}) copy-start(f32[2,256,256]{2,1,0:T(8,128)} %get-tuple-element.113.exact_ref) | copy-start | bytes 1572868
  24.4 10.4 %copy-start.5 = (bf16[2,256,256]{2,1,0:T(8,128)(2,1)S(1)}, bf16[2,256,256]{2,1,0:T(8,128)(2,1)}, u32[]{:S(2)}) copy-start(bf16[2,256,256]{2,1,0:T(8,128)(2,1)} %get-tuple-element.130) | copy-start | bytes 786436
  24.4 9.3 %collective-permute-start.6 = (bf16[512,128]{1,0:T(8,128)(2,1)S(1)}, bf16[512,128]{1,0:T(8,128)(2,1)S(1)}, u32[]{:S(2)}, u32[]{:S(2)}) collective-permute-start(bf16[512,128]{1,0:T(8,128)(2,1)S(1)} %maximum_select_fusion.4.refs_0_), channel_id=1, source_target_pairs={{0,8},{4,12},{8,0},{12,4},{16,24},{20,28},{24,16},{28,20},{1,9},{5... | collective-permute-start | bytes 393224 | tf_op jit(solution)/shard_map/ppermute | solution.py:292
  26.0 8.1 %collective-permute-start.7 = (bf16[512,128]{1,0:T(8,128)(2,1)S(1)}, bf16[512,128]{1,0:T(8,128)(2,1)S(1)}, u32[]{:S(2)}, u32[]{:S(2)}) collective-permute-start(bf16[512,128]{1,0:T(8,128)(2,1)S(1)} %maximum_select_fusion.4.refs_0_), channel_id=1, source_target_pairs={{0,16},{4,20},{8,24},{12,28},{16,0},{20,4},{24,8},{28,12},{1,17},{... | collective-permute-start | bytes 393224 | tf_op jit(solution)/shard_map/ppermute | solution.py:292
  27.5 6.6 %collective-permute-start.8 = (bf16[512,128]{1,0:T(8,128)(2,1)S(1)}, bf16[512,128]{1,0:T(8,128)(2,1)S(1)}, u32[]{:S(2)}, u32[]{:S(2)}) collective-permute-start(bf16[512,128]{1,0:T(8,128)(2,1)S(1)} %maximum_select_fusion.4.refs_0_), channel_id=1, source_target_pairs={{0,24},{4,28},{8,16},{12,20},{16,8},{20,12},{24,0},{28,4},{1,25},{... | collective-permute-start | bytes 393224 | tf_op jit(solution)/shard_map/ppermute | solution.py:292
  31.7 8.9 %collective-permute-start.13 = (bf16[1,256,256]{2,1,0:T(8,128)(2,1)S(1)}, bf16[1,256,256]{2,1,0:T(8,128)(2,1)S(1)}, u32[]{:S(2)}, u32[]{:S(2)}) collective-permute-start(bf16[1,256,256]{2,1,0:T(8,128)(2,1)S(1)} %get-tuple-element.117), channel_id=1, source_target_pairs={{0,2},{1,3},{2,0},{3,1},{4,6},{5,7},{6,4},{7,5},{8,10},{9,11},{10,... | collective-permute-start | bytes 393224 | tf_op jit(solution)/shard_map/ppermute | solution.py:365
  34.8 16.3 %collective-permute-start.21 = (bf16[2,256,256]{2,1,0:T(8,128)(2,1)S(1)}, bf16[2,256,256]{2,1,0:T(8,128)(2,1)S(1)}, u32[]{:S(2)}, u32[]{:S(2)}) collective-permute-start(bf16[2,256,256]{2,1,0:T(8,128)(2,1)S(1)} %copy-done.5), channel_id=1, source_target_pairs={{0,1},{1,0},{2,3},{3,2},{4,5},{5,4},{6,7},{7,6},{8,9},{9,8},{10,11... | collective-permute-start | bytes 786440 | tf_op jit(solution)/shard_map/ppermute | solution.py:365
  36.0 6.2 %collective-permute-start.9 = (bf16[512,128]{1,0:T(8,128)(2,1)S(1)}, bf16[512,128]{1,0:T(8,128)(2,1)S(1)}, u32[]{:S(2)}, u32[]{:S(2)}) collective-permute-start(bf16[512,128]{1,0:T(8,128)(2,1)S(1)} %get-tuple-element.111.refs_0_), channel_id=1, source_target_pairs={{0,8},{4,12},{8,0},{12,4},{16,24},{20,28},{24,16},{28,20},{1,9},{5... | collective-permute-start | bytes 393224 | tf_op jit(solution)/shard_map/ppermute | solution.py:292
  37.3 7.3 %collective-permute-start.10 = (bf16[512,128]{1,0:T(8,128)(2,1)S(1)}, bf16[512,128]{1,0:T(8,128)(2,1)S(1)}, u32[]{:S(2)}, u32[]{:S(2)}) collective-permute-start(bf16[512,128]{1,0:T(8,128)(2,1)S(1)} %get-tuple-element.111.refs_0_), channel_id=1, source_target_pairs={{0,16},{4,20},{8,24},{12,28},{16,0},{20,4},{24,8},{28,12},{1,17},{... | collective-permute-start | bytes 393224 | tf_op jit(solution)/shard_map/ppermute | solution.py:292
  38.1 6.5 %collective-permute-start.11 = (bf16[512,128]{1,0:T(8,128)(2,1)S(1)}, bf16[512,128]{1,0:T(8,128)(2,1)S(1)}, u32[]{:S(2)}, u32[]{:S(2)}) collective-permute-start(bf16[512,128]{1,0:T(8,128)(2,1)S(1)} %get-tuple-element.111.refs_0_), channel_id=1, source_target_pairs={{0,24},{4,28},{8,16},{12,20},{16,8},{20,12},{24,0},{28,4},{1,25},{... | collective-permute-start | bytes 393224 | tf_op jit(solution)/shard_map/ppermute | solution.py:292
  40.7 3.9 %collective-permute-start.14 = (f32[256,128]{1,0:T(8,128)S(1)}, f32[256,128]{1,0:T(8,128)S(1)}, u32[]{:S(2)}, u32[]{:S(2)}) collective-permute-start(f32[256,128]{1,0:T(8,128)S(1)} %get-tuple-element.119), channel_id=1, source_target_pairs={{0,4},{4,0},{8,12},{12,8},{16,20},{20,16},{24,28},{28,24},{1,5},{5... | collective-permute-start | bytes 393224 | tf_op jit(solution)/shard_map/ppermute | solution.py:283
  45.3 5.8 %copy-start.2 = (f32[2,256,256]{2,1,0:T(8,128)S(1)}, f32[2,256,256]{2,1,0:T(8,128)}, u32[]{:S(2)}) copy-start(f32[2,256,256]{2,1,0:T(8,128)} %get-tuple-element.128.exact_ref) | copy-start | bytes 1572868
  45.3 7.7 %collective-permute-start.15 = (bf16[512,128]{1,0:T(8,128)(2,1)S(1)}, bf16[512,128]{1,0:T(8,128)(2,1)S(1)}, u32[]{:S(2)}, u32[]{:S(2)}) collective-permute-start(bf16[512,128]{1,0:T(8,128)(2,1)S(1)} %shard_map.62.refs_0_), channel_id=1, source_target_pairs={{0,8},{4,12},{8,0},{12,4},{16,24},{20,28},{24,16},{28,20},{1,9},{5... | collective-permute-start | bytes 393224 | tf_op jit(solution)/shard_map/ppermute | solution.py:292
  46.4 7.1 %collective-permute-start.16 = (bf16[512,128]{1,0:T(8,128)(2,1)S(1)}, bf16[512,128]{1,0:T(8,128)(2,1)S(1)}, u32[]{:S(2)}, u32[]{:S(2)}) collective-permute-start(bf16[512,128]{1,0:T(8,128)(2,1)S(1)} %shard_map.62.refs_0_), channel_id=1, source_target_pairs={{0,16},{4,20},{8,24},{12,28},{16,0},{20,4},{24,8},{28,12},{1,17},{... | collective-permute-start | bytes 393224 | tf_op jit(solution)/shard_map/ppermute | solution.py:292
  47.2 6.3 %collective-permute-start.17 = (bf16[512,128]{1,0:T(8,128)(2,1)S(1)}, bf16[512,128]{1,0:T(8,128)(2,1)S(1)}, u32[]{:S(2)}, u32[]{:S(2)}) collective-permute-start(bf16[512,128]{1,0:T(8,128)(2,1)S(1)} %shard_map.62.refs_0_), channel_id=1, source_target_pairs={{0,24},{4,28},{8,16},{12,20},{16,8},{20,12},{24,0},{28,4},{1,25},{... | collective-permute-start | bytes 393224 | tf_op jit(solution)/shard_map/ppermute | solution.py:292
  51.1 7.3 %collective-permute-start.22 = (bf16[1,256,256]{2,1,0:T(8,128)(2,1)S(1)}, bf16[1,256,256]{2,1,0:T(8,128)(2,1)S(1)}, u32[]{:S(2)}, u32[]{:S(2)}) collective-permute-start(bf16[1,256,256]{2,1,0:T(8,128)(2,1)S(1)} %get-tuple-element.133), channel_id=1, source_target_pairs={{0,2},{1,3},{2,0},{3,1},{4,6},{5,7},{6,4},{7,5},{8,10},{9,11},{10,... | collective-permute-start | bytes 393224 | tf_op jit(solution)/shard_map/ppermute | solution.py:365
  54.2 6.7 %collective-permute-start.18 = (bf16[512,128]{1,0:T(8,128)(2,1)S(1)}, bf16[512,128]{1,0:T(8,128)(2,1)S(1)}, u32[]{:S(2)}, u32[]{:S(2)}) collective-permute-start(bf16[512,128]{1,0:T(8,128)(2,1)S(1)} %get-tuple-element.126.refs_0_), channel_id=1, source_target_pairs={{0,8},{4,12},{8,0},{12,4},{16,24},{20,28},{24,16},{28,20},{1,9},{5... | collective-permute-start | bytes 393224 | tf_op jit(solution)/shard_map/ppermute | solution.py:292
  55.2 5.7 %collective-permute-start.19 = (bf16[512,128]{1,0:T(8,128)(2,1)S(1)}, bf16[512,128]{1,0:T(8,128)(2,1)S(1)}, u32[]{:S(2)}, u32[]{:S(2)}) collective-permute-start(bf16[512,128]{1,0:T(8,128)(2,1)S(1)} %get-tuple-element.126.refs_0_), channel_id=1, source_target_pairs={{0,16},{4,20},{8,24},{12,28},{16,0},{20,4},{24,8},{28,12},{1,17},{... | collective-permute-start | bytes 393224 | tf_op jit(solution)/shard_map/ppermute | solution.py:292
  56.1 5.9 %collective-permute-start.20 = (bf16[512,128]{1,0:T(8,128)(2,1)S(1)}, bf16[512,128]{1,0:T(8,128)(2,1)S(1)}, u32[]{:S(2)}, u32[]{:S(2)}) collective-permute-start(bf16[512,128]{1,0:T(8,128)(2,1)S(1)} %get-tuple-element.126.refs_0_), channel_id=1, source_target_pairs={{0,24},{4,28},{8,16},{12,20},{16,8},{20,12},{24,0},{28,4},{1,25},{... | collective-permute-start | bytes 393224 | tf_op jit(solution)/shard_map/ppermute | solution.py:292
  58.5 4.1 %copy-start.4 = (bf16[2,256,256]{2,1,0:T(8,128)(2,1)S(1)}, bf16[2,256,256]{2,1,0:T(8,128)(2,1)}, u32[]{:S(2)}) copy-start(bf16[2,256,256]{2,1,0:T(8,128)(2,1)} %get-tuple-element.151) | copy-start | bytes 786436
  58.5 3.4 %collective-permute-start.23 = (f32[256,128]{1,0:T(8,128)S(1)}, f32[256,128]{1,0:T(8,128)S(1)}, u32[]{:S(2)}, u32[]{:S(2)}) collective-permute-start(f32[256,128]{1,0:T(8,128)S(1)} %get-tuple-element.135), channel_id=1, source_target_pairs={{0,4},{4,0},{8,12},{12,8},{16,20},{20,16},{24,28},{28,24},{1,5},{5... | collective-permute-start | bytes 393224 | tf_op jit(solution)/shard_map/ppermute | solution.py:283
  62.7 7.8 %copy-start.1 = (f32[2,256,256]{2,1,0:T(8,128)S(1)}, f32[2,256,256]{2,1,0:T(8,128)}, u32[]{:S(2)}) copy-start(f32[2,256,256]{2,1,0:T(8,128)} %get-tuple-element.149.exact_ref) | copy-start | bytes 1572868
  62.7 7.8 %collective-permute-start.30 = (bf16[2,256,256]{2,1,0:T(8,128)(2,1)S(1)}, bf16[2,256,256]{2,1,0:T(8,128)(2,1)S(1)}, u32[]{:S(2)}, u32[]{:S(2)}) collective-permute-start(bf16[2,256,256]{2,1,0:T(8,128)(2,1)S(1)} %copy-done.4), channel_id=1, source_target_pairs={{0,1},{1,0},{2,3},{3,2},{4,5},{5,4},{6,7},{7,6},{8,9},{9,8},{10,11... | collective-permute-start | bytes 786440 | tf_op jit(solution)/shard_map/ppermute | solution.py:365
  64.2 7.3 %collective-permute-start.24 = (bf16[512,128]{1,0:T(8,128)(2,1)S(1)}, bf16[512,128]{1,0:T(8,128)(2,1)S(1)}, u32[]{:S(2)}, u32[]{:S(2)}) collective-permute-start(bf16[512,128]{1,0:T(8,128)(2,1)S(1)} %shard_map.69.refs_0_), channel_id=1, source_target_pairs={{0,8},{4,12},{8,0},{12,4},{16,24},{20,28},{24,16},{28,20},{1,9},{5... | collective-permute-start | bytes 393224 | tf_op jit(solution)/shard_map/ppermute | solution.py:292
  64.7 6.8 %collective-permute-start.25 = (bf16[512,128]{1,0:T(8,128)(2,1)S(1)}, bf16[512,128]{1,0:T(8,128)(2,1)S(1)}, u32[]{:S(2)}, u32[]{:S(2)}) collective-permute-start(bf16[512,128]{1,0:T(8,128)(2,1)S(1)} %shard_map.69.refs_0_), channel_id=1, source_target_pairs={{0,16},{4,20},{8,24},{12,28},{16,0},{20,4},{24,8},{28,12},{1,17},{... | collective-permute-start | bytes 393224 | tf_op jit(solution)/shard_map/ppermute | solution.py:292
  65.5 6.2 %collective-permute-start.26 = (bf16[512,128]{1,0:T(8,128)(2,1)S(1)}, bf16[512,128]{1,0:T(8,128)(2,1)S(1)}, u32[]{:S(2)}, u32[]{:S(2)}) collective-permute-start(bf16[512,128]{1,0:T(8,128)(2,1)S(1)} %shard_map.69.refs_0_), channel_id=1, source_target_pairs={{0,24},{4,28},{8,16},{12,20},{16,8},{20,12},{24,0},{28,4},{1,25},{... | collective-permute-start | bytes 393224 | tf_op jit(solution)/shard_map/ppermute | solution.py:292
  70.5 7.1 %collective-permute-start.31 = (bf16[1,256,256]{2,1,0:T(8,128)(2,1)S(1)}, bf16[1,256,256]{2,1,0:T(8,128)(2,1)S(1)}, u32[]{:S(2)}, u32[]{:S(2)}) collective-permute-start(bf16[1,256,256]{2,1,0:T(8,128)(2,1)S(1)} %get-tuple-element.154), channel_id=1, source_target_pairs={{0,2},{1,3},{2,0},{3,1},{4,6},{5,7},{6,4},{7,5},{8,10},{9,11},{10,... | collective-permute-start | bytes 393224 | tf_op jit(solution)/shard_map/ppermute | solution.py:365
  72.4 9.0 %collective-permute-start.27 = (bf16[512,128]{1,0:T(8,128)(2,1)S(1)}, bf16[512,128]{1,0:T(8,128)(2,1)S(1)}, u32[]{:S(2)}, u32[]{:S(2)}) collective-permute-start(bf16[512,128]{1,0:T(8,128)(2,1)S(1)} %get-tuple-element.147.refs_0_), channel_id=1, source_target_pairs={{0,8},{4,12},{8,0},{12,4},{16,24},{20,28},{24,16},{28,20},{1,9},{5... | collective-permute-start | bytes 393224 | tf_op jit(solution)/shard_map/ppermute | solution.py:292
  74.0 7.4 %collective-permute-start.28 = (bf16[512,128]{1,0:T(8,128)(2,1)S(1)}, bf16[512,128]{1,0:T(8,128)(2,1)S(1)}, u32[]{:S(2)}, u32[]{:S(2)}) collective-permute-start(bf16[512,128]{1,0:T(8,128)(2,1)S(1)} %get-tuple-element.147.refs_0_), channel_id=1, source_target_pairs={{0,16},{4,20},{8,24},{12,28},{16,0},{20,4},{24,8},{28,12},{1,17},{... | collective-permute-start | bytes 393224 | tf_op jit(solution)/shard_map/ppermute | solution.py:292
  74.9 6.5 %collective-permute-start.29 = (bf16[512,128]{1,0:T(8,128)(2,1)S(1)}, bf16[512,128]{1,0:T(8,128)(2,1)S(1)}, u32[]{:S(2)}, u32[]{:S(2)}) collective-permute-start(bf16[512,128]{1,0:T(8,128)(2,1)S(1)} %get-tuple-element.147.refs_0_), channel_id=1, source_target_pairs={{0,24},{4,28},{8,16},{12,20},{16,8},{20,12},{24,0},{28,4},{1,25},{... | collective-permute-start | bytes 393224 | tf_op jit(solution)/shard_map/ppermute | solution.py:292
  77.6 3.8 %collective-permute-start.32 = (f32[256,128]{1,0:T(8,128)S(1)}, f32[256,128]{1,0:T(8,128)S(1)}, u32[]{:S(2)}, u32[]{:S(2)}) collective-permute-start(f32[256,128]{1,0:T(8,128)S(1)} %get-tuple-element.156), channel_id=1, source_target_pairs={{0,4},{4,0},{8,12},{12,8},{16,20},{20,16},{24,28},{28,24},{1,5},{5... | collective-permute-start | bytes 393224 | tf_op jit(solution)/shard_map/ppermute | solution.py:283
  82.1 7.6 %collective-permute-start.33 = (f32[3,256,128]{2,1,0:T(8,128)S(1)}, f32[3,256,128]{2,1,0:T(8,128)S(1)}, u32[]{:S(2)}, u32[]{:S(2)}) collective-permute-start(f32[3,256,128]{2,1,0:T(8,128)S(1)} %pad_maximum_fusion), channel_id=1, source_target_pairs={{0,4},{4,0},{8,12},{12,8},{16,20},{20,16},{24,28},{28,24},{1,5},{5... | collective-permute-start | bytes 1179656 | tf_op jit(solution)/shard_map/ppermute | solution.py:283
  82.8 8.2 %collective-permute-start.34 = (bf16[512,128]{1,0:T(8,128)(2,1)S(1)}, bf16[512,128]{1,0:T(8,128)(2,1)S(1)}, u32[]{:S(2)}, u32[]{:S(2)}) collective-permute-start(bf16[512,128]{1,0:T(8,128)(2,1)S(1)} %shard_map.77.refs_0_), channel_id=1, source_target_pairs={{0,8},{4,12},{8,0},{12,4},{16,24},{20,28},{24,16},{28,20},{1,9},{5... | collective-permute-start | bytes 393224 | tf_op jit(solution)/shard_map/ppermute | solution.py:292
  83.9 7.1 %collective-permute-start.35 = (bf16[512,128]{1,0:T(8,128)(2,1)S(1)}, bf16[512,128]{1,0:T(8,128)(2,1)S(1)}, u32[]{:S(2)}, u32[]{:S(2)}) collective-permute-start(bf16[512,128]{1,0:T(8,128)(2,1)S(1)} %shard_map.77.refs_0_), channel_id=1, source_target_pairs={{0,16},{4,20},{8,24},{12,28},{16,0},{20,4},{24,8},{28,12},{1,17},{... | collective-permute-start | bytes 393224 | tf_op jit(solution)/shard_map/ppermute | solution.py:292
  84.8 6.1 %collective-permute-start.36 = (bf16[512,128]{1,0:T(8,128)(2,1)S(1)}, bf16[512,128]{1,0:T(8,128)(2,1)S(1)}, u32[]{:S(2)}, u32[]{:S(2)}) collective-permute-start(bf16[512,128]{1,0:T(8,128)(2,1)S(1)} %shard_map.77.refs_0_), channel_id=1, source_target_pairs={{0,24},{4,28},{8,16},{12,20},{1,25},{5,29},{9,17},{13,21},{2,26},{... | collective-permute-start | bytes 393224 | tf_op jit(solution)/shard_map/ppermute | solution.py:292
  91.4 1.4 %collective-permute-start.37 = (f32[256,128]{1,0:T(8,128)S(1)}, f32[256,128]{1,0:T(8,128)S(1)}, u32[]{:S(2)}, u32[]{:S(2)}) collective-permute-start(f32[256,128]{1,0:T(8,128)S(1)} %shard_map.79), channel_id=1, source_target_pairs={{0,4},{4,0},{8,12},{12,8},{16,20},{20,16},{24,28},{28,24},{1,5},{5... | collective-permute-start | bytes 393224 | tf_op jit(solution)/shard_map/ppermute | solution.py:283
